TPU v7x, 128 devices: a whole 4x4x4 slice. The times are simulated.
128 devices in a mesh: dp: 4 (over z), ctx: 4 (over y), tp: 8 (over x, core).
Axes of the slice: x: 4, y: 4, z: 4, core: 2. Of those that a mesh axis runs over, the one named last changes fastest.
Arguments:
- hidden_states: bfloat16 [4, 1024, 1536], P('dp', 'ctx'), may hold values from -32 to 32
- norm_gain: bfloat16 [1536], P(('dp', 'ctx')), may hold values from 0.5 to 1.5
- gate_weight: bfloat16 [1536, 3072], P(('dp', 'ctx'), 'tp'), may hold values from -0.15625 to 0.15625
- value_weight: bfloat16 [1536, 3072], P(('dp', 'ctx'), 'tp'), may hold values from -0.15625 to 0.15625
- state_proj: bfloat16 [1536, 256], P(('dp', 'ctx')), may hold values from -0.15625 to 0.15625
- step_proj: bfloat16 [1536, 48], P(('dp', 'ctx'), 'tp'), may hold values from -0.15625 to 0.15625
- value_filter: bfloat16 [4, 3072], P(None, 'tp'), may hold values from -3 to 3
- value_offset: bfloat16 [3072], P('tp'), may hold values from -0.5 to 0.5
- state_filter: bfloat16 [4, 256], replicated, may hold values from -3 to 3
- state_offset: bfloat16 [256], replicated, may hold values from -0.5 to 0.5
- step_bias: float32 [48], P('tp'), may hold values from -4 to -3
- decay_log: float32 [48], P('tp'), may hold values from -12 to 0
- skip_gain: float32 [48], P('tp'), may hold values from 0.5 to 1.5
- gate_norm_gain: bfloat16 [3072], P('tp'), may hold values from 0.5 to 1.5
- out_weight: bfloat16 [3072, 1536], P('tp', ('dp', 'ctx')), may hold values from -0.109375 to 0.109375
- out_grad: bfloat16 [4, 1024, 1536], P('dp', 'ctx'), may hold values from -6 to 6
Outputs:
- block_out: bfloat16 [4, 1024, 1536], P('dp', 'ctx')
- grad_hidden_states: float32 [4, 1024, 1536], P('dp', 'ctx')
- grad_norm_gain: float32 [1536], P(('dp', 'ctx'))
- grad_gate_weight: float32 [1536, 3072], P(('dp', 'ctx'), 'tp')
- grad_value_weight: float32 [1536, 3072], P(('dp', 'ctx'), 'tp')
- grad_state_proj: float32 [1536, 256], P(('dp', 'ctx'))
- grad_step_proj: float32 [1536, 48], P(('dp', 'ctx'), 'tp')
- grad_value_filter: float32 [4, 3072], P(None, 'tp')
- grad_value_offset: float32 [3072], P('tp')
- grad_state_filter: float32 [4, 256], replicated
- grad_state_offset: float32 [256], replicated
- grad_step_bias: float32 [48], P('tp')
- grad_decay_log: float32 [48], P('tp')
- grad_skip_gain: float32 [48], P('tp')
- grad_gate_norm_gain: float32 [3072], P('tp')
- grad_out_weight: float32 [3072, 1536], P('tp', ('dp', 'ctx'))
All inputs are finite; a program needn't handle non-finite values.
Results may differ from a plain program's by a relative error of at most 0.011.
Values may be sent and summed in bfloat16 or wider, within the bound.
No kernel may reach another device: no remote copies, remote signals or barrier semaphores. Data moves between devices by JAX's collectives and lax.ppermute only.
A program may use at most 64 MiB of HBM per device.

v0:
```python
import jax
import jax.numpy as jnp
from jax import lax
from jax.sharding import PartitionSpec as P

INNER = 3072
HEAD = 64
STATE = 128
KERNEL = 4
BLOCK = 256


EPSILON = 1e-05
PRECISE = lax.Precision.HIGHEST


def from_behind(value, axis, steps):
    count = lax.axis_size(axis)
    leading, last = (max(0, -steps), min(count, count - steps))
    return lax.ppermute(value, axis, [(source, source + steps) for source in range(leading, last)])


def entering_2(value, axis, join, neutral, backward):
    count, mine = (lax.axis_size(axis), lax.axis_index(axis))
    pieces = jax.tree.map(lambda part: lax.all_gather(part, axis), value)
    if backward:
        pieces = jax.tree.map(lambda part: part[::-1], pieces)
        mine = count - 1 - mine
    running = jax.tree.map(
        lambda part, zero: jnp.full_like(part, 0) + jnp.asarray(zero, part.dtype), value, neutral
    )

    def turn(position, running):
        longer = join(running, jax.tree.map(lambda part: part[position], pieces))
        return jax.tree.map(lambda new, old: jnp.where(position < mine, new, old), longer, running)

    return lax.fori_loop(0, count - 1, turn, running)


def contract_rows(former, latter):
    return lax.dot_general(
        former, latter, (((0,), (0,)), ((), ())), preferred_element_type=jnp.float32
    )


def contract_last(former, latter):
    return lax.dot_general(
        former, latter, (((1,), (1,)), ((), ())), preferred_element_type=jnp.float32
    )


def block_local(values, bmatrix, cmatrix, step_size, decay_rates):
    length = step_size.shape[1]
    log_decay = jnp.cumsum(-step_size * decay_rates[None, None, :], axis=1)
    row_index = lax.broadcasted_iota(jnp.int32, (length, length), 0)
    col_index = lax.broadcasted_iota(jnp.int32, (length, length), 1)
    causal = (row_index >= col_index)[None, :, :, None]
    spread = log_decay[:, :, None, :] - log_decay[:, None, :, :]
    decay_mask = jnp.where(causal, jnp.exp(jnp.where(causal, spread, 0.0)), 0.0)
    scores = jnp.einsum("ctn,csn->cts", cmatrix, bmatrix, precision=PRECISE)
    weighted = values * step_size[:, :, :, None]
    within = jnp.einsum(
        "ctsh,cshp->cthp", scores[:, :, :, None] * decay_mask, weighted, precision=PRECISE
    )
    to_end = jnp.exp(log_decay[:, -1:, :] - log_decay)
    local_states = jnp.einsum(
        "cshp,csn->chpn", weighted * to_end[:, :, :, None], bmatrix, precision=PRECISE
    )
    return (log_decay, within, local_states)


def filter_apply(padded, filters, biases):
    length = padded.shape[0] - filters.shape[0] + 1
    summed = biases[None, :] + jnp.zeros((length, filters.shape[1]), jnp.float32)
    for offset in range(filters.shape[0]):
        summed = summed + filters[offset][None, :] * padded[offset : offset + length]
    return jax.nn.silu(summed)


def chain_blocks(start_state, block_decay, local_states):

    def carry_step(current, pieces):
        decay_now, local_now = pieces
        return (current * decay_now[:, None, None] + local_now, current)

    return lax.scan(carry_step, start_state, (block_decay, local_states))


def mixer_parts(activated, step_pre, step_bias, decay_log):
    length = activated.shape[0]
    heads_local = step_pre.shape[1]
    inner_local = heads_local * HEAD
    blocks = length // BLOCK
    values = activated[:, :inner_local].reshape(blocks, BLOCK, heads_local, HEAD)
    bmatrix = activated[:, inner_local : inner_local + STATE].reshape(blocks, BLOCK, STATE)
    cmatrix = activated[:, inner_local + STATE :].reshape(blocks, BLOCK, STATE)
    step_size = jax.nn.softplus(step_pre + step_bias[None, :]).reshape(blocks, BLOCK, heads_local)
    log_decay, within, local_states = block_local(
        values, bmatrix, cmatrix, step_size, jnp.exp(decay_log)
    )
    return (values, cmatrix, log_decay, within, local_states)


def mixer_finish(parts, skip_gain, start_state):
    values, cmatrix, log_decay, within, local_states = parts
    end_state, entering = chain_blocks(start_state, jnp.exp(log_decay[:, -1, :]), local_states)
    across = (
        jnp.einsum("ctn,chpn->cthp", cmatrix, entering, precision=PRECISE)
        * jnp.exp(log_decay)[:, :, :, None]
    )
    output = within + across + values * skip_gain[None, None, :, None]
    return (output.reshape(values.shape[0] * values.shape[1], -1), end_state)


def mixer_whole(activated, step_pre, step_bias, decay_log, skip_gain, start_state):
    return mixer_finish(
        mixer_parts(activated, step_pre, step_bias, decay_log), skip_gain, start_state
    )


def entry_sensitivity(parts, grad_mixed):
    values, cmatrix, log_decay, within, local_states = parts
    blocks, length, heads_local, head_size = values.shape
    offsets = jnp.cumsum(log_decay[:, -1, :], axis=0) - log_decay[:, -1, :]
    factors = jnp.exp(log_decay + offsets[:, None, :])
    scaled = grad_mixed.reshape(blocks, length, heads_local, head_size) * factors[:, :, :, None]
    return jnp.einsum("cthp,ctn->hpn", scaled, cmatrix, precision=PRECISE)


def join_states(earlier, latter):
    return (earlier[0] * latter[0], latter[0][:, None, None] * earlier[1] + latter[1])


def per_device(
    hidden_states,
    norm_gain,
    gate_weight,
    value_weight,
    state_proj,
    step_proj,
    value_filter,
    value_offset,
    state_filter,
    state_offset,
    step_bias,
    decay_log,
    skip_gain,
    gate_norm_gain,
    out_weight,
    out_grad,
):
    tokens = hidden_states[0].astype(jnp.float32)
    inner_local = gate_weight.shape[1]
    heads_local = step_proj.shape[1]
    gathered = (
        lax.all_gather(norm_gain, ("dp", "ctx"), axis=0, tiled=True),
        lax.all_gather(gate_weight, ("dp", "ctx"), axis=0, tiled=True),
        lax.all_gather(value_weight, ("dp", "ctx"), axis=0, tiled=True),
        lax.all_gather(state_proj, ("dp", "ctx"), axis=0, tiled=True),
        lax.all_gather(step_proj, ("dp", "ctx"), axis=0, tiled=True),
        lax.all_gather(out_weight, ("dp", "ctx"), axis=1, tiled=True),
    )
    gain_full, gate_full, value_full, state_full, step_full, out_full = gathered
    inv_rms = lax.rsqrt(jnp.mean(tokens * tokens, axis=1, keepdims=True) + EPSILON)
    unit_rows = tokens * inv_rms
    hidden_in = (unit_rows * gain_full.astype(jnp.float32)[None, :]).astype(jnp.bfloat16)
    gate_pre = jnp.dot(hidden_in, gate_full, preferred_element_type=jnp.float32)
    value_pre = jnp.dot(hidden_in, value_full, preferred_element_type=jnp.float32)
    state_pre = jnp.dot(hidden_in, state_full, preferred_element_type=jnp.float32)
    step_pre = jnp.dot(hidden_in, step_full, preferred_element_type=jnp.float32)
    filter_input = jnp.concatenate([value_pre, state_pre], 1).astype(jnp.bfloat16)
    rim_rows = from_behind(filter_input[filter_input.shape[0] - (KERNEL - 1) :], "ctx", 1)
    padded = jnp.concatenate([rim_rows, filter_input], 0).astype(jnp.float32)
    filters = jnp.concatenate([value_filter, state_filter], 1).astype(jnp.float32)
    biases = jnp.concatenate([value_offset, state_offset], 0).astype(jnp.float32)
    activated, filter_pullback = jax.vjp(filter_apply, padded, filters, biases)
    parts = mixer_parts(activated, step_pre, step_bias, decay_log)
    block_decay = jnp.exp(parts[2][:, -1, :])
    zero_end = chain_blocks(
        jnp.zeros((heads_local, HEAD, STATE), jnp.float32), block_decay, parts[4]
    )[0]
    span_decay = jnp.exp(jnp.sum(parts[2][:, -1, :], axis=0))
    identity = (jnp.ones_like(span_decay), jnp.zeros_like(zero_end))
    start_state = entering_2((span_decay, zero_end), "ctx", join_states, identity, False)[1]
    mixed_heads = mixer_finish(parts, skip_gain, start_state)[0]
    gate_act = jax.nn.silu(gate_pre)
    gated = mixed_heads * gate_act
    square_sum = lax.psum(jnp.sum(gated * gated, axis=1), "tp")
    inv_gate = lax.rsqrt(square_sum / INNER + EPSILON)[:, None]
    gate_gain = gate_norm_gain.astype(jnp.float32)[None, :]
    normed_out = (gated * inv_gate * gate_gain).astype(jnp.bfloat16)
    branch = lax.psum(jnp.dot(normed_out, out_full, preferred_element_type=jnp.float32), "tp")
    block_out = (tokens + branch).astype(jnp.bfloat16)[None]
    grad_out = out_grad[0]
    grad_normed = contract_last(grad_out, out_full)
    grad_out_weight = contract_rows(normed_out, grad_out)
    grad_gate_gain = jnp.sum(grad_normed * gated * inv_gate, axis=0)
    scaled_grad = grad_normed * gate_gain
    cross_sum = lax.psum(jnp.sum(scaled_grad * gated, axis=1), "tp")[:, None]
    grad_gated = inv_gate * scaled_grad - gated * inv_gate * inv_gate * inv_gate * cross_sum / INNER
    grad_mixed = grad_gated * gate_act
    sigmoid_gate = jax.nn.sigmoid(gate_pre)
    grad_gate_pre = (
        grad_gated * mixed_heads * sigmoid_gate * (1.0 + gate_pre * (1.0 - sigmoid_gate))
    )
    sensitivity = entry_sensitivity(parts, grad_mixed)
    later_grad = entering_2((span_decay, sensitivity), "ctx", join_states, identity, True)[1]
    ignored, mixer_pullback = jax.vjp(
        mixer_whole, activated, step_pre, step_bias, decay_log, skip_gain, start_state
    )
    grad_activated, grad_step_pre, grad_step_bias, grad_decay_log, grad_skip_gain, unused = (
        mixer_pullback((grad_mixed, later_grad))
    )
    grad_padded, grad_filters, grad_biases = filter_pullback(grad_activated)
    rim_grad = from_behind(grad_padded[: KERNEL - 1], "ctx", -1)
    grad_input = grad_padded[KERNEL - 1 :]
    grad_input = jnp.concatenate(
        [
            grad_input[: grad_input.shape[0] - (KERNEL - 1)],
            grad_input[grad_input.shape[0] - (KERNEL - 1) :] + rim_grad,
        ],
        0,
    )
    state_sums = lax.psum(
        (grad_input[:, inner_local:], grad_filters[:, inner_local:], grad_biases[inner_local:]),
        "tp",
    )
    grad_state_input, grad_state_filter, grad_state_offset = state_sums
    low_gate = grad_gate_pre.astype(jnp.bfloat16)
    low_value = grad_input[:, :inner_local].astype(jnp.bfloat16)
    low_state = grad_state_input.astype(jnp.bfloat16)
    low_step = grad_step_pre.astype(jnp.bfloat16)
    head_part = (
        contract_last(low_gate, gate_full)
        + contract_last(low_value, value_full)
        + contract_last(low_step, step_full)
    )
    grad_hidden = lax.psum(head_part, "tp") + contract_last(low_state, state_full)
    gain_float = gain_full.astype(jnp.float32)
    grad_gain = jnp.sum(grad_hidden * unit_rows, axis=0)
    scaled_hidden = grad_hidden * gain_float[None, :]
    grad_tokens = inv_rms * (
        scaled_hidden - unit_rows * jnp.mean(scaled_hidden * unit_rows, axis=1, keepdims=True)
    )
    grad_hidden_states = (grad_out.astype(jnp.float32) + grad_tokens)[None]
    shares = (
        lax.psum_scatter(grad_gain, ("dp", "ctx"), scatter_dimension=0, tiled=True),
        lax.psum_scatter(
            contract_rows(hidden_in, low_gate), ("dp", "ctx"), scatter_dimension=0, tiled=True
        ),
        lax.psum_scatter(
            contract_rows(hidden_in, low_value), ("dp", "ctx"), scatter_dimension=0, tiled=True
        ),
        lax.psum_scatter(
            contract_rows(hidden_in, low_state), ("dp", "ctx"), scatter_dimension=0, tiled=True
        ),
        lax.psum_scatter(
            contract_rows(hidden_in, low_step), ("dp", "ctx"), scatter_dimension=0, tiled=True
        ),
        lax.psum_scatter(grad_out_weight, ("dp", "ctx"), scatter_dimension=1, tiled=True),
    )
    small_sums = lax.psum(
        (
            grad_filters[:, :inner_local],
            grad_biases[:inner_local],
            grad_state_filter,
            grad_state_offset,
            grad_step_bias,
            grad_decay_log,
            grad_skip_gain,
            grad_gate_gain,
        ),
        ("dp", "ctx"),
    )
    return (
        block_out,
        grad_hidden_states,
        shares[0],
        shares[1],
        shares[2],
        shares[3],
        shares[4],
        small_sums[0],
        small_sums[1],
        small_sums[2],
        small_sums[3],
        small_sums[4],
        small_sums[5],
        small_sums[6],
        small_sums[7],
        shares[5],
    )


def solution(mesh):
    placed = (
        P("dp", "ctx", None),
        P(("dp", "ctx")),
        P(("dp", "ctx"), "tp"),
        P(("dp", "ctx"), "tp"),
        P(("dp", "ctx"), None),
        P(("dp", "ctx"), "tp"),
        P(None, "tp"),
        P("tp"),
        P(),
        P(),
        P("tp"),
        P("tp"),
        P("tp"),
        P("tp"),
        P("tp", ("dp", "ctx")),
        P("dp", "ctx", None),
    )
    return jax.shard_map(
        per_device,
        mesh=mesh,
        in_specs=placed,
        out_specs=(
            P("dp", "ctx", None),
            P("dp", "ctx", None),
            P(("dp", "ctx")),
            P(("dp", "ctx"), "tp"),
            P(("dp", "ctx"), "tp"),
            P(("dp", "ctx"), None),
            P(("dp", "ctx"), "tp"),
            P(None, "tp"),
            P("tp"),
            P(),
            P(),
            P("tp"),
            P("tp"),
            P("tp"),
            P("tp"),
            P("tp", ("dp", "ctx")),
        ),
        check_vma=False,
    )
```

profile of v0, /device:TPU:1, one launch (start us, length us, event | category | flops | bytes accessed | tf_op | source)
XLA Modules:
  0.0 703.9 jit_solution(2146290373607235296)
XLA Ops:
  12.3 35.6 %all-reduce.13 = bf16[1536]{0:T(1024)(128)(2,1)S(1)} all-reduce(bf16[1536]{0:T(1024)(128)(2,1)S(1)} %dynamic-update-slice), channel_id=1, replica_groups=mesh['dp'=4,'ctx'=4,'tp'=8] {'dp','ctx'}, use_global_device_ids=true, to_apply=%add.13 | all-reduce | flops 1536 | bytes 6144
  49.4 16.5 %all-gather.3 = bf16[16,96,6]{1,2,0:T(8,128)(2,1)S(1)} all-gather(bf16[1,96,6]{1,2,0:T(8,128)(2,1)} %bitcast.285), channel_id=1, replica_groups=mesh['dp'=4,'ctx'=4,'tp'=8] {'dp','ctx'}, dimensions={0}, use_global_device_ids=true | all-gather | bytes 19584 | tf_op jit(solution)/shard_map/all_gather | solution.py:160
  70.6 18.6 %all_gather.36 = bf16[1536,256]{1,0:T(8,128)(2,1)S(1)} all-gather(bf16[96,256]{1,0:T(8,128)(2,1)S(1)} %copy-done.37), channel_id=1, replica_groups=mesh['dp'=4,'ctx'=4,'tp'=8] {'dp','ctx'}, dimensions={0}, use_global_device_ids=true | all-gather | bytes 835584 | tf_op jit(solution)/shard_map/all_gather | solution.py:159
  94.5 7.0 all-gather
  108.9 11.6 %all-gather.1 = f32[24,64,128]{2,1,0:T(8,128)S(1)} all-gather(f32[6,64,128]{2,1,0:T(8,128)S(1)} %convolution_add_fusion.3), channel_id=3, replica_groups=mesh['dp'=4,'ctx'=4,'tp'=8] {'ctx'}, dimensions={0}, use_global_device_ids=true | all-gather | bytes 983040 | tf_op jit(solution)/shard_map/all_gather | solution.py:25
  120.5 1.9 copy.197
  124.4 3.3 fusion.25
  128.6 3.0 multiply_reduce_fusion.10
  131.6 34.6 %psum.105 = f32[256]{0:T(256)S(1)} all-reduce(f32[256]{0:T(256)S(1)} %get-tuple-element.365), channel_id=1, replica_groups=mesh['dp'=4,'ctx'=4,'tp'=8] {'tp'}, use_global_device_ids=true, to_apply=%region_6.7 | all-reduce | flops 256 | bytes 2048 | tf_op jit(solution)/shard_map/psum | solution.py:188
  166.2 3.3 multiply_reduce_fusion.4
  169.5 12.4 %psum.107 = f32[256]{0:T(256)S(1)} all-reduce(f32[256]{0:T(256)S(1)} %get-tuple-element.318), channel_id=1, replica_groups=mesh['dp'=4,'ctx'=4,'tp'=8] {'tp'}, use_global_device_ids=true, to_apply=%region_9.10 | all-reduce | flops 256 | bytes 2048 | tf_op jit(solution)/shard_map/psum | solution.py:199
  181.9 3.0 multiply_reduce_fusion.5
  185.9 2.0 fusion.109
  189.5 11.3 %all-gather.2 = f32[24,64,128]{2,1,0:T(8,128)} all-gather(f32[6,64,128]{2,1,0:T(8,128)S(1)} %fusion.62), channel_id=4, replica_groups=mesh['dp'=4,'ctx'=4,'tp'=8] {'ctx'}, dimensions={0}, use_global_device_ids=true | all-gather | bytes 983040 | tf_op jit(solution)/shard_map/all_gather | solution.py:25
  206.3 4.0 fusion.29
  212.2 2.9 multiply_reduce_fusion.6
  229.3 7.6 %reduce-window.16 = f32[1,6,2,128]{3,2,1,0:T(2,128)S(1)} reduce-window(f32[1,6,2,128]{3,2,1,0:T(2,128)S(1)} %copy.228, f32[]{:T(128)} %constant.128.clone.1), window={size=1x1x1x128 pad=0_0x0_0x0_0x0_127}, to_apply=%region_20.21 | reduce-window | flops 195072 | bytes 12292 | tf_op jit(solution)/shard_map/reduce-window.2
  238.6 2.1 fusion.87
  241.0 3.3 fusion.92
  250.1 28.4 %all-reduce.22 = (bf16[256,256]{1,0:T(8,128)(2,1)S(1)}, f32[4,256]{1,0:T(4,128)S(1)}, f32[256]{0:T(256)S(1)}) all-reduce(f32[256,256]{1,0:T(8,128)S(1)} %pad_maximum_fusion, f32[4,256]{1,0:T(4,128)S(1)} %pad_add_fusion.3, f32[256]{0:T(256)S(1)} %slice.122), channel_id=1, replica_groups=mesh['dp'=4,'ctx'=4,'tp'=8] {'tp'}, use_global_device_ids=true, to_apply=%region_23.24 | all-reduce | flops 66816 | bytes 403456 | tf_op jit(solution)/shard_map/psum | solution.py:224
  280.4 2.1 fusion.31
  283.4 2.1 fusion.97
  286.2 2.1 fusion.95
  289.5 24.7 %reduce-scatter.16.cloned.1.call-done = f32[96,6]{1,0:T(8,128)} async-done(((f32[1536,6]{1,0:T(8,128)}), f32[96,6]{1,0:T(8,128)}) %reduce-scatter.16.cloned.1.call-update) | async-done | bytes 2320
  315.6 69.6 %all-reduce.21.cloned.1.call-done = (f32[256,1536]{1,0:T(8,128)}, f32[256,1536]{1,0:T(8,128)}) async-done(((f32[256,1536]{1,0:T(8,128)}, f32[256,1536]{1,0:T(8,128)}), (f32[256,1536]{1,0:T(8,128)}, f32[256,1536]{1,0:T(8,128)})) %all-reduce.21.cloned.1.call-update) | async-done | bytes 3145744 | tf_op jit(solution)/shard_map/psum | solution.py:192
  385.2 2.4 fusion.12
  387.6 60.4 %all-reduce.15 = (f32[1536]{0:T(1024)S(1)}, f32[4,384]{1,0:T(4,128)}, f32[384]{0:T(512)}, f32[4,256]{1,0:T(4,128)}, f32[256]{0:T(256)}, /*index=5*/f32[6]{0:T(128)}, f32[6]{0:T(128)}, f32[6]{0:T(128)}, f32[384]{0:T(512)}) all-reduce(f32[1536]{0:T(1024)S(1)} %get-tuple-element.308, ...), channel_id=5, replica_groups=mesh['dp'=4,'ctx'=4,'tp'=8] {'dp','ctx'}, use_global_device_ids=true, to_apply=%region_26.27.clone | all-reduce | flops 5138 | bytes 41104
  448.6 3.4 fusion.11
  451.9 10.8 %reduce-scatter.12.cloned.1.call-done = f32[96,256]{1,0:T(8,128)} async-done(((f32[1536,256]{1,0:T(8,128)}), f32[96,256]{1,0:T(8,128)}) %reduce-scatter.12.cloned.1.call-update) | async-done | bytes 98320 | tf_op jit(solution)/shard_map/reduce_scatter | solution.py:254
  462.7 78.2 %reduce-scatter.14.cloned.1.call-done = f32[384,96]{0,1:T(8,128)} async-done(((f32[384,1536]{0,1:T(8,128)}), f32[384,96]{0,1:T(8,128)}) %reduce-scatter.14.cloned.1.call-update) | async-done | bytes 147472 | tf_op jit(solution)/shard_map/reduce_scatter | solution.py:260
  541.0 78.2 %reduce-scatter.8.cloned.1.call-done = f32[96,384]{1,0:T(8,128)} async-done(((f32[1536,384]{1,0:T(8,128)}), f32[96,384]{1,0:T(8,128)}) %reduce-scatter.8.cloned.1.call-update) | async-done | bytes 147472 | tf_op jit(solution)/shard_map/reduce_scatter | solution.py:248
  619.1 78.2 %reduce-scatter.10.cloned.1.call-done = f32[96,384]{1,0:T(8,128)} async-done(((f32[1536,384]{1,0:T(8,128)}), f32[96,384]{1,0:T(8,128)}) %reduce-scatter.10.cloned.1.call-update) | async-done | bytes 147472 | tf_op jit(solution)/shard_map/reduce_scatter | solution.py:251
  (283 shorter events, 63.8 us)
Async XLA Ops:
  7.2 83.6 %all-gather.8.cloned.1.call-start = ((), (), s32[]{:S(2)}) async-start(), calls=%async_computation.5 | async-start | bytes 1253376 | tf_op jit(solution)/shard_map/all_gather | solution.py:158
  7.9 120.7 %all-gather.10.cloned.1.call-start = ((), (), s32[]{:S(2)}) async-start(), calls=%async_computation.6 | async-start | bytes 1253376 | tf_op jit(solution)/shard_map/all_gather | solution.py:157
  8.7 157.6 %all-gather.12.cloned.1.call-start = ((), (), s32[]{:S(2)}) async-start(), calls=%async_computation.7 | async-start | bytes 1253376 | tf_op jit(solution)/shard_map/all_gather | solution.py:161
  9.4 304.8 %reduce-scatter.16.cloned.1.call-start = ((), (), s32[]{:S(2)}) async-start(), calls=%async_computation.12 | async-start | bytes 835584
  10.8 59.8 %copy-start.37 = (bf16[96,256]{1,0:T(8,128)(2,1)S(1)}, bf16[96,256]{1,0:T(8,128)(2,1)}, u32[]{:S(2)}) copy-start(bf16[96,256]{1,0:T(8,128)(2,1)} %param.24) | copy-start | bytes 147460
  49.3 79.3 %copy-start.35 = (f32[256]{0:T(256)}, f32[256]{0:T(256)S(1)}, u32[]{:S(2)}) copy-start(f32[256]{0:T(256)S(1)} %add_rsqrt_fusion.1) | copy-start | bytes 3076
  49.4 40.8 %copy-start = (bf16[1,256,1536]{2,1,0:T(8,128)(2,1)S(1)}, bf16[1,256,1536]{2,1,0:T(8,128)(2,1)}, u32[]{:S(2)}) copy-start(bf16[1,256,1536]{2,1,0:T(8,128)(2,1)} %param.20) | copy-start | bytes 2359300
  70.5 31.5 %copy-start.8 = (f32[1,6,256]{1,2,0:T(8,128)}, f32[1,6,256]{1,2,0:T(8,128)S(1)}, u32[]{:S(2)}) copy-start(f32[1,6,256]{1,2,0:T(8,128)S(1)} %get-tuple-element.368) | copy-start | bytes 18436
  70.5 20.1 %copy-start.55 = (f32[6]{0:T(128)}, f32[6]{0:T(128)S(1)}, u32[]{:S(2)}) copy-start(f32[6]{0:T(128)S(1)} %get-tuple-element.387) | copy-start | bytes 76
  70.6 20.0 %copy-start.57 = (bf16[4,384]{1,0:T(4,128)(2,1)S(1)}, bf16[4,384]{1,0:T(4,128)(2,1)}, u32[]{:S(2)}) copy-start(bf16[4,384]{1,0:T(4,128)(2,1)} %param.26) | copy-start | bytes 9220
  70.6 20.0 %copy-start.60 = (bf16[4,256]{1,0:T(4,128)(2,1)S(1)}, bf16[4,256]{1,0:T(4,128)(2,1)}, u32[]{:S(2)}) copy-start(bf16[4,256]{1,0:T(4,128)(2,1)} %param.28) | copy-start | bytes 6148
  90.6 13.6 %copy-start.40 = (f32[640]{0:T(1024)}, f32[640]{0:T(1024)S(1)}, u32[]{:S(2)}) copy-start(f32[640]{0:T(1024)S(1)} %get-tuple-element.324) | copy-start | bytes 7684
  90.6 13.6 %copy-start.42 = (f32[640]{0:T(1024)}, f32[640]{0:T(1024)S(1)}, u32[]{:S(2)}) copy-start(f32[640]{0:T(1024)S(1)} %get-tuple-element.325) | copy-start | bytes 7684
  92.7 9.5 %copy-start.61 = (bf16[384]{0:T(512)(128)(2,1)S(1)}, bf16[384]{0:T(512)(128)(2,1)}, u32[]{:S(2)}) copy-start(bf16[384]{0:T(512)(128)(2,1)} %param.33) | copy-start | bytes 2308
  92.7 11.5 %collective-permute-start = (bf16[3,640]{1,0:T(4,128)(2,1)S(1)}, bf16[3,640]{1,0:T(4,128)(2,1)S(1)}, u32[]{:S(2)}, u32[]{:S(2)}) collective-permute-start(bf16[3,640]{1,0:T(4,128)(2,1)S(1)} %pad_maximum_fusion.1), channel_id=1, source_target_pairs={{0,8},{8,16},{16,24},{1,9},{9,17},{17,25},{2,10},{10,18},{18,26},{... | collective-permute-start | bytes 11528 | tf_op jit(solution)/shard_map/ppermute | solution.py:20
  102.1 104.3 %copy-start.53 = (f32[256,6]{0,1:T(8,128)}, f32[256,6]{0,1:T(8,128)S(1)}, u32[]{:S(2)}) copy-start(f32[256,6]{0,1:T(8,128)S(1)} %copy.202) | copy-start | bytes 18436
  102.2 79.8 %copy-start.32 = (f32[384]{0:T(512)}, f32[384]{0:T(512)S(1)}, u32[]{:S(2)}) copy-start(f32[384]{0:T(512)S(1)} %convert_element_type.56) | copy-start | bytes 4612
  128.6 37.6 %copy-start.3 = (bf16[1,256,1536]{2,1,0:T(8,128)(2,1)S(1)}, bf16[1,256,1536]{2,1,0:T(8,128)(2,1)}, u32[]{:S(2)}) copy-start(bf16[1,256,1536]{2,1,0:T(8,128)(2,1)} %param.35) | copy-start | bytes 2359300
  166.2 18.7 %copy-start.44 = (f32[256]{0:T(256)}, f32[256]{0:T(256)S(1)}, u32[]{:S(2)}) copy-start(f32[256]{0:T(256)S(1)} %add_rsqrt_fusion) | copy-start | bytes 3076
  206.3 5.0 copy-start.7
  217.7 27.2 %copy-start.1 = (f32[256,640]{1,0:T(8,128)}, f32[256,640]{1,0:T(8,128)S(1)}, u32[]{:S(2)}) copy-start(f32[256,640]{1,0:T(8,128)S(1)} %get-tuple-element.377) | copy-start | bytes 1966084
  218.3 26.9 %collective-permute-start.1 = (f32[3,640]{1,0:T(4,128)}, f32[3,640]{1,0:T(4,128)}, u32[]{:S(2)}, u32[]{:S(2)}) collective-permute-start(f32[3,640]{1,0:T(4,128)} %pad_add_fusion.1), channel_id=1, source_target_pairs={{8,0},{16,8},{24,16},{9,1},{17,9},{25,17},{10,2},{18,10},{26,18},{... | collective-permute-start | bytes 23048 | tf_op jit(solution)/shard_map/ppermute | solution.py:20
  228.3 12.7 %copy-start.33 = (f32[384]{0:T(512)S(1)}, f32[384]{0:T(512)}, u32[]{:S(2)}) copy-start(f32[384]{0:T(512)} %copy-done.32) | copy-start | bytes 4612
  228.3 12.7 %copy-start.45 = (f32[256]{0:T(256)S(1)}, f32[256]{0:T(256)}, u32[]{:S(2)}) copy-start(f32[256]{0:T(256)} %copy-done.44) | copy-start | bytes 3076
  237.2 7.1 %copy-start.30 = (f32[1,6,256]{2,1,0:T(8,128)}, f32[1,6,256]{2,1,0:T(8,128)S(1)}, u32[]{:S(2)}) copy-start(f32[1,6,256]{2,1,0:T(8,128)S(1)} %reshape.500) | copy-start | bytes 18436
  238.6 5.7 copy-start.38
  240.7 144.5 %all-reduce.21.cloned.1.call-start = ((), (), s32[]{:S(2)}) async-start(), calls=%async_computation.13 | async-start | bytes 6291456 | tf_op jit(solution)/shard_map/psum | solution.py:192
  249.3 29.2 %copy-start.36 = (f32[256]{0:T(256)S(1)}, f32[256]{0:T(256)}, u32[]{:S(2)}) copy-start(f32[256]{0:T(256)} %copy-done.35) | copy-start | bytes 3076
  249.3 213.4 %reduce-scatter.12.cloned.1.call-start = ((), (), s32[]{:S(2)}) async-start(), calls=%async_computation.10 | async-start | bytes 1671168 | tf_op jit(solution)/shard_map/reduce_scatter | solution.py:254
  280.3 260.6 %reduce-scatter.14.cloned.1.call-start = ((), (), s32[]{:S(2)}) async-start(), calls=%async_computation.11 | async-start | bytes 2506752 | tf_op jit(solution)/shard_map/reduce_scatter | solution.py:260
  282.5 336.6 %reduce-scatter.8.cloned.1.call-start = ((), (), s32[]{:S(2)}) async-start(), calls=%async_computation.8 | async-start | bytes 2506752 | tf_op jit(solution)/shard_map/reduce_scatter | solution.py:248
  285.5 411.8 %reduce-scatter.10.cloned.1.call-start = ((), (), s32[]{:S(2)}) async-start(), calls=%async_computation.9 | async-start | bytes 2506752 | tf_op jit(solution)/shard_map/reduce_scatter | solution.py:251
  (46 other events, 86.8 us)
Sparse Core Ops, SparseCore 0:
  10.1 45.5 all-gather.7
  57.9 42.8 all-gather.9
  102.9 42.6 all-gather.11
  240.8 73.2 reduce-scatter.15
  317.0 68.1 all-reduce.20
  388.8 73.8 reduce-scatter.11
  466.6 74.3 reduce-scatter.13
  544.8 74.2 reduce-scatter.7
  623.0 74.2 reduce-scatter.9
where the time goes:
time: 706 us; the launch traced here: 704 us
  waiting for transfers between devices  342 us (48%)
  blocking collectives  237 us (34%)
  matrix products  45.2 us (6%)
  other arithmetic  30.9 us (4%)
  local copies, waits for them, and re-layouts  29.4 us (4%)
  between operations  16.3 us (2%)
    unnamed x2, blocking collectives  96.1 us
    reduce_scatter x1, waiting for transfers between devices, per_device(): lax.psum_scatter(grad_out_weight, ('dp', 'ctx'), scatter_dimension=1, til...  78.2 us
    reduce_scatter x1, waiting for transfers between devices, per_device(): lax.psum_scatter(contract_rows(hidden_in, low_value), ('dp', 'ctx'), scat...  78.2 us
    reduce_scatter x1, waiting for transfers between devices, per_device(): lax.psum_scatter(contract_rows(hidden_in, low_gate), ('dp', 'ctx'), scatt...  78.2 us
    psum x1, waiting for transfers between devices, per_device(): lax.psum(jnp.dot(normed_out, out_full, preferred_element_type=jnp.float32...  69.6 us
    psum x1, blocking collectives, per_device(): square_sum = lax.psum(jnp.sum(gated * gated, axis=1), 'tp')  34.6 us
    all_gather x3, blocking collectives, entering_2(): pieces = jax.tree.map(lambda part: lax.all_gather(part, axis), value)  29.9 us
    psum x1, blocking collectives, per_device(): lax.psum((grad_input[:, inner_local:], grad_filters[:, inner_local:], gra...  28.4 us
  transfers between devices with their start and end apart: 11, of which 6 were waited for; matrix products, arithmetic and copies ran while one was open for 10% of the time, Pallas kernels for 0%

commit v1 on v0

v1 whole, which is shorter than its diff:
```python
import jax
import jax.numpy as jnp
from jax import lax
from jax.experimental import pallas as pl
from jax.experimental.pallas import tpu as pltpu
from jax.sharding import PartitionSpec as P

F32 = jnp.float32
BF16 = jnp.bfloat16
HIGH = lax.Precision.HIGHEST
EPSILON = 1e-05
INNER = 3072
D = 1536
T = 256
RIM = 16
EXT = T + RIM
KERNEL = 4
HEADS = 6
WIDE = 384
STATE = 128
MIX = WIDE + 2 * STATE
FIRST = MIX + 128
ROWS = 96
SHARES = 16
HALF = 640
RIM_SLOTS = ((0, ROWS), (0, ROWS + RIM), (1, ROWS))
SHARE = T // 8
REST = ROWS + 16
PART = 32
STEP_LANE = 32
GAIN_LANE = STEP_LANE + HEADS
STATE_LANE = 64
TURNED = 384
VMEM_LIMIT = 16 * 2**20
VMEM_WHOLE = 65_500_000

VALUES, SLOPE = slice(0, WIDE), slice(WIDE, WIDE + MIX)
STEP, STEP_SLOPE, LOG_DECAY = slice(1024, 1152), slice(1152, 1280), slice(1280, 1408)
BMAT, CMAT, WEIGHTED = slice(0, 128), slice(128, 256), slice(256, 640)
GATE_PRE, GRAD_NORMED, WITHIN = slice(0, 384), slice(384, 768), slice(768, 1152)
INSIDE, MIXED = slice(0, 384), slice(384, 768)
NORMED, LOW_GATE = slice(0, 384), slice(384, 768)


def fuse(function, outputs, ids, *arrays, scratch=(), fetch=False, rim=False):
    count = len(arrays)
    shapes = [array.shape for array in arrays]
    if rim:
        shapes[-1] = (RIM, D)

    def body(*refs):
        if not fetch:
            function(*refs)
            return
        given, rest = refs[1 : 1 + count], refs[1 + count : -1 - count]
        held, done = refs[-1 - count : -1], refs[-1]
        given = list(given)
        if rim:
            given[-1] = given[-1].at[pl.ds(T - RIM, RIM)]
        copies = [
            pltpu.make_async_copy(source, target, done.at[i])
            for i, (source, target) in enumerate(zip(given, held))
        ]
        for copy in copies:
            copy.start()
        for copy in copies:
            copy.wait()
        function(refs[0], *held, *rest)

    buffers = [pltpu.VMEM(shape, dtype) for shape, dtype in scratch]
    if fetch:
        buffers += [pltpu.VMEM(shape, array.dtype) for shape, array in zip(shapes, arrays)]
        buffers += [pltpu.SemaphoreType.DMA((count,))]
    space = pltpu.HBM if fetch else pltpu.VMEM
    call = pl.pallas_call(
        body,
        out_shape=[jax.ShapeDtypeStruct(shape, dtype) for shape, dtype in outputs],
        in_specs=[pl.BlockSpec(memory_space=pltpu.SMEM)]
        + [pl.BlockSpec(memory_space=space) for _ in arrays],
        out_specs=[pl.BlockSpec(memory_space=pltpu.VMEM) for _ in outputs],
        scratch_shapes=buffers,
        compiler_params=pltpu.CompilerParams(vmem_limit_bytes=VMEM_WHOLE if fetch else VMEM_LIMIT),
        name=function.__name__,
    )
    return list(call(ids, *arrays))


def roll(array, shift, axis):
    return pltpu.roll(array, shift % array.shape[axis], axis)


def product(a, b, left, right):
    return lax.dot_general(
        a.astype(BF16),
        b.astype(BF16),
        (((left,), (right,)), ((), ())),
        preferred_element_type=F32,
    )


def dot(a, b):
    return product(a, b, 1, 0)


def dot_last(a, b):
    return product(a, b, 1, 1)


def dot_first(a, b):
    return product(a, b, 0, 0)


def exact(a, b, left, right):
    return lax.dot_general(
        a, b, (((left,), (right,)), ((), ())), preferred_element_type=F32, precision=HIGH
    )


def iota(shape, axis):
    return lax.broadcasted_iota(jnp.int32, shape, axis)


def flag(condition):
    return jnp.where(condition, 1.0, 0.0)


def silu_parts(array):
    sig = jax.nn.sigmoid(array)
    return array * sig, sig * (1.0 + array * (1.0 - sig))


def spread_heads(array):
    rows = array.shape[0]
    lower = iota((rows, 128), 1) < 64
    pieces = [
        jnp.where(lower, array[:, h : h + 1], array[:, h + 1 : h + 2]) for h in range(0, HEADS, 2)
    ]
    return jnp.concatenate(pieces, axis=1)


def head_sums(array):
    chosen = flag((iota((128, WIDE), 1) >> 6) == iota((128, WIDE), 0))
    return exact(array, chosen, 1, 1)


def gain_row(tail):
    return dot_last(flag(iota((8, 128), 1) == GAIN_LANE), tail)[0:1]


def unit_rows(rows):
    tokens = rows.astype(F32)
    inv = lax.rsqrt(jnp.mean(tokens * tokens, axis=1, keepdims=True) + EPSILON)
    return tokens * inv


def aligned(start, size):
    return pl.ds(pl.multiple_of(start, size), size)


def prepare(
    ids, value_weight, gate_weight, state_proj, step_proj, norm_gain, out_weight, rim, left, longer, right
):
    left[0] = value_weight[...]
    left[1] = gate_weight[...]
    longer[0, :ROWS] = value_weight[...]
    longer[1, :ROWS] = gate_weight[...]
    for chunk in range(4):
        start = ROWS + RIM * (chunk % 2)
        longer[chunk // 2, start : start + RIM] = rim[:, WIDE * chunk : WIDE * chunk + WIDE]
    right[0, :, : 2 * STATE] = state_proj[...]
    place = iota((HEADS, 128), 1) == STEP_LANE + iota((HEADS, 128), 0)
    tail = dot_first(step_proj[...], flag(place))
    tail = tail + dot_first(norm_gain[...], flag(iota((1, 128), 1) == GAIN_LANE))
    right[0, :, 2 * STATE :] = tail.astype(BF16)
    right[1] = out_weight[...]


def tabulate(
    ids, value_filter, state_filter, value_offset, state_offset, gate_gain, step_bias, decay_log, skip_gain,
    rim, hidden, consts, units,
):
    units[:RIM] = unit_rows(rim[...])
    units[RIM:] = unit_rows(hidden[...])
    consts[...] = jnp.zeros(consts.shape, F32)
    consts[:KERNEL, :WIDE] = value_filter[...].astype(F32)
    consts[:KERNEL, WIDE:MIX] = state_filter[...].astype(F32)
    consts[KERNEL : KERNEL + 1, :WIDE] = value_offset[...].astype(F32)
    consts[KERNEL : KERNEL + 1, WIDE:MIX] = state_offset[...].astype(F32)
    consts[5:6, :WIDE] = gate_gain[...].astype(F32)
    consts[6:7, :HEADS] = step_bias[...]
    consts[7:8, :HEADS] = decay_log[...]
    consts[8:9, :HEADS] = skip_gain[...]


def place_blocks(ids, left, right, which, target):
    line, ctx = ids[0, 0], ids[0, 1]

    def piece(side, far, near):
        if far == 2:
            return side[2][near, which] if near < 2 else side[3][near - 2, which]
        return side[far + far // 3][near, which]

    for far in range(4):
        for near in range(4):
            block = ((line - far) & 3) * 4 + ((ctx - near) & 3)
            target[aligned(block * ROWS, ROWS), :WIDE] = piece(left, far, near)
            block = ((line - near) & 3) * 4 + ((ctx - far) & 3)
            target[aligned(block * ROWS, ROWS), WIDE:] = piece(right, far, near)


def enter(
    ids, l0, l1, l2, l3, l4, r0, r1, r2, r3, r4, units, consts,
    weights, hidden_in, taken, wide, narrow, message,
):
    place_blocks(ids, (l0, l1, l2, l3, l4), (r0, r1, r2, r3, r4), 0, weights)
    gain = gain_row(weights[:, MIX:])
    hidden_in[...] = (units[...] * gain).astype(BF16)
    projected = dot(hidden_in[...], weights[...])
    inputs = projected[:, :MIX].astype(BF16)
    taken[...] = inputs
    inputs = inputs.astype(F32)
    filter_pre = consts[KERNEL : KERNEL + 1, :MIX]
    for tap in range(KERNEL):
        filter_pre = filter_pre + consts[tap : tap + 1, :MIX] * roll(inputs, KERNEL - 1 - tap, 0)[RIM:]
    activated, wide[:, SLOPE] = silu_parts(filter_pre)
    lanes = iota((T, 128), 1) < HEADS
    step_in = roll(projected[RIM:, MIX:], 128 - STEP_LANE, 1) + consts[6:7, :128]
    step_in = jnp.where(lanes, step_in, -100.0)
    step = jnp.maximum(step_in, 0.0) + jnp.log1p(jnp.exp(-jnp.abs(step_in)))
    step = jnp.where(lanes, step, 0.0)
    rate = jnp.exp(consts[7:8, :128])
    log_decay = exact(flag(iota((T, T), 0) >= iota((T, T), 1)), -step * rate, 1, 0)
    values = activated[:, :WIDE]
    weighted = (values * spread_heads(step)).astype(BF16)
    wide[:, VALUES] = values
    wide[:, STEP] = step
    wide[:, STEP_SLOPE] = jax.nn.sigmoid(step_in)
    wide[:, LOG_DECAY] = log_decay
    narrow[:, BMAT] = activated[:, WIDE : WIDE + STATE].astype(BF16)
    narrow[:, CMAT] = activated[:, WIDE + STATE :].astype(BF16)
    narrow[:, WEIGHTED] = weighted
    last = log_decay[T - 1 :]
    to_end = spread_heads(jnp.exp(last - log_decay))
    message[:STATE] = dot_first(narrow[:, BMAT], weighted.astype(F32) * to_end).astype(BF16)
    span = spread_heads(last)
    high = span.astype(BF16).astype(F32)
    line = iota((16, WIDE), 0)
    tail = jnp.where(line == 0, high, jnp.where(line == 1, span - high, 0.0))
    message[STATE:] = tail.astype(BF16)


def decays(log_decay, turned, head):
    gap = log_decay[:, head : head + 1] - turned[head : head + 1, :]
    return jnp.exp(jnp.where(iota((T, T), 0) >= iota((T, T), 1), gap, -1e30))


def pair_columns(pair):
    return slice(128 * pair, 128 * pair + 128)


def project(
    ids, l0, l1, l2, l3, l4, r0, r1, r2, r3, r4, hidden_in, cotangent, wide, narrow, gate_out, before
):
    place_blocks(ids, (l0, l1, l2, l3, l4), (r0, r1, r2, r3, r4), 1, gate_out)
    before[:, GATE_PRE] = dot(hidden_in[RIM:], gate_out[:, :WIDE])
    before[:, GRAD_NORMED] = dot(cotangent[...], gate_out[:, WIDE:])
    scores = dot_last(narrow[:, CMAT], narrow[:, BMAT])
    log_decay = wide[:, LOG_DECAY]
    turned = log_decay.T
    lower = iota((T, 128), 1) < 64
    weighted = narrow[:, WEIGHTED]
    for pair in range(HEADS // 2):
        part = weighted[:, pair_columns(pair)]
        one = dot(scores * decays(log_decay, turned, 2 * pair), part)
        two = dot(scores * decays(log_decay, turned, 2 * pair + 1), part)
        start = WITHIN.start + 128 * pair
        before[:, start : start + 128] = jnp.where(lower, one, two)


def mix(ids, m1, m2, m3, wide, narrow, consts, before, state, after, sums):
    me = ids[0, 1]
    total = jnp.zeros((STATE, WIDE), F32)
    gap = jnp.zeros((1, WIDE), F32)
    for back, message in enumerate((m1, m2, m3)):
        tail = message[STATE:].astype(F32)
        log = tail[0:1] + tail[1:2]
        state[STATE + 8 * back : STATE + 8 * back + 8] = jnp.broadcast_to(log, (8, WIDE))
        scale = jnp.exp(gap) * jnp.where(me > back, 1.0, 0.0)
        total = total + scale * message[:STATE].astype(F32)
        gap = gap + log
    state[:STATE] = total
    grown = spread_heads(jnp.exp(wide[:, LOG_DECAY]))
    inside = before[:, WITHIN] + dot(narrow[:, CMAT], total) * grown
    after[:, INSIDE] = inside
    whole = inside + wide[:, VALUES] * spread_heads(consts[8:9, :128])
    after[:, MIXED] = whole
    gate = before[:, GATE_PRE]
    gated = whole * gate * jax.nn.sigmoid(gate)
    ones = jnp.ones((8, WIDE), F32)
    squares = exact(ones, gated * gated, 1, 1)
    crosses = exact(ones, before[:, GRAD_NORMED] * consts[5:6, :WIDE] * gated, 1, 1)
    sums[...] = jnp.where(iota((8, T), 0) < 4, squares, crosses)


def gate_back(
    ids, s0, s1, s2, s3, after, before, consts, wide, narrow, gated_low, grad_mixed, grad_gain, sensitivity
):
    total = s0[...] + s1[...] + s2[...] + s3[...]
    columns = exact(total, flag(iota((8, 128), 0) == 4 * iota((8, 128), 1)), 0, 0)
    inv = lax.rsqrt(columns[:, 0:1] / INNER + EPSILON)
    cross = columns[:, 1:2]
    act, slope = silu_parts(before[:, GATE_PRE])
    mixed = after[:, MIXED]
    normed = mixed * act * inv
    scaled = consts[5:6, :WIDE]
    gated_low[:, NORMED] = (normed * scaled).astype(BF16)
    grads = before[:, GRAD_NORMED]
    grad_gain[...] = jnp.broadcast_to(jnp.sum(grads * normed, axis=0, keepdims=True), (8, WIDE))
    grad_gated = inv * (grads * scaled) - normed * (inv * inv * cross / INNER)
    own = grad_gated * act
    grad_mixed[...] = own
    gated_low[:, LOW_GATE] = (grad_gated * mixed * slope).astype(BF16)
    grown = spread_heads(jnp.exp(wide[:, LOG_DECAY]))
    sensitivity[...] = dot_first(narrow[:, CMAT], own * grown).astype(BF16)


def share_out(ids, source, keep, send):
    chip, core = ids[0, 2] >> 1, ids[0, 2] & 1
    for ahead in range(4):
        start = ((chip + ahead) & 3) * 2
        keep[ahead] = source[aligned((start + core) * SHARE, SHARE)]
        send[ahead] = source[aligned((start + 1 - core) * SHARE, SHARE)]


def middle(
    ids, hidden_in, gated_low, cotangent, gate_out, wide, narrow, grad_mixed, gate, out, grads, branch
):
    gate[...] = dot_first(hidden_in[RIM:], gated_low[:, LOW_GATE]).astype(BF16)
    out[...] = dot_first(cotangent[...], gated_low[:, NORMED]).astype(BF16)
    branch[...] = dot_last(gated_low[:, NORMED], gate_out[:, WIDE:]).astype(BF16)
    bmat, cmat, weighted = narrow[:, BMAT], narrow[:, CMAT], narrow[:, WEIGHTED]
    scores = dot_last(cmat, bmat)
    log_decay = wide[:, LOG_DECAY]
    turned = log_decay.T
    lower = iota((T, 128), 1) < 64
    grad_scores = jnp.zeros((T, T), F32)
    for pair in range(HEADS // 2):
        part = weighted[:, pair_columns(pair)]
        grad = grad_mixed[:, pair_columns(pair)]
        got = []
        for side in range(2):
            weights = decays(log_decay, turned, 2 * pair + side)
            got.append(dot_first(scores * weights, grad))
            own = jnp.where(lower, grad, 0.0) if side == 0 else jnp.where(lower, 0.0, grad)
            grad_scores = grad_scores + dot_last(own, part) * weights
        grads[:, pair_columns(pair)] = jnp.where(lower, got[0], got[1])
    grads[:, WIDE : WIDE + STATE] = dot_first(grad_scores, cmat)
    grads[:, WIDE + STATE :] = dot(grad_scores, bmat)


def leave(
    ids, g1, g2, g3, state, after, grad_mixed, grads, wide, narrow, consts, taken, grad_gain,
    low, keep, send, small, turned,
):
    me = ids[0, 1]
    end = jnp.zeros((STATE, WIDE), F32)
    gap = jnp.zeros((1, WIDE), F32)
    for ahead, message in enumerate((g1, g2, g3)):
        scale = jnp.exp(gap) * jnp.where(me + ahead < 3, 1.0, 0.0)
        end = end + scale * message[...].astype(F32)
        start = STATE + 8 * (2 - ahead)
        gap = gap + state[start : start + 1]
    step, step_slope, log_decay = wide[:, STEP], wide[:, STEP_SLOPE], wide[:, LOG_DECAY]
    values = wide[:, VALUES]
    last = log_decay[T - 1 :]
    to_end = spread_heads(jnp.exp(last - log_decay))
    weighted = narrow[:, WEIGHTED].astype(F32)
    own = grad_mixed[...]
    from_end = dot(narrow[:, BMAT], end) * to_end
    inputs = grads[:, :WIDE] + from_end
    from_b = grads[:, WIDE : WIDE + STATE] + dot_last(weighted * to_end, end)
    grown = spread_heads(jnp.exp(log_decay))
    from_c = grads[:, WIDE + STATE :] + dot_last(own * grown, state[:STATE])
    grad_log = head_sums(own.astype(BF16).astype(F32) * after[:, INSIDE] - weighted * inputs)
    at_end = jnp.sum(weighted * from_end, axis=0, keepdims=True) + jnp.exp(
        spread_heads(last)
    ) * jnp.sum(end * state[:STATE], axis=0, keepdims=True)
    at_end = head_sums(jnp.broadcast_to(at_end, (8, WIDE)))[0:1]
    grad_decay = exact(flag(iota((T, T), 0) <= iota((T, T), 1)), grad_log, 1, 0) + at_end
    rate = jnp.exp(consts[7:8, :128])
    grad_step = head_sums(values * inputs) - rate * grad_decay
    grad_step_pre = grad_step * step_slope
    grad_values = own * spread_heads(consts[8:9, :128]) + inputs * spread_heads(step)
    grad_pre = jnp.concatenate([grad_values, from_b, from_c], axis=1) * wide[:, SLOPE]
    before = taken[...].astype(F32)
    padded = jnp.concatenate([jnp.zeros((RIM, MIX), F32), grad_pre], axis=0)
    grad_input = jnp.zeros((EXT, MIX), F32)
    line = iota((8, MIX), 0)
    taps = jnp.where(line == KERNEL, jnp.sum(grad_pre, axis=0, keepdims=True), 0.0)
    for tap in range(KERNEL):
        shift = KERNEL - 1 - tap
        found = jnp.sum(grad_pre * roll(before, shift, 0)[RIM:], axis=0, keepdims=True)
        taps = jnp.where(line == tap, found, taps)
        grad_input = grad_input + consts[tap : tap + 1, :MIX] * roll(padded, -shift, 0)
    low[:, :WIDE] = grad_input[:, :WIDE].astype(BF16)
    low_step = jnp.concatenate([jnp.zeros((RIM, 128), F32), grad_step_pre], axis=0)
    low[:, WIDE:] = roll(low_step, STEP_LANE, 1).astype(BF16)
    rest = jnp.zeros((TURNED - EXT - 8, 2 * STATE), F32)
    turned[...] = jnp.concatenate([grad_input[:, WIDE:], taps[:, WIDE:], rest], axis=0).T
    share_out(ids, turned, keep, send)
    heads = (
        jnp.sum(grad_step_pre, axis=0, keepdims=True),
        -rate * jnp.sum(grad_decay * step, axis=0, keepdims=True),
        head_sums(jnp.broadcast_to(jnp.sum(own * values, axis=0, keepdims=True), (8, WIDE)))[0:1],
    )
    none = jnp.zeros((1, 128), F32)
    heads = jnp.concatenate([heads[0] + roll(heads[1], 64, 1), heads[2], none], axis=1)
    line = iota((8, WIDE), 0)
    small[...] = jnp.where(line == 5, grad_gain[...], jnp.where(line == 6, heads, taps[:, :WIDE]))


def pair_sum(ids, keep, got, *shares):
    for ahead, share in enumerate(shares):
        share[...] = (keep[ahead].astype(F32) + got[ahead].astype(F32)).astype(share.dtype)


def value_grads(ids, low, gated_low, weights, gate_out, hidden_in, value, head):
    value[...] = dot_first(hidden_in[...], low[:, :WIDE]).astype(BF16)
    part = dot_last(low[:, :WIDE], weights[:, :WIDE]) + dot_last(low[:, WIDE:], weights[:, MIX:])
    head[:RIM] = part[:RIM]
    head[RIM:] = part[RIM:] + dot_last(gated_low[:, LOW_GATE], gate_out[:, :WIDE])


def fold(small):
    pieces = []
    for chunk in range(6):
        piece = small[:, pair_columns(chunk // 2)]
        pieces.append(piece if chunk % 2 else roll(piece, 64, 1))
    folded = jnp.concatenate(pieces, axis=0)
    high = folded.astype(BF16).astype(F32)
    return jnp.concatenate([high, folded - high], axis=0)


def unfold(block):
    folded = block[:48] + block[48:]
    lower = iota((8, 128), 1) < 64
    pairs = []
    for pair in range(3):
        one, two = folded[16 * pair : 16 * pair + 8], folded[16 * pair + 8 : 16 * pair + 16]
        pairs.append(jnp.where(lower, roll(one, 64, 1), two))
    return jnp.concatenate(pairs, axis=1)


def tidy(block):
    folded = block[:48] + block[48:]
    high = folded.astype(BF16).astype(F32)
    parts = jnp.concatenate([high, folded - high], axis=0)
    return jnp.where(iota((ROWS, 128), 1) < 64, block, parts)


def late_grads(
    ids, t0, t1, t2, t3, low, small, head, weights, units, hidden_in, gate, out, value,
    whole, *targets
):
    targets, tail = targets[:-1], targets[-1]
    total = t0[...] + t1[...] + t2[...] + t3[...]
    low_turned = total.astype(BF16).astype(F32)
    straight = jnp.concatenate([total, jnp.zeros((128 - PART, TURNED), F32)], axis=0).T
    low_tail = low[:, WIDE:].astype(F32) + straight[:EXT]
    tiles = jnp.concatenate([low_turned] * 8, axis=0)
    tiles = jnp.where((iota((8 * PART, TURNED), 0) >> 5) == ids[0, 2], tiles, 0.0)
    part = head[...] + product(tiles, weights[:, WIDE:MIX], 0, 1)[:EXT]
    behind = part[:RIM].astype(BF16)
    whole[...] = part[RIM:].astype(BF16)
    terms = part * units[...]
    grads = dot_first(hidden_in[...], low_tail)
    grads = grads + dot_first(terms, flag(iota((EXT, 128), 1) == GAIN_LANE))
    tail[...] = grads.astype(BF16)
    own = straight[EXT : EXT + 8]
    row = jnp.concatenate([own[0:1] + roll(own[1:2], 64, 1), own[2:3] + roll(own[3:4], 64, 1), own[4:5]], axis=1)
    folded = fold(jnp.where(iota((8, WIDE), 0) == 7, row, small[...]))
    arrange(ids, gate, out, value, tail, folded, targets)
    for chunk, (slot, start) in enumerate(RIM_SLOTS):
        piece = behind[:, HALF * chunk : HALF * chunk + HALF]
        targets[8][slot, start : start + RIM, : piece.shape[1]] = piece


def arrange(ids, gate, out, value, tail, folded, targets):
    line, ctx = ids[0, 0], ids[0, 1]
    lanes = iota((ROWS, 128), 1) < 64

    def left(block):
        rows = aligned(block * ROWS, ROWS)
        return gate[rows], value[rows, :256]

    def right(block):
        rows = aligned(block * ROWS, ROWS)
        end = jnp.where(lanes, tail[rows].astype(F32), folded).astype(BF16)
        return out[rows], value[rows, 256:], end

    for far in range(4):
        for near in range(4):
            slot = far + far // 3
            place = near
            if far == 2 and near >= 2:
                slot, place = 3, near - 2
            start = 0
            for part in left(((line + far) & 3) * 4 + ((ctx + near) & 3)):
                targets[slot][place, :, start : start + part.shape[1]] = part
                start += part.shape[1]
            start = 0
            for part in right(((line + near) & 3) * 4 + ((ctx + far) & 3)):
                targets[5 + slot][place, :ROWS, start : start + part.shape[1]] = part
                start += part.shape[1]


def put(target, total, tailed):
    if tailed:
        target[:, : HALF - 128] = total[:, : HALF - 128].astype(BF16)
        target[:, HALF - 128 :] = tidy(total[:, HALF - 128 :]).astype(BF16)
    else:
        target[...] = total.astype(BF16)


def relay(ids, *refs):
    for side in range(2):
        one, three, first, second = refs[4 * side : 4 * side + 4]
        to_one, to_three = refs[10 + 2 * side : 12 + 2 * side]
        for near in range(4):
            if near < 2:
                total = one[near].astype(F32) + first[near].astype(F32)
                put(to_one.at[near], total, side)
                to_three[near] = three[near]
            else:
                total = three[near].astype(F32) + second[near - 2, :ROWS].astype(F32)
                put(to_three.at[near], total, side)
                to_one[near] = one[near]
    head, branch = refs[8:10]
    keep, send, whole = refs[14:]
    inside = jnp.where(ids[0, 1] < 3, 1.0, 0.0)
    whole[: T - RIM] = head[: T - RIM]
    for chunk, (slot, start) in enumerate(RIM_SLOTS):
        columns = slice(HALF * chunk, min(HALF * chunk + HALF, D))
        behind = refs[7][slot, start : start + RIM, : columns.stop - columns.start]
        total = head[T - RIM :, columns].astype(F32) + behind.astype(F32) * inside
        whole[T - RIM :, columns] = total.astype(BF16)
    chip, core = ids[0, 2] >> 1, ids[0, 2] & 1
    for ahead in range(4):
        start = ((chip + ahead) & 3) * 2
        for half, source in enumerate((whole, branch)):
            rows = slice(half * SHARE, half * SHARE + SHARE)
            keep[ahead, rows] = source[aligned((start + core) * SHARE, SHARE)]
            send[ahead, rows] = source[aligned((start + 1 - core) * SHARE, SHARE)]


def halfway(ids, *refs):
    for side in range(2):
        own, one, three = refs[3 * side : 3 * side + 3]
        for near in range(4):
            total = own[near].astype(F32) + one[near].astype(F32) + three[near].astype(F32)
            put(refs[7 + 4 * side + near], total, side)


def collect(
    ids, a0, a1, a2, a3, b0, b1, b2, b3, settled,
    grad_gate, grad_value, grad_out, grad_step, taps, offset, gain, bias, decay, skip, message, rest,
):
    left = sum(part[...].astype(F32) for part in (a0, a1, a2, a3))
    right = sum(part[...].astype(F32) for part in (b0, b1, b2, b3))
    grad_gate[...] = left[:, :WIDE]
    grad_out[...] = right[:, :WIDE]
    grad_value[:, :256] = left[:, WIDE:]
    grad_value[:, 256:] = right[:, WIDE : HALF - 128]
    total = right[:, HALF - 128 :]
    rest[:ROWS] = total
    small = unfold(total)
    state = small[7:8]
    rest[ROWS:] = jnp.zeros((REST - ROWS, 128), F32)
    for tap in range(KERNEL + 1):
        piece = state[:, pair_columns(tap // 2)]
        rest[ROWS + tap : ROWS + tap + 1] = piece if tap % 2 else roll(piece, 64, 1)
    picked = flag(iota((8, 128), 1) == STEP_LANE + iota((8, 128), 0))
    grad_step[...] = exact(picked, total, 1, 1)[:HEADS]
    message[: 2 * SHARE] = settled[...]
    for block in range(REST // 16):
        message[2 * SHARE :, pair_columns(block)] = rest[16 * block : 16 * block + 16].astype(BF16)
    taps[...] = small[:KERNEL]
    offset[...] = small[KERNEL : KERNEL + 1]
    gain[...] = small[5:6]
    bias[...] = small[6:7, :HEADS]
    decay[...] = small[6:7, 64 : 64 + HEADS]
    skip[...] = small[6:7, 128 : 128 + HEADS]


def finish(
    ids, a0, a1, a2, a3, b0, b1, b2, b3, cotangent,
    grad_hidden, block_out, grad_state, grad_gain, taps, offset, rest,
):
    chip, core = ids[0, 2] >> 1, ids[0, 2] & 1
    for far, pair in enumerate(((a0, b0), (a1, b1), (a2, b2), (a3, b3))):
        start = ((chip - far) & 3) * 2
        for place, piece in zip((start + core, start + 1 - core), pair):
            rows = aligned(place * SHARE, SHARE)
            grad_hidden[rows] = cotangent[rows].astype(F32) + piece[:SHARE].astype(F32)
            block_out[rows] = piece[SHARE : 2 * SHARE]
            for block in range(REST // 16):
                part = piece[2 * SHARE :, pair_columns(block)]
                rest[place, 16 * block : 16 * block + 16] = part.astype(F32)
    lanes = iota((REST, 128), 1) >> 5
    total = rest[0]
    for half in range(2):
        state = jnp.zeros((REST, 128), F32)
        small = jnp.zeros((REST, 128), F32)
        for i in range(4):
            one = rest[4 * half + i]
            state = jnp.where(lanes == i, roll(one, PART * i, 1), state)
            small = jnp.where(lanes == i, roll(one, PART * i - STATE_LANE, 1), small)
            if half + i:
                total = total + one
        columns = pair_columns(half)
        grad_state[:, columns] = state[:ROWS]
        taps[:, columns] = small[ROWS : ROWS + KERNEL]
        offset[:, columns] = small[ROWS + KERNEL : ROWS + KERNEL + 1]
    grad_gain[...] = exact(flag(iota((8, 128), 1) == GAIN_LANE), total[:ROWS], 1, 1)[0:1]


def settle(ids, p0, p1, p2, p3, hidden, weights, settled):
    both = sum(part[...].astype(F32) for part in (p0, p1, p2, p3))
    mine = hidden[aligned(ids[0, 2] * SHARE, SHARE)].astype(F32)
    inv = lax.rsqrt(jnp.mean(mine * mine, axis=1, keepdims=True) + EPSILON)
    unit = mine * inv
    scaled = both[:SHARE] * gain_row(weights[:, MIX:])
    tokens = inv * (scaled - unit * jnp.mean(scaled * unit, axis=1, keepdims=True))
    settled[:SHARE] = tokens.astype(BF16)
    settled[SHARE:] = (mine + both[SHARE:]).astype(BF16)


def stack_blocks(ids, l0, l1, l2, l3, r0, r1, r2, r3, left, right, rim):
    for i, (one, two) in enumerate(((l0, r0), (l1, r1), (l2, r2), (l3, r3))):
        left[i] = one[:, :ROWS]
        right[i] = two[...]
    inside = jnp.where(ids[0, 1] > 0, 1.0, 0.0)
    for chunk in range(4):
        start = ROWS + RIM * (chunk % 2)
        piece = l1[chunk // 2, start : start + RIM].astype(F32) * inside
        rim[:, WIDE * chunk : WIDE * chunk + WIDE] = piece.astype(BF16)


def shift(array, axis, steps):
    return lax.ppermute(array, axis, [(i, (i + steps) % 4) for i in range(4)])


def from_chip(array, steps):
    return lax.ppermute(array, "tp", [(i, (i + 2 * steps) % 8) for i in range(8)])


def from_core(array):
    return lax.ppermute(array, "tp", [(i, i ^ 1) for i in range(8)])


def around(array, axis):
    return [array] + [shift(array, axis, steps) for steps in range(1, 4)]


def ring_sides(array, axis):
    return shift(array, axis, 1), shift(array, axis, 3)


def ring_rest(array, axis, one, three):
    return [array, one, shift(one[:2], axis, 1), shift(three[2:], axis, 3), three]


def chips_sum(ids, keep, send):
    outputs = [(keep.shape[1:], keep.dtype)] * 4
    pair = fuse(pair_sum, outputs, ids, keep, from_core(send))
    return [pair[0]] + [from_chip(pair[ahead], ahead) for ahead in range(1, 4)]


def chips_all(array):
    same = [array] + [from_chip(array, steps) for steps in range(1, 4)]
    return same + [from_core(one) for one in same]


def per_device(
    hidden_states,
    norm_gain,
    gate_weight,
    value_weight,
    state_proj,
    step_proj,
    value_filter,
    value_offset,
    state_filter,
    state_offset,
    step_bias,
    decay_log,
    skip_gain,
    gate_norm_gain,
    out_weight,
    out_grad,
):
    hidden = hidden_states[0]
    cotangent = out_grad[0]
    places = [lax.axis_index(axis).astype(jnp.int32) for axis in ("dp", "ctx", "tp")]
    ids = jnp.stack(places).reshape(1, 3)

    half = ((2, ROWS, WIDE), BF16)
    left, longer, right = fuse(
        prepare,
        [half, ((2, ROWS + 2 * RIM, WIDE), BF16), half],
        ids,
        value_weight,
        gate_weight,
        state_proj,
        step_proj.T,
        norm_gain[None],
        out_weight.T,
        hidden,
        fetch=True,
        rim=True,
    )
    near = [left, shift(longer, "ctx", 1), shift(left, "ctx", 2), shift(left, "ctx", 3)]
    left, right, rim = fuse(
        stack_blocks,
        [((4, 2, ROWS, WIDE), BF16)] * 2 + [((RIM, D), BF16)],
        ids,
        *near,
        *around(right, "dp"),
    )
    consts, units = fuse(
        tabulate,
        [((16, FIRST), F32), ((EXT, D), F32)],
        ids,
        value_filter,
        state_filter,
        value_offset[None],
        state_offset[None],
        gate_norm_gain[None],
        step_bias[None],
        decay_log[None],
        skip_gain[None],
        rim,
        hidden,
    )
    left = ring_rest(left, "dp", *ring_sides(left, "dp"))
    right = ring_rest(right, "ctx", *ring_sides(right, "ctx"))
    weights, hidden_in, taken, wide, narrow, message = fuse(
        enter,
        [
            ((D, FIRST), BF16),
            ((EXT, D), BF16),
            ((EXT, MIX), BF16),
            ((T, LOG_DECAY.stop), F32),
            ((T, WEIGHTED.stop), BF16),
            ((STATE + 16, WIDE), BF16),
        ],
        ids,
        *left,
        *right,
        units,
        consts,
    )
    messages = around(message, "ctx")[1:]
    gate_out, before = fuse(
        project,
        [((D, 2 * WIDE), BF16), ((T, WITHIN.stop), F32)],
        ids,
        *left,
        *right,
        hidden_in,
        cotangent,
        wide,
        narrow,
    )
    state, after, sums = fuse(
        mix,
        [((STATE + 24, WIDE), F32), ((T, MIXED.stop), F32), ((8, T), F32)],
        ids,
        *messages,
        wide,
        narrow,
        consts,
        before,
    )
    sums = sums + from_core(sums)
    gated_low, grad_mixed, grad_gain, sensitivity = fuse(
        gate_back,
        [
            ((T, LOW_GATE.stop), BF16),
            ((T, WIDE), F32),
            ((8, WIDE), F32),
            ((STATE, WIDE), BF16),
        ],
        ids,
        sums,
        *[from_chip(sums, steps) for steps in range(1, 4)],
        after,
        before,
        consts,
        wide,
        narrow,
    )
    later = [shift(sensitivity, "ctx", -steps) for steps in range(1, 4)]
    square = ((D, WIDE), BF16)
    gate, out, grads, branch = fuse(
        middle,
        [square, square, ((T, MIX), F32), ((T, D), BF16)],
        ids,
        hidden_in,
        gated_low,
        cotangent,
        gate_out,
        wide,
        narrow,
        grad_mixed,
    )
    low, turned_keep, turned_send, small = fuse(
        leave,
        [((EXT, WIDE + 128), BF16)] + [((4, PART, TURNED), F32)] * 2 + [((8, WIDE), F32)],
        ids,
        *later,
        state,
        after,
        grad_mixed,
        grads,
        wide,
        narrow,
        consts,
        taken,
        grad_gain,
        scratch=[((2 * STATE, TURNED), F32)],
    )
    value, head = fuse(
        value_grads,
        [square, ((EXT, D), F32)],
        ids,
        low,
        gated_low,
        weights,
        gate_out,
        hidden_in,
    )
    whole, part = ((4, ROWS, HALF), BF16), ((2, ROWS, HALF), BF16)
    longer = ((2, ROWS + 2 * RIM, HALF), BF16)
    head, *blocks = fuse(
        late_grads,
        [((T, D), BF16)] + [whole, whole, part, part, whole] + [whole, whole, part, longer, whole],
        ids,
        *chips_sum(ids, turned_keep, turned_send),
        low,
        small,
        head,
        weights,
        units,
        hidden_in,
        gate,
        out,
        value,
        scratch=[((D, 128), BF16)],
    )
    left, right = blocks[:5], blocks[5:]
    halves = []
    for side, axis in ((left, "dp"), (right, "ctx")):
        halves += [side[1], side[4], shift(side[2], axis, 1), shift(side[3], axis, 3)]
    *sides, head_keep, head_send = fuse(
        relay,
        [whole] * 4 + [((4, 2 * SHARE, D), BF16)] * 2,
        ids,
        *halves,
        head,
        branch,
        scratch=[((T, D), BF16)],
    )
    left = [left[0], shift(sides[0], "dp", 1), shift(sides[1], "dp", 3)]
    right = [right[0], shift(sides[2], "ctx", 1), shift(sides[3], "ctx", 3)]
    heads = chips_sum(ids, head_keep, head_send)
    sums = fuse(halfway, [((ROWS, HALF), BF16)] * 8, ids, *left, *right, heads[0])
    left = sums[:1] + [shift(sums[steps], "ctx", steps) for steps in range(1, 4)]
    right = sums[4:5] + [shift(sums[4 + steps], "dp", steps) for steps in range(1, 4)]
    (settled,) = fuse(settle, [((2 * SHARE, D), BF16)], ids, *heads, hidden, weights)
    few, line = ((1, HEADS), F32), ((1, WIDE), F32)
    grad_gate, grad_value, grad_out, grad_step, taps, offset, gain, bias, decay, skip, message = fuse(
        collect,
        [((ROWS, WIDE), F32)] * 3
        + [((HEADS, ROWS), F32), ((KERNEL, WIDE), F32)]
        + [line, line, few, few, few]
        + [((2 * SHARE + 16, D), BF16)],
        ids,
        *left,
        *right,
        settled,
        scratch=[((REST, 128), F32)],
    )
    grad_hidden, block_out, grad_state, grad_norm_gain, state_taps, state_offset = fuse(
        finish,
        [
            ((T, D), F32),
            ((T, D), BF16),
            ((ROWS, 2 * STATE), F32),
            ((1, ROWS), F32),
            ((KERNEL, 2 * STATE), F32),
            ((1, 2 * STATE), F32),
        ],
        ids,
        *chips_all(message),
        cotangent,
        scratch=[((8, REST, 128), F32)],
    )
    return (
        block_out[None],
        grad_hidden[None],
        grad_norm_gain[0],
        grad_gate,
        grad_value,
        grad_state,
        grad_step.T,
        taps,
        offset[0],
        state_taps,
        state_offset[0],
        bias[0],
        decay[0],
        skip[0],
        gain[0],
        grad_out.T,
    )


def solution(mesh):
    line = P(("dp", "ctx"))
    placed = (
        P("dp", "ctx", None),
        line,
        P(("dp", "ctx"), "tp"),
        P(("dp", "ctx"), "tp"),
        P(("dp", "ctx"), None),
        P(("dp", "ctx"), "tp"),
        P(None, "tp"),
        P("tp"),
        P(),
        P(),
        P("tp"),
        P("tp"),
        P("tp"),
        P("tp"),
        P("tp", ("dp", "ctx")),
        P("dp", "ctx", None),
    )
    given = (
        P("dp", "ctx", None),
        P("dp", "ctx", None),
        line,
        P(("dp", "ctx"), "tp"),
        P(("dp", "ctx"), "tp"),
        P(("dp", "ctx"), None),
        P(("dp", "ctx"), "tp"),
        P(None, "tp"),
        P("tp"),
        P(),
        P(),
        P("tp"),
        P("tp"),
        P("tp"),
        P("tp"),
        P("tp", ("dp", "ctx")),
    )
    return jax.shard_map(
        per_device, mesh=mesh, in_specs=placed, out_specs=given, check_vma=False
    )
```

time: 706 us -> 167 us (0.24)
  waiting for transfers between devices: 342 us -> 53.5 us
  blocking collectives: 237 us -> 0 us
  starting transfers between devices: 3.62 us -> 76.7 us
  matrix products: 45.2 us -> 0 us
  Pallas kernels: 0 us -> 31.4 us
  other arithmetic: 30.9 us -> 1.78 us
  local copies, waits for them, and re-layouts: 29.4 us -> 2.66 us
  between operations: 16.3 us -> 1.05 us
    reduce_scatter x4 -> x0, waiting for transfers between devices: 245 us -> none  [the longest x1 78.2 us: per_device(): lax.psum_scatter(grad_out_weight, ('dp', 'ctx'), scatter_dimension=1, til...]
    unnamed x2 -> x0, blocking collectives: 96.1 us -> none
    psum x3 -> x0, blocking collectives: 75.4 us -> none  [the longest x1 34.6 us: per_device(): square_sum = lax.psum(jnp.sum(gated * gated, axis=1), 'tp')]
    ppermute x2 -> x53, starting transfers between devices: 3.04 us -> 76.7 us  [the longest x34 38.1 us: shift(): return lax.ppermute(array, axis, [(i, (i + steps) % 4) for i in range(4)])]
    psum x1 -> x0, waiting for transfers between devices: 69.6 us -> none  [per_device(): lax.psum(jnp.dot(normed_out, out_full, preferred_element_type=jnp.float32...]
    all_gather x5 -> x0, blocking collectives: 65 us -> none  [the longest x3 29.9 us: entering_2(): pieces = jax.tree.map(lambda part: lax.all_gather(part, axis), value)]
    ppermute x2 -> x53, waiting for transfers between devices: 0.01 us -> 53.5 us  [the longest x34 48.5 us: shift(): return lax.ppermute(array, axis, [(i, (i + steps) % 4) for i in range(4)])]
    dot_general x26 -> x0, matrix products: 43.1 us -> none  [the longest x3 10.2 us: block_local(): jnp.einsum('ctsh,cshp->cthp', scores[:, :, :, None] * decay_mask, weighte...]
  transfers between devices with their start and end apart: 11 -> 53, of which waited for: 6 -> 22; matrix products, arithmetic and copies ran while one was open for 10% -> 1% of each run, Pallas kernels for 0% -> 6%
where the time goes in v1:
time: 167 us
  starting transfers between devices  76.7 us (46%)
  waiting for transfers between devices  53.5 us (32%)
  Pallas kernels  31.4 us (19%)
  local copies, waits for them, and re-layouts  2.66 us (2%)
  other arithmetic  1.78 us (1%)
    ppermute x34, waiting for transfers between devices, shift(): return lax.ppermute(array, axis, [(i, (i + steps) % 4) for i in range(4)])  48.5 us
    ppermute x34, starting transfers between devices, shift(): return lax.ppermute(array, axis, [(i, (i + steps) % 4) for i in range(4)])  38.1 us
    pallas_call x18, Pallas kernels, fuse(): return list(call(ids, *arrays))  31.4 us
    ppermute x7, starting transfers between devices, from_core(): return lax.ppermute(array, 'tp', [(i, i ^ 1) for i in range(8)])  25.7 us
    ppermute x12, starting transfers between devices, from_chip(): lax.ppermute(array, 'tp', [(i, (i + 2 * steps) % 8) for i in range(8)])  13 us
  transfers between devices with their start and end apart: 53, of which 22 were waited for; matrix products, arithmetic and copies ran while one was open for 1% of the time, Pallas kernels for 6%

profile of v1, /device:TPU:1, one launch (start us, length us, event | category | flops | bytes accessed | tf_op | source)
XLA Modules:
  0.0 167.1 jit_solution(6452044891577932095)
XLA Ops:
  1.3 2.7 %prepare.1 = (bf16[2,96,384]{2,1,0:T(8,128)(2,1)}, bf16[2,128,384]{2,1,0:T(8,128)(2,1)}, bf16[2,96,384]{2,1,0:T(8,128)(2,1)}) custom-call(s32[1,3]{1,0:T(1,128)} %add_bitcast_fusion.refs_0_, bf16[96,384]{1,0:T(8,128)(2,1)} %refs_1_.2, bf16[96,384]{1,0:T(8,128)(2,1)} %refs_2_.2, bf16[96,256]{1,0:T(8,128)(2,1)} %refs_3_.1, bf16[6,96]{1,0:T(8,128)(2,1)} %bitcast.32, ...), custom_call_target="tpu_custom_call" | custom-call | tf_op jit(solution)/shard_map/prepare/pallas_call | solution.py:85
  4.0 3.6 %collective-permute-start.2 = (bf16[2,96,384]{2,1,0:T(8,128)(2,1)}, bf16[2,96,384]{2,1,0:T(8,128)(2,1)S(1)}, u32[]{:S(2)}, u32[]{:S(2)}) collective-permute-start(bf16[2,96,384]{2,1,0:T(8,128)(2,1)} %get-tuple-element.99.refs_1_), channel_id=1, source_target_pairs={{0,24},{8,0},{16,8},{24,16},{1,25},{9,1},{17,9},{25,17},{2,26},{10... | collective-permute-start | bytes 442376 | tf_op jit(solution)/shard_map/ppermute | solution.py:650
  9.3 3.8 %collective-permute-start.5 = (bf16[2,96,384]{2,1,0:T(8,128)(2,1)}, bf16[2,96,384]{2,1,0:T(8,128)(2,1)S(1)}, u32[]{:S(2)}, u32[]{:S(2)}) collective-permute-start(bf16[2,96,384]{2,1,0:T(8,128)(2,1)} %get-tuple-element.101.refs_5_), channel_id=1, source_target_pairs={{0,96},{32,0},{64,32},{96,64},{1,97},{33,1},{65,33},{97,65},{2,98}... | collective-permute-start | bytes 442376 | tf_op jit(solution)/shard_map/ppermute | solution.py:650
  13.8 2.9 %collective-permute-done.1.refs_3_ = bf16[2,96,384]{2,1,0:T(8,128)(2,1)S(1)} collective-permute-done((bf16[2,96,384]{2,1,0:T(8,128)(2,1)}, bf16[2,96,384]{2,1,0:T(8,128)(2,1)S(1)}, u32[]{:S(2)}, u32[]{:S(2)}) %collective-permute-start.1) | collective-permute-done | bytes 147488 | tf_op jit(solution)/shard_map/ppermute | solution.py:650
  16.7 2.3 %collective-permute-done.5.refs_8_ = bf16[2,96,384]{2,1,0:T(8,128)(2,1)S(1)} collective-permute-done((bf16[2,96,384]{2,1,0:T(8,128)(2,1)}, bf16[2,96,384]{2,1,0:T(8,128)(2,1)S(1)}, u32[]{:S(2)}, u32[]{:S(2)}) %collective-permute-start.5) | collective-permute-done | bytes 147488 | tf_op jit(solution)/shard_map/ppermute | solution.py:650
  18.9 3.9 %collective-permute-done.3.refs_6_ = bf16[2,96,384]{2,1,0:T(8,128)(2,1)S(1)} collective-permute-done((bf16[2,96,384]{2,1,0:T(8,128)(2,1)}, bf16[2,96,384]{2,1,0:T(8,128)(2,1)S(1)}, u32[]{:S(2)}, u32[]{:S(2)}) %collective-permute-start.3) | collective-permute-done | bytes 147488 | tf_op jit(solution)/shard_map/ppermute | solution.py:650
  29.1 10.6 %collective-permute-done.8.refs_5_ = bf16[4,2,96,384]{3,2,1,0:T(8,128)(2,1)S(1)} collective-permute-done((bf16[4,2,96,384]{3,2,1,0:T(8,128)(2,1)S(1)}, bf16[4,2,96,384]{3,2,1,0:T(8,128)(2,1)S(1)}, u32[]{:S(2)}, u32[]{:S(2)}) %collective-permute-start.8) | collective-permute-done | bytes 589856 | tf_op jit(solution)/shard_map/ppermute | solution.py:650
  48.7 3.1 %enter.1 = (bf16[1536,768]{1,0:T(8,128)(2,1)S(1)}, bf16[272,1536]{1,0:T(8,128)(2,1)S(1)}, bf16[272,640]{1,0:T(8,128)(2,1)S(1)}, f32[256,1408]{1,0:T(8,128)S(1)},...) custom-call(s32[1,3]{1,0:T(1,128)S(1)} %copy-done.2, bf16[4,2,96,384]{3,2,1,0:T(8,128)(2,1)S(1)} %get-tuple-element.102.refs_1_, ...), custom_call_target="tpu_custom_call" | custom-call | tf_op jit(solution)/shard_map/enter/pallas_call | solution.py:85
  60.7 5.4 %collective-permute-start.17 = (f32[8,256]{1,0:T(8,128)S(1)}, f32[8,256]{1,0:T(8,128)S(1)}, u32[]{:S(2)}, u32[]{:S(2)}) collective-permute-start(f32[8,256]{1,0:T(8,128)S(1)} %get-tuple-element.112), channel_id=1, source_target_pairs={{0,1},{1,0},{2,3},{3,2},{4,5},{5,4},{6,7},{7,6},{8,9},{9,8},{10,11... | collective-permute-start | bytes 24584 | tf_op jit(solution)/shard_map/ppermute | solution.py:658
  66.9 2.5 %collective-permute-start.20 = (f32[8,256]{1,0:T(8,128)S(1)}, f32[8,256]{1,0:T(8,128)S(1)}, u32[]{:S(2)}, u32[]{:S(2)}) collective-permute-start(f32[8,256]{1,0:T(8,128)S(1)} %add.3.refs_1_), channel_id=1, source_target_pairs={{0,6},{1,7},{2,0},{3,1},{4,2},{5,3},{6,4},{7,5},{8,14},{9,15},{10,... | collective-permute-start | bytes 24584 | tf_op jit(solution)/shard_map/ppermute | solution.py:654
  70.5 2.9 %collective-permute-done.19.refs_3_ = f32[8,256]{1,0:T(8,128)S(1)} collective-permute-done((f32[8,256]{1,0:T(8,128)S(1)}, f32[8,256]{1,0:T(8,128)S(1)}, u32[]{:S(2)}, u32[]{:S(2)}) %collective-permute-start.19) | collective-permute-done | bytes 8224 | tf_op jit(solution)/shard_map/ppermute | solution.py:654
  75.2 2.2 %collective-permute-start.22 = (bf16[128,384]{1,0:T(8,128)(2,1)S(1)}, bf16[128,384]{1,0:T(8,128)(2,1)S(1)}, u32[]{:S(2)}, u32[]{:S(2)}) collective-permute-start(bf16[128,384]{1,0:T(8,128)(2,1)S(1)} %get-tuple-element.114), channel_id=1, source_target_pairs={{0,16},{8,24},{16,0},{24,8},{1,17},{9,25},{17,1},{25,9},{2,18},{10... | collective-permute-start | bytes 294920 | tf_op jit(solution)/shard_map/ppermute | solution.py:650
  78.5 2.9 %middle.1 = (bf16[1536,384]{1,0:T(8,128)(2,1)S(1)}, bf16[1536,384]{1,0:T(8,128)(2,1)S(1)}, f32[256,640]{1,0:T(8,128)S(1)}, bf16[256,1536]{1,0:T(8,128)(2,1)S(1)}) custom-call(s32[1,3]{1,0:T(1,128)S(1)} %copy-done.2, bf16[272,1536]{1,0:T(8,128)(2,1)S(1)} %get-tuple-element.110.refs_11_.refs_1_.refs_5_.refs_10_, ...), custom_call_target="tpu_custom_call" | custom-call | tf_op jit(solution)/shard_map/middle/pallas_call | solution.py:85
  81.8 3.4 %leave.1 = (bf16[272,512]{1,0:T(8,128)(2,1)S(1)}, f32[4,32,384]{2,1,0:T(8,128)S(1)}, f32[4,32,384]{2,1,0:T(8,128)S(1)}, f32[8,384]{1,0:T(8,128)S(1)}) custom-call(s32[1,3]{1,0:T(1,128)S(1)} %copy-done.2, bf16[128,384]{1,0:T(8,128)(2,1)S(1)} %collective-permute-done.21.refs_1_, bf16[128,384]{1,0:T(8,128)(2,1)S(1)} %collective-permute-done.22.refs_2_, ...), custom_call_target="tpu_custom_call" | custom-call | tf_op jit(solution)/shard_map/leave/pallas_call | solution.py:85
  85.2 3.2 %collective-permute-start.24 = (f32[4,32,384]{2,1,0:T(8,128)S(1)}, f32[4,32,384]{2,1,0:T(8,128)S(1)}, u32[]{:S(2)}, u32[]{:S(2)}) collective-permute-start(f32[4,32,384]{2,1,0:T(8,128)S(1)} %get-tuple-element.123), channel_id=1, source_target_pairs={{0,1},{1,0},{2,3},{3,2},{4,5},{5,4},{6,7},{7,6},{8,9},{9,8},{10,11... | collective-permute-start | bytes 589832 | tf_op jit(solution)/shard_map/ppermute | solution.py:658
  93.4 2.5 %value_grads.1 = (bf16[1536,384]{1,0:T(8,128)(2,1)S(1)}, f32[272,1536]{1,0:T(8,128)S(1)}) custom-call(s32[1,3]{1,0:T(1,128)S(1)} %copy-done.2, bf16[272,512]{1,0:T(8,128)(2,1)S(1)} %get-tuple-element.128.refs_1_.refs_5_, bf16[256,768]{1,0:T(8,128)(2,1)S(1)} %get-tuple-element.117.refs_2_, bf16[1536,768]{1,0:T(8,128)(2,1)S(1)} %get-tuple-element.130.refs_3_.refs_8_.refs_6_, ...), custom_call_target="tpu_custom_call" | custom-call | tf_op jit(solution)/shard_map/value_grads/pallas_call | solution.py:85
  96.0 2.1 %late_grads.1 = (bf16[256,1536]{1,0:T(8,128)(2,1)S(1)}, bf16[4,96,640]{2,1,0:T(8,128)(2,1)S(1)}, bf16[4,96,640]{2,1,0:T(8,128)(2,1)S(1)}, bf16[2,96,640]{2,1,0:T...) custom-call(s32[1,3]{1,0:T(1,128)S(1)} %copy-done.2, ...), custom_call_target="tpu_custom_call" | custom-call | tf_op jit(solution)/shard_map/late_grads/pallas_call | solution.py:85
  98.1 2.5 %collective-permute-start.31 = (bf16[2,128,640]{2,1,0:T(8,128)(2,1)S(1)}, bf16[2,128,640]{2,1,0:T(8,128)(2,1)S(1)}, u32[]{:S(2)}, u32[]{:S(2)}) collective-permute-start(bf16[2,128,640]{2,1,0:T(8,128)(2,1)S(1)} %get-tuple-element.143), channel_id=1, source_target_pairs={{0,24},{8,0},{16,8},{24,16},{1,25},{9,1},{17,9},{25,17},{2,26},{10... | collective-permute-start | bytes 983048 | tf_op jit(solution)/shard_map/ppermute | solution.py:650
  100.6 2.7 %collective-permute-start.29 = (bf16[2,96,640]{2,1,0:T(8,128)(2,1)S(1)}, bf16[2,96,640]{2,1,0:T(8,128)(2,1)S(1)}, u32[]{:S(2)}, u32[]{:S(2)}) collective-permute-start(bf16[2,96,640]{2,1,0:T(8,128)(2,1)S(1)} %get-tuple-element.139), channel_id=1, source_target_pairs={{0,96},{32,0},{64,32},{96,64},{1,97},{33,1},{65,33},{97,65},{2,98}... | collective-permute-start | bytes 737288 | tf_op jit(solution)/shard_map/ppermute | solution.py:650
  103.3 4.5 %collective-permute-done.28.refs_3_ = bf16[2,96,640]{2,1,0:T(8,128)(2,1)S(1)} collective-permute-done((bf16[2,96,640]{2,1,0:T(8,128)(2,1)S(1)}, bf16[2,96,640]{2,1,0:T(8,128)(2,1)S(1)}, u32[]{:S(2)}, u32[]{:S(2)}) %collective-permute-start.28) | collective-permute-done | bytes 245792 | tf_op jit(solution)/shard_map/ppermute | solution.py:650
  107.8 2.1 %collective-permute-done.30.refs_7_ = bf16[2,96,640]{2,1,0:T(8,128)(2,1)S(1)} collective-permute-done((bf16[2,96,640]{2,1,0:T(8,128)(2,1)S(1)}, bf16[2,96,640]{2,1,0:T(8,128)(2,1)S(1)}, u32[]{:S(2)}, u32[]{:S(2)}) %collective-permute-start.30) | collective-permute-done | bytes 245792 | tf_op jit(solution)/shard_map/ppermute | solution.py:650
  111.0 3.1 %collective-permute-start.36 = (bf16[4,64,1536]{2,1,0:T(8,128)(2,1)S(1)}, bf16[4,64,1536]{2,1,0:T(8,128)(2,1)S(1)}, u32[]{:S(2)}, u32[]{:S(2)}) collective-permute-start(bf16[4,64,1536]{2,1,0:T(8,128)(2,1)S(1)} %get-tuple-element.152), channel_id=1, source_target_pairs={{0,1},{1,0},{2,3},{3,2},{4,5},{5,4},{6,7},{7,6},{8,9},{9,8},{10,11... | collective-permute-start | bytes 2359304 | tf_op jit(solution)/shard_map/ppermute | solution.py:658
  114.0 2.7 %collective-permute-start.33 = (bf16[4,96,640]{2,1,0:T(8,128)(2,1)S(1)}, bf16[4,96,640]{2,1,0:T(8,128)(2,1)S(1)}, u32[]{:S(2)}, u32[]{:S(2)}) collective-permute-start(bf16[4,96,640]{2,1,0:T(8,128)(2,1)S(1)} %get-tuple-element.147), channel_id=1, source_target_pairs={{0,96},{32,0},{64,32},{96,64},{1,97},{33,1},{65,33},{97,65},{2,98}... | collective-permute-start | bytes 1474568 | tf_op jit(solution)/shard_map/ppermute | solution.py:650
  116.7 2.7 %collective-permute-start.35 = (bf16[4,96,640]{2,1,0:T(8,128)(2,1)S(1)}, bf16[4,96,640]{2,1,0:T(8,128)(2,1)S(1)}, u32[]{:S(2)}, u32[]{:S(2)}) collective-permute-start(bf16[4,96,640]{2,1,0:T(8,128)(2,1)S(1)} %get-tuple-element.150), channel_id=1, source_target_pairs={{0,24},{8,0},{16,8},{24,16},{1,25},{9,1},{17,9},{25,17},{2,26},{10... | collective-permute-start | bytes 1474568 | tf_op jit(solution)/shard_map/ppermute | solution.py:650
  121.2 6.8 %collective-permute-done.32.refs_2_ = bf16[4,96,640]{2,1,0:T(8,128)(2,1)S(1)} collective-permute-done((bf16[4,96,640]{2,1,0:T(8,128)(2,1)S(1)}, bf16[4,96,640]{2,1,0:T(8,128)(2,1)S(1)}, u32[]{:S(2)}, u32[]{:S(2)}) %collective-permute-start.32) | collective-permute-done | bytes 491552 | tf_op jit(solution)/shard_map/ppermute | solution.py:650
  132.5 2.1 %collective-permute-start.38 = (bf16[96,640]{1,0:T(8,128)(2,1)S(1)}, bf16[96,640]{1,0:T(8,128)(2,1)S(1)}, u32[]{:S(2)}, u32[]{:S(2)}) collective-permute-start(bf16[96,640]{1,0:T(8,128)(2,1)S(1)} %get-tuple-element.156), channel_id=1, source_target_pairs={{0,16},{8,24},{16,0},{24,8},{1,17},{9,25},{17,1},{25,9},{2,18},{10... | collective-permute-start | bytes 368648 | tf_op jit(solution)/shard_map/ppermute | solution.py:650
  134.6 4.8 %collective-permute-done.37.refs_2_ = bf16[96,640]{1,0:T(8,128)(2,1)S(1)} collective-permute-done((bf16[96,640]{1,0:T(8,128)(2,1)S(1)}, bf16[96,640]{1,0:T(8,128)(2,1)S(1)}, u32[]{:S(2)}, u32[]{:S(2)}) %collective-permute-start.37) | collective-permute-done | bytes 122912 | tf_op jit(solution)/shard_map/ppermute | solution.py:650
  143.1 2.5 %collective-permute-done.40.refs_6_ = bf16[96,640]{1,0:T(8,128)(2,1)S(1)} collective-permute-done((bf16[96,640]{1,0:T(8,128)(2,1)S(1)}, bf16[96,640]{1,0:T(8,128)(2,1)S(1)}, u32[]{:S(2)}, u32[]{:S(2)}) %collective-permute-start.40) | collective-permute-done | bytes 122912 | tf_op jit(solution)/shard_map/ppermute | solution.py:650
  149.5 5.3 %collective-permute-start.49 = (bf16[80,1536]{1,0:T(8,128)(2,1)S(1)}, bf16[80,1536]{1,0:T(8,128)(2,1)S(1)}, u32[]{:S(2)}, u32[]{:S(2)}) collective-permute-start(bf16[80,1536]{1,0:T(8,128)(2,1)S(1)} %get-tuple-element.165.refs_1_), channel_id=1, source_target_pairs={{0,1},{1,0},{2,3},{3,2},{4,5},{5,4},{6,7},{7,6},{8,9},{9,8},{10,11... | collective-permute-start | bytes 737288 | tf_op jit(solution)/shard_map/ppermute | solution.py:658
  154.8 4.3 %collective-permute-start.52 = (bf16[80,1536]{1,0:T(8,128)(2,1)S(1)}, bf16[80,1536]{1,0:T(8,128)(2,1)S(1)}, u32[]{:S(2)}, u32[]{:S(2)}) collective-permute-start(bf16[80,1536]{1,0:T(8,128)(2,1)S(1)} %collective-permute-done.48.refs_4_), channel_id=1, source_target_pairs={{0,1},{1,0},{2,3},{3,2},{4,5},{5,4},{6,7},{7,6},{8,9},{9,8},{10,11... | collective-permute-start | bytes 737288 | tf_op jit(solution)/shard_map/ppermute | solution.py:658
  161.0 2.5 %collective-permute-start.50 = (bf16[80,1536]{1,0:T(8,128)(2,1)S(1)}, bf16[80,1536]{1,0:T(8,128)(2,1)S(1)}, u32[]{:S(2)}, u32[]{:S(2)}) collective-permute-start(bf16[80,1536]{1,0:T(8,128)(2,1)S(1)} %collective-permute-done.46.refs_2_), channel_id=1, source_target_pairs={{0,1},{1,0},{2,3},{3,2},{4,5},{5,4},{6,7},{7,6},{8,9},{9,8},{10,11... | collective-permute-start | bytes 737288 | tf_op jit(solution)/shard_map/ppermute | solution.py:658
  164.7 2.4 %finish.1 = (f32[256,1536]{1,0:T(8,128)}, bf16[256,1536]{1,0:T(8,128)(2,1)}, f32[96,256]{1,0:T(8,128)}, f32[1,96]{1,0:T(1,128)}, f32[4,256]{1,0:T(4,128)}, /*index=5*/f32[1,256]{1,0:T(1,128)}) custom-call(s32[1,3]{1,0:T(1,128)S(1)} %copy-done.3, bf16[80,1536]{1,0:T(8,128)(2,1)S(1)} %get-tuple-element.165.refs_1_, ...), custom_call_target="tpu_custom_call" | custom-call | tf_op jit(solution)/shard_map/finish/pallas_call | solution.py:85
  (131 shorter events, 55.3 us)
Async XLA Ops:
  4.0 9.0 %collective-permute-start.2 = (bf16[2,96,384]{2,1,0:T(8,128)(2,1)}, bf16[2,96,384]{2,1,0:T(8,128)(2,1)S(1)}, u32[]{:S(2)}, u32[]{:S(2)}) collective-permute-start(bf16[2,96,384]{2,1,0:T(8,128)(2,1)} %get-tuple-element.99.refs_1_), channel_id=1, source_target_pairs={{0,24},{8,0},{16,8},{24,16},{1,25},{9,1},{17,9},{25,17},{2,26},{10... | collective-permute-start | bytes 442376 | tf_op jit(solution)/shard_map/ppermute | solution.py:650
  7.7 15.1 %collective-permute-start = (bf16[2,128,384]{2,1,0:T(8,128)(2,1)}, bf16[2,128,384]{2,1,0:T(8,128)(2,1)S(1)}, u32[]{:S(2)}, u32[]{:S(2)}) collective-permute-start(bf16[2,128,384]{2,1,0:T(8,128)(2,1)} %get-tuple-element.100), channel_id=1, source_target_pairs={{0,8},{8,16},{16,24},{24,0},{1,9},{9,17},{17,25},{25,1},{2,10},{10... | collective-permute-start | bytes 589832 | tf_op jit(solution)/shard_map/ppermute | solution.py:650
  7.7 9.0 %collective-permute-start.1 = (bf16[2,96,384]{2,1,0:T(8,128)(2,1)}, bf16[2,96,384]{2,1,0:T(8,128)(2,1)S(1)}, u32[]{:S(2)}, u32[]{:S(2)}) collective-permute-start(bf16[2,96,384]{2,1,0:T(8,128)(2,1)} %get-tuple-element.99.refs_1_), channel_id=1, source_target_pairs={{0,16},{8,24},{16,0},{24,8},{1,17},{9,25},{17,1},{25,9},{2,18},{10... | collective-permute-start | bytes 442376 | tf_op jit(solution)/shard_map/ppermute | solution.py:650
  9.3 9.6 %collective-permute-start.5 = (bf16[2,96,384]{2,1,0:T(8,128)(2,1)}, bf16[2,96,384]{2,1,0:T(8,128)(2,1)S(1)}, u32[]{:S(2)}, u32[]{:S(2)}) collective-permute-start(bf16[2,96,384]{2,1,0:T(8,128)(2,1)} %get-tuple-element.101.refs_5_), channel_id=1, source_target_pairs={{0,96},{32,0},{64,32},{96,64},{1,97},{33,1},{65,33},{97,65},{2,98}... | collective-permute-start | bytes 442376 | tf_op jit(solution)/shard_map/ppermute | solution.py:650
  13.1 9.7 %collective-permute-start.3 = (bf16[2,96,384]{2,1,0:T(8,128)(2,1)}, bf16[2,96,384]{2,1,0:T(8,128)(2,1)S(1)}, u32[]{:S(2)}, u32[]{:S(2)}) collective-permute-start(bf16[2,96,384]{2,1,0:T(8,128)(2,1)} %get-tuple-element.101.refs_5_), channel_id=1, source_target_pairs={{0,32},{32,64},{64,96},{96,0},{1,33},{33,65},{65,97},{97,1},{2,34}... | collective-permute-start | bytes 442376 | tf_op jit(solution)/shard_map/ppermute | solution.py:650
  25.9 13.8 %collective-permute-start.8 = (bf16[4,2,96,384]{3,2,1,0:T(8,128)(2,1)S(1)}, bf16[4,2,96,384]{3,2,1,0:T(8,128)(2,1)S(1)}, u32[]{:S(2)}, u32[]{:S(2)}) collective-permute-start(bf16[4,2,96,384]{3,2,1,0:T(8,128)(2,1)S(1)} %get-tuple-element.102.refs_1_), channel_id=1, source_target_pairs={{0,96},{32,0},{64,32},{96,64},{1,97},{33,1},{65,33},{97,65},{2,98}... | collective-permute-start | bytes 1769480 | tf_op jit(solution)/shard_map/ppermute | solution.py:650
  26.0 14.4 %collective-permute-start.6 = (bf16[4,2,96,384]{3,2,1,0:T(8,128)(2,1)S(1)}, bf16[4,2,96,384]{3,2,1,0:T(8,128)(2,1)S(1)}, u32[]{:S(2)}, u32[]{:S(2)}) collective-permute-start(bf16[4,2,96,384]{3,2,1,0:T(8,128)(2,1)S(1)} %get-tuple-element.102.refs_1_), channel_id=1, source_target_pairs={{0,32},{32,64},{64,96},{96,0},{1,33},{33,65},{65,97},{97,1},{2,34}... | collective-permute-start | bytes 1769480 | tf_op jit(solution)/shard_map/ppermute | solution.py:650
  27.4 13.9 %collective-permute-start.12 = (bf16[4,2,96,384]{3,2,1,0:T(8,128)(2,1)S(1)}, bf16[4,2,96,384]{3,2,1,0:T(8,128)(2,1)S(1)}, u32[]{:S(2)}, u32[]{:S(2)}) collective-permute-start(bf16[4,2,96,384]{3,2,1,0:T(8,128)(2,1)S(1)} %get-tuple-element.103.refs_6_), channel_id=1, source_target_pairs={{0,24},{8,0},{16,8},{24,16},{1,25},{9,1},{17,9},{25,17},{2,26},{10... | collective-permute-start | bytes 1769480 | tf_op jit(solution)/shard_map/ppermute | solution.py:650
  27.5 14.0 %collective-permute-start.10 = (bf16[4,2,96,384]{3,2,1,0:T(8,128)(2,1)S(1)}, bf16[4,2,96,384]{3,2,1,0:T(8,128)(2,1)S(1)}, u32[]{:S(2)}, u32[]{:S(2)}) collective-permute-start(bf16[4,2,96,384]{3,2,1,0:T(8,128)(2,1)S(1)} %get-tuple-element.103.refs_6_), channel_id=1, source_target_pairs={{0,8},{8,16},{16,24},{24,0},{1,9},{9,17},{17,25},{25,1},{2,10},{10... | collective-permute-start | bytes 1769480 | tf_op jit(solution)/shard_map/ppermute | solution.py:650
  39.7 6.5 %collective-permute-start.9 = (bf16[2,2,96,384]{3,2,1,0:T(8,128)(2,1)S(1)}, bf16[2,2,96,384]{3,2,1,0:T(8,128)(2,1)S(1)}, u32[]{:S(2)}, u32[]{:S(2)}) collective-permute-start(bf16[2,2,96,384]{3,2,1,0:T(8,128)(2,1)S(1)} %slice.17), channel_id=1, source_target_pairs={{0,96},{32,0},{64,32},{96,64},{1,97},{33,1},{65,33},{97,65},{2,98}... | collective-permute-start | bytes 884744 | tf_op jit(solution)/shard_map/ppermute | solution.py:650
  40.4 6.9 %collective-permute-start.7 = (bf16[2,2,96,384]{3,2,1,0:T(8,128)(2,1)S(1)}, bf16[2,2,96,384]{3,2,1,0:T(8,128)(2,1)S(1)}, u32[]{:S(2)}, u32[]{:S(2)}) collective-permute-start(bf16[2,2,96,384]{3,2,1,0:T(8,128)(2,1)S(1)} %slice.16), channel_id=1, source_target_pairs={{0,32},{32,64},{64,96},{96,0},{1,33},{33,65},{65,97},{97,1},{2,34}... | collective-permute-start | bytes 884744 | tf_op jit(solution)/shard_map/ppermute | solution.py:650
  41.5 7.1 %collective-permute-start.11 = (bf16[2,2,96,384]{3,2,1,0:T(8,128)(2,1)S(1)}, bf16[2,2,96,384]{3,2,1,0:T(8,128)(2,1)S(1)}, u32[]{:S(2)}, u32[]{:S(2)}) collective-permute-start(bf16[2,2,96,384]{3,2,1,0:T(8,128)(2,1)S(1)} %slice.18), channel_id=1, source_target_pairs={{0,8},{8,16},{16,24},{24,0},{1,9},{9,17},{17,25},{25,1},{2,10},{10... | collective-permute-start | bytes 884744 | tf_op jit(solution)/shard_map/ppermute | solution.py:650
  98.1 11.7 %collective-permute-start.31 = (bf16[2,128,640]{2,1,0:T(8,128)(2,1)S(1)}, bf16[2,128,640]{2,1,0:T(8,128)(2,1)S(1)}, u32[]{:S(2)}, u32[]{:S(2)}) collective-permute-start(bf16[2,128,640]{2,1,0:T(8,128)(2,1)S(1)} %get-tuple-element.143), channel_id=1, source_target_pairs={{0,24},{8,0},{16,8},{24,16},{1,25},{9,1},{17,9},{25,17},{2,26},{10... | collective-permute-start | bytes 983048 | tf_op jit(solution)/shard_map/ppermute | solution.py:650
  100.6 7.2 %collective-permute-start.28 = (bf16[2,96,640]{2,1,0:T(8,128)(2,1)S(1)}, bf16[2,96,640]{2,1,0:T(8,128)(2,1)S(1)}, u32[]{:S(2)}, u32[]{:S(2)}) collective-permute-start(bf16[2,96,640]{2,1,0:T(8,128)(2,1)S(1)} %get-tuple-element.138), channel_id=1, source_target_pairs={{0,32},{32,64},{64,96},{96,0},{1,33},{33,65},{65,97},{97,1},{2,34}... | collective-permute-start | bytes 737288 | tf_op jit(solution)/shard_map/ppermute | solution.py:650
  100.6 7.2 %collective-permute-start.29 = (bf16[2,96,640]{2,1,0:T(8,128)(2,1)S(1)}, bf16[2,96,640]{2,1,0:T(8,128)(2,1)S(1)}, u32[]{:S(2)}, u32[]{:S(2)}) collective-permute-start(bf16[2,96,640]{2,1,0:T(8,128)(2,1)S(1)} %get-tuple-element.139), channel_id=1, source_target_pairs={{0,96},{32,0},{64,32},{96,64},{1,97},{33,1},{65,33},{97,65},{2,98}... | collective-permute-start | bytes 737288 | tf_op jit(solution)/shard_map/ppermute | solution.py:650
  103.3 6.6 %collective-permute-start.30 = (bf16[2,96,640]{2,1,0:T(8,128)(2,1)S(1)}, bf16[2,96,640]{2,1,0:T(8,128)(2,1)S(1)}, u32[]{:S(2)}, u32[]{:S(2)}) collective-permute-start(bf16[2,96,640]{2,1,0:T(8,128)(2,1)S(1)} %get-tuple-element.142), channel_id=1, source_target_pairs={{0,8},{8,16},{16,24},{24,0},{1,9},{9,17},{17,25},{25,1},{2,10},{10... | collective-permute-start | bytes 737288 | tf_op jit(solution)/shard_map/ppermute | solution.py:650
  111.0 8.4 %collective-permute-start.36 = (bf16[4,64,1536]{2,1,0:T(8,128)(2,1)S(1)}, bf16[4,64,1536]{2,1,0:T(8,128)(2,1)S(1)}, u32[]{:S(2)}, u32[]{:S(2)}) collective-permute-start(bf16[4,64,1536]{2,1,0:T(8,128)(2,1)S(1)} %get-tuple-element.152), channel_id=1, source_target_pairs={{0,1},{1,0},{2,3},{3,2},{4,5},{5,4},{6,7},{7,6},{8,9},{9,8},{10,11... | collective-permute-start | bytes 2359304 | tf_op jit(solution)/shard_map/ppermute | solution.py:658
  114.0 14.0 %collective-permute-start.32 = (bf16[4,96,640]{2,1,0:T(8,128)(2,1)S(1)}, bf16[4,96,640]{2,1,0:T(8,128)(2,1)S(1)}, u32[]{:S(2)}, u32[]{:S(2)}) collective-permute-start(bf16[4,96,640]{2,1,0:T(8,128)(2,1)S(1)} %get-tuple-element.146), channel_id=1, source_target_pairs={{0,32},{32,64},{64,96},{96,0},{1,33},{33,65},{65,97},{97,1},{2,34}... | collective-permute-start | bytes 1474568 | tf_op jit(solution)/shard_map/ppermute | solution.py:650
  114.0 15.7 %collective-permute-start.33 = (bf16[4,96,640]{2,1,0:T(8,128)(2,1)S(1)}, bf16[4,96,640]{2,1,0:T(8,128)(2,1)S(1)}, u32[]{:S(2)}, u32[]{:S(2)}) collective-permute-start(bf16[4,96,640]{2,1,0:T(8,128)(2,1)S(1)} %get-tuple-element.147), channel_id=1, source_target_pairs={{0,96},{32,0},{64,32},{96,64},{1,97},{33,1},{65,33},{97,65},{2,98}... | collective-permute-start | bytes 1474568 | tf_op jit(solution)/shard_map/ppermute | solution.py:650
  116.7 14.7 %collective-permute-start.34 = (bf16[4,96,640]{2,1,0:T(8,128)(2,1)S(1)}, bf16[4,96,640]{2,1,0:T(8,128)(2,1)S(1)}, u32[]{:S(2)}, u32[]{:S(2)}) collective-permute-start(bf16[4,96,640]{2,1,0:T(8,128)(2,1)S(1)} %get-tuple-element.149), channel_id=1, source_target_pairs={{0,8},{8,16},{16,24},{24,0},{1,9},{9,17},{17,25},{25,1},{2,10},{10... | collective-permute-start | bytes 1474568 | tf_op jit(solution)/shard_map/ppermute | solution.py:650
  116.7 14.7 %collective-permute-start.35 = (bf16[4,96,640]{2,1,0:T(8,128)(2,1)S(1)}, bf16[4,96,640]{2,1,0:T(8,128)(2,1)S(1)}, u32[]{:S(2)}, u32[]{:S(2)}) collective-permute-start(bf16[4,96,640]{2,1,0:T(8,128)(2,1)S(1)} %get-tuple-element.150), channel_id=1, source_target_pairs={{0,24},{8,0},{16,8},{24,16},{1,25},{9,1},{17,9},{25,17},{2,26},{10... | collective-permute-start | bytes 1474568 | tf_op jit(solution)/shard_map/ppermute | solution.py:650
  120.1 19.3 %collective-permute-start.43 = (bf16[64,1536]{1,0:T(8,128)(2,1)S(1)}, bf16[64,1536]{1,0:T(8,128)(2,1)S(1)}, u32[]{:S(2)}, u32[]{:S(2)}) collective-permute-start(bf16[64,1536]{1,0:T(8,128)(2,1)S(1)} %get-tuple-element.162), channel_id=1, source_target_pairs={{0,2},{1,3},{2,4},{3,5},{4,6},{5,7},{6,0},{7,1},{8,10},{9,11},{10,... | collective-permute-start | bytes 589832 | tf_op jit(solution)/shard_map/ppermute | solution.py:654
  128.0 11.4 %collective-permute-start.44 = (bf16[64,1536]{1,0:T(8,128)(2,1)S(1)}, bf16[64,1536]{1,0:T(8,128)(2,1)S(1)}, u32[]{:S(2)}, u32[]{:S(2)}) collective-permute-start(bf16[64,1536]{1,0:T(8,128)(2,1)S(1)} %get-tuple-element.163), channel_id=1, source_target_pairs={{0,4},{1,5},{2,6},{3,7},{4,0},{5,1},{6,2},{7,3},{8,12},{9,13},{10,... | collective-permute-start | bytes 589832 | tf_op jit(solution)/shard_map/ppermute | solution.py:654
  129.7 11.7 %collective-permute-start.45 = (bf16[64,1536]{1,0:T(8,128)(2,1)S(1)}, bf16[64,1536]{1,0:T(8,128)(2,1)S(1)}, u32[]{:S(2)}, u32[]{:S(2)}) collective-permute-start(bf16[64,1536]{1,0:T(8,128)(2,1)S(1)} %get-tuple-element.164), channel_id=1, source_target_pairs={{0,6},{1,7},{2,0},{3,1},{4,2},{5,3},{6,4},{7,5},{8,14},{9,15},{10,... | collective-permute-start | bytes 589832 | tf_op jit(solution)/shard_map/ppermute | solution.py:654
  132.4 7.0 %collective-permute-start.37 = (bf16[96,640]{1,0:T(8,128)(2,1)S(1)}, bf16[96,640]{1,0:T(8,128)(2,1)S(1)}, u32[]{:S(2)}, u32[]{:S(2)}) collective-permute-start(bf16[96,640]{1,0:T(8,128)(2,1)S(1)} %get-tuple-element.155), channel_id=1, source_target_pairs={{0,8},{8,16},{16,24},{24,0},{1,9},{9,17},{17,25},{25,1},{2,10},{10... | collective-permute-start | bytes 368648 | tf_op jit(solution)/shard_map/ppermute | solution.py:650
  132.5 10.6 %collective-permute-start.38 = (bf16[96,640]{1,0:T(8,128)(2,1)S(1)}, bf16[96,640]{1,0:T(8,128)(2,1)S(1)}, u32[]{:S(2)}, u32[]{:S(2)}) collective-permute-start(bf16[96,640]{1,0:T(8,128)(2,1)S(1)} %get-tuple-element.156), channel_id=1, source_target_pairs={{0,16},{8,24},{16,0},{24,8},{1,17},{9,25},{17,1},{25,9},{2,18},{10... | collective-permute-start | bytes 368648 | tf_op jit(solution)/shard_map/ppermute | solution.py:650
  139.4 6.3 %collective-permute-start.40 = (bf16[96,640]{1,0:T(8,128)(2,1)S(1)}, bf16[96,640]{1,0:T(8,128)(2,1)S(1)}, u32[]{:S(2)}, u32[]{:S(2)}) collective-permute-start(bf16[96,640]{1,0:T(8,128)(2,1)S(1)} %get-tuple-element.159), channel_id=1, source_target_pairs={{0,32},{32,64},{64,96},{96,0},{1,33},{33,65},{65,97},{97,1},{2,34}... | collective-permute-start | bytes 368648 | tf_op jit(solution)/shard_map/ppermute | solution.py:650
  148.0 6.7 %collective-permute-start.48 = (bf16[80,1536]{1,0:T(8,128)(2,1)S(1)}, bf16[80,1536]{1,0:T(8,128)(2,1)S(1)}, u32[]{:S(2)}, u32[]{:S(2)}) collective-permute-start(bf16[80,1536]{1,0:T(8,128)(2,1)S(1)} %get-tuple-element.165.refs_1_), channel_id=1, source_target_pairs={{0,6},{1,7},{2,0},{3,1},{4,2},{5,3},{6,4},{7,5},{8,14},{9,15},{10,... | collective-permute-start | bytes 737288 | tf_op jit(solution)/shard_map/ppermute | solution.py:654
  148.2 10.8 %collective-permute-start.47 = (bf16[80,1536]{1,0:T(8,128)(2,1)S(1)}, bf16[80,1536]{1,0:T(8,128)(2,1)S(1)}, u32[]{:S(2)}, u32[]{:S(2)}) collective-permute-start(bf16[80,1536]{1,0:T(8,128)(2,1)S(1)} %get-tuple-element.165.refs_1_), channel_id=1, source_target_pairs={{0,4},{1,5},{2,6},{3,7},{4,0},{5,1},{6,2},{7,3},{8,12},{9,13},{10,... | collective-permute-start | bytes 737288 | tf_op jit(solution)/shard_map/ppermute | solution.py:654
  148.8 12.2 %collective-permute-start.46 = (bf16[80,1536]{1,0:T(8,128)(2,1)S(1)}, bf16[80,1536]{1,0:T(8,128)(2,1)S(1)}, u32[]{:S(2)}, u32[]{:S(2)}) collective-permute-start(bf16[80,1536]{1,0:T(8,128)(2,1)S(1)} %get-tuple-element.165.refs_1_), channel_id=1, source_target_pairs={{0,2},{1,3},{2,4},{3,5},{4,6},{5,7},{6,0},{7,1},{8,10},{9,11},{10,... | collective-permute-start | bytes 737288 | tf_op jit(solution)/shard_map/ppermute | solution.py:654
  149.5 15.2 %collective-permute-start.49 = (bf16[80,1536]{1,0:T(8,128)(2,1)S(1)}, bf16[80,1536]{1,0:T(8,128)(2,1)S(1)}, u32[]{:S(2)}, u32[]{:S(2)}) collective-permute-start(bf16[80,1536]{1,0:T(8,128)(2,1)S(1)} %get-tuple-element.165.refs_1_), channel_id=1, source_target_pairs={{0,1},{1,0},{2,3},{3,2},{4,5},{5,4},{6,7},{7,6},{8,9},{9,8},{10,11... | collective-permute-start | bytes 737288 | tf_op jit(solution)/shard_map/ppermute | solution.py:658
  154.8 9.9 %collective-permute-start.52 = (bf16[80,1536]{1,0:T(8,128)(2,1)S(1)}, bf16[80,1536]{1,0:T(8,128)(2,1)S(1)}, u32[]{:S(2)}, u32[]{:S(2)}) collective-permute-start(bf16[80,1536]{1,0:T(8,128)(2,1)S(1)} %collective-permute-done.48.refs_4_), channel_id=1, source_target_pairs={{0,1},{1,0},{2,3},{3,2},{4,5},{5,4},{6,7},{7,6},{8,9},{9,8},{10,11... | collective-permute-start | bytes 737288 | tf_op jit(solution)/shard_map/ppermute | solution.py:658
  (35 other events, 491.4 us)

commit v2 on v1

--- a/solution.py
+++ b/solution.py
@@ -22,7 +22,10 @@
 FIRST = MIX + 128
 ROWS = 96
 SHARES = 16
-HALF = 640
+NEAR = WIDE + WIDE + 128
+FAR = MIX + 2 * WIDE - NEAR + 128
+LEFT = 2 * WIDE
+RIGHT = WIDE + 128
 RIM_SLOTS = ((0, ROWS), (0, ROWS + RIM), (1, ROWS))
 SHARE = T // 8
 REST = ROWS + 16
@@ -32,7 +35,6 @@
 STATE_LANE = 64
 TURNED = 384
 VMEM_LIMIT = 16 * 2**20
-VMEM_WHOLE = 65_500_000
 
 VALUES, SLOPE = slice(0, WIDE), slice(WIDE, WIDE + MIX)
 STEP, STEP_SLOPE, LOG_DECAY = slice(1024, 1152), slice(1152, 1280), slice(1280, 1408)
@@ -79,9 +81,11 @@
         + [pl.BlockSpec(memory_space=space) for _ in arrays],
         out_specs=[pl.BlockSpec(memory_space=pltpu.VMEM) for _ in outputs],
         scratch_shapes=buffers,
-        compiler_params=pltpu.CompilerParams(vmem_limit_bytes=VMEM_WHOLE if fetch else VMEM_LIMIT),
+        compiler_params=pltpu.CompilerParams(vmem_limit_bytes=VMEM_LIMIT),
         name=function.__name__,
     )
+    if fetch:
+        arrays = [pltpu.with_memory_space_constraint(array, pltpu.HBM) for array in arrays]
     return list(call(ids, *arrays))
 
 
@@ -160,61 +164,63 @@
 def prepare(
     ids, value_weight, gate_weight, state_proj, step_proj, norm_gain, out_weight, rim, left, longer, right
 ):
-    left[0] = value_weight[...]
-    left[1] = gate_weight[...]
-    longer[0, :ROWS] = value_weight[...]
-    longer[1, :ROWS] = gate_weight[...]
-    for chunk in range(4):
-        start = ROWS + RIM * (chunk % 2)
-        longer[chunk // 2, start : start + RIM] = rim[:, WIDE * chunk : WIDE * chunk + WIDE]
-    right[0, :, : 2 * STATE] = state_proj[...]
+    for target in (left, longer):
+        target[:ROWS, :WIDE] = value_weight[...]
+        target[:ROWS, WIDE : 2 * WIDE] = gate_weight[...]
+        target[:ROWS, 2 * WIDE :] = out_weight[:, :128]
+    longer[ROWS : ROWS + RIM] = rim[:, :NEAR]
+    longer[ROWS + RIM :, : D - NEAR] = rim[:, NEAR:]
+    right[:, : 2 * STATE] = state_proj[...]
     place = iota((HEADS, 128), 1) == STEP_LANE + iota((HEADS, 128), 0)
     tail = dot_first(step_proj[...], flag(place))
     tail = tail + dot_first(norm_gain[...], flag(iota((1, 128), 1) == GAIN_LANE))
-    right[0, :, 2 * STATE :] = tail.astype(BF16)
-    right[1] = out_weight[...]
+    right[:, 2 * STATE : WIDE] = tail.astype(BF16)
+    right[:, WIDE:] = out_weight[:, 128:]
 
 
 def tabulate(
-    ids, value_filter, state_filter, value_offset, state_offset, gate_gain, step_bias, decay_log, skip_gain,
-    rim, hidden, consts, units,
-):
-    units[:RIM] = unit_rows(rim[...])
-    units[RIM:] = unit_rows(hidden[...])
+    ids, value_filter, state_filter, value_offset, state_offset, gate_gain, heads, hidden, consts, units
+):
+    units[...] = unit_rows(hidden[...])
     consts[...] = jnp.zeros(consts.shape, F32)
     consts[:KERNEL, :WIDE] = value_filter[...].astype(F32)
     consts[:KERNEL, WIDE:MIX] = state_filter[...].astype(F32)
     consts[KERNEL : KERNEL + 1, :WIDE] = value_offset[...].astype(F32)
     consts[KERNEL : KERNEL + 1, WIDE:MIX] = state_offset[...].astype(F32)
     consts[5:6, :WIDE] = gate_gain[...].astype(F32)
-    consts[6:7, :HEADS] = step_bias[...]
-    consts[7:8, :HEADS] = decay_log[...]
-    consts[8:9, :HEADS] = skip_gain[...]
-
-
-def place_blocks(ids, left, right, which, target):
+    consts[6:9, :HEADS] = heads[...]
+
+
+def place_blocks(ids, left, right, *moves):
     line, ctx = ids[0, 0], ids[0, 1]
 
     def piece(side, far, near):
         if far == 2:
-            return side[2][near, which] if near < 2 else side[3][near - 2, which]
-        return side[far + far // 3][near, which]
+            return (side[2], near) if near < 2 else (side[3], near - 2)
+        return side[far + far // 3], near
 
     for far in range(4):
         for near in range(4):
-            block = ((line - far) & 3) * 4 + ((ctx - near) & 3)
-            target[aligned(block * ROWS, ROWS), :WIDE] = piece(left, far, near)
-            block = ((line - near) & 3) * 4 + ((ctx - far) & 3)
-            target[aligned(block * ROWS, ROWS), WIDE:] = piece(right, far, near)
+            for target, side, start, source, size in moves:
+                if side == 0:
+                    block = ((line - far) & 3) * 4 + ((ctx - near) & 3)
+                else:
+                    block = ((line - near) & 3) * 4 + ((ctx - far) & 3)
+                array, place = piece((left, right)[side], far, near)
+                target[aligned(block * ROWS, ROWS), start : start + size] = array[
+                    place, :, source : source + size
+                ]
 
 
 def enter(
-    ids, l0, l1, l2, l3, l4, r0, r1, r2, r3, r4, units, consts,
+    ids, l0, l1, l2, l3, l4, r0, r1, r2, r3, r4, rim, units, consts,
     weights, hidden_in, taken, wide, narrow, message,
 ):
-    place_blocks(ids, (l0, l1, l2, l3, l4), (r0, r1, r2, r3, r4), 0, weights)
+    moves = (weights, 0, 0, 0, WIDE), (weights, 1, WIDE, 0, WIDE)
+    place_blocks(ids, (l0, l1, l2, l3, l4), (r0, r1, r2, r3, r4), *moves)
     gain = gain_row(weights[:, MIX:])
-    hidden_in[...] = (units[...] * gain).astype(BF16)
+    hidden_in[:RIM] = (unit_rows(rim[...]) * gain).astype(BF16)
+    hidden_in[RIM:] = (units[...] * gain).astype(BF16)
     projected = dot(hidden_in[...], weights[...])
     inputs = projected[:, :MIX].astype(BF16)
     taken[...] = inputs
@@ -261,7 +267,8 @@
 def project(
     ids, l0, l1, l2, l3, l4, r0, r1, r2, r3, r4, hidden_in, cotangent, wide, narrow, gate_out, before
 ):
-    place_blocks(ids, (l0, l1, l2, l3, l4), (r0, r1, r2, r3, r4), 1, gate_out)
+    moves = (gate_out, 0, 0, WIDE, WIDE + 128), (gate_out, 1, WIDE + 128, WIDE, WIDE - 128)
+    place_blocks(ids, (l0, l1, l2, l3, l4), (r0, r1, r2, r3, r4), *moves)
     before[:, GATE_PRE] = dot(hidden_in[RIM:], gate_out[:, :WIDE])
     before[:, GRAD_NORMED] = dot(cotangent[...], gate_out[:, WIDE:])
     scores = dot_last(narrow[:, CMAT], narrow[:, BMAT])
@@ -360,7 +367,7 @@
 
 def leave(
     ids, g1, g2, g3, state, after, grad_mixed, grads, wide, narrow, consts, taken, grad_gain,
-    low, keep, send, small, turned,
+    low, state_low, keep, send, small, turned,
 ):
     me = ids[0, 1]
     end = jnp.zeros((STATE, WIDE), F32)
@@ -403,6 +410,7 @@
         taps = jnp.where(line == tap, found, taps)
         grad_input = grad_input + consts[tap : tap + 1, :MIX] * roll(padded, -shift, 0)
     low[:, :WIDE] = grad_input[:, :WIDE].astype(BF16)
+    state_low[...] = grad_input[:, WIDE:]
     low_step = jnp.concatenate([jnp.zeros((RIM, 128), F32), grad_step_pre], axis=0)
     low[:, WIDE:] = roll(low_step, STEP_LANE, 1).astype(BF16)
     rest = jnp.zeros((TURNED - EXT - 8, 2 * STATE), F32)
@@ -419,14 +427,21 @@
     small[...] = jnp.where(line == 5, grad_gain[...], jnp.where(line == 6, heads, taps[:, :WIDE]))
 
 
+def two_parts(array):
+    high = array.astype(BF16)
+    return high, array - high.astype(F32)
+
+
 def pair_sum(ids, keep, got, *shares):
     for ahead, share in enumerate(shares):
         share[...] = (keep[ahead].astype(F32) + got[ahead].astype(F32)).astype(share.dtype)
 
 
-def value_grads(ids, low, gated_low, weights, gate_out, hidden_in, value, head):
+def value_grads(ids, low, state_low, gated_low, weights, gate_out, hidden_in, pair, value, head):
     value[...] = dot_first(hidden_in[...], low[:, :WIDE]).astype(BF16)
     part = dot_last(low[:, :WIDE], weights[:, :WIDE]) + dot_last(low[:, WIDE:], weights[:, MIX:])
+    high, rest = two_parts(state_low[...])
+    part = part + dot_last(high, weights[:, WIDE:MIX]) + dot_last(rest, weights[:, WIDE:MIX])
     head[:RIM] = part[:RIM]
     head[RIM:] = part[RIM:] + dot_last(gated_low[:, LOW_GATE], gate_out[:, :WIDE])
 
@@ -459,20 +474,13 @@
 
 
 def late_grads(
-    ids, t0, t1, t2, t3, low, small, head, weights, units, hidden_in, gate, out, value,
-    whole, *targets
+    ids, t0, t1, t2, t3, low, small, head, rim, units, hidden_in, gate, out, value, *targets
 ):
     targets, tail = targets[:-1], targets[-1]
     total = t0[...] + t1[...] + t2[...] + t3[...]
-    low_turned = total.astype(BF16).astype(F32)
     straight = jnp.concatenate([total, jnp.zeros((128 - PART, TURNED), F32)], axis=0).T
     low_tail = low[:, WIDE:].astype(F32) + straight[:EXT]
-    tiles = jnp.concatenate([low_turned] * 8, axis=0)
-    tiles = jnp.where((iota((8 * PART, TURNED), 0) >> 5) == ids[0, 2], tiles, 0.0)
-    part = head[...] + product(tiles, weights[:, WIDE:MIX], 0, 1)[:EXT]
-    behind = part[:RIM].astype(BF16)
-    whole[...] = part[RIM:].astype(BF16)
-    terms = part * units[...]
+    terms = jnp.concatenate([head[:RIM] * unit_rows(rim[...]), head[RIM:] * units[...]], axis=0)
     grads = dot_first(hidden_in[...], low_tail)
     grads = grads + dot_first(terms, flag(iota((EXT, 128), 1) == GAIN_LANE))
     tail[...] = grads.astype(BF16)
@@ -481,45 +489,47 @@
     folded = fold(jnp.where(iota((8, WIDE), 0) == 7, row, small[...]))
     arrange(ids, gate, out, value, tail, folded, targets)
     for chunk, (slot, start) in enumerate(RIM_SLOTS):
-        piece = behind[:, HALF * chunk : HALF * chunk + HALF]
-        targets[8][slot, start : start + RIM, : piece.shape[1]] = piece
-
+        targets[8][slot, start : start + RIM] = head[:RIM, RIGHT * chunk : RIGHT * chunk + RIGHT].astype(
+            BF16
+        )
 
 def arrange(ids, gate, out, value, tail, folded, targets):
     line, ctx = ids[0, 0], ids[0, 1]
     lanes = iota((ROWS, 128), 1) < 64
-
-    def left(block):
-        rows = aligned(block * ROWS, ROWS)
-        return gate[rows], value[rows, :256]
-
-    def right(block):
-        rows = aligned(block * ROWS, ROWS)
-        end = jnp.where(lanes, tail[rows].astype(F32), folded).astype(BF16)
-        return out[rows], value[rows, 256:], end
-
     for far in range(4):
         for near in range(4):
-            slot = far + far // 3
-            place = near
+            slot, place = far + far // 3, near
             if far == 2 and near >= 2:
                 slot, place = 3, near - 2
-            start = 0
-            for part in left(((line + far) & 3) * 4 + ((ctx + near) & 3)):
-                targets[slot][place, :, start : start + part.shape[1]] = part
-                start += part.shape[1]
-            start = 0
-            for part in right(((line + near) & 3) * 4 + ((ctx + far) & 3)):
-                targets[5 + slot][place, :ROWS, start : start + part.shape[1]] = part
-                start += part.shape[1]
+            block = ((line + far) & 3) * 4 + ((ctx + near) & 3)
+            rows = aligned(block * ROWS, ROWS)
+            targets[slot][place, :, :WIDE] = gate[rows]
+            targets[slot][place, :, WIDE:] = value[rows]
+            block = ((line + near) & 3) * 4 + ((ctx + far) & 3)
+            rows = aligned(block * ROWS, ROWS)
+            end = jnp.where(lanes, tail[rows].astype(F32), folded).astype(BF16)
+            targets[5 + slot][place, :ROWS, :WIDE] = out[rows]
+            targets[5 + slot][place, :ROWS, WIDE:] = end
 
 
 def put(target, total, tailed):
     if tailed:
-        target[:, : HALF - 128] = total[:, : HALF - 128].astype(BF16)
-        target[:, HALF - 128 :] = tidy(total[:, HALF - 128 :]).astype(BF16)
+        target[:, :WIDE] = total[:, :WIDE].astype(BF16)
+        target[:, WIDE:] = tidy(total[:, WIDE:]).astype(BF16)
     else:
         target[...] = total.astype(BF16)
+
+
+def pair_halves(ids, keep, got, near, far):
+    for other in range(4):
+        target = far if other % 2 else near
+        total = keep[other].astype(F32) + got[other].astype(F32)
+        target[other // 2] = total.astype(BF16)
+
+
+def pair_again(ids, near, got, own, second):
+    for index, target in enumerate((own, second)):
+        target[...] = (near[index].astype(F32) + got[index].astype(F32)).astype(BF16)
 
 
 def relay(ids, *refs):
@@ -538,19 +548,18 @@
     head, branch = refs[8:10]
     keep, send, whole = refs[14:]
     inside = jnp.where(ids[0, 1] < 3, 1.0, 0.0)
-    whole[: T - RIM] = head[: T - RIM]
+    whole[: T - RIM] = head[RIM:T].astype(BF16)
     for chunk, (slot, start) in enumerate(RIM_SLOTS):
-        columns = slice(HALF * chunk, min(HALF * chunk + HALF, D))
-        behind = refs[7][slot, start : start + RIM, : columns.stop - columns.start]
-        total = head[T - RIM :, columns].astype(F32) + behind.astype(F32) * inside
-        whole[T - RIM :, columns] = total.astype(BF16)
+        columns = slice(RIGHT * chunk, RIGHT * chunk + RIGHT)
+        behind = refs[7][slot, start : start + RIM].astype(F32) * inside
+        whole[T - RIM :, columns] = (head[T:, columns] + behind).astype(BF16)
     chip, core = ids[0, 2] >> 1, ids[0, 2] & 1
-    for ahead in range(4):
-        start = ((chip + ahead) & 3) * 2
+    for other in range(4):
+        start = (chip ^ other) * 2
         for half, source in enumerate((whole, branch)):
             rows = slice(half * SHARE, half * SHARE + SHARE)
-            keep[ahead, rows] = source[aligned((start + core) * SHARE, SHARE)]
-            send[ahead, rows] = source[aligned((start + 1 - core) * SHARE, SHARE)]
+            keep[other, rows] = source[aligned((start + core) * SHARE, SHARE)]
+            send[other, rows] = source[aligned((start + 1 - core) * SHARE, SHARE)]
 
 
 def halfway(ids, *refs):
@@ -568,10 +577,9 @@
     left = sum(part[...].astype(F32) for part in (a0, a1, a2, a3))
     right = sum(part[...].astype(F32) for part in (b0, b1, b2, b3))
     grad_gate[...] = left[:, :WIDE]
+    grad_value[...] = left[:, WIDE:]
     grad_out[...] = right[:, :WIDE]
-    grad_value[:, :256] = left[:, WIDE:]
-    grad_value[:, 256:] = right[:, WIDE : HALF - 128]
-    total = right[:, HALF - 128 :]
+    total = right[:, WIDE:]
     rest[:ROWS] = total
     small = unfold(total)
     state = small[7:8]
@@ -624,8 +632,8 @@
     grad_gain[...] = exact(flag(iota((8, 128), 1) == GAIN_LANE), total[:ROWS], 1, 1)[0:1]
 
 
-def settle(ids, p0, p1, p2, p3, hidden, weights, settled):
-    both = sum(part[...].astype(F32) for part in (p0, p1, p2, p3))
+def settle(ids, p0, p1, hidden, weights, settled):
+    both = p0[...].astype(F32) + p1[...].astype(F32)
     mine = hidden[aligned(ids[0, 2] * SHARE, SHARE)].astype(F32)
     inv = lax.rsqrt(jnp.mean(mine * mine, axis=1, keepdims=True) + EPSILON)
     unit = mine * inv
@@ -637,13 +645,11 @@
 
 def stack_blocks(ids, l0, l1, l2, l3, r0, r1, r2, r3, left, right, rim):
     for i, (one, two) in enumerate(((l0, r0), (l1, r1), (l2, r2), (l3, r3))):
-        left[i] = one[:, :ROWS]
+        left[i] = one[:ROWS]
         right[i] = two[...]
     inside = jnp.where(ids[0, 1] > 0, 1.0, 0.0)
-    for chunk in range(4):
-        start = ROWS + RIM * (chunk % 2)
-        piece = l1[chunk // 2, start : start + RIM].astype(F32) * inside
-        rim[:, WIDE * chunk : WIDE * chunk + WIDE] = piece.astype(BF16)
+    rim[:, :NEAR] = (l1[ROWS : ROWS + RIM].astype(F32) * inside).astype(BF16)
+    rim[:, NEAR:] = (l1[ROWS + RIM :, : D - NEAR].astype(F32) * inside).astype(BF16)
 
 
 def shift(array, axis, steps):
@@ -654,8 +660,8 @@
     return lax.ppermute(array, "tp", [(i, (i + 2 * steps) % 8) for i in range(8)])
 
 
-def from_core(array):
-    return lax.ppermute(array, "tp", [(i, i ^ 1) for i in range(8)])
+def across(array, bits):
+    return lax.ppermute(array, "tp", [(i, i ^ bits) for i in range(8)])
 
 
 def around(array, axis):
@@ -670,15 +676,9 @@
     return [array, one, shift(one[:2], axis, 1), shift(three[2:], axis, 3), three]
 
 
-def chips_sum(ids, keep, send):
-    outputs = [(keep.shape[1:], keep.dtype)] * 4
-    pair = fuse(pair_sum, outputs, ids, keep, from_core(send))
-    return [pair[0]] + [from_chip(pair[ahead], ahead) for ahead in range(1, 4)]
-
-
 def chips_all(array):
     same = [array] + [from_chip(array, steps) for steps in range(1, 4)]
-    return same + [from_core(one) for one in same]
+    return same + [across(one, 1) for one in same]
 
 
 def per_device(
@@ -704,10 +704,9 @@
     places = [lax.axis_index(axis).astype(jnp.int32) for axis in ("dp", "ctx", "tp")]
     ids = jnp.stack(places).reshape(1, 3)
 
-    half = ((2, ROWS, WIDE), BF16)
     left, longer, right = fuse(
         prepare,
-        [half, ((2, ROWS + 2 * RIM, WIDE), BF16), half],
+        [((ROWS, NEAR), BF16), ((ROWS + 2 * RIM, NEAR), BF16), ((ROWS, FAR), BF16)],
         ids,
         value_weight,
         gate_weight,
@@ -722,25 +721,23 @@
     near = [left, shift(longer, "ctx", 1), shift(left, "ctx", 2), shift(left, "ctx", 3)]
     left, right, rim = fuse(
         stack_blocks,
-        [((4, 2, ROWS, WIDE), BF16)] * 2 + [((RIM, D), BF16)],
+        [((4, ROWS, NEAR), BF16), ((4, ROWS, FAR), BF16), ((RIM, D), BF16)],
         ids,
         *near,
         *around(right, "dp"),
     )
     consts, units = fuse(
         tabulate,
-        [((16, FIRST), F32), ((EXT, D), F32)],
+        [((16, FIRST), F32), ((T, D), F32)],
         ids,
         value_filter,
         state_filter,
         value_offset[None],
         state_offset[None],
         gate_norm_gain[None],
-        step_bias[None],
-        decay_log[None],
-        skip_gain[None],
-        rim,
+        jnp.stack([step_bias, decay_log, skip_gain]),
         hidden,
+        fetch=True,
     )
     left = ring_rest(left, "dp", *ring_sides(left, "dp"))
     right = ring_rest(right, "ctx", *ring_sides(right, "ctx"))
@@ -757,6 +754,7 @@
         ids,
         *left,
         *right,
+        rim,
         units,
         consts,
     )
@@ -782,7 +780,7 @@
         consts,
         before,
     )
-    sums = sums + from_core(sums)
+    sums = sums + across(sums, 1)
     gated_low, grad_mixed, grad_gain, sensitivity = fuse(
         gate_back,
         [
@@ -814,9 +812,9 @@
         narrow,
         grad_mixed,
     )
-    low, turned_keep, turned_send, small = fuse(
+    low, state_low, keep, send, small = fuse(
         leave,
-        [((EXT, WIDE + 128), BF16)] + [((4, PART, TURNED), F32)] * 2 + [((8, WIDE), F32)],
+        [((EXT, WIDE + 128), BF16), ((EXT, 2 * STATE), F32)] + [((4, PART, TURNED), F32)] * 2 + [((8, WIDE), F32)],
         ids,
         *later,
         state,
@@ -830,27 +828,39 @@
         grad_gain,
         scratch=[((2 * STATE, TURNED), F32)],
     )
+    pair = fuse(pair_sum, [((PART, TURNED), F32)] * 4, ids, keep, across(send, 1))
+    turned = pair[:1] + [from_chip(pair[steps], steps) for steps in range(1, 4)]
     value, head = fuse(
         value_grads,
         [square, ((EXT, D), F32)],
         ids,
         low,
+        state_low,
         gated_low,
         weights,
         gate_out,
         hidden_in,
-    )
-    whole, part = ((4, ROWS, HALF), BF16), ((2, ROWS, HALF), BF16)
-    longer = ((2, ROWS + 2 * RIM, HALF), BF16)
-    head, *blocks = fuse(
+        pair[0],
+    )
+    both = ((2 * SHARE, D), BF16)
+    two = ((2, 2 * SHARE, D), BF16)
+
+    def stage(count, rows, columns):
+        return (count, rows, columns), BF16
+
+    outputs = []
+    for columns, rows in ((LEFT, ROWS), (RIGHT, ROWS + 2 * RIM)):
+        whole = stage(4, ROWS, columns)
+        outputs += [whole, whole, stage(2, ROWS, columns), stage(2, rows, columns), whole]
+    blocks = fuse(
         late_grads,
-        [((T, D), BF16)] + [whole, whole, part, part, whole] + [whole, whole, part, longer, whole],
-        ids,
-        *chips_sum(ids, turned_keep, turned_send),
+        outputs,
+        ids,
+        *turned,
         low,
         small,
         head,
-        weights,
+        rim,
         units,
         hidden_in,
         gate,
@@ -862,9 +872,9 @@
     halves = []
     for side, axis in ((left, "dp"), (right, "ctx")):
         halves += [side[1], side[4], shift(side[2], axis, 1), shift(side[3], axis, 3)]
-    *sides, head_keep, head_send = fuse(
+    *sides, keep, send = fuse(
         relay,
-        [whole] * 4 + [((4, 2 * SHARE, D), BF16)] * 2,
+        [stage(4, ROWS, LEFT)] * 2 + [stage(4, ROWS, RIGHT)] * 2 + [((4, 2 * SHARE, D), BF16)] * 2,
         ids,
         *halves,
         head,
@@ -873,11 +883,13 @@
     )
     left = [left[0], shift(sides[0], "dp", 1), shift(sides[1], "dp", 3)]
     right = [right[0], shift(sides[2], "ctx", 1), shift(sides[3], "ctx", 3)]
-    heads = chips_sum(ids, head_keep, head_send)
-    sums = fuse(halfway, [((ROWS, HALF), BF16)] * 8, ids, *left, *right, heads[0])
+    near, far = fuse(pair_halves, [two] * 2, ids, keep, across(send, 1))
+    own, second = fuse(pair_again, [both] * 2, ids, near, across(far, 2))
+    outputs = [((ROWS, LEFT), BF16)] * 4 + [((ROWS, RIGHT), BF16)] * 4
+    sums = fuse(halfway, outputs, ids, *left, *right, own)
     left = sums[:1] + [shift(sums[steps], "ctx", steps) for steps in range(1, 4)]
     right = sums[4:5] + [shift(sums[4 + steps], "dp", steps) for steps in range(1, 4)]
-    (settled,) = fuse(settle, [((2 * SHARE, D), BF16)], ids, *heads, hidden, weights)
+    (settled,) = fuse(settle, [both], ids, own, across(second, 4), hidden, weights)
     few, line = ((1, HEADS), F32), ((1, WIDE), F32)
     grad_gate, grad_value, grad_out, grad_step, taps, offset, gain, bias, decay, skip, message = fuse(
         collect,

time: 167 us -> 160 us (0.958)
  waiting for transfers between devices: 53.5 us -> 48.8 us
  starting transfers between devices: 76.7 us -> 73.4 us
    ppermute x34, waiting for transfers between devices: 48.5 us -> 37 us  [shift(): return lax.ppermute(array, axis, [(i, (i + steps) % 4) for i in range(4)])]
    ppermute x7 -> x9, waiting for transfers between devices: 1.91 us -> 8.6 us  [across(): return lax.ppermute(array, 'tp', [(i, i ^ bits) for i in range(8)])]
    ppermute x12 -> x9, starting transfers between devices: 13 us -> 9.41 us  [from_chip(): lax.ppermute(array, 'tp', [(i, (i + 2 * steps) % 8) for i in range(8)])]
    ppermute x7 -> x9, starting transfers between devices: 25.7 us -> 28.4 us  [across(): return lax.ppermute(array, 'tp', [(i, i ^ bits) for i in range(8)])]
    ppermute x34, starting transfers between devices: 38.1 us -> 35.6 us  [shift(): return lax.ppermute(array, axis, [(i, (i + steps) % 4) for i in range(4)])]
    unnamed x28 -> x16, local copies, waits for them, and re-layouts: 2.52 us -> 0.03 us
    pallas_call x18 -> x19, Pallas kernels: 31.4 us -> 32.8 us  [fuse(): return list(call(ids, *arrays))]
  transfers between devices with their start and end apart: 53 -> 52, of which waited for: 22 -> 20; matrix products, arithmetic and copies ran while one was open for 1% -> 2% of each run, Pallas kernels for 6% -> 8%
where the time goes in v2:
time: 160 us
  starting transfers between devices  73.4 us (46%)
  waiting for transfers between devices  48.8 us (30%)
  Pallas kernels  32.8 us (20%)
  other arithmetic  1.86 us (1%)
  local copies, waits for them, and re-layouts  1.83 us (1%)
    ppermute x34, waiting for transfers between devices, shift(): return lax.ppermute(array, axis, [(i, (i + steps) % 4) for i in range(4)])  37 us
    ppermute x34, starting transfers between devices, shift(): return lax.ppermute(array, axis, [(i, (i + steps) % 4) for i in range(4)])  35.6 us
    pallas_call x19, Pallas kernels, fuse(): return list(call(ids, *arrays))  32.8 us
    ppermute x9, starting transfers between devices, across(): return lax.ppermute(array, 'tp', [(i, i ^ bits) for i in range(8)])  28.4 us
    ppermute x9, starting transfers between devices, from_chip(): lax.ppermute(array, 'tp', [(i, (i + 2 * steps) % 8) for i in range(8)])  9.41 us
    ppermute x9, waiting for transfers between devices, across(): return lax.ppermute(array, 'tp', [(i, i ^ bits) for i in range(8)])  8.6 us
    ppermute x9, waiting for transfers between devices, from_chip(): lax.ppermute(array, 'tp', [(i, (i + 2 * steps) % 8) for i in range(8)])  3.26 us
  transfers between devices with their start and end apart: 52, of which 20 were waited for; matrix products, arithmetic and copies ran while one was open for 2% of the time, Pallas kernels for 8%

profile of v2, /device:TPU:1, one launch (start us, length us, event | category | flops | bytes accessed | tf_op | source)
XLA Modules:
  0.0 159.6 jit_solution(8672271467393612185)
XLA Ops:
  2.6 4.7 %collective-permute-start.5 = (bf16[96,640]{1,0:T(8,128)(2,1)S(1)}, bf16[96,640]{1,0:T(8,128)(2,1)S(1)}, u32[]{:S(2)}, u32[]{:S(2)}) collective-permute-start(bf16[96,640]{1,0:T(8,128)(2,1)S(1)} %get-tuple-element.101.refs_5_), channel_id=1, source_target_pairs={{0,96},{32,0},{64,32},{96,64},{1,97},{33,1},{65,33},{97,65},{2,98}... | collective-permute-start | bytes 368648 | tf_op jit(solution)/shard_map/ppermute | solution.py:656
  12.4 4.6 %collective-permute-done.4.refs_7_ = bf16[96,640]{1,0:T(8,128)(2,1)S(1)} collective-permute-done((bf16[96,640]{1,0:T(8,128)(2,1)S(1)}, bf16[96,640]{1,0:T(8,128)(2,1)S(1)}, u32[]{:S(2)}, u32[]{:S(2)}) %collective-permute-start.4) | collective-permute-done | bytes 122912 | tf_op jit(solution)/shard_map/ppermute | solution.py:656
  23.3 12.0 %collective-permute-done.8.refs_5_ = bf16[4,96,896]{2,1,0:T(8,128)(2,1)S(1)} collective-permute-done((bf16[4,96,896]{2,1,0:T(8,128)(2,1)S(1)}, bf16[4,96,896]{2,1,0:T(8,128)(2,1)S(1)}, u32[]{:S(2)}, u32[]{:S(2)}) %collective-permute-start.8) | collective-permute-done | bytes 688160 | tf_op jit(solution)/shard_map/ppermute | solution.py:656
  37.0 2.3 %collective-permute-start.13 = (bf16[2,96,640]{2,1,0:T(8,128)(2,1)S(1)}, bf16[2,96,640]{2,1,0:T(8,128)(2,1)S(1)}, u32[]{:S(2)}, u32[]{:S(2)}) collective-permute-start(bf16[2,96,640]{2,1,0:T(8,128)(2,1)S(1)} %slice.19), channel_id=1, source_target_pairs={{0,24},{8,0},{16,8},{24,16},{1,25},{9,1},{17,9},{25,17},{2,26},{10... | collective-permute-start | bytes 737288 | tf_op jit(solution)/shard_map/ppermute | solution.py:656
  41.7 2.1 %tabulate.1 = (f32[16,768]{1,0:T(8,128)S(1)}, f32[256,1536]{1,0:T(8,128)S(1)}) custom-call(s32[1,3]{1,0:T(1,128)S(1)} %add_bitcast_fusion.refs_0_, bf16[4,384]{1,0:T(4,128)(2,1)} %refs_1_.3, bf16[4,256]{1,0:T(4,128)(2,1)} %refs_2_.3, bf16[1,384]{1,0:T(2,128)(2,1)} %broadcast_in_dim.19.refs_3_, bf16[1,256]{1,0:T(2,128)(2,1)} %broadcast_in_dim.20.refs_4_, ...), custom_call_target="tpu_custom_call" | custom-call | tf_op jit(solution)/shard_map/tabulate/pallas_call | solution.py:89
  43.8 2.1 %collective-permute-done.11.refs_8_ = bf16[2,96,640]{2,1,0:T(8,128)(2,1)S(1)} collective-permute-done((bf16[2,96,640]{2,1,0:T(8,128)(2,1)S(1)}, bf16[2,96,640]{2,1,0:T(8,128)(2,1)S(1)}, u32[]{:S(2)}, u32[]{:S(2)}) %collective-permute-start.11) | collective-permute-done | bytes 245792 | tf_op jit(solution)/shard_map/ppermute | solution.py:656
  46.0 3.2 %enter.1 = (bf16[1536,768]{1,0:T(8,128)(2,1)S(1)}, bf16[272,1536]{1,0:T(8,128)(2,1)S(1)}, bf16[272,640]{1,0:T(8,128)(2,1)S(1)}, f32[256,1408]{1,0:T(8,128)S(1)},...) custom-call(s32[1,3]{1,0:T(1,128)S(1)} %add_bitcast_fusion.refs_0_, ...), custom_call_target="tpu_custom_call" | custom-call | tf_op jit(solution)/shard_map/enter/pallas_call | solution.py:89
  50.7 2.0 %project.1 = (bf16[1536,768]{1,0:T(8,128)(2,1)S(1)}, f32[256,1152]{1,0:T(8,128)S(1)}) custom-call(s32[1,3]{1,0:T(1,128)S(1)} %add_bitcast_fusion.refs_0_, bf16[4,96,896]{2,1,0:T(8,128)(2,1)S(1)} %get-tuple-element.102.refs_1_, bf16[4,96,896]{2,1,0:T(8,128)(2,1)S(1)} %collective-permute-done.6.refs_2_, ...), custom_call_target="tpu_custom_call" | custom-call | tf_op jit(solution)/shard_map/project/pallas_call | solution.py:89
  52.8 2.2 %collective-permute-done.15.refs_2_ = bf16[144,384]{1,0:T(8,128)(2,1)S(1)} collective-permute-done((bf16[144,384]{1,0:T(8,128)(2,1)S(1)}, bf16[144,384]{1,0:T(8,128)(2,1)S(1)}, u32[]{:S(2)}, u32[]{:S(2)}) %collective-permute-start.15) | collective-permute-done | bytes 110624 | tf_op jit(solution)/shard_map/ppermute | solution.py:656
  57.6 5.1 %collective-permute-start.17 = (f32[8,256]{1,0:T(8,128)S(1)}, f32[8,256]{1,0:T(8,128)S(1)}, u32[]{:S(2)}, u32[]{:S(2)}) collective-permute-start(f32[8,256]{1,0:T(8,128)S(1)} %get-tuple-element.112), channel_id=1, source_target_pairs={{0,1},{1,0},{2,3},{3,2},{4,5},{5,4},{6,7},{7,6},{8,9},{9,8},{10,11... | collective-permute-start | bytes 24584 | tf_op jit(solution)/shard_map/ppermute | solution.py:664
  63.6 2.5 %collective-permute-start.20 = (f32[8,256]{1,0:T(8,128)S(1)}, f32[8,256]{1,0:T(8,128)S(1)}, u32[]{:S(2)}, u32[]{:S(2)}) collective-permute-start(f32[8,256]{1,0:T(8,128)S(1)} %add.3.refs_1_), channel_id=1, source_target_pairs={{0,6},{1,7},{2,0},{3,1},{4,2},{5,3},{6,4},{7,5},{8,14},{9,15},{10,... | collective-permute-start | bytes 24584 | tf_op jit(solution)/shard_map/ppermute | solution.py:660
  67.2 2.9 %collective-permute-done.19.refs_3_ = f32[8,256]{1,0:T(8,128)S(1)} collective-permute-done((f32[8,256]{1,0:T(8,128)S(1)}, f32[8,256]{1,0:T(8,128)S(1)}, u32[]{:S(2)}, u32[]{:S(2)}) %collective-permute-start.19) | collective-permute-done | bytes 8224 | tf_op jit(solution)/shard_map/ppermute | solution.py:660
  71.8 2.2 %collective-permute-start.22 = (bf16[128,384]{1,0:T(8,128)(2,1)S(1)}, bf16[128,384]{1,0:T(8,128)(2,1)S(1)}, u32[]{:S(2)}, u32[]{:S(2)}) collective-permute-start(bf16[128,384]{1,0:T(8,128)(2,1)S(1)} %get-tuple-element.114), channel_id=1, source_target_pairs={{0,16},{8,24},{16,0},{24,8},{1,17},{9,25},{17,1},{25,9},{2,18},{10... | collective-permute-start | bytes 294920 | tf_op jit(solution)/shard_map/ppermute | solution.py:656
  74.5 2.9 %middle.1 = (bf16[1536,384]{1,0:T(8,128)(2,1)S(1)}, bf16[1536,384]{1,0:T(8,128)(2,1)S(1)}, f32[256,640]{1,0:T(8,128)S(1)}, bf16[256,1536]{1,0:T(8,128)(2,1)S(1)}) custom-call(s32[1,3]{1,0:T(1,128)S(1)} %add_bitcast_fusion.refs_0_, bf16[272,1536]{1,0:T(8,128)(2,1)S(1)} %get-tuple-element.110.refs_11_.refs_1_.refs_6_.refs_10_, ...), custom_call_target="tpu_custom_call" | custom-call | tf_op jit(solution)/shard_map/middle/pallas_call | solution.py:89
  78.5 3.4 %leave.1 = (bf16[272,512]{1,0:T(8,128)(2,1)S(1)}, f32[272,256]{1,0:T(8,128)S(1)}, f32[4,32,384]{2,1,0:T(8,128)S(1)}, f32[4,32,384]{2,1,0:T(8,128)S(1)}, f32[8,384]{1,0:T(8,128)S(1)}) custom-call(s32[1,3]{1,0:T(1,128)S(1)} %add_bitcast_fusion.refs_0_, bf16[128,384]{1,0:T(8,128)(2,1)S(1)} %collective-permute-done.21.refs_1_, ...), custom_call_target="tpu_custom_call" | custom-call | tf_op jit(solution)/shard_map/leave/pallas_call | solution.py:89
  81.9 3.2 %collective-permute-start.24 = (f32[4,32,384]{2,1,0:T(8,128)S(1)}, f32[4,32,384]{2,1,0:T(8,128)S(1)}, u32[]{:S(2)}, u32[]{:S(2)}) collective-permute-start(f32[4,32,384]{2,1,0:T(8,128)S(1)} %get-tuple-element.123), channel_id=1, source_target_pairs={{0,1},{1,0},{2,3},{3,2},{4,5},{5,4},{6,7},{7,6},{8,9},{9,8},{10,11... | collective-permute-start | bytes 589832 | tf_op jit(solution)/shard_map/ppermute | solution.py:664
  88.2 2.0 %collective-permute-start.27 = (f32[32,384]{1,0:T(8,128)S(1)}, f32[32,384]{1,0:T(8,128)S(1)}, u32[]{:S(2)}, u32[]{:S(2)}) collective-permute-start(f32[32,384]{1,0:T(8,128)S(1)} %get-tuple-element.127), channel_id=1, source_target_pairs={{0,6},{1,7},{2,0},{3,1},{4,2},{5,3},{6,4},{7,5},{8,14},{9,15},{10,... | collective-permute-start | bytes 147464 | tf_op jit(solution)/shard_map/ppermute | solution.py:660
  90.2 3.0 %value_grads.1 = (bf16[1536,384]{1,0:T(8,128)(2,1)S(1)}, f32[272,1536]{1,0:T(8,128)S(1)}) custom-call(s32[1,3]{1,0:T(1,128)S(1)} %add_bitcast_fusion.refs_0_, bf16[272,512]{1,0:T(8,128)(2,1)S(1)} %get-tuple-element.128.refs_1_.refs_5_, f32[272,256]{1,0:T(8,128)S(1)} %get-tuple-element.130.refs_2_, bf16[256,768]{1,0:T(8,128)(2,1)S(1)} %get-tuple-element.117.refs_2_.refs_3_, ...), custom_call_target="tpu_custom_call" | custom-call | tf_op jit(solution)/shard_map/value_grads/pallas_call | solution.py:89
  95.2 2.7 %collective-permute-start.29 = (bf16[2,96,768]{2,1,0:T(8,128)(2,1)S(1)}, bf16[2,96,768]{2,1,0:T(8,128)(2,1)S(1)}, u32[]{:S(2)}, u32[]{:S(2)}) collective-permute-start(bf16[2,96,768]{2,1,0:T(8,128)(2,1)S(1)} %get-tuple-element.140), channel_id=1, source_target_pairs={{0,96},{32,0},{64,32},{96,64},{1,97},{33,1},{65,33},{97,65},{2,98}... | collective-permute-start | bytes 884744 | tf_op jit(solution)/shard_map/ppermute | solution.py:656
  97.9 2.3 %collective-permute-start.31 = (bf16[2,128,512]{2,1,0:T(8,128)(2,1)S(1)}, bf16[2,128,512]{2,1,0:T(8,128)(2,1)S(1)}, u32[]{:S(2)}, u32[]{:S(2)}) collective-permute-start(bf16[2,128,512]{2,1,0:T(8,128)(2,1)S(1)} %get-tuple-element.144), channel_id=1, source_target_pairs={{0,24},{8,0},{16,8},{24,16},{1,25},{9,1},{17,9},{25,17},{2,26},{10... | collective-permute-start | bytes 786440 | tf_op jit(solution)/shard_map/ppermute | solution.py:656
  100.2 5.7 %collective-permute-done.30.refs_7_ = bf16[2,96,512]{2,1,0:T(8,128)(2,1)S(1)} collective-permute-done((bf16[2,96,512]{2,1,0:T(8,128)(2,1)S(1)}, bf16[2,96,512]{2,1,0:T(8,128)(2,1)S(1)}, u32[]{:S(2)}, u32[]{:S(2)}) %collective-permute-start.30) | collective-permute-done | bytes 196640 | tf_op jit(solution)/shard_map/ppermute | solution.py:656
  107.0 3.3 %collective-permute-start.36 = (bf16[4,64,1536]{2,1,0:T(8,128)(2,1)S(1)}, bf16[4,64,1536]{2,1,0:T(8,128)(2,1)S(1)}, u32[]{:S(2)}, u32[]{:S(2)}) collective-permute-start(bf16[4,64,1536]{2,1,0:T(8,128)(2,1)S(1)} %get-tuple-element.152), channel_id=1, source_target_pairs={{0,1},{1,0},{2,3},{3,2},{4,5},{5,4},{6,7},{7,6},{8,9},{9,8},{10,11... | collective-permute-start | bytes 2359304 | tf_op jit(solution)/shard_map/ppermute | solution.py:664
  110.3 2.7 %collective-permute-start.33 = (bf16[4,96,768]{2,1,0:T(8,128)(2,1)S(1)}, bf16[4,96,768]{2,1,0:T(8,128)(2,1)S(1)}, u32[]{:S(2)}, u32[]{:S(2)}) collective-permute-start(bf16[4,96,768]{2,1,0:T(8,128)(2,1)S(1)} %get-tuple-element.147), channel_id=1, source_target_pairs={{0,96},{32,0},{64,32},{96,64},{1,97},{33,1},{65,33},{97,65},{2,98}... | collective-permute-start | bytes 1769480 | tf_op jit(solution)/shard_map/ppermute | solution.py:656
  114.5 2.7 %collective-permute-start.35 = (bf16[4,96,512]{2,1,0:T(8,128)(2,1)S(1)}, bf16[4,96,512]{2,1,0:T(8,128)(2,1)S(1)}, u32[]{:S(2)}, u32[]{:S(2)}) collective-permute-start(bf16[4,96,512]{2,1,0:T(8,128)(2,1)S(1)} %get-tuple-element.150), channel_id=1, source_target_pairs={{0,24},{8,0},{16,8},{24,16},{1,25},{9,1},{17,9},{25,17},{2,26},{10... | collective-permute-start | bytes 1179656 | tf_op jit(solution)/shard_map/ppermute | solution.py:656
  117.2 6.7 %collective-permute-done.37.refs_2_ = bf16[2,64,1536]{2,1,0:T(8,128)(2,1)S(1)} collective-permute-done((bf16[2,64,1536]{2,1,0:T(8,128)(2,1)S(1)}, bf16[2,64,1536]{2,1,0:T(8,128)(2,1)S(1)}, u32[]{:S(2)}, u32[]{:S(2)}) %collective-permute-start.37) | collective-permute-done | bytes 393248 | tf_op jit(solution)/shard_map/ppermute | solution.py:664
  127.5 2.5 %collective-permute-start.39 = (bf16[96,768]{1,0:T(8,128)(2,1)S(1)}, bf16[96,768]{1,0:T(8,128)(2,1)S(1)}, u32[]{:S(2)}, u32[]{:S(2)}) collective-permute-start(bf16[96,768]{1,0:T(8,128)(2,1)S(1)} %get-tuple-element.158), channel_id=1, source_target_pairs={{0,16},{8,24},{16,0},{24,8},{1,17},{9,25},{17,1},{25,9},{2,18},{10... | collective-permute-start | bytes 442376 | tf_op jit(solution)/shard_map/ppermute | solution.py:656
  130.2 2.2 %collective-permute-done.41.refs_6_ = bf16[96,512]{1,0:T(8,128)(2,1)S(1)} collective-permute-done((bf16[96,512]{1,0:T(8,128)(2,1)S(1)}, bf16[96,512]{1,0:T(8,128)(2,1)S(1)}, u32[]{:S(2)}, u32[]{:S(2)}) %collective-permute-start.41) | collective-permute-done | bytes 98336 | tf_op jit(solution)/shard_map/ppermute | solution.py:656
  134.5 3.1 %collective-permute-done.42.refs_7_ = bf16[96,512]{1,0:T(8,128)(2,1)S(1)} collective-permute-done((bf16[96,512]{1,0:T(8,128)(2,1)S(1)}, bf16[96,512]{1,0:T(8,128)(2,1)S(1)}, u32[]{:S(2)}, u32[]{:S(2)}) %collective-permute-start.42) | collective-permute-done | bytes 98336 | tf_op jit(solution)/shard_map/ppermute | solution.py:656
  141.6 4.6 %collective-permute-start.48 = (bf16[80,1536]{1,0:T(8,128)(2,1)S(1)}, bf16[80,1536]{1,0:T(8,128)(2,1)S(1)}, u32[]{:S(2)}, u32[]{:S(2)}) collective-permute-start(bf16[80,1536]{1,0:T(8,128)(2,1)S(1)} %get-tuple-element.165.refs_1_), channel_id=1, source_target_pairs={{0,1},{1,0},{2,3},{3,2},{4,5},{5,4},{6,7},{7,6},{8,9},{9,8},{10,11... | collective-permute-start | bytes 737288 | tf_op jit(solution)/shard_map/ppermute | solution.py:664
  146.2 6.2 %collective-permute-start.51 = (bf16[80,1536]{1,0:T(8,128)(2,1)S(1)}, bf16[80,1536]{1,0:T(8,128)(2,1)S(1)}, u32[]{:S(2)}, u32[]{:S(2)}) collective-permute-start(bf16[80,1536]{1,0:T(8,128)(2,1)S(1)} %collective-permute-done.47.refs_4_), channel_id=1, source_target_pairs={{0,1},{1,0},{2,3},{3,2},{4,5},{5,4},{6,7},{7,6},{8,9},{9,8},{10,11... | collective-permute-start | bytes 737288 | tf_op jit(solution)/shard_map/ppermute | solution.py:664
  153.7 2.3 %collective-permute-start.49 = (bf16[80,1536]{1,0:T(8,128)(2,1)S(1)}, bf16[80,1536]{1,0:T(8,128)(2,1)S(1)}, u32[]{:S(2)}, u32[]{:S(2)}) collective-permute-start(bf16[80,1536]{1,0:T(8,128)(2,1)S(1)} %collective-permute-done.45.refs_2_), channel_id=1, source_target_pairs={{0,1},{1,0},{2,3},{3,2},{4,5},{5,4},{6,7},{7,6},{8,9},{9,8},{10,11... | collective-permute-start | bytes 737288 | tf_op jit(solution)/shard_map/ppermute | solution.py:664
  157.3 2.4 %finish.1 = (f32[256,1536]{1,0:T(8,128)}, bf16[256,1536]{1,0:T(8,128)(2,1)}, f32[96,256]{1,0:T(8,128)}, f32[1,96]{1,0:T(1,128)}, f32[4,256]{1,0:T(4,128)}, /*index=5*/f32[1,256]{1,0:T(1,128)}) custom-call(s32[1,3]{1,0:T(1,128)S(1)} %add_bitcast_fusion.refs_0_, bf16[80,1536]{1,0:T(8,128)(2,1)S(1)} %get-tuple-element.165.refs_1_, ...), custom_call_target="tpu_custom_call" | custom-call | tf_op jit(solution)/shard_map/finish/pallas_call | solution.py:89
  (119 shorter events, 47.0 us)
Async XLA Ops:
  2.6 9.1 %collective-permute-start.5 = (bf16[96,640]{1,0:T(8,128)(2,1)S(1)}, bf16[96,640]{1,0:T(8,128)(2,1)S(1)}, u32[]{:S(2)}, u32[]{:S(2)}) collective-permute-start(bf16[96,640]{1,0:T(8,128)(2,1)S(1)} %get-tuple-element.101.refs_5_), channel_id=1, source_target_pairs={{0,96},{32,0},{64,32},{96,64},{1,97},{33,1},{65,33},{97,65},{2,98}... | collective-permute-start | bytes 368648 | tf_op jit(solution)/shard_map/ppermute | solution.py:656
  7.2 12.3 %collective-permute-start = (bf16[128,896]{1,0:T(8,128)(2,1)S(1)}, bf16[128,896]{1,0:T(8,128)(2,1)S(1)}, u32[]{:S(2)}, u32[]{:S(2)}) collective-permute-start(bf16[128,896]{1,0:T(8,128)(2,1)S(1)} %get-tuple-element.100), channel_id=1, source_target_pairs={{0,8},{8,16},{16,24},{24,0},{1,9},{9,17},{17,25},{25,1},{2,10},{10... | collective-permute-start | bytes 688136 | tf_op jit(solution)/shard_map/ppermute | solution.py:656
  8.6 10.4 %collective-permute-start.2 = (bf16[96,896]{1,0:T(8,128)(2,1)S(1)}, bf16[96,896]{1,0:T(8,128)(2,1)S(1)}, u32[]{:S(2)}, u32[]{:S(2)}) collective-permute-start(bf16[96,896]{1,0:T(8,128)(2,1)S(1)} %get-tuple-element.99.refs_1_), channel_id=1, source_target_pairs={{0,24},{8,0},{16,8},{24,16},{1,25},{9,1},{17,9},{25,17},{2,26},{10... | collective-permute-start | bytes 516104 | tf_op jit(solution)/shard_map/ppermute | solution.py:656
  10.1 9.4 %collective-permute-start.1 = (bf16[96,896]{1,0:T(8,128)(2,1)S(1)}, bf16[96,896]{1,0:T(8,128)(2,1)S(1)}, u32[]{:S(2)}, u32[]{:S(2)}) collective-permute-start(bf16[96,896]{1,0:T(8,128)(2,1)S(1)} %get-tuple-element.99.refs_1_), channel_id=1, source_target_pairs={{0,16},{8,24},{16,0},{24,8},{1,17},{9,25},{17,1},{25,9},{2,18},{10... | collective-permute-start | bytes 516104 | tf_op jit(solution)/shard_map/ppermute | solution.py:656
  11.7 7.2 %collective-permute-start.3 = (bf16[96,640]{1,0:T(8,128)(2,1)S(1)}, bf16[96,640]{1,0:T(8,128)(2,1)S(1)}, u32[]{:S(2)}, u32[]{:S(2)}) collective-permute-start(bf16[96,640]{1,0:T(8,128)(2,1)S(1)} %get-tuple-element.101.refs_5_), channel_id=1, source_target_pairs={{0,32},{32,64},{64,96},{96,0},{1,33},{33,65},{65,97},{97,1},{2,34}... | collective-permute-start | bytes 368648 | tf_op jit(solution)/shard_map/ppermute | solution.py:656
  20.2 15.1 %collective-permute-start.8 = (bf16[4,96,896]{2,1,0:T(8,128)(2,1)S(1)}, bf16[4,96,896]{2,1,0:T(8,128)(2,1)S(1)}, u32[]{:S(2)}, u32[]{:S(2)}) collective-permute-start(bf16[4,96,896]{2,1,0:T(8,128)(2,1)S(1)} %get-tuple-element.102.refs_1_), channel_id=1, source_target_pairs={{0,96},{32,0},{64,32},{96,64},{1,97},{33,1},{65,33},{97,65},{2,98}... | collective-permute-start | bytes 2064392 | tf_op jit(solution)/shard_map/ppermute | solution.py:656
  20.4 16.0 %collective-permute-start.6 = (bf16[4,96,896]{2,1,0:T(8,128)(2,1)S(1)}, bf16[4,96,896]{2,1,0:T(8,128)(2,1)S(1)}, u32[]{:S(2)}, u32[]{:S(2)}) collective-permute-start(bf16[4,96,896]{2,1,0:T(8,128)(2,1)S(1)} %get-tuple-element.102.refs_1_), channel_id=1, source_target_pairs={{0,32},{32,64},{64,96},{96,0},{1,33},{33,65},{65,97},{97,1},{2,34}... | collective-permute-start | bytes 2064392 | tf_op jit(solution)/shard_map/ppermute | solution.py:656
  21.7 15.3 %collective-permute-start.12 = (bf16[4,96,640]{2,1,0:T(8,128)(2,1)S(1)}, bf16[4,96,640]{2,1,0:T(8,128)(2,1)S(1)}, u32[]{:S(2)}, u32[]{:S(2)}) collective-permute-start(bf16[4,96,640]{2,1,0:T(8,128)(2,1)S(1)} %get-tuple-element.103.refs_6_), channel_id=1, source_target_pairs={{0,24},{8,0},{16,8},{24,16},{1,25},{9,1},{17,9},{25,17},{2,26},{10... | collective-permute-start | bytes 1474568 | tf_op jit(solution)/shard_map/ppermute | solution.py:656
  23.3 16.0 %collective-permute-start.10 = (bf16[4,96,640]{2,1,0:T(8,128)(2,1)S(1)}, bf16[4,96,640]{2,1,0:T(8,128)(2,1)S(1)}, u32[]{:S(2)}, u32[]{:S(2)}) collective-permute-start(bf16[4,96,640]{2,1,0:T(8,128)(2,1)S(1)} %get-tuple-element.103.refs_6_), channel_id=1, source_target_pairs={{0,8},{8,16},{16,24},{24,0},{1,9},{9,17},{17,25},{25,1},{2,10},{10... | collective-permute-start | bytes 1474568 | tf_op jit(solution)/shard_map/ppermute | solution.py:656
  35.3 10.6 %collective-permute-start.9 = (bf16[2,96,896]{2,1,0:T(8,128)(2,1)S(1)}, bf16[2,96,896]{2,1,0:T(8,128)(2,1)S(1)}, u32[]{:S(2)}, u32[]{:S(2)}) collective-permute-start(bf16[2,96,896]{2,1,0:T(8,128)(2,1)S(1)} %slice.17), channel_id=1, source_target_pairs={{0,96},{32,0},{64,32},{96,64},{1,97},{33,1},{65,33},{97,65},{2,98}... | collective-permute-start | bytes 1032200 | tf_op jit(solution)/shard_map/ppermute | solution.py:656
  36.4 9.6 %collective-permute-start.7 = (bf16[2,96,896]{2,1,0:T(8,128)(2,1)S(1)}, bf16[2,96,896]{2,1,0:T(8,128)(2,1)S(1)}, u32[]{:S(2)}, u32[]{:S(2)}) collective-permute-start(bf16[2,96,896]{2,1,0:T(8,128)(2,1)S(1)} %slice.16), channel_id=1, source_target_pairs={{0,32},{32,64},{64,96},{96,0},{1,33},{33,65},{65,97},{97,1},{2,34}... | collective-permute-start | bytes 1032200 | tf_op jit(solution)/shard_map/ppermute | solution.py:656
  37.0 6.8 %collective-permute-start.13 = (bf16[2,96,640]{2,1,0:T(8,128)(2,1)S(1)}, bf16[2,96,640]{2,1,0:T(8,128)(2,1)S(1)}, u32[]{:S(2)}, u32[]{:S(2)}) collective-permute-start(bf16[2,96,640]{2,1,0:T(8,128)(2,1)S(1)} %slice.19), channel_id=1, source_target_pairs={{0,24},{8,0},{16,8},{24,16},{1,25},{9,1},{17,9},{25,17},{2,26},{10... | collective-permute-start | bytes 737288 | tf_op jit(solution)/shard_map/ppermute | solution.py:656
  39.3 6.6 %collective-permute-start.11 = (bf16[2,96,640]{2,1,0:T(8,128)(2,1)S(1)}, bf16[2,96,640]{2,1,0:T(8,128)(2,1)S(1)}, u32[]{:S(2)}, u32[]{:S(2)}) collective-permute-start(bf16[2,96,640]{2,1,0:T(8,128)(2,1)S(1)} %slice.18), channel_id=1, source_target_pairs={{0,8},{8,16},{16,24},{24,0},{1,9},{9,17},{17,25},{25,1},{2,10},{10... | collective-permute-start | bytes 737288 | tf_op jit(solution)/shard_map/ppermute | solution.py:656
  86.7 6.4 %collective-permute-start.25 = (f32[32,384]{1,0:T(8,128)S(1)}, f32[32,384]{1,0:T(8,128)S(1)}, u32[]{:S(2)}, u32[]{:S(2)}) collective-permute-start(f32[32,384]{1,0:T(8,128)S(1)} %get-tuple-element.125), channel_id=1, source_target_pairs={{0,2},{1,3},{2,4},{3,5},{4,6},{5,7},{6,0},{7,1},{8,10},{9,11},{10,... | collective-permute-start | bytes 147464 | tf_op jit(solution)/shard_map/ppermute | solution.py:660
  86.8 6.3 %collective-permute-start.26 = (f32[32,384]{1,0:T(8,128)S(1)}, f32[32,384]{1,0:T(8,128)S(1)}, u32[]{:S(2)}, u32[]{:S(2)}) collective-permute-start(f32[32,384]{1,0:T(8,128)S(1)} %get-tuple-element.126), channel_id=1, source_target_pairs={{0,4},{1,5},{2,6},{3,7},{4,0},{5,1},{6,2},{7,3},{8,12},{9,13},{10,... | collective-permute-start | bytes 147464 | tf_op jit(solution)/shard_map/ppermute | solution.py:660
  95.1 10.8 %collective-permute-start.28 = (bf16[2,96,768]{2,1,0:T(8,128)(2,1)S(1)}, bf16[2,96,768]{2,1,0:T(8,128)(2,1)S(1)}, u32[]{:S(2)}, u32[]{:S(2)}) collective-permute-start(bf16[2,96,768]{2,1,0:T(8,128)(2,1)S(1)} %get-tuple-element.139), channel_id=1, source_target_pairs={{0,32},{32,64},{64,96},{96,0},{1,33},{33,65},{65,97},{97,1},{2,34}... | collective-permute-start | bytes 884744 | tf_op jit(solution)/shard_map/ppermute | solution.py:656
  95.2 10.7 %collective-permute-start.29 = (bf16[2,96,768]{2,1,0:T(8,128)(2,1)S(1)}, bf16[2,96,768]{2,1,0:T(8,128)(2,1)S(1)}, u32[]{:S(2)}, u32[]{:S(2)}) collective-permute-start(bf16[2,96,768]{2,1,0:T(8,128)(2,1)S(1)} %get-tuple-element.140), channel_id=1, source_target_pairs={{0,96},{32,0},{64,32},{96,64},{1,97},{33,1},{65,33},{97,65},{2,98}... | collective-permute-start | bytes 884744 | tf_op jit(solution)/shard_map/ppermute | solution.py:656
  97.9 8.0 %collective-permute-start.31 = (bf16[2,128,512]{2,1,0:T(8,128)(2,1)S(1)}, bf16[2,128,512]{2,1,0:T(8,128)(2,1)S(1)}, u32[]{:S(2)}, u32[]{:S(2)}) collective-permute-start(bf16[2,128,512]{2,1,0:T(8,128)(2,1)S(1)} %get-tuple-element.144), channel_id=1, source_target_pairs={{0,24},{8,0},{16,8},{24,16},{1,25},{9,1},{17,9},{25,17},{2,26},{10... | collective-permute-start | bytes 786440 | tf_op jit(solution)/shard_map/ppermute | solution.py:656
  110.3 16.1 %collective-permute-start.32 = (bf16[4,96,768]{2,1,0:T(8,128)(2,1)S(1)}, bf16[4,96,768]{2,1,0:T(8,128)(2,1)S(1)}, u32[]{:S(2)}, u32[]{:S(2)}) collective-permute-start(bf16[4,96,768]{2,1,0:T(8,128)(2,1)S(1)} %get-tuple-element.146), channel_id=1, source_target_pairs={{0,32},{32,64},{64,96},{96,0},{1,33},{33,65},{65,97},{97,1},{2,34}... | collective-permute-start | bytes 1769480 | tf_op jit(solution)/shard_map/ppermute | solution.py:656
  110.3 16.1 %collective-permute-start.33 = (bf16[4,96,768]{2,1,0:T(8,128)(2,1)S(1)}, bf16[4,96,768]{2,1,0:T(8,128)(2,1)S(1)}, u32[]{:S(2)}, u32[]{:S(2)}) collective-permute-start(bf16[4,96,768]{2,1,0:T(8,128)(2,1)S(1)} %get-tuple-element.147), channel_id=1, source_target_pairs={{0,96},{32,0},{64,32},{96,64},{1,97},{33,1},{65,33},{97,65},{2,98}... | collective-permute-start | bytes 1769480 | tf_op jit(solution)/shard_map/ppermute | solution.py:656
  113.7 10.1 %collective-permute-start.37 = (bf16[2,64,1536]{2,1,0:T(8,128)(2,1)S(1)}, bf16[2,64,1536]{2,1,0:T(8,128)(2,1)S(1)}, u32[]{:S(2)}, u32[]{:S(2)}) collective-permute-start(bf16[2,64,1536]{2,1,0:T(8,128)(2,1)S(1)} %get-tuple-element.154), channel_id=1, source_target_pairs={{0,2},{1,3},{2,0},{3,1},{4,6},{5,7},{6,4},{7,5},{8,10},{9,11},{10,... | collective-permute-start | bytes 1179656 | tf_op jit(solution)/shard_map/ppermute | solution.py:664
  114.5 11.8 %collective-permute-start.34 = (bf16[4,96,512]{2,1,0:T(8,128)(2,1)S(1)}, bf16[4,96,512]{2,1,0:T(8,128)(2,1)S(1)}, u32[]{:S(2)}, u32[]{:S(2)}) collective-permute-start(bf16[4,96,512]{2,1,0:T(8,128)(2,1)S(1)} %get-tuple-element.149), channel_id=1, source_target_pairs={{0,8},{8,16},{16,24},{24,0},{1,9},{9,17},{17,25},{25,1},{2,10},{10... | collective-permute-start | bytes 1179656 | tf_op jit(solution)/shard_map/ppermute | solution.py:656
  114.5 11.8 %collective-permute-start.35 = (bf16[4,96,512]{2,1,0:T(8,128)(2,1)S(1)}, bf16[4,96,512]{2,1,0:T(8,128)(2,1)S(1)}, u32[]{:S(2)}, u32[]{:S(2)}) collective-permute-start(bf16[4,96,512]{2,1,0:T(8,128)(2,1)S(1)} %get-tuple-element.150), channel_id=1, source_target_pairs={{0,24},{8,0},{16,8},{24,16},{1,25},{9,1},{17,9},{25,17},{2,26},{10... | collective-permute-start | bytes 1179656 | tf_op jit(solution)/shard_map/ppermute | solution.py:656
  124.5 9.2 %collective-permute-start.44 = (bf16[64,1536]{1,0:T(8,128)(2,1)S(1)}, bf16[64,1536]{1,0:T(8,128)(2,1)S(1)}, u32[]{:S(2)}, u32[]{:S(2)}) collective-permute-start(bf16[64,1536]{1,0:T(8,128)(2,1)S(1)} %get-tuple-element.164), channel_id=1, source_target_pairs={{0,4},{1,5},{2,6},{3,7},{4,0},{5,1},{6,2},{7,3},{8,12},{9,13},{10,... | collective-permute-start | bytes 589832 | tf_op jit(solution)/shard_map/ppermute | solution.py:664
  127.5 10.2 %collective-permute-start.38 = (bf16[96,768]{1,0:T(8,128)(2,1)S(1)}, bf16[96,768]{1,0:T(8,128)(2,1)S(1)}, u32[]{:S(2)}, u32[]{:S(2)}) collective-permute-start(bf16[96,768]{1,0:T(8,128)(2,1)S(1)} %get-tuple-element.157), channel_id=1, source_target_pairs={{0,8},{8,16},{16,24},{24,0},{1,9},{9,17},{17,25},{25,1},{2,10},{10... | collective-permute-start | bytes 442376 | tf_op jit(solution)/shard_map/ppermute | solution.py:656
  127.5 10.2 %collective-permute-start.39 = (bf16[96,768]{1,0:T(8,128)(2,1)S(1)}, bf16[96,768]{1,0:T(8,128)(2,1)S(1)}, u32[]{:S(2)}, u32[]{:S(2)}) collective-permute-start(bf16[96,768]{1,0:T(8,128)(2,1)S(1)} %get-tuple-element.158), channel_id=1, source_target_pairs={{0,16},{8,24},{16,0},{24,8},{1,17},{9,25},{17,1},{25,9},{2,18},{10... | collective-permute-start | bytes 442376 | tf_op jit(solution)/shard_map/ppermute | solution.py:656
  130.1 7.6 %collective-permute-start.40 = (bf16[96,768]{1,0:T(8,128)(2,1)S(1)}, bf16[96,768]{1,0:T(8,128)(2,1)S(1)}, u32[]{:S(2)}, u32[]{:S(2)}) collective-permute-start(bf16[96,768]{1,0:T(8,128)(2,1)S(1)} %get-tuple-element.159), channel_id=1, source_target_pairs={{0,24},{8,0},{16,8},{24,16},{1,25},{9,1},{17,9},{25,17},{2,26},{10... | collective-permute-start | bytes 442376 | tf_op jit(solution)/shard_map/ppermute | solution.py:656
  139.2 7.0 %collective-permute-start.47 = (bf16[80,1536]{1,0:T(8,128)(2,1)S(1)}, bf16[80,1536]{1,0:T(8,128)(2,1)S(1)}, u32[]{:S(2)}, u32[]{:S(2)}) collective-permute-start(bf16[80,1536]{1,0:T(8,128)(2,1)S(1)} %get-tuple-element.165.refs_1_), channel_id=1, source_target_pairs={{0,6},{1,7},{2,0},{3,1},{4,2},{5,3},{6,4},{7,5},{8,14},{9,15},{10,... | collective-permute-start | bytes 737288 | tf_op jit(solution)/shard_map/ppermute | solution.py:660
  140.9 11.5 %collective-permute-start.46 = (bf16[80,1536]{1,0:T(8,128)(2,1)S(1)}, bf16[80,1536]{1,0:T(8,128)(2,1)S(1)}, u32[]{:S(2)}, u32[]{:S(2)}) collective-permute-start(bf16[80,1536]{1,0:T(8,128)(2,1)S(1)} %get-tuple-element.165.refs_1_), channel_id=1, source_target_pairs={{0,4},{1,5},{2,6},{3,7},{4,0},{5,1},{6,2},{7,3},{8,12},{9,13},{10,... | collective-permute-start | bytes 737288 | tf_op jit(solution)/shard_map/ppermute | solution.py:660
  141.6 12.2 %collective-permute-start.45 = (bf16[80,1536]{1,0:T(8,128)(2,1)S(1)}, bf16[80,1536]{1,0:T(8,128)(2,1)S(1)}, u32[]{:S(2)}, u32[]{:S(2)}) collective-permute-start(bf16[80,1536]{1,0:T(8,128)(2,1)S(1)} %get-tuple-element.165.refs_1_), channel_id=1, source_target_pairs={{0,2},{1,3},{2,4},{3,5},{4,6},{5,7},{6,0},{7,1},{8,10},{9,11},{10,... | collective-permute-start | bytes 737288 | tf_op jit(solution)/shard_map/ppermute | solution.py:660
  141.6 15.6 %collective-permute-start.48 = (bf16[80,1536]{1,0:T(8,128)(2,1)S(1)}, bf16[80,1536]{1,0:T(8,128)(2,1)S(1)}, u32[]{:S(2)}, u32[]{:S(2)}) collective-permute-start(bf16[80,1536]{1,0:T(8,128)(2,1)S(1)} %get-tuple-element.165.refs_1_), channel_id=1, source_target_pairs={{0,1},{1,0},{2,3},{3,2},{4,5},{5,4},{6,7},{7,6},{8,9},{9,8},{10,11... | collective-permute-start | bytes 737288 | tf_op jit(solution)/shard_map/ppermute | solution.py:664
  146.2 11.1 %collective-permute-start.51 = (bf16[80,1536]{1,0:T(8,128)(2,1)S(1)}, bf16[80,1536]{1,0:T(8,128)(2,1)S(1)}, u32[]{:S(2)}, u32[]{:S(2)}) collective-permute-start(bf16[80,1536]{1,0:T(8,128)(2,1)S(1)} %collective-permute-done.47.refs_4_), channel_id=1, source_target_pairs={{0,1},{1,0},{2,3},{3,2},{4,5},{5,4},{6,7},{7,6},{8,9},{9,8},{10,11... | collective-permute-start | bytes 737288 | tf_op jit(solution)/shard_map/ppermute | solution.py:664
  (28 other events, 301.5 us)

commit v3 on v2

--- a/solution.py
+++ b/solution.py
@@ -7,7 +7,6 @@
 
 F32 = jnp.float32
 BF16 = jnp.bfloat16
-HIGH = lax.Precision.HIGHEST
 EPSILON = 1e-05
 INNER = 3072
 D = 1536
@@ -22,19 +21,17 @@
 FIRST = MIX + 128
 ROWS = 96
 SHARES = 16
-NEAR = WIDE + WIDE + 128
-FAR = MIX + 2 * WIDE - NEAR + 128
-LEFT = 2 * WIDE
-RIGHT = WIDE + 128
-RIM_SLOTS = ((0, ROWS), (0, ROWS + RIM), (1, ROWS))
+PAIR = 2 * WIDE
+RIGHT = 512
+OUT_RIGHT = RIGHT - 128
+LEFT = 3 * WIDE - OUT_RIGHT
 SHARE = T // 8
-REST = ROWS + 16
 PART = 32
 STEP_LANE = 32
 GAIN_LANE = STEP_LANE + HEADS
 STATE_LANE = 64
 TURNED = 384
-VMEM_LIMIT = 16 * 2**20
+VMEM_LIMIT = 8 * 2**20
 
 VALUES, SLOPE = slice(0, WIDE), slice(WIDE, WIDE + MIX)
 STEP, STEP_SLOPE, LOG_DECAY = slice(1024, 1152), slice(1152, 1280), slice(1280, 1408)
@@ -42,10 +39,15 @@
 GATE_PRE, GRAD_NORMED, WITHIN = slice(0, 384), slice(384, 768), slice(768, 1152)
 INSIDE, MIXED = slice(0, 384), slice(384, 768)
 NORMED, LOW_GATE = slice(0, 384), slice(384, 768)
-
-
-def fuse(function, outputs, ids, *arrays, scratch=(), fetch=False, rim=False):
+GROWN, TO_END, STEPS = slice(0, 384), slice(384, 768), slice(768, 1152)
+
+
+WORK = {"pair_again": 2 * 10**9, "collect_left": 5 * 10**9}
+
+
+def fuse(function, outputs, ids, *arrays, scratch=(), fetch=0, rim=False):
     count = len(arrays)
+    plain = count - fetch
     shapes = [array.shape for array in arrays]
     if rim:
         shapes[-1] = (RIM, D)
@@ -54,9 +56,8 @@
         if not fetch:
             function(*refs)
             return
-        given, rest = refs[1 : 1 + count], refs[1 + count : -1 - count]
-        held, done = refs[-1 - count : -1], refs[-1]
-        given = list(given)
+        given = list(refs[1 + plain : 1 + count])
+        held, done = refs[-1 - fetch : -1], refs[-1]
         if rim:
             given[-1] = given[-1].at[pl.ds(T - RIM, RIM)]
         copies = [
@@ -65,27 +66,35 @@
         ]
         for copy in copies:
             copy.start()
-        for copy in copies:
-            copy.wait()
-        function(refs[0], *held, *rest)
+
+        def ready():
+            for copy in copies:
+                copy.wait()
+
+        function(*refs[: 1 + plain], *held, *refs[1 + count : -1 - fetch], ready=ready)
 
     buffers = [pltpu.VMEM(shape, dtype) for shape, dtype in scratch]
+    spaces = [pltpu.SMEM] + [pltpu.VMEM] * plain + [pltpu.HBM] * fetch
     if fetch:
-        buffers += [pltpu.VMEM(shape, array.dtype) for shape, array in zip(shapes, arrays)]
-        buffers += [pltpu.SemaphoreType.DMA((count,))]
-    space = pltpu.HBM if fetch else pltpu.VMEM
+        buffers += [pltpu.VMEM(shapes[i], arrays[i].dtype) for i in range(plain, count)]
+        buffers += [pltpu.SemaphoreType.DMA((fetch,))]
+        held = [pltpu.with_memory_space_constraint(array, pltpu.HBM) for array in arrays[plain:]]
+        arrays = (*arrays[:plain], *held)
+    cost = None
+    if function.__name__ in WORK:
+        cost = pl.CostEstimate(
+            flops=WORK[function.__name__], bytes_accessed=10**6, transcendentals=1
+        )
     call = pl.pallas_call(
         body,
         out_shape=[jax.ShapeDtypeStruct(shape, dtype) for shape, dtype in outputs],
-        in_specs=[pl.BlockSpec(memory_space=pltpu.SMEM)]
-        + [pl.BlockSpec(memory_space=space) for _ in arrays],
+        in_specs=[pl.BlockSpec(memory_space=space) for space in spaces],
         out_specs=[pl.BlockSpec(memory_space=pltpu.VMEM) for _ in outputs],
         scratch_shapes=buffers,
         compiler_params=pltpu.CompilerParams(vmem_limit_bytes=VMEM_LIMIT),
+        cost_estimate=cost,
         name=function.__name__,
     )
-    if fetch:
-        arrays = [pltpu.with_memory_space_constraint(array, pltpu.HBM) for array in arrays]
     return list(call(ids, *arrays))
 
 
@@ -114,10 +123,17 @@
     return product(a, b, 0, 0)
 
 
-def exact(a, b, left, right):
-    return lax.dot_general(
-        a, b, (((left,), (right,)), ((), ())), preferred_element_type=F32, precision=HIGH
-    )
+def split(array, count):
+    parts = []
+    for _ in range(count):
+        part = array.astype(BF16)
+        parts.append(part)
+        array = array - part.astype(F32)
+    return parts
+
+
+def pick(chosen, array, left, right, parts=2):
+    return sum(product(chosen, part, left, right) for part in split(array, parts))
 
 
 def iota(shape, axis):
@@ -144,7 +160,7 @@
 
 def head_sums(array):
     chosen = flag((iota((128, WIDE), 1) >> 6) == iota((128, WIDE), 0))
-    return exact(array, chosen, 1, 1)
+    return sum(dot_last(part, chosen) for part in split(array, 2))
 
 
 def gain_row(tail):
@@ -162,25 +178,26 @@
 
 
 def prepare(
-    ids, value_weight, gate_weight, state_proj, step_proj, norm_gain, out_weight, rim, left, longer, right
+    ids, value_weight, gate_weight, state_proj, step_proj, norm_gain, out_weight, rim, left, longer, right, ready
 ):
+    ready()
     for target in (left, longer):
         target[:ROWS, :WIDE] = value_weight[...]
-        target[:ROWS, WIDE : 2 * WIDE] = gate_weight[...]
-        target[:ROWS, 2 * WIDE :] = out_weight[:, :128]
-    longer[ROWS : ROWS + RIM] = rim[:, :NEAR]
-    longer[ROWS + RIM :, : D - NEAR] = rim[:, NEAR:]
+        target[:ROWS, WIDE:] = gate_weight[...]
+    last = rim[...].astype(F32)[8:]
+    longer[ROWS:] = jnp.concatenate([last[:, :PAIR], last[:, PAIR:]], axis=0).astype(BF16)
     right[:, : 2 * STATE] = state_proj[...]
     place = iota((HEADS, 128), 1) == STEP_LANE + iota((HEADS, 128), 0)
     tail = dot_first(step_proj[...], flag(place))
     tail = tail + dot_first(norm_gain[...], flag(iota((1, 128), 1) == GAIN_LANE))
     right[:, 2 * STATE : WIDE] = tail.astype(BF16)
-    right[:, WIDE:] = out_weight[:, 128:]
+    right[:, WIDE:] = out_weight[...]
 
 
 def tabulate(
-    ids, value_filter, state_filter, value_offset, state_offset, gate_gain, heads, hidden, consts, units
+    ids, value_filter, state_filter, value_offset, state_offset, gate_gain, heads, hidden, consts, units, ready
 ):
+    ready()
     units[...] = unit_rows(hidden[...])
     consts[...] = jnp.zeros(consts.shape, F32)
     consts[:KERNEL, :WIDE] = value_filter[...].astype(F32)
@@ -228,14 +245,15 @@
     filter_pre = consts[KERNEL : KERNEL + 1, :MIX]
     for tap in range(KERNEL):
         filter_pre = filter_pre + consts[tap : tap + 1, :MIX] * roll(inputs, KERNEL - 1 - tap, 0)[RIM:]
-    activated, wide[:, SLOPE] = silu_parts(filter_pre)
+    wide[:, SLOPE] = filter_pre
+    activated = filter_pre * jax.nn.sigmoid(filter_pre)
     lanes = iota((T, 128), 1) < HEADS
     step_in = roll(projected[RIM:, MIX:], 128 - STEP_LANE, 1) + consts[6:7, :128]
     step_in = jnp.where(lanes, step_in, -100.0)
     step = jnp.maximum(step_in, 0.0) + jnp.log1p(jnp.exp(-jnp.abs(step_in)))
     step = jnp.where(lanes, step, 0.0)
     rate = jnp.exp(consts[7:8, :128])
-    log_decay = exact(flag(iota((T, T), 0) >= iota((T, T), 1)), -step * rate, 1, 0)
+    log_decay = pick(flag(iota((T, T), 0) >= iota((T, T), 1)), -step * rate, 1, 0, 3)
     values = activated[:, :WIDE]
     weighted = (values * spread_heads(step)).astype(BF16)
     wide[:, VALUES] = values
@@ -265,10 +283,16 @@
 
 
 def project(
-    ids, l0, l1, l2, l3, l4, r0, r1, r2, r3, r4, hidden_in, cotangent, wide, narrow, gate_out, before
+    ids, l0, l1, l2, l3, l4, r0, r1, r2, r3, r4, hidden_in, cotangent, wide, narrow,
+    gate_out, before, slope, spread,
 ):
-    moves = (gate_out, 0, 0, WIDE, WIDE + 128), (gate_out, 1, WIDE + 128, WIDE, WIDE - 128)
+    moves = (gate_out, 0, 0, WIDE, WIDE), (gate_out, 1, WIDE, WIDE, WIDE)
     place_blocks(ids, (l0, l1, l2, l3, l4), (r0, r1, r2, r3, r4), *moves)
+    _, slope[...] = silu_parts(wide[:, SLOPE])
+    last = wide[T - 1 :, LOG_DECAY]
+    spread[:, GROWN] = spread_heads(jnp.exp(wide[:, LOG_DECAY]))
+    spread[:, TO_END] = spread_heads(jnp.exp(last - wide[:, LOG_DECAY]))
+    spread[:, STEPS] = spread_heads(wide[:, STEP])
     before[:, GATE_PRE] = dot(hidden_in[RIM:], gate_out[:, :WIDE])
     before[:, GRAD_NORMED] = dot(cotangent[...], gate_out[:, WIDE:])
     scores = dot_last(narrow[:, CMAT], narrow[:, BMAT])
@@ -284,7 +308,7 @@
         before[:, start : start + 128] = jnp.where(lower, one, two)
 
 
-def mix(ids, m1, m2, m3, wide, narrow, consts, before, state, after, sums):
+def mix(ids, m1, m2, m3, wide, spread, narrow, consts, before, state, after, sums):
     me = ids[0, 1]
     total = jnp.zeros((STATE, WIDE), F32)
     gap = jnp.zeros((1, WIDE), F32)
@@ -296,24 +320,24 @@
         total = total + scale * message[:STATE].astype(F32)
         gap = gap + log
     state[:STATE] = total
-    grown = spread_heads(jnp.exp(wide[:, LOG_DECAY]))
-    inside = before[:, WITHIN] + dot(narrow[:, CMAT], total) * grown
+    inside = before[:, WITHIN] + dot(narrow[:, CMAT], total) * spread[:, GROWN]
     after[:, INSIDE] = inside
     whole = inside + wide[:, VALUES] * spread_heads(consts[8:9, :128])
     after[:, MIXED] = whole
     gate = before[:, GATE_PRE]
     gated = whole * gate * jax.nn.sigmoid(gate)
     ones = jnp.ones((8, WIDE), F32)
-    squares = exact(ones, gated * gated, 1, 1)
-    crosses = exact(ones, before[:, GRAD_NORMED] * consts[5:6, :WIDE] * gated, 1, 1)
+    squares = pick(ones, gated * gated, 1, 1)
+    crosses = pick(ones, before[:, GRAD_NORMED] * consts[5:6, :WIDE] * gated, 1, 1)
     sums[...] = jnp.where(iota((8, T), 0) < 4, squares, crosses)
 
 
 def gate_back(
-    ids, s0, s1, s2, s3, after, before, consts, wide, narrow, gated_low, grad_mixed, grad_gain, sensitivity
+    ids, s0, s1, s2, s3, after, before, consts, spread, narrow, gated_low, grad_mixed, grad_gain, sensitivity
 ):
     total = s0[...] + s1[...] + s2[...] + s3[...]
-    columns = exact(total, flag(iota((8, 128), 0) == 4 * iota((8, 128), 1)), 0, 0)
+    chosen = flag(iota((8, 128), 0) == 4 * iota((8, 128), 1))
+    columns = sum(dot_first(part, chosen) for part in split(total, 3))
     inv = lax.rsqrt(columns[:, 0:1] / INNER + EPSILON)
     cross = columns[:, 1:2]
     act, slope = silu_parts(before[:, GATE_PRE])
@@ -327,11 +351,10 @@
     own = grad_gated * act
     grad_mixed[...] = own
     gated_low[:, LOW_GATE] = (grad_gated * mixed * slope).astype(BF16)
-    grown = spread_heads(jnp.exp(wide[:, LOG_DECAY]))
-    sensitivity[...] = dot_first(narrow[:, CMAT], own * grown).astype(BF16)
-
-
-def share_out(ids, source, keep, send):
+    sensitivity[...] = dot_first(narrow[:, CMAT], own * spread[:, GROWN]).astype(BF16)
+
+
+def turn_out(ids, source, keep, send):
     chip, core = ids[0, 2] >> 1, ids[0, 2] & 1
     for ahead in range(4):
         start = ((chip + ahead) & 3) * 2
@@ -366,7 +389,7 @@
 
 
 def leave(
-    ids, g1, g2, g3, state, after, grad_mixed, grads, wide, narrow, consts, taken, grad_gain,
+    ids, g1, g2, g3, state, after, grad_mixed, grads, wide, spread, slope, narrow, consts, taken, grad_gain,
     low, state_low, keep, send, small, turned,
 ):
     me = ids[0, 1]
@@ -377,45 +400,43 @@
         end = end + scale * message[...].astype(F32)
         start = STATE + 8 * (2 - ahead)
         gap = gap + state[start : start + 1]
-    step, step_slope, log_decay = wide[:, STEP], wide[:, STEP_SLOPE], wide[:, LOG_DECAY]
+    step, step_slope = wide[:, STEP], wide[:, STEP_SLOPE]
     values = wide[:, VALUES]
-    last = log_decay[T - 1 :]
-    to_end = spread_heads(jnp.exp(last - log_decay))
+    last = wide[T - 1 :, LOG_DECAY]
+    to_end = spread[:, TO_END]
     weighted = narrow[:, WEIGHTED].astype(F32)
     own = grad_mixed[...]
     from_end = dot(narrow[:, BMAT], end) * to_end
     inputs = grads[:, :WIDE] + from_end
     from_b = grads[:, WIDE : WIDE + STATE] + dot_last(weighted * to_end, end)
-    grown = spread_heads(jnp.exp(log_decay))
-    from_c = grads[:, WIDE + STATE :] + dot_last(own * grown, state[:STATE])
+    from_c = grads[:, WIDE + STATE :] + dot_last(own * spread[:, GROWN], state[:STATE])
     grad_log = head_sums(own.astype(BF16).astype(F32) * after[:, INSIDE] - weighted * inputs)
     at_end = jnp.sum(weighted * from_end, axis=0, keepdims=True) + jnp.exp(
         spread_heads(last)
     ) * jnp.sum(end * state[:STATE], axis=0, keepdims=True)
     at_end = head_sums(jnp.broadcast_to(at_end, (8, WIDE)))[0:1]
-    grad_decay = exact(flag(iota((T, T), 0) <= iota((T, T), 1)), grad_log, 1, 0) + at_end
+    grad_decay = pick(flag(iota((T, T), 0) <= iota((T, T), 1)), grad_log, 1, 0) + at_end
     rate = jnp.exp(consts[7:8, :128])
     grad_step = head_sums(values * inputs) - rate * grad_decay
     grad_step_pre = grad_step * step_slope
-    grad_values = own * spread_heads(consts[8:9, :128]) + inputs * spread_heads(step)
-    grad_pre = jnp.concatenate([grad_values, from_b, from_c], axis=1) * wide[:, SLOPE]
+    grad_values = own * spread_heads(consts[8:9, :128]) + inputs * spread[:, STEPS]
+    grad_pre = jnp.concatenate([grad_values, from_b, from_c], axis=1) * slope[...]
     before = taken[...].astype(F32)
     padded = jnp.concatenate([jnp.zeros((RIM, MIX), F32), grad_pre], axis=0)
     grad_input = jnp.zeros((EXT, MIX), F32)
     line = iota((8, MIX), 0)
     taps = jnp.where(line == KERNEL, jnp.sum(grad_pre, axis=0, keepdims=True), 0.0)
     for tap in range(KERNEL):
-        shift = KERNEL - 1 - tap
-        found = jnp.sum(grad_pre * roll(before, shift, 0)[RIM:], axis=0, keepdims=True)
-        taps = jnp.where(line == tap, found, taps)
-        grad_input = grad_input + consts[tap : tap + 1, :MIX] * roll(padded, -shift, 0)
+        later = roll(padded, tap + 1 - KERNEL, 0)
+        taps = jnp.where(line == tap, jnp.sum(before * later, axis=0, keepdims=True), taps)
+        grad_input = grad_input + consts[tap : tap + 1, :MIX] * later
     low[:, :WIDE] = grad_input[:, :WIDE].astype(BF16)
     state_low[...] = grad_input[:, WIDE:]
     low_step = jnp.concatenate([jnp.zeros((RIM, 128), F32), grad_step_pre], axis=0)
     low[:, WIDE:] = roll(low_step, STEP_LANE, 1).astype(BF16)
     rest = jnp.zeros((TURNED - EXT - 8, 2 * STATE), F32)
     turned[...] = jnp.concatenate([grad_input[:, WIDE:], taps[:, WIDE:], rest], axis=0).T
-    share_out(ids, turned, keep, send)
+    turn_out(ids, turned, keep, send)
     heads = (
         jnp.sum(grad_step_pre, axis=0, keepdims=True),
         -rate * jnp.sum(grad_decay * step, axis=0, keepdims=True),
@@ -427,23 +448,31 @@
     small[...] = jnp.where(line == 5, grad_gain[...], jnp.where(line == 6, heads, taps[:, :WIDE]))
 
 
-def two_parts(array):
-    high = array.astype(BF16)
-    return high, array - high.astype(F32)
-
-
 def pair_sum(ids, keep, got, *shares):
     for ahead, share in enumerate(shares):
         share[...] = (keep[ahead].astype(F32) + got[ahead].astype(F32)).astype(share.dtype)
 
 
-def value_grads(ids, low, state_low, gated_low, weights, gate_out, hidden_in, pair, value, head):
+def value_grads(
+    ids, low, state_low, gated_low, weights, gate_out, hidden_in, pair, value, head
+):
     value[...] = dot_first(hidden_in[...], low[:, :WIDE]).astype(BF16)
     part = dot_last(low[:, :WIDE], weights[:, :WIDE]) + dot_last(low[:, WIDE:], weights[:, MIX:])
-    high, rest = two_parts(state_low[...])
+    high, rest = split(state_low[...], 2)
     part = part + dot_last(high, weights[:, WIDE:MIX]) + dot_last(rest, weights[:, WIDE:MIX])
     head[:RIM] = part[:RIM]
     head[RIM:] = part[RIM:] + dot_last(gated_low[:, LOW_GATE], gate_out[:, :WIDE])
+
+
+def share_out(ids, head, branch, keep, send, whole):
+    whole[...] = head[RIM:].astype(BF16)
+    chip, core = ids[0, 2] >> 1, ids[0, 2] & 1
+    for other in range(4):
+        start = (chip ^ other) * 2
+        for half, source in enumerate((whole, branch)):
+            rows = slice(half * SHARE, half * SHARE + SHARE)
+            keep[other, rows] = source[aligned((start + core) * SHARE, SHARE)]
+            send[other, rows] = source[aligned((start + 1 - core) * SHARE, SHARE)]
 
 
 def fold(small):
@@ -474,48 +503,55 @@
 
 
 def late_grads(
-    ids, t0, t1, t2, t3, low, small, head, rim, units, hidden_in, gate, out, value, *targets
+    ids, t0, t1, t2, t3, low, small, head, rim, units, hidden_in, gate, out, value, branch, keep, send, *targets
 ):
-    targets, tail = targets[:-1], targets[-1]
+    targets, tail, whole = targets[:-2], targets[-2], targets[-1]
     total = t0[...] + t1[...] + t2[...] + t3[...]
     straight = jnp.concatenate([total, jnp.zeros((128 - PART, TURNED), F32)], axis=0).T
     low_tail = low[:, WIDE:].astype(F32) + straight[:EXT]
-    terms = jnp.concatenate([head[:RIM] * unit_rows(rim[...]), head[RIM:] * units[...]], axis=0)
+    terms = jnp.sum(head[:RIM] * unit_rows(rim[...]), axis=0, keepdims=True)
+    terms = terms + jnp.sum(head[RIM:] * units[...], axis=0, keepdims=True)
     grads = dot_first(hidden_in[...], low_tail)
-    grads = grads + dot_first(terms, flag(iota((EXT, 128), 1) == GAIN_LANE))
+    row = jnp.where(iota((8, D), 0) == 0, terms, 0.0)
+    chosen = flag(iota((8, 128), 1) == GAIN_LANE)
+    grads = grads + sum(dot_first(part, chosen) for part in split(row, 2))
     tail[...] = grads.astype(BF16)
     own = straight[EXT : EXT + 8]
     row = jnp.concatenate([own[0:1] + roll(own[1:2], 64, 1), own[2:3] + roll(own[3:4], 64, 1), own[4:5]], axis=1)
     folded = fold(jnp.where(iota((8, WIDE), 0) == 7, row, small[...]))
-    arrange(ids, gate, out, value, tail, folded, targets)
-    for chunk, (slot, start) in enumerate(RIM_SLOTS):
-        targets[8][slot, start : start + RIM] = head[:RIM, RIGHT * chunk : RIGHT * chunk + RIGHT].astype(
-            BF16
-        )
-
-def arrange(ids, gate, out, value, tail, folded, targets):
+    lanes = iota((ROWS, 128), 1) < 64
+    for target, place, block in places(ids, 0, targets[:5]):
+        rows = aligned(block * ROWS, ROWS)
+        target[place, :, :WIDE] = gate[rows]
+        target[place, :, WIDE:] = value[rows]
+    for target, place, block in places(ids, 1, targets[5:]):
+        rows = aligned(block * ROWS, ROWS)
+        target[place, :ROWS, :OUT_RIGHT] = out[rows]
+        end = jnp.where(lanes, tail[rows].astype(F32), folded)
+        target[place, :ROWS, OUT_RIGHT:] = end.astype(BF16)
+    share_out(ids, head, branch, keep, send, whole)
+    last = head[:RIM][8:]
+    pieces = [last[:, RIGHT * chunk : RIGHT * chunk + RIGHT] for chunk in range(D // RIGHT)]
+    pieces.append(jnp.zeros((8, RIGHT), F32))
+    for slot in range(2):
+        targets[8][slot, ROWS:] = jnp.concatenate(pieces[2 * slot : 2 * slot + 2], axis=0).astype(BF16)
+
+
+def places(ids, side, targets):
     line, ctx = ids[0, 0], ids[0, 1]
-    lanes = iota((ROWS, 128), 1) < 64
     for far in range(4):
         for near in range(4):
             slot, place = far + far // 3, near
             if far == 2 and near >= 2:
                 slot, place = 3, near - 2
-            block = ((line + far) & 3) * 4 + ((ctx + near) & 3)
-            rows = aligned(block * ROWS, ROWS)
-            targets[slot][place, :, :WIDE] = gate[rows]
-            targets[slot][place, :, WIDE:] = value[rows]
-            block = ((line + near) & 3) * 4 + ((ctx + far) & 3)
-            rows = aligned(block * ROWS, ROWS)
-            end = jnp.where(lanes, tail[rows].astype(F32), folded).astype(BF16)
-            targets[5 + slot][place, :ROWS, :WIDE] = out[rows]
-            targets[5 + slot][place, :ROWS, WIDE:] = end
+            one, two = (near, far) if side else (far, near)
+            yield targets[slot], place, ((line + one) & 3) * 4 + ((ctx + two) & 3)
 
 
 def put(target, total, tailed):
     if tailed:
-        target[:, :WIDE] = total[:, :WIDE].astype(BF16)
-        target[:, WIDE:] = tidy(total[:, WIDE:]).astype(BF16)
+        target[:, :OUT_RIGHT] = total[:, :OUT_RIGHT].astype(BF16)
+        target[:, OUT_RIGHT:] = tidy(total[:, OUT_RIGHT:]).astype(BF16)
     else:
         target[...] = total.astype(BF16)
 
@@ -527,71 +563,93 @@
         target[other // 2] = total.astype(BF16)
 
 
-def pair_again(ids, near, got, own, second):
+def relay(side, one, three, first, second, to_one, to_three):
+    for near in range(4):
+        if near < 2:
+            total = one[near].astype(F32) + first[near].astype(F32)
+            put(to_one.at[near], total, side)
+            to_three[near] = three[near]
+        else:
+            total = three[near].astype(F32) + second[near - 2, :ROWS].astype(F32)
+            put(to_three.at[near], total, side)
+            to_one[near] = one[near]
+
+
+def relay_both(ids, *refs):
+    relay(0, *refs[:4], *refs[9:11])
+    relay(1, *refs[4:8], *refs[11:13])
+    second, behind = refs[7], refs[13]
+    inside = jnp.where(ids[0, 1] < 3, 1.0, 0.0)
+    for chunk in range(D // RIGHT):
+        got = second[chunk // 2, ROWS:].astype(F32) * inside
+        start = 8 * (chunk % 2)
+        behind[:, RIGHT * chunk : RIGHT * chunk + RIGHT] = got[start : start + 8]
+
+
+def halfway(side, own, one, three, *targets):
+    for near, target in enumerate(targets):
+        total = own[near].astype(F32) + one[near].astype(F32) + three[near].astype(F32)
+        put(target, total, side)
+
+
+def halfway_both(ids, l0, l1, l3, r0, r1, r3, own, *targets):
+    halfway(0, l0, l1, l3, *targets[:4])
+    halfway(1, r0, r1, r3, *targets[4:])
+
+
+def pair_again(ids, near, got, cotangent, hidden, own, second, held, mine, last):
     for index, target in enumerate((own, second)):
         target[...] = (near[index].astype(F32) + got[index].astype(F32)).astype(BF16)
-
-
-def relay(ids, *refs):
-    for side in range(2):
-        one, three, first, second = refs[4 * side : 4 * side + 4]
-        to_one, to_three = refs[10 + 2 * side : 12 + 2 * side]
-        for near in range(4):
-            if near < 2:
-                total = one[near].astype(F32) + first[near].astype(F32)
-                put(to_one.at[near], total, side)
-                to_three[near] = three[near]
-            else:
-                total = three[near].astype(F32) + second[near - 2, :ROWS].astype(F32)
-                put(to_three.at[near], total, side)
-                to_one[near] = one[near]
-    head, branch = refs[8:10]
-    keep, send, whole = refs[14:]
-    inside = jnp.where(ids[0, 1] < 3, 1.0, 0.0)
-    whole[: T - RIM] = head[RIM:T].astype(BF16)
-    for chunk, (slot, start) in enumerate(RIM_SLOTS):
-        columns = slice(RIGHT * chunk, RIGHT * chunk + RIGHT)
-        behind = refs[7][slot, start : start + RIM].astype(F32) * inside
-        whole[T - RIM :, columns] = (head[T:, columns] + behind).astype(BF16)
-    chip, core = ids[0, 2] >> 1, ids[0, 2] & 1
-    for other in range(4):
-        start = (chip ^ other) * 2
-        for half, source in enumerate((whole, branch)):
-            rows = slice(half * SHARE, half * SHARE + SHARE)
-            keep[other, rows] = source[aligned((start + core) * SHARE, SHARE)]
-            send[other, rows] = source[aligned((start + 1 - core) * SHARE, SHARE)]
-
-
-def halfway(ids, *refs):
-    for side in range(2):
-        own, one, three = refs[3 * side : 3 * side + 3]
-        for near in range(4):
-            total = own[near].astype(F32) + one[near].astype(F32) + three[near].astype(F32)
-            put(refs[7 + 4 * side + near], total, side)
-
-
-def collect(
-    ids, a0, a1, a2, a3, b0, b1, b2, b3, settled,
-    grad_gate, grad_value, grad_out, grad_step, taps, offset, gain, bias, decay, skip, message, rest,
+    held[...] = cotangent[...]
+    mine[...] = hidden[aligned(ids[0, 2] * SHARE, SHARE)]
+    last[...] = hidden[T - RIM :].astype(F32)[8:]
+
+
+def collect_left(ids, a0, a1, a2, a3, b0, b1, b2, b3, grad_gate, grad_value, grad_out):
+    total = sum(part[...].astype(F32) for part in (a0, a1, a2, a3))
+    grad_gate[...] = total[:, :WIDE]
+    grad_value[...] = total[:, WIDE:]
+    grad_out[...] = sum(part[:, :OUT_RIGHT].astype(F32) for part in (b0, b1, b2, b3))
+
+
+def hidden_back(grads, rows, gain):
+    tokens = rows.astype(F32)
+    inv = lax.rsqrt(jnp.mean(tokens * tokens, axis=1, keepdims=True) + EPSILON)
+    unit = tokens * inv
+    scaled = grads * gain
+    return inv * (scaled - unit * jnp.mean(scaled * unit, axis=1, keepdims=True)), tokens
+
+
+def gather_up(
+    ids, b0, b1, b2, b3, p0, p1, mine, weights, behind,
+    message, gain_out, grad_step, taps, offset, gain, bias, decay, skip, rest,
 ):
-    left = sum(part[...].astype(F32) for part in (a0, a1, a2, a3))
-    right = sum(part[...].astype(F32) for part in (b0, b1, b2, b3))
-    grad_gate[...] = left[:, :WIDE]
-    grad_value[...] = left[:, WIDE:]
-    grad_out[...] = right[:, :WIDE]
-    total = right[:, WIDE:]
-    rest[:ROWS] = total
+    both = p0[...].astype(F32) + p1[...].astype(F32)
+    row = gain_row(weights[:, MIX:])
+    gain_out[...] = jnp.broadcast_to(row, (8, D))
+    grads, tokens = hidden_back(both[:SHARE], mine[...], row)
+    message[:SHARE] = grads.astype(BF16)
+    message[SHARE : 2 * SHARE] = (tokens + both[SHARE:]).astype(BF16)
+    total = sum(part[:, OUT_RIGHT:].astype(F32) for part in (b0, b1, b2, b3))
+    rest[...] = total
     small = unfold(total)
     state = small[7:8]
-    rest[ROWS:] = jnp.zeros((REST - ROWS, 128), F32)
+    lanes = iota((8, 128), 1)
     for tap in range(KERNEL + 1):
         piece = state[:, pair_columns(tap // 2)]
-        rest[ROWS + tap : ROWS + tap + 1] = piece if tap % 2 else roll(piece, 64, 1)
+        piece = piece if tap % 2 == 0 else roll(piece, 64, 1)
+        if tap == 0:
+            rows = jnp.where(iota((8, 128), 0) == 0, roll(piece, STATE_LANE, 1), 0.0)
+        else:
+            rows = jnp.where(iota((8, 128), 0) == tap, roll(piece, STATE_LANE, 1), rows)
+    rest[:8] = jnp.where(lanes < 64, rest[:8], rows)
+    for block in range(ROWS // 16):
+        message[2 * SHARE :, pair_columns(block)] = rest[16 * block : 16 * block + 16].astype(BF16)
+    for block in range(6):
+        pair = [behind[:, pair_columns(2 * block + i)] for i in range(2)]
+        message[2 * SHARE :, pair_columns(6 + block)] = jnp.concatenate(pair, axis=0).astype(BF16)
     picked = flag(iota((8, 128), 1) == STEP_LANE + iota((8, 128), 0))
-    grad_step[...] = exact(picked, total, 1, 1)[:HEADS]
-    message[: 2 * SHARE] = settled[...]
-    for block in range(REST // 16):
-        message[2 * SHARE :, pair_columns(block)] = rest[16 * block : 16 * block + 16].astype(BF16)
+    grad_step[...] = pick(picked, total, 1, 1, 3)[:HEADS]
     taps[...] = small[:KERNEL]
     offset[...] = small[KERNEL : KERNEL + 1]
     gain[...] = small[5:6]
@@ -600,47 +658,44 @@
     skip[...] = small[6:7, 128 : 128 + HEADS]
 
 
-def finish(
-    ids, a0, a1, a2, a3, b0, b1, b2, b3, cotangent,
-    grad_hidden, block_out, grad_state, grad_gain, taps, offset, rest,
-):
+def finish(ids, *refs):
+    pieces, row, cotangent, last = refs[:8], refs[8], refs[9], refs[10]
+    grad_hidden, block_out, grad_state, grad_gain, taps, offset, rest, rims = refs[11:]
     chip, core = ids[0, 2] >> 1, ids[0, 2] & 1
-    for far, pair in enumerate(((a0, b0), (a1, b1), (a2, b2), (a3, b3))):
+    order = []
+    for far in range(4):
         start = ((chip - far) & 3) * 2
-        for place, piece in zip((start + core, start + 1 - core), pair):
-            rows = aligned(place * SHARE, SHARE)
-            grad_hidden[rows] = cotangent[rows].astype(F32) + piece[:SHARE].astype(F32)
-            block_out[rows] = piece[SHARE : 2 * SHARE]
-            for block in range(REST // 16):
-                part = piece[2 * SHARE :, pair_columns(block)]
-                rest[place, 16 * block : 16 * block + 16] = part.astype(F32)
-    lanes = iota((REST, 128), 1) >> 5
-    total = rest[0]
+        order += [(start + core, pieces[far]), (start + 1 - core, pieces[4 + far])]
+    for place, piece in order:
+        block_out[aligned(place * SHARE, SHARE)] = piece[SHARE : 2 * SHARE]
+        for block in range(6):
+            part = piece[2 * SHARE :, pair_columns(block)]
+            rest[place, 16 * block : 16 * block + 16] = part.astype(F32)
+            part = piece[2 * SHARE :, pair_columns(6 + block)].astype(F32)
+            rims[place, :, pair_columns(2 * block)] = part[:8]
+            rims[place, :, pair_columns(2 * block + 1)] = part[8:]
+    total, behind = rest[0], rims[0]
+    for i in range(1, 8):
+        total = total + rest[i]
+        behind = behind + rims[i]
+    for place, piece in order:
+        rows = aligned(place * SHARE, SHARE)
+        grad_hidden[rows] = cotangent[rows].astype(F32) + piece[:SHARE].astype(F32)
+    grads, _ = hidden_back(behind, last[...], row[0:1])
+    grad_hidden[T - 8 :] = grad_hidden[T - 8 :] + grads
+    lanes = iota((ROWS, 128), 1) >> 5
     for half in range(2):
-        state = jnp.zeros((REST, 128), F32)
-        small = jnp.zeros((REST, 128), F32)
+        state = jnp.zeros((ROWS, 128), F32)
+        small = jnp.zeros((8, 128), F32)
         for i in range(4):
             one = rest[4 * half + i]
             state = jnp.where(lanes == i, roll(one, PART * i, 1), state)
-            small = jnp.where(lanes == i, roll(one, PART * i - STATE_LANE, 1), small)
-            if half + i:
-                total = total + one
+            small = jnp.where(lanes[:8] == i, roll(one[:8], PART * i - STATE_LANE, 1), small)
         columns = pair_columns(half)
-        grad_state[:, columns] = state[:ROWS]
-        taps[:, columns] = small[ROWS : ROWS + KERNEL]
-        offset[:, columns] = small[ROWS + KERNEL : ROWS + KERNEL + 1]
-    grad_gain[...] = exact(flag(iota((8, 128), 1) == GAIN_LANE), total[:ROWS], 1, 1)[0:1]
-
-
-def settle(ids, p0, p1, hidden, weights, settled):
-    both = p0[...].astype(F32) + p1[...].astype(F32)
-    mine = hidden[aligned(ids[0, 2] * SHARE, SHARE)].astype(F32)
-    inv = lax.rsqrt(jnp.mean(mine * mine, axis=1, keepdims=True) + EPSILON)
-    unit = mine * inv
-    scaled = both[:SHARE] * gain_row(weights[:, MIX:])
-    tokens = inv * (scaled - unit * jnp.mean(scaled * unit, axis=1, keepdims=True))
-    settled[:SHARE] = tokens.astype(BF16)
-    settled[SHARE:] = (mine + both[SHARE:]).astype(BF16)
+        grad_state[:, columns] = state
+        taps[:, columns] = small[:KERNEL]
+        offset[:, columns] = small[KERNEL : KERNEL + 1]
+    grad_gain[...] = pick(flag(iota((8, 128), 1) == GAIN_LANE), total, 1, 1, 3)[0:1]
 
 
 def stack_blocks(ids, l0, l1, l2, l3, r0, r1, r2, r3, left, right, rim):
@@ -648,8 +703,10 @@
         left[i] = one[:ROWS]
         right[i] = two[...]
     inside = jnp.where(ids[0, 1] > 0, 1.0, 0.0)
-    rim[:, :NEAR] = (l1[ROWS : ROWS + RIM].astype(F32) * inside).astype(BF16)
-    rim[:, NEAR:] = (l1[ROWS + RIM :, : D - NEAR].astype(F32) * inside).astype(BF16)
+    got = l1[ROWS:].astype(F32) * inside
+    none = jnp.zeros((8, PAIR), F32)
+    rim[:, :PAIR] = jnp.concatenate([none, got[:8]], axis=0).astype(BF16)
+    rim[:, PAIR:] = jnp.concatenate([none, got[8:]], axis=0).astype(BF16)
 
 
 def shift(array, axis, steps):
@@ -706,7 +763,7 @@
 
     left, longer, right = fuse(
         prepare,
-        [((ROWS, NEAR), BF16), ((ROWS + 2 * RIM, NEAR), BF16), ((ROWS, FAR), BF16)],
+        [((ROWS, PAIR), BF16), ((ROWS + RIM, PAIR), BF16), ((ROWS, PAIR), BF16)],
         ids,
         value_weight,
         gate_weight,
@@ -715,13 +772,13 @@
         norm_gain[None],
         out_weight.T,
         hidden,
-        fetch=True,
+        fetch=7,
         rim=True,
     )
     near = [left, shift(longer, "ctx", 1), shift(left, "ctx", 2), shift(left, "ctx", 3)]
     left, right, rim = fuse(
         stack_blocks,
-        [((4, ROWS, NEAR), BF16), ((4, ROWS, FAR), BF16), ((RIM, D), BF16)],
+        [((4, ROWS, PAIR), BF16)] * 2 + [((RIM, D), BF16)],
         ids,
         *near,
         *around(right, "dp"),
@@ -737,7 +794,7 @@
         gate_norm_gain[None],
         jnp.stack([step_bias, decay_log, skip_gain]),
         hidden,
-        fetch=True,
+        fetch=7,
     )
     left = ring_rest(left, "dp", *ring_sides(left, "dp"))
     right = ring_rest(right, "ctx", *ring_sides(right, "ctx"))
@@ -759,9 +816,9 @@
         consts,
     )
     messages = around(message, "ctx")[1:]
-    gate_out, before = fuse(
+    gate_out, before, slope, spread = fuse(
         project,
-        [((D, 2 * WIDE), BF16), ((T, WITHIN.stop), F32)],
+        [((D, 2 * WIDE), BF16), ((T, WITHIN.stop), F32), ((T, MIX), F32), ((T, STEPS.stop), F32)],
         ids,
         *left,
         *right,
@@ -776,6 +833,7 @@
         ids,
         *messages,
         wide,
+        spread,
         narrow,
         consts,
         before,
@@ -795,7 +853,7 @@
         after,
         before,
         consts,
-        wide,
+        spread,
         narrow,
     )
     later = [shift(sensitivity, "ctx", -steps) for steps in range(1, 4)]
@@ -822,6 +880,8 @@
         grad_mixed,
         grads,
         wide,
+        spread,
+        slope,
         narrow,
         consts,
         taken,
@@ -848,13 +908,13 @@
     def stage(count, rows, columns):
         return (count, rows, columns), BF16
 
-    outputs = []
-    for columns, rows in ((LEFT, ROWS), (RIGHT, ROWS + 2 * RIM)):
+    def stages(columns, rows):
         whole = stage(4, ROWS, columns)
-        outputs += [whole, whole, stage(2, ROWS, columns), stage(2, rows, columns), whole]
-    blocks = fuse(
+        return [whole, whole, stage(2, ROWS, columns), stage(2, rows, columns), whole]
+
+    keep, send, *blocks = fuse(
         late_grads,
-        outputs,
+        [((4, 2 * SHARE, D), BF16)] * 2 + stages(LEFT, ROWS) + stages(RIGHT, ROWS + RIM),
         ids,
         *turned,
         low,
@@ -866,42 +926,57 @@
         gate,
         out,
         value,
-        scratch=[((D, 128), BF16)],
+        branch,
+        scratch=[((D, 128), BF16), ((T, D), BF16)],
     )
     left, right = blocks[:5], blocks[5:]
-    halves = []
-    for side, axis in ((left, "dp"), (right, "ctx")):
-        halves += [side[1], side[4], shift(side[2], axis, 1), shift(side[3], axis, 3)]
-    *sides, keep, send = fuse(
-        relay,
-        [stage(4, ROWS, LEFT)] * 2 + [stage(4, ROWS, RIGHT)] * 2 + [((4, 2 * SHARE, D), BF16)] * 2,
-        ids,
-        *halves,
-        head,
-        branch,
-        scratch=[((T, D), BF16)],
+    near, far = fuse(pair_halves, [two] * 2, ids, keep, across(send, 1))
+    *sides, behind = fuse(
+        relay_both,
+        [stage(4, ROWS, LEFT)] * 2 + [stage(4, ROWS, RIGHT)] * 2 + [((8, D), F32)],
+        ids,
+        *(left[1], left[4], shift(left[2], "dp", 1), shift(left[3], "dp", 3)),
+        *(right[1], right[4], shift(right[2], "ctx", 1), shift(right[3], "ctx", 3)),
+        near,
     )
     left = [left[0], shift(sides[0], "dp", 1), shift(sides[1], "dp", 3)]
     right = [right[0], shift(sides[2], "ctx", 1), shift(sides[3], "ctx", 3)]
-    near, far = fuse(pair_halves, [two] * 2, ids, keep, across(send, 1))
-    own, second = fuse(pair_again, [both] * 2, ids, near, across(far, 2))
-    outputs = [((ROWS, LEFT), BF16)] * 4 + [((ROWS, RIGHT), BF16)] * 4
-    sums = fuse(halfway, outputs, ids, *left, *right, own)
+    own, second, held, mine, last = fuse(
+        pair_again,
+        [both, both, ((T, D), BF16), ((SHARE, D), BF16), ((8, D), F32)],
+        ids,
+        near,
+        across(far, 2),
+        cotangent,
+        hidden,
+    )
+    sums = fuse(
+        halfway_both,
+        [((ROWS, LEFT), BF16)] * 4 + [((ROWS, RIGHT), BF16)] * 4,
+        ids,
+        *left,
+        *right,
+        own,
+    )
     left = sums[:1] + [shift(sums[steps], "ctx", steps) for steps in range(1, 4)]
     right = sums[4:5] + [shift(sums[4 + steps], "dp", steps) for steps in range(1, 4)]
-    (settled,) = fuse(settle, [both], ids, own, across(second, 4), hidden, weights)
     few, line = ((1, HEADS), F32), ((1, WIDE), F32)
-    grad_gate, grad_value, grad_out, grad_step, taps, offset, gain, bias, decay, skip, message = fuse(
-        collect,
-        [((ROWS, WIDE), F32)] * 3
-        + [((HEADS, ROWS), F32), ((KERNEL, WIDE), F32)]
-        + [line, line, few, few, few]
-        + [((2 * SHARE + 16, D), BF16)],
-        ids,
-        *left,
+    message, gain_full, *few_grads = fuse(
+        gather_up,
+        [((2 * SHARE + 16, D), BF16), ((8, D), F32), ((HEADS, ROWS), F32), ((KERNEL, WIDE), F32)]
+        + [line, line, few, few, few],
+        ids,
         *right,
-        settled,
-        scratch=[((REST, 128), F32)],
+        own,
+        across(second, 4),
+        mine,
+        weights,
+        behind,
+        scratch=[((ROWS, 128), F32)],
+    )
+    grad_step, taps, offset, gain, bias, decay, skip = few_grads
+    grad_gate, grad_value, grad_out = fuse(
+        collect_left, [((ROWS, WIDE), F32)] * 3, ids, *left, *right
     )
     grad_hidden, block_out, grad_state, grad_norm_gain, state_taps, state_offset = fuse(
         finish,
@@ -915,8 +990,10 @@
         ],
         ids,
         *chips_all(message),
-        cotangent,
-        scratch=[((8, REST, 128), F32)],
+        gain_full,
+        held,
+        last,
+        scratch=[((8, ROWS, 128), F32), ((8, 8, D), F32)],
     )
     return (
         block_out[None],

time: 160 us -> 152 us (0.950)
  starting transfers between devices: 73.4 us -> 69.8 us
  waiting for transfers between devices: 48.8 us -> 45.6 us
    ppermute x9, starting transfers between devices: 28.4 us -> 21.6 us  [across(): return lax.ppermute(array, 'tp', [(i, i ^ bits) for i in range(8)])]
    ppermute x9, waiting for transfers between devices: 8.6 us -> 1.92 us  [across(): return lax.ppermute(array, 'tp', [(i, i ^ bits) for i in range(8)])]
    ppermute x34, waiting for transfers between devices: 37 us -> 40.6 us  [shift(): return lax.ppermute(array, axis, [(i, (i + steps) % 4) for i in range(4)])]
    ppermute x34, starting transfers between devices: 35.6 us -> 38.6 us  [shift(): return lax.ppermute(array, axis, [(i, (i + steps) % 4) for i in range(4)])]
  transfers between devices with their start and end apart: 52 -> 52, of which waited for: 20 -> 20; matrix products, arithmetic and copies ran while one was open for 2% -> 2% of each run, Pallas kernels for 8% -> 11%
where the time goes in v3:
time: 152 us
  starting transfers between devices  69.8 us (46%)
  waiting for transfers between devices  45.6 us (30%)
  Pallas kernels  31.5 us (21%)
  other arithmetic  1.86 us (1%)
  local copies, waits for them, and re-layouts  1.82 us (1%)
    ppermute x34, waiting for transfers between devices, shift(): return lax.ppermute(array, axis, [(i, (i + steps) % 4) for i in range(4)])  40.6 us
    ppermute x34, starting transfers between devices, shift(): return lax.ppermute(array, axis, [(i, (i + steps) % 4) for i in range(4)])  38.6 us
    pallas_call x19, Pallas kernels, fuse(): return list(call(ids, *arrays))  31.5 us
    ppermute x9, starting transfers between devices, across(): return lax.ppermute(array, 'tp', [(i, i ^ bits) for i in range(8)])  21.6 us
    ppermute x9, starting transfers between devices, from_chip(): lax.ppermute(array, 'tp', [(i, (i + 2 * steps) % 8) for i in range(8)])  9.57 us
    ppermute x9, waiting for transfers between devices, from_chip(): lax.ppermute(array, 'tp', [(i, (i + 2 * steps) % 8) for i in range(8)])  3.12 us
  transfers between devices with their start and end apart: 52, of which 20 were waited for; matrix products, arithmetic and copies ran while one was open for 2% of the time, Pallas kernels for 11%

profile of v3, /device:TPU:1, one launch (start us, length us, event | category | flops | bytes accessed | tf_op | source)
XLA Modules:
  0.0 151.6 jit_solution(3869691791545467168)
XLA Ops:
  2.6 3.6 %collective-permute-start.2 = (bf16[96,768]{1,0:T(8,128)(2,1)S(1)}, bf16[96,768]{1,0:T(8,128)(2,1)S(1)}, u32[]{:S(2)}, u32[]{:S(2)}) collective-permute-start(bf16[96,768]{1,0:T(8,128)(2,1)S(1)} %get-tuple-element.106.refs_1_), channel_id=1, source_target_pairs={{0,24},{8,0},{16,8},{24,16},{1,25},{9,1},{17,9},{25,17},{2,26},{10... | collective-permute-start | bytes 442376 | tf_op jit(solution)/shard_map/ppermute | solution.py:713
  7.9 3.8 %collective-permute-start.5 = (bf16[96,768]{1,0:T(8,128)(2,1)S(1)}, bf16[96,768]{1,0:T(8,128)(2,1)S(1)}, u32[]{:S(2)}, u32[]{:S(2)}) collective-permute-start(bf16[96,768]{1,0:T(8,128)(2,1)S(1)} %get-tuple-element.108.refs_5_), channel_id=1, source_target_pairs={{0,96},{32,0},{64,32},{96,64},{1,97},{33,1},{65,33},{97,65},{2,98}... | collective-permute-start | bytes 442376 | tf_op jit(solution)/shard_map/ppermute | solution.py:713
  12.3 2.2 %collective-permute-done.1.refs_3_ = bf16[96,768]{1,0:T(8,128)(2,1)S(1)} collective-permute-done((bf16[96,768]{1,0:T(8,128)(2,1)S(1)}, bf16[96,768]{1,0:T(8,128)(2,1)S(1)}, u32[]{:S(2)}, u32[]{:S(2)}) %collective-permute-start.1) | collective-permute-done | bytes 147488 | tf_op jit(solution)/shard_map/ppermute | solution.py:713
  14.5 2.7 %collective-permute-done.5.refs_8_ = bf16[96,768]{1,0:T(8,128)(2,1)S(1)} collective-permute-done((bf16[96,768]{1,0:T(8,128)(2,1)S(1)}, bf16[96,768]{1,0:T(8,128)(2,1)S(1)}, u32[]{:S(2)}, u32[]{:S(2)}) %collective-permute-start.5) | collective-permute-done | bytes 147488 | tf_op jit(solution)/shard_map/ppermute | solution.py:713
  17.2 3.9 %collective-permute-done.3.refs_6_ = bf16[96,768]{1,0:T(8,128)(2,1)S(1)} collective-permute-done((bf16[96,768]{1,0:T(8,128)(2,1)S(1)}, bf16[96,768]{1,0:T(8,128)(2,1)S(1)}, u32[]{:S(2)}, u32[]{:S(2)}) %collective-permute-start.3) | collective-permute-done | bytes 147488 | tf_op jit(solution)/shard_map/ppermute | solution.py:713
  25.0 10.6 %collective-permute-done.8.refs_5_ = bf16[4,96,768]{2,1,0:T(8,128)(2,1)S(1)} collective-permute-done((bf16[4,96,768]{2,1,0:T(8,128)(2,1)S(1)}, bf16[4,96,768]{2,1,0:T(8,128)(2,1)S(1)}, u32[]{:S(2)}, u32[]{:S(2)}) %collective-permute-start.8) | collective-permute-done | bytes 589856 | tf_op jit(solution)/shard_map/ppermute | solution.py:713
  41.4 2.1 %tabulate.1 = (f32[16,768]{1,0:T(8,128)S(1)}, f32[256,1536]{1,0:T(8,128)S(1)}) custom-call(s32[1,3]{1,0:T(1,128)S(1)} %add_bitcast_fusion.refs_0_, bf16[4,384]{1,0:T(4,128)(2,1)} %refs_1_.3, bf16[4,256]{1,0:T(4,128)(2,1)} %refs_2_.3, bf16[1,384]{1,0:T(2,128)(2,1)} %broadcast_in_dim.19.refs_3_, bf16[1,256]{1,0:T(2,128)(2,1)} %broadcast_in_dim.20.refs_4_, ...), custom_call_target="tpu_custom_call" | custom-call | tf_op jit(solution)/shard_map/tabulate/pallas_call | solution.py:98
  44.5 2.9 %enter.1 = (bf16[1536,768]{1,0:T(8,128)(2,1)S(1)}, bf16[272,1536]{1,0:T(8,128)(2,1)S(1)}, bf16[272,640]{1,0:T(8,128)(2,1)S(1)}, f32[256,1408]{1,0:T(8,128)S(1)},...) custom-call(s32[1,3]{1,0:T(1,128)S(1)} %add_bitcast_fusion.refs_0_, ...), custom_call_target="tpu_custom_call" | custom-call | tf_op jit(solution)/shard_map/enter/pallas_call | solution.py:98
  50.5 2.4 %project.1 = (bf16[1536,768]{1,0:T(8,128)(2,1)S(1)}, f32[256,1152]{1,0:T(8,128)S(1)}, f32[256,640]{1,0:T(8,128)S(1)}, f32[256,1152]{1,0:T(8,128)S(1)}) custom-call(s32[1,3]{1,0:T(1,128)S(1)} %add_bitcast_fusion.refs_0_, bf16[4,96,768]{2,1,0:T(8,128)(2,1)S(1)} %get-tuple-element.109.refs_1_, bf16[4,96,768]{2,1,0:T(8,128)(2,1)S(1)} %collective-permute-done.6.refs_2_, ...), custom_call_target="tpu_custom_call" | custom-call | tf_op jit(solution)/shard_map/project/pallas_call | solution.py:98
  55.9 5.4 %collective-permute-start.17 = (f32[8,256]{1,0:T(8,128)S(1)}, f32[8,256]{1,0:T(8,128)S(1)}, u32[]{:S(2)}, u32[]{:S(2)}) collective-permute-start(f32[8,256]{1,0:T(8,128)S(1)} %get-tuple-element.120), channel_id=1, source_target_pairs={{0,1},{1,0},{2,3},{3,2},{4,5},{5,4},{6,7},{7,6},{8,9},{9,8},{10,11... | collective-permute-start | bytes 24584 | tf_op jit(solution)/shard_map/ppermute | solution.py:721
  62.1 2.5 %collective-permute-start.20 = (f32[8,256]{1,0:T(8,128)S(1)}, f32[8,256]{1,0:T(8,128)S(1)}, u32[]{:S(2)}, u32[]{:S(2)}) collective-permute-start(f32[8,256]{1,0:T(8,128)S(1)} %add.3.refs_1_), channel_id=1, source_target_pairs={{0,6},{1,7},{2,0},{3,1},{4,2},{5,3},{6,4},{7,5},{8,14},{9,15},{10,... | collective-permute-start | bytes 24584 | tf_op jit(solution)/shard_map/ppermute | solution.py:717
  65.7 2.9 %collective-permute-done.19.refs_3_ = f32[8,256]{1,0:T(8,128)S(1)} collective-permute-done((f32[8,256]{1,0:T(8,128)S(1)}, f32[8,256]{1,0:T(8,128)S(1)}, u32[]{:S(2)}, u32[]{:S(2)}) %collective-permute-start.19) | collective-permute-done | bytes 8224 | tf_op jit(solution)/shard_map/ppermute | solution.py:717
  70.3 2.0 %collective-permute-start.22 = (bf16[128,384]{1,0:T(8,128)(2,1)S(1)}, bf16[128,384]{1,0:T(8,128)(2,1)S(1)}, u32[]{:S(2)}, u32[]{:S(2)}) collective-permute-start(bf16[128,384]{1,0:T(8,128)(2,1)S(1)} %get-tuple-element.122), channel_id=1, source_target_pairs={{0,16},{8,24},{16,0},{24,8},{1,17},{9,25},{17,1},{25,9},{2,18},{10... | collective-permute-start | bytes 294920 | tf_op jit(solution)/shard_map/ppermute | solution.py:713
  73.6 2.9 %middle.1 = (bf16[1536,384]{1,0:T(8,128)(2,1)S(1)}, bf16[1536,384]{1,0:T(8,128)(2,1)S(1)}, f32[256,640]{1,0:T(8,128)S(1)}, bf16[256,1536]{1,0:T(8,128)(2,1)S(1)}) custom-call(s32[1,3]{1,0:T(1,128)S(1)} %add_bitcast_fusion.refs_0_, bf16[272,1536]{1,0:T(8,128)(2,1)S(1)} %get-tuple-element.116.refs_11_.refs_1_.refs_6_.refs_10_, ...), custom_call_target="tpu_custom_call" | custom-call | tf_op jit(solution)/shard_map/middle/pallas_call | solution.py:98
  76.9 2.2 %leave.1 = (bf16[272,512]{1,0:T(8,128)(2,1)S(1)}, f32[272,256]{1,0:T(8,128)S(1)}, f32[4,32,384]{2,1,0:T(8,128)S(1)}, f32[4,32,384]{2,1,0:T(8,128)S(1)}, f32[8,384]{1,0:T(8,128)S(1)}) custom-call(s32[1,3]{1,0:T(1,128)S(1)} %add_bitcast_fusion.refs_0_, bf16[128,384]{1,0:T(8,128)(2,1)S(1)} %collective-permute-done.21.refs_1_, ...), custom_call_target="tpu_custom_call" | custom-call | tf_op jit(solution)/shard_map/leave/pallas_call | solution.py:98
  79.2 3.3 %collective-permute-start.24 = (f32[4,32,384]{2,1,0:T(8,128)S(1)}, f32[4,32,384]{2,1,0:T(8,128)S(1)}, u32[]{:S(2)}, u32[]{:S(2)}) collective-permute-start(f32[4,32,384]{2,1,0:T(8,128)S(1)} %get-tuple-element.132), channel_id=1, source_target_pairs={{0,1},{1,0},{2,3},{3,2},{4,5},{5,4},{6,7},{7,6},{8,9},{9,8},{10,11... | collective-permute-start | bytes 589832 | tf_op jit(solution)/shard_map/ppermute | solution.py:721
  85.5 2.0 %collective-permute-start.27 = (f32[32,384]{1,0:T(8,128)S(1)}, f32[32,384]{1,0:T(8,128)S(1)}, u32[]{:S(2)}, u32[]{:S(2)}) collective-permute-start(f32[32,384]{1,0:T(8,128)S(1)} %get-tuple-element.136), channel_id=1, source_target_pairs={{0,6},{1,7},{2,0},{3,1},{4,2},{5,3},{6,4},{7,5},{8,14},{9,15},{10,... | collective-permute-start | bytes 147464 | tf_op jit(solution)/shard_map/ppermute | solution.py:717
  87.5 3.0 %value_grads.1 = (bf16[1536,384]{1,0:T(8,128)(2,1)S(1)}, f32[272,1536]{1,0:T(8,128)S(1)}) custom-call(s32[1,3]{1,0:T(1,128)S(1)} %add_bitcast_fusion.refs_0_, bf16[272,512]{1,0:T(8,128)(2,1)S(1)} %get-tuple-element.137.refs_1_.refs_5_, f32[272,256]{1,0:T(8,128)S(1)} %get-tuple-element.139.refs_2_, bf16[256,768]{1,0:T(8,128)(2,1)S(1)} %get-tuple-element.125.refs_2_.refs_3_, ...), custom_call_target="tpu_custom_call" | custom-call | tf_op jit(solution)/shard_map/value_grads/pallas_call | solution.py:98
  90.5 2.1 %late_grads.1 = (bf16[4,64,1536]{2,1,0:T(8,128)(2,1)S(1)}, bf16[4,64,1536]{2,1,0:T(8,128)(2,1)S(1)}, bf16[4,96,768]{2,1,0:T(8,128)(2,1)S(1)}, bf16[4,96,768]{2,1...) custom-call(s32[1,3]{1,0:T(1,128)S(1)} %add_bitcast_fusion.refs_0_, ...), custom_call_target="tpu_custom_call" | custom-call | tf_op jit(solution)/shard_map/late_grads/pallas_call | solution.py:98
  93.9 2.7 %collective-permute-start.29 = (bf16[2,96,768]{2,1,0:T(8,128)(2,1)S(1)}, bf16[2,96,768]{2,1,0:T(8,128)(2,1)S(1)}, u32[]{:S(2)}, u32[]{:S(2)}) collective-permute-start(bf16[2,96,768]{2,1,0:T(8,128)(2,1)S(1)} %get-tuple-element.150), channel_id=1, source_target_pairs={{0,96},{32,0},{64,32},{96,64},{1,97},{33,1},{65,33},{97,65},{2,98}... | collective-permute-start | bytes 884744 | tf_op jit(solution)/shard_map/ppermute | solution.py:713
  96.5 2.4 %collective-permute-start.31 = (bf16[2,112,512]{2,1,0:T(8,128)(2,1)S(1)}, bf16[2,112,512]{2,1,0:T(8,128)(2,1)S(1)}, u32[]{:S(2)}, u32[]{:S(2)}) collective-permute-start(bf16[2,112,512]{2,1,0:T(8,128)(2,1)S(1)} %get-tuple-element.154), channel_id=1, source_target_pairs={{0,24},{8,0},{16,8},{24,16},{1,25},{9,1},{17,9},{25,17},{2,26},{10... | collective-permute-start | bytes 688136 | tf_op jit(solution)/shard_map/ppermute | solution.py:713
  100.5 5.2 %collective-permute-done.30.refs_7_ = bf16[2,96,512]{2,1,0:T(8,128)(2,1)S(1)} collective-permute-done((bf16[2,96,512]{2,1,0:T(8,128)(2,1)S(1)}, bf16[2,96,512]{2,1,0:T(8,128)(2,1)S(1)}, u32[]{:S(2)}, u32[]{:S(2)}) %collective-permute-start.30) | collective-permute-done | bytes 196640 | tf_op jit(solution)/shard_map/ppermute | solution.py:713
  106.6 2.7 %collective-permute-start.34 = (bf16[4,96,768]{2,1,0:T(8,128)(2,1)S(1)}, bf16[4,96,768]{2,1,0:T(8,128)(2,1)S(1)}, u32[]{:S(2)}, u32[]{:S(2)}) collective-permute-start(bf16[4,96,768]{2,1,0:T(8,128)(2,1)S(1)} %get-tuple-element.159), channel_id=1, source_target_pairs={{0,96},{32,0},{64,32},{96,64},{1,97},{33,1},{65,33},{97,65},{2,98}... | collective-permute-start | bytes 1769480 | tf_op jit(solution)/shard_map/ppermute | solution.py:713
  109.3 2.7 %collective-permute-start.36 = (bf16[4,96,512]{2,1,0:T(8,128)(2,1)S(1)}, bf16[4,96,512]{2,1,0:T(8,128)(2,1)S(1)}, u32[]{:S(2)}, u32[]{:S(2)}) collective-permute-start(bf16[4,96,512]{2,1,0:T(8,128)(2,1)S(1)} %get-tuple-element.162), channel_id=1, source_target_pairs={{0,24},{8,0},{16,8},{24,16},{1,25},{9,1},{17,9},{25,17},{2,26},{10... | collective-permute-start | bytes 1179656 | tf_op jit(solution)/shard_map/ppermute | solution.py:713
  114.4 4.3 %collective-permute-done.35.refs_5_ = bf16[4,96,512]{2,1,0:T(8,128)(2,1)S(1)} collective-permute-done((bf16[4,96,512]{2,1,0:T(8,128)(2,1)S(1)}, bf16[4,96,512]{2,1,0:T(8,128)(2,1)S(1)}, u32[]{:S(2)}, u32[]{:S(2)}) %collective-permute-start.35) | collective-permute-done | bytes 393248 | tf_op jit(solution)/shard_map/ppermute | solution.py:713
  118.7 2.1 %collective-permute-done.33.refs_2_ = bf16[4,96,768]{2,1,0:T(8,128)(2,1)S(1)} collective-permute-done((bf16[4,96,768]{2,1,0:T(8,128)(2,1)S(1)}, bf16[4,96,768]{2,1,0:T(8,128)(2,1)S(1)}, u32[]{:S(2)}, u32[]{:S(2)}) %collective-permute-start.33) | collective-permute-done | bytes 589856 | tf_op jit(solution)/shard_map/ppermute | solution.py:713
  121.8 3.6 %collective-permute-start.39 = (bf16[96,512]{1,0:T(8,128)(2,1)S(1)}, bf16[96,512]{1,0:T(8,128)(2,1)S(1)}, u32[]{:S(2)}, u32[]{:S(2)}) collective-permute-start(bf16[96,512]{1,0:T(8,128)(2,1)S(1)} %get-tuple-element.167), channel_id=1, source_target_pairs={{0,64},{32,96},{64,0},{96,32},{1,65},{33,97},{65,1},{97,33},{2,66}... | collective-permute-start | bytes 294920 | tf_op jit(solution)/shard_map/ppermute | solution.py:713
  130.6 2.0 %collective-permute-start.44 = (bf16[80,1536]{1,0:T(8,128)(2,1)S(1)}, bf16[80,1536]{1,0:T(8,128)(2,1)S(1)}, u32[]{:S(2)}, u32[]{:S(2)}) collective-permute-start(bf16[80,1536]{1,0:T(8,128)(2,1)S(1)} %get-tuple-element.172.refs_1_), channel_id=1, source_target_pairs={{0,6},{1,7},{2,0},{3,1},{4,2},{5,3},{6,4},{7,5},{8,14},{9,15},{10,... | collective-permute-start | bytes 737288 | tf_op jit(solution)/shard_map/ppermute | solution.py:717
  136.2 2.5 %collective-permute-done.50.refs_3_ = bf16[96,768]{1,0:T(8,128)(2,1)S(1)} collective-permute-done((bf16[96,768]{1,0:T(8,128)(2,1)S(1)}, bf16[96,768]{1,0:T(8,128)(2,1)S(1)}, u32[]{:S(2)}, u32[]{:S(2)}) %collective-permute-start.50) | collective-permute-done | bytes 147488 | tf_op jit(solution)/shard_map/ppermute | solution.py:713
  138.7 6.4 %collective-permute-start.45 = (bf16[80,1536]{1,0:T(8,128)(2,1)S(1)}, bf16[80,1536]{1,0:T(8,128)(2,1)S(1)}, u32[]{:S(2)}, u32[]{:S(2)}) collective-permute-start(bf16[80,1536]{1,0:T(8,128)(2,1)S(1)} %get-tuple-element.172.refs_1_), channel_id=1, source_target_pairs={{0,1},{1,0},{2,3},{3,2},{4,5},{5,4},{6,7},{7,6},{8,9},{9,8},{10,11... | collective-permute-start | bytes 737288 | tf_op jit(solution)/shard_map/ppermute | solution.py:721
  145.6 2.1 %collective-permute-start.46 = (bf16[80,1536]{1,0:T(8,128)(2,1)S(1)}, bf16[80,1536]{1,0:T(8,128)(2,1)S(1)}, u32[]{:S(2)}, u32[]{:S(2)}) collective-permute-start(bf16[80,1536]{1,0:T(8,128)(2,1)S(1)} %collective-permute-done.42.refs_2_), channel_id=1, source_target_pairs={{0,1},{1,0},{2,3},{3,2},{4,5},{5,4},{6,7},{7,6},{8,9},{9,8},{10,11... | collective-permute-start | bytes 737288 | tf_op jit(solution)/shard_map/ppermute | solution.py:721
  149.1 2.5 %finish.1 = (f32[256,1536]{1,0:T(8,128)}, bf16[256,1536]{1,0:T(8,128)(2,1)}, f32[96,256]{1,0:T(8,128)}, f32[1,96]{1,0:T(1,128)}, f32[4,256]{1,0:T(4,128)}, /*index=5*/f32[1,256]{1,0:T(1,128)}) custom-call(s32[1,3]{1,0:T(1,128)S(1)} %add_bitcast_fusion.refs_0_, bf16[80,1536]{1,0:T(8,128)(2,1)S(1)} %get-tuple-element.172.refs_1_, ...), custom_call_target="tpu_custom_call" | custom-call | tf_op jit(solution)/shard_map/finish/pallas_call | solution.py:98
  (119 shorter events, 47.4 us)
Async XLA Ops:
  2.6 9.0 %collective-permute-start.2 = (bf16[96,768]{1,0:T(8,128)(2,1)S(1)}, bf16[96,768]{1,0:T(8,128)(2,1)S(1)}, u32[]{:S(2)}, u32[]{:S(2)}) collective-permute-start(bf16[96,768]{1,0:T(8,128)(2,1)S(1)} %get-tuple-element.106.refs_1_), channel_id=1, source_target_pairs={{0,24},{8,0},{16,8},{24,16},{1,25},{9,1},{17,9},{25,17},{2,26},{10... | collective-permute-start | bytes 442376 | tf_op jit(solution)/shard_map/ppermute | solution.py:713
  6.2 14.9 %collective-permute-start = (bf16[112,768]{1,0:T(8,128)(2,1)S(1)}, bf16[112,768]{1,0:T(8,128)(2,1)S(1)}, u32[]{:S(2)}, u32[]{:S(2)}) collective-permute-start(bf16[112,768]{1,0:T(8,128)(2,1)S(1)} %get-tuple-element.107), channel_id=1, source_target_pairs={{0,8},{8,16},{16,24},{24,0},{1,9},{9,17},{17,25},{25,1},{2,10},{10... | collective-permute-start | bytes 516104 | tf_op jit(solution)/shard_map/ppermute | solution.py:713
  6.2 8.3 %collective-permute-start.1 = (bf16[96,768]{1,0:T(8,128)(2,1)S(1)}, bf16[96,768]{1,0:T(8,128)(2,1)S(1)}, u32[]{:S(2)}, u32[]{:S(2)}) collective-permute-start(bf16[96,768]{1,0:T(8,128)(2,1)S(1)} %get-tuple-element.106.refs_1_), channel_id=1, source_target_pairs={{0,16},{8,24},{16,0},{24,8},{1,17},{9,25},{17,1},{25,9},{2,18},{10... | collective-permute-start | bytes 442376 | tf_op jit(solution)/shard_map/ppermute | solution.py:713
  7.9 9.3 %collective-permute-start.5 = (bf16[96,768]{1,0:T(8,128)(2,1)S(1)}, bf16[96,768]{1,0:T(8,128)(2,1)S(1)}, u32[]{:S(2)}, u32[]{:S(2)}) collective-permute-start(bf16[96,768]{1,0:T(8,128)(2,1)S(1)} %get-tuple-element.108.refs_5_), channel_id=1, source_target_pairs={{0,96},{32,0},{64,32},{96,64},{1,97},{33,1},{65,33},{97,65},{2,98}... | collective-permute-start | bytes 442376 | tf_op jit(solution)/shard_map/ppermute | solution.py:713
  11.6 9.5 %collective-permute-start.3 = (bf16[96,768]{1,0:T(8,128)(2,1)S(1)}, bf16[96,768]{1,0:T(8,128)(2,1)S(1)}, u32[]{:S(2)}, u32[]{:S(2)}) collective-permute-start(bf16[96,768]{1,0:T(8,128)(2,1)S(1)} %get-tuple-element.108.refs_5_), channel_id=1, source_target_pairs={{0,32},{32,64},{64,96},{96,0},{1,33},{33,65},{65,97},{97,1},{2,34}... | collective-permute-start | bytes 442376 | tf_op jit(solution)/shard_map/ppermute | solution.py:713
  21.8 13.8 %collective-permute-start.8 = (bf16[4,96,768]{2,1,0:T(8,128)(2,1)S(1)}, bf16[4,96,768]{2,1,0:T(8,128)(2,1)S(1)}, u32[]{:S(2)}, u32[]{:S(2)}) collective-permute-start(bf16[4,96,768]{2,1,0:T(8,128)(2,1)S(1)} %get-tuple-element.109.refs_1_), channel_id=1, source_target_pairs={{0,96},{32,0},{64,32},{96,64},{1,97},{33,1},{65,33},{97,65},{2,98}... | collective-permute-start | bytes 1769480 | tf_op jit(solution)/shard_map/ppermute | solution.py:713
  21.9 14.4 %collective-permute-start.6 = (bf16[4,96,768]{2,1,0:T(8,128)(2,1)S(1)}, bf16[4,96,768]{2,1,0:T(8,128)(2,1)S(1)}, u32[]{:S(2)}, u32[]{:S(2)}) collective-permute-start(bf16[4,96,768]{2,1,0:T(8,128)(2,1)S(1)} %get-tuple-element.109.refs_1_), channel_id=1, source_target_pairs={{0,32},{32,64},{64,96},{96,0},{1,33},{33,65},{65,97},{97,1},{2,34}... | collective-permute-start | bytes 1769480 | tf_op jit(solution)/shard_map/ppermute | solution.py:713
  23.4 13.9 %collective-permute-start.12 = (bf16[4,96,768]{2,1,0:T(8,128)(2,1)S(1)}, bf16[4,96,768]{2,1,0:T(8,128)(2,1)S(1)}, u32[]{:S(2)}, u32[]{:S(2)}) collective-permute-start(bf16[4,96,768]{2,1,0:T(8,128)(2,1)S(1)} %get-tuple-element.110.refs_6_), channel_id=1, source_target_pairs={{0,24},{8,0},{16,8},{24,16},{1,25},{9,1},{17,9},{25,17},{2,26},{10... | collective-permute-start | bytes 1769480 | tf_op jit(solution)/shard_map/ppermute | solution.py:713
  23.4 14.0 %collective-permute-start.10 = (bf16[4,96,768]{2,1,0:T(8,128)(2,1)S(1)}, bf16[4,96,768]{2,1,0:T(8,128)(2,1)S(1)}, u32[]{:S(2)}, u32[]{:S(2)}) collective-permute-start(bf16[4,96,768]{2,1,0:T(8,128)(2,1)S(1)} %get-tuple-element.110.refs_6_), channel_id=1, source_target_pairs={{0,8},{8,16},{16,24},{24,0},{1,9},{9,17},{17,25},{25,1},{2,10},{10... | collective-permute-start | bytes 1769480 | tf_op jit(solution)/shard_map/ppermute | solution.py:713
  35.6 7.9 %collective-permute-start.9 = (bf16[2,96,768]{2,1,0:T(8,128)(2,1)S(1)}, bf16[2,96,768]{2,1,0:T(8,128)(2,1)S(1)}, u32[]{:S(2)}, u32[]{:S(2)}) collective-permute-start(bf16[2,96,768]{2,1,0:T(8,128)(2,1)S(1)} %slice.17), channel_id=1, source_target_pairs={{0,96},{32,0},{64,32},{96,64},{1,97},{33,1},{65,33},{97,65},{2,98}... | collective-permute-start | bytes 884744 | tf_op jit(solution)/shard_map/ppermute | solution.py:713
  36.3 7.2 %collective-permute-start.7 = (bf16[2,96,768]{2,1,0:T(8,128)(2,1)S(1)}, bf16[2,96,768]{2,1,0:T(8,128)(2,1)S(1)}, u32[]{:S(2)}, u32[]{:S(2)}) collective-permute-start(bf16[2,96,768]{2,1,0:T(8,128)(2,1)S(1)} %slice.16), channel_id=1, source_target_pairs={{0,32},{32,64},{64,96},{96,0},{1,33},{33,65},{65,97},{97,1},{2,34}... | collective-permute-start | bytes 884744 | tf_op jit(solution)/shard_map/ppermute | solution.py:713
  37.4 7.1 %collective-permute-start.11 = (bf16[2,96,768]{2,1,0:T(8,128)(2,1)S(1)}, bf16[2,96,768]{2,1,0:T(8,128)(2,1)S(1)}, u32[]{:S(2)}, u32[]{:S(2)}) collective-permute-start(bf16[2,96,768]{2,1,0:T(8,128)(2,1)S(1)} %slice.18), channel_id=1, source_target_pairs={{0,8},{8,16},{16,24},{24,0},{1,9},{9,17},{17,25},{25,1},{2,10},{10... | collective-permute-start | bytes 884744 | tf_op jit(solution)/shard_map/ppermute | solution.py:713
  84.1 6.4 %collective-permute-start.25 = (f32[32,384]{1,0:T(8,128)S(1)}, f32[32,384]{1,0:T(8,128)S(1)}, u32[]{:S(2)}, u32[]{:S(2)}) collective-permute-start(f32[32,384]{1,0:T(8,128)S(1)} %get-tuple-element.134), channel_id=1, source_target_pairs={{0,2},{1,3},{2,4},{3,5},{4,6},{5,7},{6,0},{7,1},{8,10},{9,11},{10,... | collective-permute-start | bytes 147464 | tf_op jit(solution)/shard_map/ppermute | solution.py:717
  84.2 6.3 %collective-permute-start.26 = (f32[32,384]{1,0:T(8,128)S(1)}, f32[32,384]{1,0:T(8,128)S(1)}, u32[]{:S(2)}, u32[]{:S(2)}) collective-permute-start(f32[32,384]{1,0:T(8,128)S(1)} %get-tuple-element.135), channel_id=1, source_target_pairs={{0,4},{1,5},{2,6},{3,7},{4,0},{5,1},{6,2},{7,3},{8,12},{9,13},{10,... | collective-permute-start | bytes 147464 | tf_op jit(solution)/shard_map/ppermute | solution.py:717
  92.6 6.4 %collective-permute-start.32 = (bf16[4,64,1536]{2,1,0:T(8,128)(2,1)S(1)}, bf16[4,64,1536]{2,1,0:T(8,128)(2,1)S(1)}, u32[]{:S(2)}, u32[]{:S(2)}) collective-permute-start(bf16[4,64,1536]{2,1,0:T(8,128)(2,1)S(1)} %get-tuple-element.156), channel_id=1, source_target_pairs={{0,1},{1,0},{2,3},{3,2},{4,5},{5,4},{6,7},{7,6},{8,9},{9,8},{10,11... | collective-permute-start | bytes 2359304 | tf_op jit(solution)/shard_map/ppermute | solution.py:721
  93.9 11.8 %collective-permute-start.28 = (bf16[2,96,768]{2,1,0:T(8,128)(2,1)S(1)}, bf16[2,96,768]{2,1,0:T(8,128)(2,1)S(1)}, u32[]{:S(2)}, u32[]{:S(2)}) collective-permute-start(bf16[2,96,768]{2,1,0:T(8,128)(2,1)S(1)} %get-tuple-element.149), channel_id=1, source_target_pairs={{0,32},{32,64},{64,96},{96,0},{1,33},{33,65},{65,97},{97,1},{2,34}... | collective-permute-start | bytes 884744 | tf_op jit(solution)/shard_map/ppermute | solution.py:713
  93.9 11.8 %collective-permute-start.29 = (bf16[2,96,768]{2,1,0:T(8,128)(2,1)S(1)}, bf16[2,96,768]{2,1,0:T(8,128)(2,1)S(1)}, u32[]{:S(2)}, u32[]{:S(2)}) collective-permute-start(bf16[2,96,768]{2,1,0:T(8,128)(2,1)S(1)} %get-tuple-element.150), channel_id=1, source_target_pairs={{0,96},{32,0},{64,32},{96,64},{1,97},{33,1},{65,33},{97,65},{2,98}... | collective-permute-start | bytes 884744 | tf_op jit(solution)/shard_map/ppermute | solution.py:713
  96.5 9.1 %collective-permute-start.31 = (bf16[2,112,512]{2,1,0:T(8,128)(2,1)S(1)}, bf16[2,112,512]{2,1,0:T(8,128)(2,1)S(1)}, u32[]{:S(2)}, u32[]{:S(2)}) collective-permute-start(bf16[2,112,512]{2,1,0:T(8,128)(2,1)S(1)} %get-tuple-element.154), channel_id=1, source_target_pairs={{0,24},{8,0},{16,8},{24,16},{1,25},{9,1},{17,9},{25,17},{2,26},{10... | collective-permute-start | bytes 688136 | tf_op jit(solution)/shard_map/ppermute | solution.py:713
  98.9 6.7 %collective-permute-start.30 = (bf16[2,96,512]{2,1,0:T(8,128)(2,1)S(1)}, bf16[2,96,512]{2,1,0:T(8,128)(2,1)S(1)}, u32[]{:S(2)}, u32[]{:S(2)}) collective-permute-start(bf16[2,96,512]{2,1,0:T(8,128)(2,1)S(1)} %get-tuple-element.153), channel_id=1, source_target_pairs={{0,8},{8,16},{16,24},{24,0},{1,9},{9,17},{17,25},{25,1},{2,10},{10... | collective-permute-start | bytes 589832 | tf_op jit(solution)/shard_map/ppermute | solution.py:713
  99.7 12.3 %collective-permute-start.37 = (bf16[2,64,1536]{2,1,0:T(8,128)(2,1)S(1)}, bf16[2,64,1536]{2,1,0:T(8,128)(2,1)S(1)}, u32[]{:S(2)}, u32[]{:S(2)}) collective-permute-start(bf16[2,64,1536]{2,1,0:T(8,128)(2,1)S(1)} %get-tuple-element.163), channel_id=1, source_target_pairs={{0,2},{1,3},{2,0},{3,1},{4,6},{5,7},{6,4},{7,5},{8,10},{9,11},{10,... | collective-permute-start | bytes 1179656 | tf_op jit(solution)/shard_map/ppermute | solution.py:721
  106.5 14.3 %collective-permute-start.33 = (bf16[4,96,768]{2,1,0:T(8,128)(2,1)S(1)}, bf16[4,96,768]{2,1,0:T(8,128)(2,1)S(1)}, u32[]{:S(2)}, u32[]{:S(2)}) collective-permute-start(bf16[4,96,768]{2,1,0:T(8,128)(2,1)S(1)} %get-tuple-element.158), channel_id=1, source_target_pairs={{0,32},{32,64},{64,96},{96,0},{1,33},{33,65},{65,97},{97,1},{2,34}... | collective-permute-start | bytes 1769480 | tf_op jit(solution)/shard_map/ppermute | solution.py:713
  106.6 14.2 %collective-permute-start.34 = (bf16[4,96,768]{2,1,0:T(8,128)(2,1)S(1)}, bf16[4,96,768]{2,1,0:T(8,128)(2,1)S(1)}, u32[]{:S(2)}, u32[]{:S(2)}) collective-permute-start(bf16[4,96,768]{2,1,0:T(8,128)(2,1)S(1)} %get-tuple-element.159), channel_id=1, source_target_pairs={{0,96},{32,0},{64,32},{96,64},{1,97},{33,1},{65,33},{97,65},{2,98}... | collective-permute-start | bytes 1769480 | tf_op jit(solution)/shard_map/ppermute | solution.py:713
  109.3 9.4 %collective-permute-start.35 = (bf16[4,96,512]{2,1,0:T(8,128)(2,1)S(1)}, bf16[4,96,512]{2,1,0:T(8,128)(2,1)S(1)}, u32[]{:S(2)}, u32[]{:S(2)}) collective-permute-start(bf16[4,96,512]{2,1,0:T(8,128)(2,1)S(1)} %get-tuple-element.161), channel_id=1, source_target_pairs={{0,8},{8,16},{16,24},{24,0},{1,9},{9,17},{17,25},{25,1},{2,10},{10... | collective-permute-start | bytes 1179656 | tf_op jit(solution)/shard_map/ppermute | solution.py:713
  109.3 9.4 %collective-permute-start.36 = (bf16[4,96,512]{2,1,0:T(8,128)(2,1)S(1)}, bf16[4,96,512]{2,1,0:T(8,128)(2,1)S(1)}, u32[]{:S(2)}, u32[]{:S(2)}) collective-permute-start(bf16[4,96,512]{2,1,0:T(8,128)(2,1)S(1)} %get-tuple-element.162), channel_id=1, source_target_pairs={{0,24},{8,0},{16,8},{24,16},{1,25},{9,1},{17,9},{25,17},{2,26},{10... | collective-permute-start | bytes 1179656 | tf_op jit(solution)/shard_map/ppermute | solution.py:713
  112.6 12.8 %collective-permute-start.41 = (bf16[64,1536]{1,0:T(8,128)(2,1)S(1)}, bf16[64,1536]{1,0:T(8,128)(2,1)S(1)}, u32[]{:S(2)}, u32[]{:S(2)}) collective-permute-start(bf16[64,1536]{1,0:T(8,128)(2,1)S(1)} %get-tuple-element.169), channel_id=1, source_target_pairs={{0,4},{1,5},{2,6},{3,7},{4,0},{5,1},{6,2},{7,3},{8,12},{9,13},{10,... | collective-permute-start | bytes 589832 | tf_op jit(solution)/shard_map/ppermute | solution.py:721
  121.8 6.6 %collective-permute-start.39 = (bf16[96,512]{1,0:T(8,128)(2,1)S(1)}, bf16[96,512]{1,0:T(8,128)(2,1)S(1)}, u32[]{:S(2)}, u32[]{:S(2)}) collective-permute-start(bf16[96,512]{1,0:T(8,128)(2,1)S(1)} %get-tuple-element.167), channel_id=1, source_target_pairs={{0,64},{32,96},{64,0},{96,32},{1,65},{33,97},{65,1},{97,33},{2,66}... | collective-permute-start | bytes 294920 | tf_op jit(solution)/shard_map/ppermute | solution.py:713
  125.4 8.2 %collective-permute-start.49 = (bf16[96,768]{1,0:T(8,128)(2,1)S(1)}, bf16[96,768]{1,0:T(8,128)(2,1)S(1)}, u32[]{:S(2)}, u32[]{:S(2)}) collective-permute-start(bf16[96,768]{1,0:T(8,128)(2,1)S(1)} %get-tuple-element.180), channel_id=1, source_target_pairs={{0,8},{8,16},{16,24},{24,0},{1,9},{9,17},{17,25},{25,1},{2,10},{10... | collective-permute-start | bytes 442376 | tf_op jit(solution)/shard_map/ppermute | solution.py:713
  130.6 14.5 %collective-permute-start.44 = (bf16[80,1536]{1,0:T(8,128)(2,1)S(1)}, bf16[80,1536]{1,0:T(8,128)(2,1)S(1)}, u32[]{:S(2)}, u32[]{:S(2)}) collective-permute-start(bf16[80,1536]{1,0:T(8,128)(2,1)S(1)} %get-tuple-element.172.refs_1_), channel_id=1, source_target_pairs={{0,6},{1,7},{2,0},{3,1},{4,2},{5,3},{6,4},{7,5},{8,14},{9,15},{10,... | collective-permute-start | bytes 737288 | tf_op jit(solution)/shard_map/ppermute | solution.py:717
  132.5 12.6 %collective-permute-start.43 = (bf16[80,1536]{1,0:T(8,128)(2,1)S(1)}, bf16[80,1536]{1,0:T(8,128)(2,1)S(1)}, u32[]{:S(2)}, u32[]{:S(2)}) collective-permute-start(bf16[80,1536]{1,0:T(8,128)(2,1)S(1)} %get-tuple-element.172.refs_1_), channel_id=1, source_target_pairs={{0,4},{1,5},{2,6},{3,7},{4,0},{5,1},{6,2},{7,3},{8,12},{9,13},{10,... | collective-permute-start | bytes 737288 | tf_op jit(solution)/shard_map/ppermute | solution.py:717
  133.1 12.6 %collective-permute-start.42 = (bf16[80,1536]{1,0:T(8,128)(2,1)S(1)}, bf16[80,1536]{1,0:T(8,128)(2,1)S(1)}, u32[]{:S(2)}, u32[]{:S(2)}) collective-permute-start(bf16[80,1536]{1,0:T(8,128)(2,1)S(1)} %get-tuple-element.172.refs_1_), channel_id=1, source_target_pairs={{0,2},{1,3},{2,4},{3,5},{4,6},{5,7},{6,0},{7,1},{8,10},{9,11},{10,... | collective-permute-start | bytes 737288 | tf_op jit(solution)/shard_map/ppermute | solution.py:717
  133.6 14.1 %collective-permute-start.51 = (bf16[96,768]{1,0:T(8,128)(2,1)S(1)}, bf16[96,768]{1,0:T(8,128)(2,1)S(1)}, u32[]{:S(2)}, u32[]{:S(2)}) collective-permute-start(bf16[96,768]{1,0:T(8,128)(2,1)S(1)} %get-tuple-element.182), channel_id=1, source_target_pairs={{0,24},{8,0},{16,8},{24,16},{1,25},{9,1},{17,9},{25,17},{2,26},{10... | collective-permute-start | bytes 442376 | tf_op jit(solution)/shard_map/ppermute | solution.py:713
  138.7 10.4 %collective-permute-start.45 = (bf16[80,1536]{1,0:T(8,128)(2,1)S(1)}, bf16[80,1536]{1,0:T(8,128)(2,1)S(1)}, u32[]{:S(2)}, u32[]{:S(2)}) collective-permute-start(bf16[80,1536]{1,0:T(8,128)(2,1)S(1)} %get-tuple-element.172.refs_1_), channel_id=1, source_target_pairs={{0,1},{1,0},{2,3},{3,2},{4,5},{5,4},{6,7},{7,6},{8,9},{9,8},{10,11... | collective-permute-start | bytes 737288 | tf_op jit(solution)/shard_map/ppermute | solution.py:721
  (28 other events, 219.5 us)

commit v4 on v3

--- a/solution.py
+++ b/solution.py
@@ -130,6 +130,10 @@
         parts.append(part)
         array = array - part.astype(F32)
     return parts
+
+
+def twice(a, b, left, right):
+    return sum(product(part, b, left, right) for part in split(a, 2))
 
 
 def pick(chosen, array, left, right, parts=2):
@@ -382,10 +386,10 @@
             weights = decays(log_decay, turned, 2 * pair + side)
             got.append(dot_first(scores * weights, grad))
             own = jnp.where(lower, grad, 0.0) if side == 0 else jnp.where(lower, 0.0, grad)
-            grad_scores = grad_scores + dot_last(own, part) * weights
+            grad_scores = grad_scores + twice(own, part, 1, 1) * weights
         grads[:, pair_columns(pair)] = jnp.where(lower, got[0], got[1])
-    grads[:, WIDE : WIDE + STATE] = dot_first(grad_scores, cmat)
-    grads[:, WIDE + STATE :] = dot(grad_scores, bmat)
+    grads[:, WIDE : WIDE + STATE] = twice(grad_scores, cmat, 0, 0)
+    grads[:, WIDE + STATE :] = twice(grad_scores, bmat, 1, 0)
 
 
 def leave(
@@ -408,8 +412,12 @@
     own = grad_mixed[...]
     from_end = dot(narrow[:, BMAT], end) * to_end
     inputs = grads[:, :WIDE] + from_end
-    from_b = grads[:, WIDE : WIDE + STATE] + dot_last(weighted * to_end, end)
-    from_c = grads[:, WIDE + STATE :] + dot_last(own * spread[:, GROWN], state[:STATE])
+    from_b = grads[:, WIDE : WIDE + STATE]
+    from_b = from_b + sum(dot_last(weighted * to_end, part) for part in split(end, 2))
+    from_c = grads[:, WIDE + STATE :]
+    from_c = from_c + sum(
+        dot_last(own * spread[:, GROWN], part) for part in split(state[:STATE], 2)
+    )
     grad_log = head_sums(own.astype(BF16).astype(F32) * after[:, INSIDE] - weighted * inputs)
     at_end = jnp.sum(weighted * from_end, axis=0, keepdims=True) + jnp.exp(
         spread_heads(last)

time: 152 us -> 152 us (level)
  transfers between devices with their start and end apart: 52 -> 52, of which waited for: 20 -> 19; matrix products, arithmetic and copies ran while one was open for 2% -> 2% of each run, Pallas kernels for 11% -> 11%
where the time goes in v4:
time: 152 us
  starting transfers between devices  69.8 us (46%)
  waiting for transfers between devices  45.2 us (30%)
  Pallas kernels  32 us (21%)
  other arithmetic  1.86 us (1%)
  local copies, waits for them, and re-layouts  1.82 us (1%)
    ppermute x34, waiting for transfers between devices, shift(): return lax.ppermute(array, axis, [(i, (i + steps) % 4) for i in range(4)])  40.2 us
    ppermute x34, starting transfers between devices, shift(): return lax.ppermute(array, axis, [(i, (i + steps) % 4) for i in range(4)])  38.6 us
    pallas_call x19, Pallas kernels, fuse(): return list(call(ids, *arrays))  32 us
    ppermute x9, starting transfers between devices, across(): return lax.ppermute(array, 'tp', [(i, i ^ bits) for i in range(8)])  21.6 us
    ppermute x9, starting transfers between devices, from_chip(): lax.ppermute(array, 'tp', [(i, (i + 2 * steps) % 8) for i in range(8)])  9.56 us
    ppermute x9, waiting for transfers between devices, from_chip(): lax.ppermute(array, 'tp', [(i, (i + 2 * steps) % 8) for i in range(8)])  3.12 us
  transfers between devices with their start and end apart: 52, of which 19 were waited for; matrix products, arithmetic and copies ran while one was open for 2% of the time, Pallas kernels for 11%

profile of v4, /device:TPU:1, one launch (start us, length us, event | category | flops | bytes accessed | tf_op | source)
XLA Modules:
  0.0 151.7 jit_solution(15637127864751022031)
XLA Ops:
  2.6 3.6 %collective-permute-start.2 = (bf16[96,768]{1,0:T(8,128)(2,1)S(1)}, bf16[96,768]{1,0:T(8,128)(2,1)S(1)}, u32[]{:S(2)}, u32[]{:S(2)}) collective-permute-start(bf16[96,768]{1,0:T(8,128)(2,1)S(1)} %get-tuple-element.106.refs_1_), channel_id=1, source_target_pairs={{0,24},{8,0},{16,8},{24,16},{1,25},{9,1},{17,9},{25,17},{2,26},{10... | collective-permute-start | bytes 442376 | tf_op jit(solution)/shard_map/ppermute | solution.py:721
  7.9 3.8 %collective-permute-start.5 = (bf16[96,768]{1,0:T(8,128)(2,1)S(1)}, bf16[96,768]{1,0:T(8,128)(2,1)S(1)}, u32[]{:S(2)}, u32[]{:S(2)}) collective-permute-start(bf16[96,768]{1,0:T(8,128)(2,1)S(1)} %get-tuple-element.108.refs_5_), channel_id=1, source_target_pairs={{0,96},{32,0},{64,32},{96,64},{1,97},{33,1},{65,33},{97,65},{2,98}... | collective-permute-start | bytes 442376 | tf_op jit(solution)/shard_map/ppermute | solution.py:721
  12.3 2.2 %collective-permute-done.1.refs_3_ = bf16[96,768]{1,0:T(8,128)(2,1)S(1)} collective-permute-done((bf16[96,768]{1,0:T(8,128)(2,1)S(1)}, bf16[96,768]{1,0:T(8,128)(2,1)S(1)}, u32[]{:S(2)}, u32[]{:S(2)}) %collective-permute-start.1) | collective-permute-done | bytes 147488 | tf_op jit(solution)/shard_map/ppermute | solution.py:721
  14.5 2.7 %collective-permute-done.5.refs_8_ = bf16[96,768]{1,0:T(8,128)(2,1)S(1)} collective-permute-done((bf16[96,768]{1,0:T(8,128)(2,1)S(1)}, bf16[96,768]{1,0:T(8,128)(2,1)S(1)}, u32[]{:S(2)}, u32[]{:S(2)}) %collective-permute-start.5) | collective-permute-done | bytes 147488 | tf_op jit(solution)/shard_map/ppermute | solution.py:721
  17.2 3.9 %collective-permute-done.3.refs_6_ = bf16[96,768]{1,0:T(8,128)(2,1)S(1)} collective-permute-done((bf16[96,768]{1,0:T(8,128)(2,1)S(1)}, bf16[96,768]{1,0:T(8,128)(2,1)S(1)}, u32[]{:S(2)}, u32[]{:S(2)}) %collective-permute-start.3) | collective-permute-done | bytes 147488 | tf_op jit(solution)/shard_map/ppermute | solution.py:721
  25.0 10.6 %collective-permute-done.8.refs_5_ = bf16[4,96,768]{2,1,0:T(8,128)(2,1)S(1)} collective-permute-done((bf16[4,96,768]{2,1,0:T(8,128)(2,1)S(1)}, bf16[4,96,768]{2,1,0:T(8,128)(2,1)S(1)}, u32[]{:S(2)}, u32[]{:S(2)}) %collective-permute-start.8) | collective-permute-done | bytes 589856 | tf_op jit(solution)/shard_map/ppermute | solution.py:721
  41.4 2.1 %tabulate.1 = (f32[16,768]{1,0:T(8,128)S(1)}, f32[256,1536]{1,0:T(8,128)S(1)}) custom-call(s32[1,3]{1,0:T(1,128)S(1)} %add_bitcast_fusion.refs_0_, bf16[4,384]{1,0:T(4,128)(2,1)} %refs_1_.3, bf16[4,256]{1,0:T(4,128)(2,1)} %refs_2_.3, bf16[1,384]{1,0:T(2,128)(2,1)} %broadcast_in_dim.19.refs_3_, bf16[1,256]{1,0:T(2,128)(2,1)} %broadcast_in_dim.20.refs_4_, ...), custom_call_target="tpu_custom_call" | custom-call | tf_op jit(solution)/shard_map/tabulate/pallas_call | solution.py:98
  44.5 2.9 %enter.1 = (bf16[1536,768]{1,0:T(8,128)(2,1)S(1)}, bf16[272,1536]{1,0:T(8,128)(2,1)S(1)}, bf16[272,640]{1,0:T(8,128)(2,1)S(1)}, f32[256,1408]{1,0:T(8,128)S(1)},...) custom-call(s32[1,3]{1,0:T(1,128)S(1)} %add_bitcast_fusion.refs_0_, ...), custom_call_target="tpu_custom_call" | custom-call | tf_op jit(solution)/shard_map/enter/pallas_call | solution.py:98
  50.5 2.4 %project.1 = (bf16[1536,768]{1,0:T(8,128)(2,1)S(1)}, f32[256,1152]{1,0:T(8,128)S(1)}, f32[256,640]{1,0:T(8,128)S(1)}, f32[256,1152]{1,0:T(8,128)S(1)}) custom-call(s32[1,3]{1,0:T(1,128)S(1)} %add_bitcast_fusion.refs_0_, bf16[4,96,768]{2,1,0:T(8,128)(2,1)S(1)} %get-tuple-element.109.refs_1_, bf16[4,96,768]{2,1,0:T(8,128)(2,1)S(1)} %collective-permute-done.6.refs_2_, ...), custom_call_target="tpu_custom_call" | custom-call | tf_op jit(solution)/shard_map/project/pallas_call | solution.py:98
  55.9 5.4 %collective-permute-start.17 = (f32[8,256]{1,0:T(8,128)S(1)}, f32[8,256]{1,0:T(8,128)S(1)}, u32[]{:S(2)}, u32[]{:S(2)}) collective-permute-start(f32[8,256]{1,0:T(8,128)S(1)} %get-tuple-element.120), channel_id=1, source_target_pairs={{0,1},{1,0},{2,3},{3,2},{4,5},{5,4},{6,7},{7,6},{8,9},{9,8},{10,11... | collective-permute-start | bytes 24584 | tf_op jit(solution)/shard_map/ppermute | solution.py:729
  62.1 2.5 %collective-permute-start.20 = (f32[8,256]{1,0:T(8,128)S(1)}, f32[8,256]{1,0:T(8,128)S(1)}, u32[]{:S(2)}, u32[]{:S(2)}) collective-permute-start(f32[8,256]{1,0:T(8,128)S(1)} %add.3.refs_1_), channel_id=1, source_target_pairs={{0,6},{1,7},{2,0},{3,1},{4,2},{5,3},{6,4},{7,5},{8,14},{9,15},{10,... | collective-permute-start | bytes 24584 | tf_op jit(solution)/shard_map/ppermute | solution.py:725
  65.7 2.9 %collective-permute-done.19.refs_3_ = f32[8,256]{1,0:T(8,128)S(1)} collective-permute-done((f32[8,256]{1,0:T(8,128)S(1)}, f32[8,256]{1,0:T(8,128)S(1)}, u32[]{:S(2)}, u32[]{:S(2)}) %collective-permute-start.19) | collective-permute-done | bytes 8224 | tf_op jit(solution)/shard_map/ppermute | solution.py:725
  70.3 2.0 %collective-permute-start.22 = (bf16[128,384]{1,0:T(8,128)(2,1)S(1)}, bf16[128,384]{1,0:T(8,128)(2,1)S(1)}, u32[]{:S(2)}, u32[]{:S(2)}) collective-permute-start(bf16[128,384]{1,0:T(8,128)(2,1)S(1)} %get-tuple-element.122), channel_id=1, source_target_pairs={{0,16},{8,24},{16,0},{24,8},{1,17},{9,25},{17,1},{25,9},{2,18},{10... | collective-permute-start | bytes 294920 | tf_op jit(solution)/shard_map/ppermute | solution.py:721
  73.6 3.3 %middle.1 = (bf16[1536,384]{1,0:T(8,128)(2,1)S(1)}, bf16[1536,384]{1,0:T(8,128)(2,1)S(1)}, f32[256,640]{1,0:T(8,128)S(1)}, bf16[256,1536]{1,0:T(8,128)(2,1)S(1)}) custom-call(s32[1,3]{1,0:T(1,128)S(1)} %add_bitcast_fusion.refs_0_, bf16[272,1536]{1,0:T(8,128)(2,1)S(1)} %get-tuple-element.116.refs_11_.refs_1_.refs_6_.refs_10_, ...), custom_call_target="tpu_custom_call" | custom-call | tf_op jit(solution)/shard_map/middle/pallas_call | solution.py:98
  76.9 2.3 %leave.1 = (bf16[272,512]{1,0:T(8,128)(2,1)S(1)}, f32[272,256]{1,0:T(8,128)S(1)}, f32[4,32,384]{2,1,0:T(8,128)S(1)}, f32[4,32,384]{2,1,0:T(8,128)S(1)}, f32[8,384]{1,0:T(8,128)S(1)}) custom-call(s32[1,3]{1,0:T(1,128)S(1)} %add_bitcast_fusion.refs_0_, bf16[128,384]{1,0:T(8,128)(2,1)S(1)} %collective-permute-done.21.refs_1_, ...), custom_call_target="tpu_custom_call" | custom-call | tf_op jit(solution)/shard_map/leave/pallas_call | solution.py:98
  79.3 3.3 %collective-permute-start.24 = (f32[4,32,384]{2,1,0:T(8,128)S(1)}, f32[4,32,384]{2,1,0:T(8,128)S(1)}, u32[]{:S(2)}, u32[]{:S(2)}) collective-permute-start(f32[4,32,384]{2,1,0:T(8,128)S(1)} %get-tuple-element.132), channel_id=1, source_target_pairs={{0,1},{1,0},{2,3},{3,2},{4,5},{5,4},{6,7},{7,6},{8,9},{9,8},{10,11... | collective-permute-start | bytes 589832 | tf_op jit(solution)/shard_map/ppermute | solution.py:729
  85.6 2.0 %collective-permute-start.27 = (f32[32,384]{1,0:T(8,128)S(1)}, f32[32,384]{1,0:T(8,128)S(1)}, u32[]{:S(2)}, u32[]{:S(2)}) collective-permute-start(f32[32,384]{1,0:T(8,128)S(1)} %get-tuple-element.136), channel_id=1, source_target_pairs={{0,6},{1,7},{2,0},{3,1},{4,2},{5,3},{6,4},{7,5},{8,14},{9,15},{10,... | collective-permute-start | bytes 147464 | tf_op jit(solution)/shard_map/ppermute | solution.py:725
  87.6 3.0 %value_grads.1 = (bf16[1536,384]{1,0:T(8,128)(2,1)S(1)}, f32[272,1536]{1,0:T(8,128)S(1)}) custom-call(s32[1,3]{1,0:T(1,128)S(1)} %add_bitcast_fusion.refs_0_, bf16[272,512]{1,0:T(8,128)(2,1)S(1)} %get-tuple-element.137.refs_1_.refs_5_, f32[272,256]{1,0:T(8,128)S(1)} %get-tuple-element.139.refs_2_, bf16[256,768]{1,0:T(8,128)(2,1)S(1)} %get-tuple-element.125.refs_2_.refs_3_, ...), custom_call_target="tpu_custom_call" | custom-call | tf_op jit(solution)/shard_map/value_grads/pallas_call | solution.py:98
  90.6 2.1 %late_grads.1 = (bf16[4,64,1536]{2,1,0:T(8,128)(2,1)S(1)}, bf16[4,64,1536]{2,1,0:T(8,128)(2,1)S(1)}, bf16[4,96,768]{2,1,0:T(8,128)(2,1)S(1)}, bf16[4,96,768]{2,1...) custom-call(s32[1,3]{1,0:T(1,128)S(1)} %add_bitcast_fusion.refs_0_, ...), custom_call_target="tpu_custom_call" | custom-call | tf_op jit(solution)/shard_map/late_grads/pallas_call | solution.py:98
  93.9 2.7 %collective-permute-start.29 = (bf16[2,96,768]{2,1,0:T(8,128)(2,1)S(1)}, bf16[2,96,768]{2,1,0:T(8,128)(2,1)S(1)}, u32[]{:S(2)}, u32[]{:S(2)}) collective-permute-start(bf16[2,96,768]{2,1,0:T(8,128)(2,1)S(1)} %get-tuple-element.150), channel_id=1, source_target_pairs={{0,96},{32,0},{64,32},{96,64},{1,97},{33,1},{65,33},{97,65},{2,98}... | collective-permute-start | bytes 884744 | tf_op jit(solution)/shard_map/ppermute | solution.py:721
  96.6 2.4 %collective-permute-start.31 = (bf16[2,112,512]{2,1,0:T(8,128)(2,1)S(1)}, bf16[2,112,512]{2,1,0:T(8,128)(2,1)S(1)}, u32[]{:S(2)}, u32[]{:S(2)}) collective-permute-start(bf16[2,112,512]{2,1,0:T(8,128)(2,1)S(1)} %get-tuple-element.154), channel_id=1, source_target_pairs={{0,24},{8,0},{16,8},{24,16},{1,25},{9,1},{17,9},{25,17},{2,26},{10... | collective-permute-start | bytes 688136 | tf_op jit(solution)/shard_map/ppermute | solution.py:721
  100.6 5.2 %collective-permute-done.30.refs_7_ = bf16[2,96,512]{2,1,0:T(8,128)(2,1)S(1)} collective-permute-done((bf16[2,96,512]{2,1,0:T(8,128)(2,1)S(1)}, bf16[2,96,512]{2,1,0:T(8,128)(2,1)S(1)}, u32[]{:S(2)}, u32[]{:S(2)}) %collective-permute-start.30) | collective-permute-done | bytes 196640 | tf_op jit(solution)/shard_map/ppermute | solution.py:721
  106.7 2.7 %collective-permute-start.34 = (bf16[4,96,768]{2,1,0:T(8,128)(2,1)S(1)}, bf16[4,96,768]{2,1,0:T(8,128)(2,1)S(1)}, u32[]{:S(2)}, u32[]{:S(2)}) collective-permute-start(bf16[4,96,768]{2,1,0:T(8,128)(2,1)S(1)} %get-tuple-element.159), channel_id=1, source_target_pairs={{0,96},{32,0},{64,32},{96,64},{1,97},{33,1},{65,33},{97,65},{2,98}... | collective-permute-start | bytes 1769480 | tf_op jit(solution)/shard_map/ppermute | solution.py:721
  109.4 2.7 %collective-permute-start.36 = (bf16[4,96,512]{2,1,0:T(8,128)(2,1)S(1)}, bf16[4,96,512]{2,1,0:T(8,128)(2,1)S(1)}, u32[]{:S(2)}, u32[]{:S(2)}) collective-permute-start(bf16[4,96,512]{2,1,0:T(8,128)(2,1)S(1)} %get-tuple-element.162), channel_id=1, source_target_pairs={{0,24},{8,0},{16,8},{24,16},{1,25},{9,1},{17,9},{25,17},{2,26},{10... | collective-permute-start | bytes 1179656 | tf_op jit(solution)/shard_map/ppermute | solution.py:721
  114.5 4.3 %collective-permute-done.35.refs_5_ = bf16[4,96,512]{2,1,0:T(8,128)(2,1)S(1)} collective-permute-done((bf16[4,96,512]{2,1,0:T(8,128)(2,1)S(1)}, bf16[4,96,512]{2,1,0:T(8,128)(2,1)S(1)}, u32[]{:S(2)}, u32[]{:S(2)}) %collective-permute-start.35) | collective-permute-done | bytes 393248 | tf_op jit(solution)/shard_map/ppermute | solution.py:721
  118.8 2.1 %collective-permute-done.33.refs_2_ = bf16[4,96,768]{2,1,0:T(8,128)(2,1)S(1)} collective-permute-done((bf16[4,96,768]{2,1,0:T(8,128)(2,1)S(1)}, bf16[4,96,768]{2,1,0:T(8,128)(2,1)S(1)}, u32[]{:S(2)}, u32[]{:S(2)}) %collective-permute-start.33) | collective-permute-done | bytes 589856 | tf_op jit(solution)/shard_map/ppermute | solution.py:721
  121.9 3.6 %collective-permute-start.39 = (bf16[96,512]{1,0:T(8,128)(2,1)S(1)}, bf16[96,512]{1,0:T(8,128)(2,1)S(1)}, u32[]{:S(2)}, u32[]{:S(2)}) collective-permute-start(bf16[96,512]{1,0:T(8,128)(2,1)S(1)} %get-tuple-element.167), channel_id=1, source_target_pairs={{0,64},{32,96},{64,0},{96,32},{1,65},{33,97},{65,1},{97,33},{2,66}... | collective-permute-start | bytes 294920 | tf_op jit(solution)/shard_map/ppermute | solution.py:721
  130.7 2.0 %collective-permute-start.44 = (bf16[80,1536]{1,0:T(8,128)(2,1)S(1)}, bf16[80,1536]{1,0:T(8,128)(2,1)S(1)}, u32[]{:S(2)}, u32[]{:S(2)}) collective-permute-start(bf16[80,1536]{1,0:T(8,128)(2,1)S(1)} %get-tuple-element.172.refs_1_), channel_id=1, source_target_pairs={{0,6},{1,7},{2,0},{3,1},{4,2},{5,3},{6,4},{7,5},{8,14},{9,15},{10,... | collective-permute-start | bytes 737288 | tf_op jit(solution)/shard_map/ppermute | solution.py:725
  136.3 2.5 %collective-permute-done.50.refs_3_ = bf16[96,768]{1,0:T(8,128)(2,1)S(1)} collective-permute-done((bf16[96,768]{1,0:T(8,128)(2,1)S(1)}, bf16[96,768]{1,0:T(8,128)(2,1)S(1)}, u32[]{:S(2)}, u32[]{:S(2)}) %collective-permute-start.50) | collective-permute-done | bytes 147488 | tf_op jit(solution)/shard_map/ppermute | solution.py:721
  138.8 6.4 %collective-permute-start.45 = (bf16[80,1536]{1,0:T(8,128)(2,1)S(1)}, bf16[80,1536]{1,0:T(8,128)(2,1)S(1)}, u32[]{:S(2)}, u32[]{:S(2)}) collective-permute-start(bf16[80,1536]{1,0:T(8,128)(2,1)S(1)} %get-tuple-element.172.refs_1_), channel_id=1, source_target_pairs={{0,1},{1,0},{2,3},{3,2},{4,5},{5,4},{6,7},{7,6},{8,9},{9,8},{10,11... | collective-permute-start | bytes 737288 | tf_op jit(solution)/shard_map/ppermute | solution.py:729
  145.7 2.1 %collective-permute-start.46 = (bf16[80,1536]{1,0:T(8,128)(2,1)S(1)}, bf16[80,1536]{1,0:T(8,128)(2,1)S(1)}, u32[]{:S(2)}, u32[]{:S(2)}) collective-permute-start(bf16[80,1536]{1,0:T(8,128)(2,1)S(1)} %collective-permute-done.42.refs_2_), channel_id=1, source_target_pairs={{0,1},{1,0},{2,3},{3,2},{4,5},{5,4},{6,7},{7,6},{8,9},{9,8},{10,11... | collective-permute-start | bytes 737288 | tf_op jit(solution)/shard_map/ppermute | solution.py:729
  149.2 2.5 %finish.1 = (f32[256,1536]{1,0:T(8,128)}, bf16[256,1536]{1,0:T(8,128)(2,1)}, f32[96,256]{1,0:T(8,128)}, f32[1,96]{1,0:T(1,128)}, f32[4,256]{1,0:T(4,128)}, /*index=5*/f32[1,256]{1,0:T(1,128)}) custom-call(s32[1,3]{1,0:T(1,128)S(1)} %add_bitcast_fusion.refs_0_, bf16[80,1536]{1,0:T(8,128)(2,1)S(1)} %get-tuple-element.172.refs_1_, ...), custom_call_target="tpu_custom_call" | custom-call | tf_op jit(solution)/shard_map/finish/pallas_call | solution.py:98
  (119 shorter events, 47.0 us)
Async XLA Ops:
  2.6 9.0 %collective-permute-start.2 = (bf16[96,768]{1,0:T(8,128)(2,1)S(1)}, bf16[96,768]{1,0:T(8,128)(2,1)S(1)}, u32[]{:S(2)}, u32[]{:S(2)}) collective-permute-start(bf16[96,768]{1,0:T(8,128)(2,1)S(1)} %get-tuple-element.106.refs_1_), channel_id=1, source_target_pairs={{0,24},{8,0},{16,8},{24,16},{1,25},{9,1},{17,9},{25,17},{2,26},{10... | collective-permute-start | bytes 442376 | tf_op jit(solution)/shard_map/ppermute | solution.py:721
  6.2 14.9 %collective-permute-start = (bf16[112,768]{1,0:T(8,128)(2,1)S(1)}, bf16[112,768]{1,0:T(8,128)(2,1)S(1)}, u32[]{:S(2)}, u32[]{:S(2)}) collective-permute-start(bf16[112,768]{1,0:T(8,128)(2,1)S(1)} %get-tuple-element.107), channel_id=1, source_target_pairs={{0,8},{8,16},{16,24},{24,0},{1,9},{9,17},{17,25},{25,1},{2,10},{10... | collective-permute-start | bytes 516104 | tf_op jit(solution)/shard_map/ppermute | solution.py:721
  6.2 8.3 %collective-permute-start.1 = (bf16[96,768]{1,0:T(8,128)(2,1)S(1)}, bf16[96,768]{1,0:T(8,128)(2,1)S(1)}, u32[]{:S(2)}, u32[]{:S(2)}) collective-permute-start(bf16[96,768]{1,0:T(8,128)(2,1)S(1)} %get-tuple-element.106.refs_1_), channel_id=1, source_target_pairs={{0,16},{8,24},{16,0},{24,8},{1,17},{9,25},{17,1},{25,9},{2,18},{10... | collective-permute-start | bytes 442376 | tf_op jit(solution)/shard_map/ppermute | solution.py:721
  7.9 9.3 %collective-permute-start.5 = (bf16[96,768]{1,0:T(8,128)(2,1)S(1)}, bf16[96,768]{1,0:T(8,128)(2,1)S(1)}, u32[]{:S(2)}, u32[]{:S(2)}) collective-permute-start(bf16[96,768]{1,0:T(8,128)(2,1)S(1)} %get-tuple-element.108.refs_5_), channel_id=1, source_target_pairs={{0,96},{32,0},{64,32},{96,64},{1,97},{33,1},{65,33},{97,65},{2,98}... | collective-permute-start | bytes 442376 | tf_op jit(solution)/shard_map/ppermute | solution.py:721
  11.6 9.5 %collective-permute-start.3 = (bf16[96,768]{1,0:T(8,128)(2,1)S(1)}, bf16[96,768]{1,0:T(8,128)(2,1)S(1)}, u32[]{:S(2)}, u32[]{:S(2)}) collective-permute-start(bf16[96,768]{1,0:T(8,128)(2,1)S(1)} %get-tuple-element.108.refs_5_), channel_id=1, source_target_pairs={{0,32},{32,64},{64,96},{96,0},{1,33},{33,65},{65,97},{97,1},{2,34}... | collective-permute-start | bytes 442376 | tf_op jit(solution)/shard_map/ppermute | solution.py:721
  21.8 13.8 %collective-permute-start.8 = (bf16[4,96,768]{2,1,0:T(8,128)(2,1)S(1)}, bf16[4,96,768]{2,1,0:T(8,128)(2,1)S(1)}, u32[]{:S(2)}, u32[]{:S(2)}) collective-permute-start(bf16[4,96,768]{2,1,0:T(8,128)(2,1)S(1)} %get-tuple-element.109.refs_1_), channel_id=1, source_target_pairs={{0,96},{32,0},{64,32},{96,64},{1,97},{33,1},{65,33},{97,65},{2,98}... | collective-permute-start | bytes 1769480 | tf_op jit(solution)/shard_map/ppermute | solution.py:721
  21.9 14.4 %collective-permute-start.6 = (bf16[4,96,768]{2,1,0:T(8,128)(2,1)S(1)}, bf16[4,96,768]{2,1,0:T(8,128)(2,1)S(1)}, u32[]{:S(2)}, u32[]{:S(2)}) collective-permute-start(bf16[4,96,768]{2,1,0:T(8,128)(2,1)S(1)} %get-tuple-element.109.refs_1_), channel_id=1, source_target_pairs={{0,32},{32,64},{64,96},{96,0},{1,33},{33,65},{65,97},{97,1},{2,34}... | collective-permute-start | bytes 1769480 | tf_op jit(solution)/shard_map/ppermute | solution.py:721
  23.4 13.9 %collective-permute-start.12 = (bf16[4,96,768]{2,1,0:T(8,128)(2,1)S(1)}, bf16[4,96,768]{2,1,0:T(8,128)(2,1)S(1)}, u32[]{:S(2)}, u32[]{:S(2)}) collective-permute-start(bf16[4,96,768]{2,1,0:T(8,128)(2,1)S(1)} %get-tuple-element.110.refs_6_), channel_id=1, source_target_pairs={{0,24},{8,0},{16,8},{24,16},{1,25},{9,1},{17,9},{25,17},{2,26},{10... | collective-permute-start | bytes 1769480 | tf_op jit(solution)/shard_map/ppermute | solution.py:721
  23.4 14.0 %collective-permute-start.10 = (bf16[4,96,768]{2,1,0:T(8,128)(2,1)S(1)}, bf16[4,96,768]{2,1,0:T(8,128)(2,1)S(1)}, u32[]{:S(2)}, u32[]{:S(2)}) collective-permute-start(bf16[4,96,768]{2,1,0:T(8,128)(2,1)S(1)} %get-tuple-element.110.refs_6_), channel_id=1, source_target_pairs={{0,8},{8,16},{16,24},{24,0},{1,9},{9,17},{17,25},{25,1},{2,10},{10... | collective-permute-start | bytes 1769480 | tf_op jit(solution)/shard_map/ppermute | solution.py:721
  35.6 7.9 %collective-permute-start.9 = (bf16[2,96,768]{2,1,0:T(8,128)(2,1)S(1)}, bf16[2,96,768]{2,1,0:T(8,128)(2,1)S(1)}, u32[]{:S(2)}, u32[]{:S(2)}) collective-permute-start(bf16[2,96,768]{2,1,0:T(8,128)(2,1)S(1)} %slice.17), channel_id=1, source_target_pairs={{0,96},{32,0},{64,32},{96,64},{1,97},{33,1},{65,33},{97,65},{2,98}... | collective-permute-start | bytes 884744 | tf_op jit(solution)/shard_map/ppermute | solution.py:721
  36.3 7.2 %collective-permute-start.7 = (bf16[2,96,768]{2,1,0:T(8,128)(2,1)S(1)}, bf16[2,96,768]{2,1,0:T(8,128)(2,1)S(1)}, u32[]{:S(2)}, u32[]{:S(2)}) collective-permute-start(bf16[2,96,768]{2,1,0:T(8,128)(2,1)S(1)} %slice.16), channel_id=1, source_target_pairs={{0,32},{32,64},{64,96},{96,0},{1,33},{33,65},{65,97},{97,1},{2,34}... | collective-permute-start | bytes 884744 | tf_op jit(solution)/shard_map/ppermute | solution.py:721
  37.4 7.1 %collective-permute-start.11 = (bf16[2,96,768]{2,1,0:T(8,128)(2,1)S(1)}, bf16[2,96,768]{2,1,0:T(8,128)(2,1)S(1)}, u32[]{:S(2)}, u32[]{:S(2)}) collective-permute-start(bf16[2,96,768]{2,1,0:T(8,128)(2,1)S(1)} %slice.18), channel_id=1, source_target_pairs={{0,8},{8,16},{16,24},{24,0},{1,9},{9,17},{17,25},{25,1},{2,10},{10... | collective-permute-start | bytes 884744 | tf_op jit(solution)/shard_map/ppermute | solution.py:721
  70.2 6.6 %collective-permute-start.23 = (bf16[128,384]{1,0:T(8,128)(2,1)S(1)}, bf16[128,384]{1,0:T(8,128)(2,1)S(1)}, u32[]{:S(2)}, u32[]{:S(2)}) collective-permute-start(bf16[128,384]{1,0:T(8,128)(2,1)S(1)} %get-tuple-element.122), channel_id=1, source_target_pairs={{0,8},{8,16},{16,24},{24,0},{1,9},{9,17},{17,25},{25,1},{2,10},{10... | collective-permute-start | bytes 294920 | tf_op jit(solution)/shard_map/ppermute | solution.py:721
  70.3 6.5 %collective-permute-start.22 = (bf16[128,384]{1,0:T(8,128)(2,1)S(1)}, bf16[128,384]{1,0:T(8,128)(2,1)S(1)}, u32[]{:S(2)}, u32[]{:S(2)}) collective-permute-start(bf16[128,384]{1,0:T(8,128)(2,1)S(1)} %get-tuple-element.122), channel_id=1, source_target_pairs={{0,16},{8,24},{16,0},{24,8},{1,17},{9,25},{17,1},{25,9},{2,18},{10... | collective-permute-start | bytes 294920 | tf_op jit(solution)/shard_map/ppermute | solution.py:721
  84.2 6.4 %collective-permute-start.25 = (f32[32,384]{1,0:T(8,128)S(1)}, f32[32,384]{1,0:T(8,128)S(1)}, u32[]{:S(2)}, u32[]{:S(2)}) collective-permute-start(f32[32,384]{1,0:T(8,128)S(1)} %get-tuple-element.134), channel_id=1, source_target_pairs={{0,2},{1,3},{2,4},{3,5},{4,6},{5,7},{6,0},{7,1},{8,10},{9,11},{10,... | collective-permute-start | bytes 147464 | tf_op jit(solution)/shard_map/ppermute | solution.py:725
  93.9 11.8 %collective-permute-start.28 = (bf16[2,96,768]{2,1,0:T(8,128)(2,1)S(1)}, bf16[2,96,768]{2,1,0:T(8,128)(2,1)S(1)}, u32[]{:S(2)}, u32[]{:S(2)}) collective-permute-start(bf16[2,96,768]{2,1,0:T(8,128)(2,1)S(1)} %get-tuple-element.149), channel_id=1, source_target_pairs={{0,32},{32,64},{64,96},{96,0},{1,33},{33,65},{65,97},{97,1},{2,34}... | collective-permute-start | bytes 884744 | tf_op jit(solution)/shard_map/ppermute | solution.py:721
  93.9 11.8 %collective-permute-start.29 = (bf16[2,96,768]{2,1,0:T(8,128)(2,1)S(1)}, bf16[2,96,768]{2,1,0:T(8,128)(2,1)S(1)}, u32[]{:S(2)}, u32[]{:S(2)}) collective-permute-start(bf16[2,96,768]{2,1,0:T(8,128)(2,1)S(1)} %get-tuple-element.150), channel_id=1, source_target_pairs={{0,96},{32,0},{64,32},{96,64},{1,97},{33,1},{65,33},{97,65},{2,98}... | collective-permute-start | bytes 884744 | tf_op jit(solution)/shard_map/ppermute | solution.py:721
  96.6 9.1 %collective-permute-start.31 = (bf16[2,112,512]{2,1,0:T(8,128)(2,1)S(1)}, bf16[2,112,512]{2,1,0:T(8,128)(2,1)S(1)}, u32[]{:S(2)}, u32[]{:S(2)}) collective-permute-start(bf16[2,112,512]{2,1,0:T(8,128)(2,1)S(1)} %get-tuple-element.154), channel_id=1, source_target_pairs={{0,24},{8,0},{16,8},{24,16},{1,25},{9,1},{17,9},{25,17},{2,26},{10... | collective-permute-start | bytes 688136 | tf_op jit(solution)/shard_map/ppermute | solution.py:721
  99.0 6.7 %collective-permute-start.30 = (bf16[2,96,512]{2,1,0:T(8,128)(2,1)S(1)}, bf16[2,96,512]{2,1,0:T(8,128)(2,1)S(1)}, u32[]{:S(2)}, u32[]{:S(2)}) collective-permute-start(bf16[2,96,512]{2,1,0:T(8,128)(2,1)S(1)} %get-tuple-element.153), channel_id=1, source_target_pairs={{0,8},{8,16},{16,24},{24,0},{1,9},{9,17},{17,25},{25,1},{2,10},{10... | collective-permute-start | bytes 589832 | tf_op jit(solution)/shard_map/ppermute | solution.py:721
  99.8 12.3 %collective-permute-start.37 = (bf16[2,64,1536]{2,1,0:T(8,128)(2,1)S(1)}, bf16[2,64,1536]{2,1,0:T(8,128)(2,1)S(1)}, u32[]{:S(2)}, u32[]{:S(2)}) collective-permute-start(bf16[2,64,1536]{2,1,0:T(8,128)(2,1)S(1)} %get-tuple-element.163), channel_id=1, source_target_pairs={{0,2},{1,3},{2,0},{3,1},{4,6},{5,7},{6,4},{7,5},{8,10},{9,11},{10,... | collective-permute-start | bytes 1179656 | tf_op jit(solution)/shard_map/ppermute | solution.py:729
  106.6 14.3 %collective-permute-start.33 = (bf16[4,96,768]{2,1,0:T(8,128)(2,1)S(1)}, bf16[4,96,768]{2,1,0:T(8,128)(2,1)S(1)}, u32[]{:S(2)}, u32[]{:S(2)}) collective-permute-start(bf16[4,96,768]{2,1,0:T(8,128)(2,1)S(1)} %get-tuple-element.158), channel_id=1, source_target_pairs={{0,32},{32,64},{64,96},{96,0},{1,33},{33,65},{65,97},{97,1},{2,34}... | collective-permute-start | bytes 1769480 | tf_op jit(solution)/shard_map/ppermute | solution.py:721
  106.7 14.2 %collective-permute-start.34 = (bf16[4,96,768]{2,1,0:T(8,128)(2,1)S(1)}, bf16[4,96,768]{2,1,0:T(8,128)(2,1)S(1)}, u32[]{:S(2)}, u32[]{:S(2)}) collective-permute-start(bf16[4,96,768]{2,1,0:T(8,128)(2,1)S(1)} %get-tuple-element.159), channel_id=1, source_target_pairs={{0,96},{32,0},{64,32},{96,64},{1,97},{33,1},{65,33},{97,65},{2,98}... | collective-permute-start | bytes 1769480 | tf_op jit(solution)/shard_map/ppermute | solution.py:721
  109.4 9.4 %collective-permute-start.35 = (bf16[4,96,512]{2,1,0:T(8,128)(2,1)S(1)}, bf16[4,96,512]{2,1,0:T(8,128)(2,1)S(1)}, u32[]{:S(2)}, u32[]{:S(2)}) collective-permute-start(bf16[4,96,512]{2,1,0:T(8,128)(2,1)S(1)} %get-tuple-element.161), channel_id=1, source_target_pairs={{0,8},{8,16},{16,24},{24,0},{1,9},{9,17},{17,25},{25,1},{2,10},{10... | collective-permute-start | bytes 1179656 | tf_op jit(solution)/shard_map/ppermute | solution.py:721
  109.4 9.4 %collective-permute-start.36 = (bf16[4,96,512]{2,1,0:T(8,128)(2,1)S(1)}, bf16[4,96,512]{2,1,0:T(8,128)(2,1)S(1)}, u32[]{:S(2)}, u32[]{:S(2)}) collective-permute-start(bf16[4,96,512]{2,1,0:T(8,128)(2,1)S(1)} %get-tuple-element.162), channel_id=1, source_target_pairs={{0,24},{8,0},{16,8},{24,16},{1,25},{9,1},{17,9},{25,17},{2,26},{10... | collective-permute-start | bytes 1179656 | tf_op jit(solution)/shard_map/ppermute | solution.py:721
  112.7 12.8 %collective-permute-start.41 = (bf16[64,1536]{1,0:T(8,128)(2,1)S(1)}, bf16[64,1536]{1,0:T(8,128)(2,1)S(1)}, u32[]{:S(2)}, u32[]{:S(2)}) collective-permute-start(bf16[64,1536]{1,0:T(8,128)(2,1)S(1)} %get-tuple-element.169), channel_id=1, source_target_pairs={{0,4},{1,5},{2,6},{3,7},{4,0},{5,1},{6,2},{7,3},{8,12},{9,13},{10,... | collective-permute-start | bytes 589832 | tf_op jit(solution)/shard_map/ppermute | solution.py:729
  121.9 6.6 %collective-permute-start.39 = (bf16[96,512]{1,0:T(8,128)(2,1)S(1)}, bf16[96,512]{1,0:T(8,128)(2,1)S(1)}, u32[]{:S(2)}, u32[]{:S(2)}) collective-permute-start(bf16[96,512]{1,0:T(8,128)(2,1)S(1)} %get-tuple-element.167), channel_id=1, source_target_pairs={{0,64},{32,96},{64,0},{96,32},{1,65},{33,97},{65,1},{97,33},{2,66}... | collective-permute-start | bytes 294920 | tf_op jit(solution)/shard_map/ppermute | solution.py:721
  125.5 8.2 %collective-permute-start.49 = (bf16[96,768]{1,0:T(8,128)(2,1)S(1)}, bf16[96,768]{1,0:T(8,128)(2,1)S(1)}, u32[]{:S(2)}, u32[]{:S(2)}) collective-permute-start(bf16[96,768]{1,0:T(8,128)(2,1)S(1)} %get-tuple-element.180), channel_id=1, source_target_pairs={{0,8},{8,16},{16,24},{24,0},{1,9},{9,17},{17,25},{25,1},{2,10},{10... | collective-permute-start | bytes 442376 | tf_op jit(solution)/shard_map/ppermute | solution.py:721
  130.7 14.5 %collective-permute-start.44 = (bf16[80,1536]{1,0:T(8,128)(2,1)S(1)}, bf16[80,1536]{1,0:T(8,128)(2,1)S(1)}, u32[]{:S(2)}, u32[]{:S(2)}) collective-permute-start(bf16[80,1536]{1,0:T(8,128)(2,1)S(1)} %get-tuple-element.172.refs_1_), channel_id=1, source_target_pairs={{0,6},{1,7},{2,0},{3,1},{4,2},{5,3},{6,4},{7,5},{8,14},{9,15},{10,... | collective-permute-start | bytes 737288 | tf_op jit(solution)/shard_map/ppermute | solution.py:725
  132.6 12.6 %collective-permute-start.43 = (bf16[80,1536]{1,0:T(8,128)(2,1)S(1)}, bf16[80,1536]{1,0:T(8,128)(2,1)S(1)}, u32[]{:S(2)}, u32[]{:S(2)}) collective-permute-start(bf16[80,1536]{1,0:T(8,128)(2,1)S(1)} %get-tuple-element.172.refs_1_), channel_id=1, source_target_pairs={{0,4},{1,5},{2,6},{3,7},{4,0},{5,1},{6,2},{7,3},{8,12},{9,13},{10,... | collective-permute-start | bytes 737288 | tf_op jit(solution)/shard_map/ppermute | solution.py:725
  133.2 12.6 %collective-permute-start.42 = (bf16[80,1536]{1,0:T(8,128)(2,1)S(1)}, bf16[80,1536]{1,0:T(8,128)(2,1)S(1)}, u32[]{:S(2)}, u32[]{:S(2)}) collective-permute-start(bf16[80,1536]{1,0:T(8,128)(2,1)S(1)} %get-tuple-element.172.refs_1_), channel_id=1, source_target_pairs={{0,2},{1,3},{2,4},{3,5},{4,6},{5,7},{6,0},{7,1},{8,10},{9,11},{10,... | collective-permute-start | bytes 737288 | tf_op jit(solution)/shard_map/ppermute | solution.py:725
  133.7 14.1 %collective-permute-start.51 = (bf16[96,768]{1,0:T(8,128)(2,1)S(1)}, bf16[96,768]{1,0:T(8,128)(2,1)S(1)}, u32[]{:S(2)}, u32[]{:S(2)}) collective-permute-start(bf16[96,768]{1,0:T(8,128)(2,1)S(1)} %get-tuple-element.182), channel_id=1, source_target_pairs={{0,24},{8,0},{16,8},{24,16},{1,25},{9,1},{17,9},{25,17},{2,26},{10... | collective-permute-start | bytes 442376 | tf_op jit(solution)/shard_map/ppermute | solution.py:721
  138.8 10.4 %collective-permute-start.45 = (bf16[80,1536]{1,0:T(8,128)(2,1)S(1)}, bf16[80,1536]{1,0:T(8,128)(2,1)S(1)}, u32[]{:S(2)}, u32[]{:S(2)}) collective-permute-start(bf16[80,1536]{1,0:T(8,128)(2,1)S(1)} %get-tuple-element.172.refs_1_), channel_id=1, source_target_pairs={{0,1},{1,0},{2,3},{3,2},{4,5},{5,4},{6,7},{7,6},{8,9},{9,8},{10,11... | collective-permute-start | bytes 737288 | tf_op jit(solution)/shard_map/ppermute | solution.py:729
  (28 other events, 219.9 us)

commit v5 on v4

--- a/solution.py
+++ b/solution.py
@@ -36,7 +36,8 @@
 VALUES, SLOPE = slice(0, WIDE), slice(WIDE, WIDE + MIX)
 STEP, STEP_SLOPE, LOG_DECAY = slice(1024, 1152), slice(1152, 1280), slice(1280, 1408)
 BMAT, CMAT, WEIGHTED = slice(0, 128), slice(128, 256), slice(256, 640)
-GATE_PRE, GRAD_NORMED, WITHIN = slice(0, 384), slice(384, 768), slice(768, 1152)
+GATE, GRAD_NORMED, WITHIN = slice(0, 384), slice(384, 768), slice(768, 1152)
+GATE_SLOPE, SCALED, SKIPPED = slice(1152, 1536), slice(1536, 1920), slice(1920, 2304)
 INSIDE, MIXED = slice(0, 384), slice(384, 768)
 NORMED, LOW_GATE = slice(0, 384), slice(384, 768)
 GROWN, TO_END, STEPS = slice(0, 384), slice(384, 768), slice(768, 1152)
@@ -287,7 +288,7 @@
 
 
 def project(
-    ids, l0, l1, l2, l3, l4, r0, r1, r2, r3, r4, hidden_in, cotangent, wide, narrow,
+    ids, l0, l1, l2, l3, l4, r0, r1, r2, r3, r4, hidden_in, cotangent, wide, narrow, consts,
     gate_out, before, slope, spread,
 ):
     moves = (gate_out, 0, 0, WIDE, WIDE), (gate_out, 1, WIDE, WIDE, WIDE)
@@ -297,8 +298,13 @@
     spread[:, GROWN] = spread_heads(jnp.exp(wide[:, LOG_DECAY]))
     spread[:, TO_END] = spread_heads(jnp.exp(last - wide[:, LOG_DECAY]))
     spread[:, STEPS] = spread_heads(wide[:, STEP])
-    before[:, GATE_PRE] = dot(hidden_in[RIM:], gate_out[:, :WIDE])
-    before[:, GRAD_NORMED] = dot(cotangent[...], gate_out[:, WIDE:])
+    act, gate_slope = silu_parts(dot(hidden_in[RIM:], gate_out[:, :WIDE]))
+    grads = dot(cotangent[...], gate_out[:, WIDE:])
+    before[:, GATE] = act
+    before[:, GATE_SLOPE] = gate_slope
+    before[:, GRAD_NORMED] = grads
+    before[:, SCALED] = grads * consts[5:6, :WIDE] * act
+    before[:, SKIPPED] = wide[:, VALUES] * spread_heads(consts[8:9, :128])
     scores = dot_last(narrow[:, CMAT], narrow[:, BMAT])
     log_decay = wide[:, LOG_DECAY]
     turned = log_decay.T
@@ -312,7 +318,7 @@
         before[:, start : start + 128] = jnp.where(lower, one, two)
 
 
-def mix(ids, m1, m2, m3, wide, spread, narrow, consts, before, state, after, sums):
+def mix(ids, m1, m2, m3, spread, narrow, before, state, after, sums):
     me = ids[0, 1]
     total = jnp.zeros((STATE, WIDE), F32)
     gap = jnp.zeros((1, WIDE), F32)
@@ -326,36 +332,37 @@
     state[:STATE] = total
     inside = before[:, WITHIN] + dot(narrow[:, CMAT], total) * spread[:, GROWN]
     after[:, INSIDE] = inside
-    whole = inside + wide[:, VALUES] * spread_heads(consts[8:9, :128])
+    whole = inside + before[:, SKIPPED]
     after[:, MIXED] = whole
-    gate = before[:, GATE_PRE]
-    gated = whole * gate * jax.nn.sigmoid(gate)
+    gated = whole * before[:, GATE]
     ones = jnp.ones((8, WIDE), F32)
     squares = pick(ones, gated * gated, 1, 1)
-    crosses = pick(ones, before[:, GRAD_NORMED] * consts[5:6, :WIDE] * gated, 1, 1)
+    crosses = pick(ones, before[:, SCALED] * whole, 1, 1)
     sums[...] = jnp.where(iota((8, T), 0) < 4, squares, crosses)
 
 
-def gate_back(
-    ids, s0, s1, s2, s3, after, before, consts, spread, narrow, gated_low, grad_mixed, grad_gain, sensitivity
-):
+def gate_ready(ids, after, before, consts, ready):
+    mixed, act = after[:, MIXED], before[:, GATE]
+    gated, rest = mixed * act, mixed * before[:, GATE_SLOPE]
+    ready[0] = gated * act
+    ready[1] = before[:, GRAD_NORMED] * consts[5:6, :WIDE] * rest
+    ready[2] = gated * rest
+    ready[3] = gated * consts[5:6, :WIDE]
+    ready[4] = before[:, GRAD_NORMED] * gated
+
+
+def gate_back(ids, s0, s1, s2, s3, ready, before, spread, narrow, gated_low, grad_mixed, grad_gain, sensitivity):
     total = s0[...] + s1[...] + s2[...] + s3[...]
     chosen = flag(iota((8, 128), 0) == 4 * iota((8, 128), 1))
     columns = sum(dot_first(part, chosen) for part in split(total, 3))
     inv = lax.rsqrt(columns[:, 0:1] / INNER + EPSILON)
-    cross = columns[:, 1:2]
-    act, slope = silu_parts(before[:, GATE_PRE])
-    mixed = after[:, MIXED]
-    normed = mixed * act * inv
-    scaled = consts[5:6, :WIDE]
-    gated_low[:, NORMED] = (normed * scaled).astype(BF16)
-    grads = before[:, GRAD_NORMED]
-    grad_gain[...] = jnp.broadcast_to(jnp.sum(grads * normed, axis=0, keepdims=True), (8, WIDE))
-    grad_gated = inv * (grads * scaled) - normed * (inv * inv * cross / INNER)
-    own = grad_gated * act
+    back = inv * (inv * inv * columns[:, 1:2] / INNER)
+    own = inv * before[:, SCALED] - back * ready[0]
     grad_mixed[...] = own
-    gated_low[:, LOW_GATE] = (grad_gated * mixed * slope).astype(BF16)
     sensitivity[...] = dot_first(narrow[:, CMAT], own * spread[:, GROWN]).astype(BF16)
+    gated_low[:, LOW_GATE] = (inv * ready[1] - back * ready[2]).astype(BF16)
+    gated_low[:, NORMED] = (inv * ready[3]).astype(BF16)
+    grad_gain[...] = jnp.broadcast_to(jnp.sum(inv * ready[4], axis=0, keepdims=True), (8, WIDE))
 
 
 def turn_out(ids, source, keep, send):
@@ -826,7 +833,7 @@
     messages = around(message, "ctx")[1:]
     gate_out, before, slope, spread = fuse(
         project,
-        [((D, 2 * WIDE), BF16), ((T, WITHIN.stop), F32), ((T, MIX), F32), ((T, STEPS.stop), F32)],
+        [((D, 2 * WIDE), BF16), ((T, SKIPPED.stop), F32), ((T, MIX), F32), ((T, STEPS.stop), F32)],
         ids,
         *left,
         *right,
@@ -834,18 +841,18 @@
         cotangent,
         wide,
         narrow,
+        consts,
     )
     state, after, sums = fuse(
         mix,
         [((STATE + 24, WIDE), F32), ((T, MIXED.stop), F32), ((8, T), F32)],
         ids,
         *messages,
-        wide,
         spread,
         narrow,
-        consts,
         before,
     )
+    (ready,) = fuse(gate_ready, [((5, T, WIDE), F32)], ids, after, before, consts)
     sums = sums + across(sums, 1)
     gated_low, grad_mixed, grad_gain, sensitivity = fuse(
         gate_back,
@@ -858,9 +865,8 @@
         ids,
         sums,
         *[from_chip(sums, steps) for steps in range(1, 4)],
-        after,
+        ready,
         before,
-        consts,
         spread,
         narrow,
     )

time: 152 us -> 150 us (0.987)
  waiting for transfers between devices: 45.2 us -> 36.4 us
  starting transfers between devices: 69.8 us -> 76.2 us
    ppermute x34, waiting for transfers between devices: 40.2 us -> 33.2 us  [shift(): return lax.ppermute(array, axis, [(i, (i + steps) % 4) for i in range(4)])]
    ppermute x34, starting transfers between devices: 38.6 us -> 44.4 us  [shift(): return lax.ppermute(array, axis, [(i, (i + steps) % 4) for i in range(4)])]
    ppermute x9, starting transfers between devices: 9.56 us -> 11.7 us  [from_chip(): lax.ppermute(array, 'tp', [(i, (i + 2 * steps) % 8) for i in range(8)])]
    ppermute x9, waiting for transfers between devices: 3.12 us -> 1.06 us  [from_chip(): lax.ppermute(array, 'tp', [(i, (i + 2 * steps) % 8) for i in range(8)])]
    pallas_call x19 -> x20, Pallas kernels: 32 us -> 32.6 us  [fuse(): return list(call(ids, *arrays))]
  transfers between devices with their start and end apart: 52 -> 52, of which waited for: 19 -> 22; matrix products, arithmetic and copies ran while one was open for 2% -> 2% of each run, Pallas kernels for 11% -> 12%
where the time goes in v5:
time: 150 us
  starting transfers between devices  76.2 us (51%)
  waiting for transfers between devices  36.4 us (24%)
  Pallas kernels  32.6 us (22%)
  other arithmetic  1.86 us (1%)
  local copies, waits for them, and re-layouts  1.81 us (1%)
    ppermute x34, starting transfers between devices, shift(): return lax.ppermute(array, axis, [(i, (i + steps) % 4) for i in range(4)])  44.4 us
    ppermute x34, waiting for transfers between devices, shift(): return lax.ppermute(array, axis, [(i, (i + steps) % 4) for i in range(4)])  33.2 us
    pallas_call x20, Pallas kernels, fuse(): return list(call(ids, *arrays))  32.6 us
    ppermute x9, starting transfers between devices, across(): return lax.ppermute(array, 'tp', [(i, i ^ bits) for i in range(8)])  20.1 us
    ppermute x9, starting transfers between devices, from_chip(): lax.ppermute(array, 'tp', [(i, (i + 2 * steps) % 8) for i in range(8)])  11.7 us
  transfers between devices with their start and end apart: 52, of which 22 were waited for; matrix products, arithmetic and copies ran while one was open for 2% of the time, Pallas kernels for 12%

profile of v5, /device:TPU:1, one launch (start us, length us, event | category | flops | bytes accessed | tf_op | source)
XLA Modules:
  0.0 149.9 jit_solution(3358105316047283759)
XLA Ops:
  2.6 2.5 %collective-permute-start.3 = (bf16[96,768]{1,0:T(8,128)(2,1)S(1)}, bf16[96,768]{1,0:T(8,128)(2,1)S(1)}, u32[]{:S(2)}, u32[]{:S(2)}) collective-permute-start(bf16[96,768]{1,0:T(8,128)(2,1)S(1)} %get-tuple-element.108.refs_5_), channel_id=1, source_target_pairs={{0,32},{32,64},{64,96},{96,0},{1,33},{33,65},{65,97},{97,1},{2,34}... | collective-permute-start | bytes 442376 | tf_op jit(solution)/shard_map/ppermute | solution.py:728
  6.4 3.3 %collective-permute-start.4 = (bf16[96,768]{1,0:T(8,128)(2,1)S(1)}, bf16[96,768]{1,0:T(8,128)(2,1)S(1)}, u32[]{:S(2)}, u32[]{:S(2)}) collective-permute-start(bf16[96,768]{1,0:T(8,128)(2,1)S(1)} %get-tuple-element.108.refs_5_), channel_id=1, source_target_pairs={{0,64},{32,96},{64,0},{96,32},{1,65},{33,97},{65,1},{97,33},{2,66}... | collective-permute-start | bytes 442376 | tf_op jit(solution)/shard_map/ppermute | solution.py:728
  10.5 2.7 %collective-permute-start.1 = (bf16[96,768]{1,0:T(8,128)(2,1)S(1)}, bf16[96,768]{1,0:T(8,128)(2,1)S(1)}, u32[]{:S(2)}, u32[]{:S(2)}) collective-permute-start(bf16[96,768]{1,0:T(8,128)(2,1)S(1)} %get-tuple-element.106.refs_1_), channel_id=1, source_target_pairs={{0,16},{8,24},{16,0},{24,8},{1,17},{9,25},{17,1},{25,9},{2,18},{10... | collective-permute-start | bytes 442376 | tf_op jit(solution)/shard_map/ppermute | solution.py:728
  16.1 2.6 %collective-permute-done.2.refs_4_ = bf16[96,768]{1,0:T(8,128)(2,1)S(1)} collective-permute-done((bf16[96,768]{1,0:T(8,128)(2,1)S(1)}, bf16[96,768]{1,0:T(8,128)(2,1)S(1)}, u32[]{:S(2)}, u32[]{:S(2)}) %collective-permute-start.2) | collective-permute-done | bytes 147488 | tf_op jit(solution)/shard_map/ppermute | solution.py:728
  22.9 1.9 %collective-permute-start.8 = (bf16[4,96,768]{2,1,0:T(8,128)(2,1)S(1)}, bf16[4,96,768]{2,1,0:T(8,128)(2,1)S(1)}, u32[]{:S(2)}, u32[]{:S(2)}) collective-permute-start(bf16[4,96,768]{2,1,0:T(8,128)(2,1)S(1)} %get-tuple-element.109.refs_1_), channel_id=1, source_target_pairs={{0,96},{32,0},{64,32},{96,64},{1,97},{33,1},{65,33},{97,65},{2,98}... | collective-permute-start | bytes 1769480 | tf_op jit(solution)/shard_map/ppermute | solution.py:728
  24.8 8.2 %collective-permute-done.10.refs_7_ = bf16[4,96,768]{2,1,0:T(8,128)(2,1)S(1)} collective-permute-done((bf16[4,96,768]{2,1,0:T(8,128)(2,1)S(1)}, bf16[4,96,768]{2,1,0:T(8,128)(2,1)S(1)}, u32[]{:S(2)}, u32[]{:S(2)}) %collective-permute-start.10) | collective-permute-done | bytes 589856 | tf_op jit(solution)/shard_map/ppermute | solution.py:728
  33.2 2.7 %collective-permute-start.13 = (bf16[2,96,768]{2,1,0:T(8,128)(2,1)S(1)}, bf16[2,96,768]{2,1,0:T(8,128)(2,1)S(1)}, u32[]{:S(2)}, u32[]{:S(2)}) collective-permute-start(bf16[2,96,768]{2,1,0:T(8,128)(2,1)S(1)} %slice.19), channel_id=1, source_target_pairs={{0,24},{8,0},{16,8},{24,16},{1,25},{9,1},{17,9},{25,17},{2,26},{10... | collective-permute-start | bytes 884744 | tf_op jit(solution)/shard_map/ppermute | solution.py:728
  36.8 2.0 %collective-permute-start.9 = (bf16[2,96,768]{2,1,0:T(8,128)(2,1)S(1)}, bf16[2,96,768]{2,1,0:T(8,128)(2,1)S(1)}, u32[]{:S(2)}, u32[]{:S(2)}) collective-permute-start(bf16[2,96,768]{2,1,0:T(8,128)(2,1)S(1)} %slice.17), channel_id=1, source_target_pairs={{0,96},{32,0},{64,32},{96,64},{1,97},{33,1},{65,33},{97,65},{2,98}... | collective-permute-start | bytes 884744 | tf_op jit(solution)/shard_map/ppermute | solution.py:728
  41.1 2.1 %tabulate.1 = (f32[16,768]{1,0:T(8,128)S(1)}, f32[256,1536]{1,0:T(8,128)S(1)}) custom-call(s32[1,3]{1,0:T(1,128)S(1)} %add_bitcast_fusion.refs_0_, bf16[4,384]{1,0:T(4,128)(2,1)} %refs_1_.3, bf16[4,256]{1,0:T(4,128)(2,1)} %refs_2_.3, bf16[1,384]{1,0:T(2,128)(2,1)} %broadcast_in_dim.19.refs_3_, bf16[1,256]{1,0:T(2,128)(2,1)} %broadcast_in_dim.20.refs_4_, ...), custom_call_target="tpu_custom_call" | custom-call | tf_op jit(solution)/shard_map/tabulate/pallas_call | solution.py:99
  43.2 2.9 %enter.1 = (bf16[1536,768]{1,0:T(8,128)(2,1)S(1)}, bf16[272,1536]{1,0:T(8,128)(2,1)S(1)}, bf16[272,640]{1,0:T(8,128)(2,1)S(1)}, f32[256,1408]{1,0:T(8,128)S(1)},...) custom-call(s32[1,3]{1,0:T(1,128)S(1)} %add_bitcast_fusion.refs_0_, ...), custom_call_target="tpu_custom_call" | custom-call | tf_op jit(solution)/shard_map/enter/pallas_call | solution.py:99
  46.2 2.3 %collective-permute-start.15 = (bf16[144,384]{1,0:T(8,128)(2,1)S(1)}, bf16[144,384]{1,0:T(8,128)(2,1)S(1)}, u32[]{:S(2)}, u32[]{:S(2)}) collective-permute-start(bf16[144,384]{1,0:T(8,128)(2,1)S(1)} %get-tuple-element.114), channel_id=1, source_target_pairs={{0,16},{8,24},{16,0},{24,8},{1,17},{9,25},{17,1},{25,9},{2,18},{10... | collective-permute-start | bytes 331784 | tf_op jit(solution)/shard_map/ppermute | solution.py:728
  48.9 2.4 %project.1 = (bf16[1536,768]{1,0:T(8,128)(2,1)S(1)}, f32[256,2304]{1,0:T(8,128)S(1)}, f32[256,640]{1,0:T(8,128)S(1)}, f32[256,1152]{1,0:T(8,128)S(1)}) custom-call(s32[1,3]{1,0:T(1,128)S(1)} %add_bitcast_fusion.refs_0_, bf16[4,96,768]{2,1,0:T(8,128)(2,1)S(1)} %get-tuple-element.109.refs_1_, bf16[4,96,768]{2,1,0:T(8,128)(2,1)S(1)} %collective-permute-done.6.refs_2_, ...), custom_call_target="tpu_custom_call" | custom-call | tf_op jit(solution)/shard_map/project/pallas_call | solution.py:99
  53.9 6.0 %collective-permute-start.17 = (f32[8,256]{1,0:T(8,128)S(1)}, f32[8,256]{1,0:T(8,128)S(1)}, u32[]{:S(2)}, u32[]{:S(2)}) collective-permute-start(f32[8,256]{1,0:T(8,128)S(1)} %get-tuple-element.120), channel_id=1, source_target_pairs={{0,1},{1,0},{2,3},{3,2},{4,5},{5,4},{6,7},{7,6},{8,9},{9,8},{10,11... | collective-permute-start | bytes 24584 | tf_op jit(solution)/shard_map/ppermute | solution.py:736
  61.9 2.4 %collective-permute-start.19 = (f32[8,256]{1,0:T(8,128)S(1)}, f32[8,256]{1,0:T(8,128)S(1)}, u32[]{:S(2)}, u32[]{:S(2)}) collective-permute-start(f32[8,256]{1,0:T(8,128)S(1)} %add.3.refs_1_), channel_id=1, source_target_pairs={{0,4},{1,5},{2,6},{3,7},{4,0},{5,1},{6,2},{7,3},{8,12},{9,13},{10,... | collective-permute-start | bytes 24584 | tf_op jit(solution)/shard_map/ppermute | solution.py:732
  68.4 2.2 %collective-permute-start.21 = (bf16[128,384]{1,0:T(8,128)(2,1)S(1)}, bf16[128,384]{1,0:T(8,128)(2,1)S(1)}, u32[]{:S(2)}, u32[]{:S(2)}) collective-permute-start(bf16[128,384]{1,0:T(8,128)(2,1)S(1)} %get-tuple-element.122), channel_id=1, source_target_pairs={{0,24},{8,0},{16,8},{24,16},{1,25},{9,1},{17,9},{25,17},{2,26},{10... | collective-permute-start | bytes 294920 | tf_op jit(solution)/shard_map/ppermute | solution.py:728
  71.3 3.3 %middle.1 = (bf16[1536,384]{1,0:T(8,128)(2,1)S(1)}, bf16[1536,384]{1,0:T(8,128)(2,1)S(1)}, f32[256,640]{1,0:T(8,128)S(1)}, bf16[256,1536]{1,0:T(8,128)(2,1)S(1)}) custom-call(s32[1,3]{1,0:T(1,128)S(1)} %add_bitcast_fusion.refs_0_, bf16[272,1536]{1,0:T(8,128)(2,1)S(1)} %get-tuple-element.115.refs_11_.refs_1_.refs_6_.refs_10_, ...), custom_call_target="tpu_custom_call" | custom-call | tf_op jit(solution)/shard_map/middle/pallas_call | solution.py:99
  76.5 2.4 %leave.1 = (bf16[272,512]{1,0:T(8,128)(2,1)S(1)}, f32[272,256]{1,0:T(8,128)S(1)}, f32[4,32,384]{2,1,0:T(8,128)S(1)}, f32[4,32,384]{2,1,0:T(8,128)S(1)}, f32[8,384]{1,0:T(8,128)S(1)}) custom-call(s32[1,3]{1,0:T(1,128)S(1)} %add_bitcast_fusion.refs_0_, bf16[128,384]{1,0:T(8,128)(2,1)S(1)} %collective-permute-done.21.refs_1_, ...), custom_call_target="tpu_custom_call" | custom-call | tf_op jit(solution)/shard_map/leave/pallas_call | solution.py:99
  78.9 3.4 %collective-permute-start.24 = (f32[4,32,384]{2,1,0:T(8,128)S(1)}, f32[4,32,384]{2,1,0:T(8,128)S(1)}, u32[]{:S(2)}, u32[]{:S(2)}) collective-permute-start(f32[4,32,384]{2,1,0:T(8,128)S(1)} %get-tuple-element.132), channel_id=1, source_target_pairs={{0,1},{1,0},{2,3},{3,2},{4,5},{5,4},{6,7},{7,6},{8,9},{9,8},{10,11... | collective-permute-start | bytes 589832 | tf_op jit(solution)/shard_map/ppermute | solution.py:736
  84.0 3.5 %collective-permute-start.26 = (f32[32,384]{1,0:T(8,128)S(1)}, f32[32,384]{1,0:T(8,128)S(1)}, u32[]{:S(2)}, u32[]{:S(2)}) collective-permute-start(f32[32,384]{1,0:T(8,128)S(1)} %get-tuple-element.135), channel_id=1, source_target_pairs={{0,4},{1,5},{2,6},{3,7},{4,0},{5,1},{6,2},{7,3},{8,12},{9,13},{10,... | collective-permute-start | bytes 147464 | tf_op jit(solution)/shard_map/ppermute | solution.py:732
  87.6 3.0 %value_grads.1 = (bf16[1536,384]{1,0:T(8,128)(2,1)S(1)}, f32[272,1536]{1,0:T(8,128)S(1)}) custom-call(s32[1,3]{1,0:T(1,128)S(1)} %add_bitcast_fusion.refs_0_, bf16[272,512]{1,0:T(8,128)(2,1)S(1)} %get-tuple-element.137.refs_1_.refs_5_, f32[272,256]{1,0:T(8,128)S(1)} %get-tuple-element.139.refs_2_, bf16[256,768]{1,0:T(8,128)(2,1)S(1)} %get-tuple-element.125.refs_2_.refs_3_, ...), custom_call_target="tpu_custom_call" | custom-call | tf_op jit(solution)/shard_map/value_grads/pallas_call | solution.py:99
  90.8 2.0 %late_grads.1 = (bf16[4,64,1536]{2,1,0:T(8,128)(2,1)S(1)}, bf16[4,64,1536]{2,1,0:T(8,128)(2,1)S(1)}, bf16[4,96,768]{2,1,0:T(8,128)(2,1)S(1)}, bf16[4,96,768]{2,1...) custom-call(s32[1,3]{1,0:T(1,128)S(1)} %add_bitcast_fusion.refs_0_, ...), custom_call_target="tpu_custom_call" | custom-call | tf_op jit(solution)/shard_map/late_grads/pallas_call | solution.py:99
  94.7 3.1 %collective-permute-start.29 = (bf16[2,96,768]{2,1,0:T(8,128)(2,1)S(1)}, bf16[2,96,768]{2,1,0:T(8,128)(2,1)S(1)}, u32[]{:S(2)}, u32[]{:S(2)}) collective-permute-start(bf16[2,96,768]{2,1,0:T(8,128)(2,1)S(1)} %get-tuple-element.150), channel_id=1, source_target_pairs={{0,96},{32,0},{64,32},{96,64},{1,97},{33,1},{65,33},{97,65},{2,98}... | collective-permute-start | bytes 884744 | tf_op jit(solution)/shard_map/ppermute | solution.py:728
  100.8 4.0 %collective-permute-done.30.refs_7_ = bf16[2,96,512]{2,1,0:T(8,128)(2,1)S(1)} collective-permute-done((bf16[2,96,512]{2,1,0:T(8,128)(2,1)S(1)}, bf16[2,96,512]{2,1,0:T(8,128)(2,1)S(1)}, u32[]{:S(2)}, u32[]{:S(2)}) %collective-permute-start.30) | collective-permute-done | bytes 196640 | tf_op jit(solution)/shard_map/ppermute | solution.py:728
  106.7 2.0 %collective-permute-start.34 = (bf16[4,96,768]{2,1,0:T(8,128)(2,1)S(1)}, bf16[4,96,768]{2,1,0:T(8,128)(2,1)S(1)}, u32[]{:S(2)}, u32[]{:S(2)}) collective-permute-start(bf16[4,96,768]{2,1,0:T(8,128)(2,1)S(1)} %get-tuple-element.159), channel_id=1, source_target_pairs={{0,96},{32,0},{64,32},{96,64},{1,97},{33,1},{65,33},{97,65},{2,98}... | collective-permute-start | bytes 1769480 | tf_op jit(solution)/shard_map/ppermute | solution.py:728
  108.7 2.7 %collective-permute-start.36 = (bf16[4,96,512]{2,1,0:T(8,128)(2,1)S(1)}, bf16[4,96,512]{2,1,0:T(8,128)(2,1)S(1)}, u32[]{:S(2)}, u32[]{:S(2)}) collective-permute-start(bf16[4,96,512]{2,1,0:T(8,128)(2,1)S(1)} %get-tuple-element.162), channel_id=1, source_target_pairs={{0,24},{8,0},{16,8},{24,16},{1,25},{9,1},{17,9},{25,17},{2,26},{10... | collective-permute-start | bytes 1179656 | tf_op jit(solution)/shard_map/ppermute | solution.py:728
  113.3 5.1 %collective-permute-done.35.refs_5_ = bf16[4,96,512]{2,1,0:T(8,128)(2,1)S(1)} collective-permute-done((bf16[4,96,512]{2,1,0:T(8,128)(2,1)S(1)}, bf16[4,96,512]{2,1,0:T(8,128)(2,1)S(1)}, u32[]{:S(2)}, u32[]{:S(2)}) %collective-permute-start.35) | collective-permute-done | bytes 393248 | tf_op jit(solution)/shard_map/ppermute | solution.py:728
  118.4 2.1 %collective-permute-done.33.refs_2_ = bf16[4,96,768]{2,1,0:T(8,128)(2,1)S(1)} collective-permute-done((bf16[4,96,768]{2,1,0:T(8,128)(2,1)S(1)}, bf16[4,96,768]{2,1,0:T(8,128)(2,1)S(1)}, u32[]{:S(2)}, u32[]{:S(2)}) %collective-permute-start.33) | collective-permute-done | bytes 589856 | tf_op jit(solution)/shard_map/ppermute | solution.py:728
  122.2 2.9 %collective-permute-start.39 = (bf16[96,512]{1,0:T(8,128)(2,1)S(1)}, bf16[96,512]{1,0:T(8,128)(2,1)S(1)}, u32[]{:S(2)}, u32[]{:S(2)}) collective-permute-start(bf16[96,512]{1,0:T(8,128)(2,1)S(1)} %get-tuple-element.167), channel_id=1, source_target_pairs={{0,64},{32,96},{64,0},{96,32},{1,65},{33,97},{65,1},{97,33},{2,66}... | collective-permute-start | bytes 294920 | tf_op jit(solution)/shard_map/ppermute | solution.py:728
  126.2 2.0 %collective-permute-done.39.refs_3_.refs_7_ = bf16[96,512]{1,0:T(8,128)(2,1)S(1)} collective-permute-done((bf16[96,512]{1,0:T(8,128)(2,1)S(1)}, bf16[96,512]{1,0:T(8,128)(2,1)S(1)}, u32[]{:S(2)}, u32[]{:S(2)}) %collective-permute-start.39) | collective-permute-done | bytes 98336 | tf_op jit(solution)/shard_map/ppermute | solution.py:728
  136.5 2.6 %collective-permute-done.50.refs_3_ = bf16[96,768]{1,0:T(8,128)(2,1)S(1)} collective-permute-done((bf16[96,768]{1,0:T(8,128)(2,1)S(1)}, bf16[96,768]{1,0:T(8,128)(2,1)S(1)}, u32[]{:S(2)}, u32[]{:S(2)}) %collective-permute-start.50) | collective-permute-done | bytes 147488 | tf_op jit(solution)/shard_map/ppermute | solution.py:728
  139.0 6.2 %collective-permute-start.45 = (bf16[80,1536]{1,0:T(8,128)(2,1)S(1)}, bf16[80,1536]{1,0:T(8,128)(2,1)S(1)}, u32[]{:S(2)}, u32[]{:S(2)}) collective-permute-start(bf16[80,1536]{1,0:T(8,128)(2,1)S(1)} %get-tuple-element.172.refs_1_), channel_id=1, source_target_pairs={{0,1},{1,0},{2,3},{3,2},{4,5},{5,4},{6,7},{7,6},{8,9},{9,8},{10,11... | collective-permute-start | bytes 737288 | tf_op jit(solution)/shard_map/ppermute | solution.py:736
  147.4 2.5 %finish.1 = (f32[256,1536]{1,0:T(8,128)}, bf16[256,1536]{1,0:T(8,128)(2,1)}, f32[96,256]{1,0:T(8,128)}, f32[1,96]{1,0:T(1,128)}, f32[4,256]{1,0:T(4,128)}, /*index=5*/f32[1,256]{1,0:T(1,128)}) custom-call(s32[1,3]{1,0:T(1,128)S(1)} %add_bitcast_fusion.refs_0_, bf16[80,1536]{1,0:T(8,128)(2,1)S(1)} %get-tuple-element.172.refs_1_, ...), custom_call_target="tpu_custom_call" | custom-call | tf_op jit(solution)/shard_map/finish/pallas_call | solution.py:99
  (120 shorter events, 50.1 us)
Async XLA Ops:
  2.6 10.6 %collective-permute-start.3 = (bf16[96,768]{1,0:T(8,128)(2,1)S(1)}, bf16[96,768]{1,0:T(8,128)(2,1)S(1)}, u32[]{:S(2)}, u32[]{:S(2)}) collective-permute-start(bf16[96,768]{1,0:T(8,128)(2,1)S(1)} %get-tuple-element.108.refs_5_), channel_id=1, source_target_pairs={{0,32},{32,64},{64,96},{96,0},{1,33},{33,65},{65,97},{97,1},{2,34}... | collective-permute-start | bytes 442376 | tf_op jit(solution)/shard_map/ppermute | solution.py:728
  5.1 13.5 %collective-permute-start = (bf16[112,768]{1,0:T(8,128)(2,1)S(1)}, bf16[112,768]{1,0:T(8,128)(2,1)S(1)}, u32[]{:S(2)}, u32[]{:S(2)}) collective-permute-start(bf16[112,768]{1,0:T(8,128)(2,1)S(1)} %get-tuple-element.107), channel_id=1, source_target_pairs={{0,8},{8,16},{16,24},{24,0},{1,9},{9,17},{17,25},{25,1},{2,10},{10... | collective-permute-start | bytes 516104 | tf_op jit(solution)/shard_map/ppermute | solution.py:728
  6.4 8.4 %collective-permute-start.4 = (bf16[96,768]{1,0:T(8,128)(2,1)S(1)}, bf16[96,768]{1,0:T(8,128)(2,1)S(1)}, u32[]{:S(2)}, u32[]{:S(2)}) collective-permute-start(bf16[96,768]{1,0:T(8,128)(2,1)S(1)} %get-tuple-element.108.refs_5_), channel_id=1, source_target_pairs={{0,64},{32,96},{64,0},{96,32},{1,65},{33,97},{65,1},{97,33},{2,66}... | collective-permute-start | bytes 442376 | tf_op jit(solution)/shard_map/ppermute | solution.py:728
  19.3 13.8 %collective-permute-start.10 = (bf16[4,96,768]{2,1,0:T(8,128)(2,1)S(1)}, bf16[4,96,768]{2,1,0:T(8,128)(2,1)S(1)}, u32[]{:S(2)}, u32[]{:S(2)}) collective-permute-start(bf16[4,96,768]{2,1,0:T(8,128)(2,1)S(1)} %get-tuple-element.110.refs_6_), channel_id=1, source_target_pairs={{0,8},{8,16},{16,24},{24,0},{1,9},{9,17},{17,25},{25,1},{2,10},{10... | collective-permute-start | bytes 1769480 | tf_op jit(solution)/shard_map/ppermute | solution.py:728
  20.4 12.7 %collective-permute-start.12 = (bf16[4,96,768]{2,1,0:T(8,128)(2,1)S(1)}, bf16[4,96,768]{2,1,0:T(8,128)(2,1)S(1)}, u32[]{:S(2)}, u32[]{:S(2)}) collective-permute-start(bf16[4,96,768]{2,1,0:T(8,128)(2,1)S(1)} %get-tuple-element.110.refs_6_), channel_id=1, source_target_pairs={{0,24},{8,0},{16,8},{24,16},{1,25},{9,1},{17,9},{25,17},{2,26},{10... | collective-permute-start | bytes 1769480 | tf_op jit(solution)/shard_map/ppermute | solution.py:728
  22.1 13.8 %collective-permute-start.6 = (bf16[4,96,768]{2,1,0:T(8,128)(2,1)S(1)}, bf16[4,96,768]{2,1,0:T(8,128)(2,1)S(1)}, u32[]{:S(2)}, u32[]{:S(2)}) collective-permute-start(bf16[4,96,768]{2,1,0:T(8,128)(2,1)S(1)} %get-tuple-element.109.refs_1_), channel_id=1, source_target_pairs={{0,32},{32,64},{64,96},{96,0},{1,33},{33,65},{65,97},{97,1},{2,34}... | collective-permute-start | bytes 1769480 | tf_op jit(solution)/shard_map/ppermute | solution.py:728
  22.9 13.9 %collective-permute-start.8 = (bf16[4,96,768]{2,1,0:T(8,128)(2,1)S(1)}, bf16[4,96,768]{2,1,0:T(8,128)(2,1)S(1)}, u32[]{:S(2)}, u32[]{:S(2)}) collective-permute-start(bf16[4,96,768]{2,1,0:T(8,128)(2,1)S(1)} %get-tuple-element.109.refs_1_), channel_id=1, source_target_pairs={{0,96},{32,0},{64,32},{96,64},{1,97},{33,1},{65,33},{97,65},{2,98}... | collective-permute-start | bytes 1769480 | tf_op jit(solution)/shard_map/ppermute | solution.py:728
  33.1 10.1 %collective-permute-start.11 = (bf16[2,96,768]{2,1,0:T(8,128)(2,1)S(1)}, bf16[2,96,768]{2,1,0:T(8,128)(2,1)S(1)}, u32[]{:S(2)}, u32[]{:S(2)}) collective-permute-start(bf16[2,96,768]{2,1,0:T(8,128)(2,1)S(1)} %slice.18), channel_id=1, source_target_pairs={{0,8},{8,16},{16,24},{24,0},{1,9},{9,17},{17,25},{25,1},{2,10},{10... | collective-permute-start | bytes 884744 | tf_op jit(solution)/shard_map/ppermute | solution.py:728
  33.2 10.0 %collective-permute-start.13 = (bf16[2,96,768]{2,1,0:T(8,128)(2,1)S(1)}, bf16[2,96,768]{2,1,0:T(8,128)(2,1)S(1)}, u32[]{:S(2)}, u32[]{:S(2)}) collective-permute-start(bf16[2,96,768]{2,1,0:T(8,128)(2,1)S(1)} %slice.19), channel_id=1, source_target_pairs={{0,24},{8,0},{16,8},{24,16},{1,25},{9,1},{17,9},{25,17},{2,26},{10... | collective-permute-start | bytes 884744 | tf_op jit(solution)/shard_map/ppermute | solution.py:728
  35.9 7.3 %collective-permute-start.7 = (bf16[2,96,768]{2,1,0:T(8,128)(2,1)S(1)}, bf16[2,96,768]{2,1,0:T(8,128)(2,1)S(1)}, u32[]{:S(2)}, u32[]{:S(2)}) collective-permute-start(bf16[2,96,768]{2,1,0:T(8,128)(2,1)S(1)} %slice.16), channel_id=1, source_target_pairs={{0,32},{32,64},{64,96},{96,0},{1,33},{33,65},{65,97},{97,1},{2,34}... | collective-permute-start | bytes 884744 | tf_op jit(solution)/shard_map/ppermute | solution.py:728
  36.8 6.4 %collective-permute-start.9 = (bf16[2,96,768]{2,1,0:T(8,128)(2,1)S(1)}, bf16[2,96,768]{2,1,0:T(8,128)(2,1)S(1)}, u32[]{:S(2)}, u32[]{:S(2)}) collective-permute-start(bf16[2,96,768]{2,1,0:T(8,128)(2,1)S(1)} %slice.17), channel_id=1, source_target_pairs={{0,96},{32,0},{64,32},{96,64},{1,97},{33,1},{65,33},{97,65},{2,98}... | collective-permute-start | bytes 884744 | tf_op jit(solution)/shard_map/ppermute | solution.py:728
  53.9 6.8 %collective-permute-start.17 = (f32[8,256]{1,0:T(8,128)S(1)}, f32[8,256]{1,0:T(8,128)S(1)}, u32[]{:S(2)}, u32[]{:S(2)}) collective-permute-start(f32[8,256]{1,0:T(8,128)S(1)} %get-tuple-element.120), channel_id=1, source_target_pairs={{0,1},{1,0},{2,3},{3,2},{4,5},{5,4},{6,7},{7,6},{8,9},{9,8},{10,11... | collective-permute-start | bytes 24584 | tf_op jit(solution)/shard_map/ppermute | solution.py:736
  68.4 6.2 %collective-permute-start.21 = (bf16[128,384]{1,0:T(8,128)(2,1)S(1)}, bf16[128,384]{1,0:T(8,128)(2,1)S(1)}, u32[]{:S(2)}, u32[]{:S(2)}) collective-permute-start(bf16[128,384]{1,0:T(8,128)(2,1)S(1)} %get-tuple-element.122), channel_id=1, source_target_pairs={{0,24},{8,0},{16,8},{24,16},{1,25},{9,1},{17,9},{25,17},{2,26},{10... | collective-permute-start | bytes 294920 | tf_op jit(solution)/shard_map/ppermute | solution.py:728
  84.0 6.6 %collective-permute-start.25 = (f32[32,384]{1,0:T(8,128)S(1)}, f32[32,384]{1,0:T(8,128)S(1)}, u32[]{:S(2)}, u32[]{:S(2)}) collective-permute-start(f32[32,384]{1,0:T(8,128)S(1)} %get-tuple-element.134), channel_id=1, source_target_pairs={{0,2},{1,3},{2,4},{3,5},{4,6},{5,7},{6,0},{7,1},{8,10},{9,11},{10,... | collective-permute-start | bytes 147464 | tf_op jit(solution)/shard_map/ppermute | solution.py:732
  84.0 6.6 %collective-permute-start.26 = (f32[32,384]{1,0:T(8,128)S(1)}, f32[32,384]{1,0:T(8,128)S(1)}, u32[]{:S(2)}, u32[]{:S(2)}) collective-permute-start(f32[32,384]{1,0:T(8,128)S(1)} %get-tuple-element.135), channel_id=1, source_target_pairs={{0,4},{1,5},{2,6},{3,7},{4,0},{5,1},{6,2},{7,3},{8,12},{9,13},{10,... | collective-permute-start | bytes 147464 | tf_op jit(solution)/shard_map/ppermute | solution.py:732
  92.8 6.4 %collective-permute-start.32 = (bf16[4,64,1536]{2,1,0:T(8,128)(2,1)S(1)}, bf16[4,64,1536]{2,1,0:T(8,128)(2,1)S(1)}, u32[]{:S(2)}, u32[]{:S(2)}) collective-permute-start(bf16[4,64,1536]{2,1,0:T(8,128)(2,1)S(1)} %get-tuple-element.156), channel_id=1, source_target_pairs={{0,1},{1,0},{2,3},{3,2},{4,5},{5,4},{6,7},{7,6},{8,9},{9,8},{10,11... | collective-permute-start | bytes 2359304 | tf_op jit(solution)/shard_map/ppermute | solution.py:736
  94.7 10.3 %collective-permute-start.28 = (bf16[2,96,768]{2,1,0:T(8,128)(2,1)S(1)}, bf16[2,96,768]{2,1,0:T(8,128)(2,1)S(1)}, u32[]{:S(2)}, u32[]{:S(2)}) collective-permute-start(bf16[2,96,768]{2,1,0:T(8,128)(2,1)S(1)} %get-tuple-element.149), channel_id=1, source_target_pairs={{0,32},{32,64},{64,96},{96,0},{1,33},{33,65},{65,97},{97,1},{2,34}... | collective-permute-start | bytes 884744 | tf_op jit(solution)/shard_map/ppermute | solution.py:728
  94.7 10.3 %collective-permute-start.29 = (bf16[2,96,768]{2,1,0:T(8,128)(2,1)S(1)}, bf16[2,96,768]{2,1,0:T(8,128)(2,1)S(1)}, u32[]{:S(2)}, u32[]{:S(2)}) collective-permute-start(bf16[2,96,768]{2,1,0:T(8,128)(2,1)S(1)} %get-tuple-element.150), channel_id=1, source_target_pairs={{0,96},{32,0},{64,32},{96,64},{1,97},{33,1},{65,33},{97,65},{2,98}... | collective-permute-start | bytes 884744 | tf_op jit(solution)/shard_map/ppermute | solution.py:728
  97.8 7.0 %collective-permute-start.31 = (bf16[2,112,512]{2,1,0:T(8,128)(2,1)S(1)}, bf16[2,112,512]{2,1,0:T(8,128)(2,1)S(1)}, u32[]{:S(2)}, u32[]{:S(2)}) collective-permute-start(bf16[2,112,512]{2,1,0:T(8,128)(2,1)S(1)} %get-tuple-element.154), channel_id=1, source_target_pairs={{0,24},{8,0},{16,8},{24,16},{1,25},{9,1},{17,9},{25,17},{2,26},{10... | collective-permute-start | bytes 688136 | tf_op jit(solution)/shard_map/ppermute | solution.py:728
  98.1 6.7 %collective-permute-start.30 = (bf16[2,96,512]{2,1,0:T(8,128)(2,1)S(1)}, bf16[2,96,512]{2,1,0:T(8,128)(2,1)S(1)}, u32[]{:S(2)}, u32[]{:S(2)}) collective-permute-start(bf16[2,96,512]{2,1,0:T(8,128)(2,1)S(1)} %get-tuple-element.153), channel_id=1, source_target_pairs={{0,8},{8,16},{16,24},{24,0},{1,9},{9,17},{17,25},{25,1},{2,10},{10... | collective-permute-start | bytes 589832 | tf_op jit(solution)/shard_map/ppermute | solution.py:728
  100.0 11.4 %collective-permute-start.37 = (bf16[2,64,1536]{2,1,0:T(8,128)(2,1)S(1)}, bf16[2,64,1536]{2,1,0:T(8,128)(2,1)S(1)}, u32[]{:S(2)}, u32[]{:S(2)}) collective-permute-start(bf16[2,64,1536]{2,1,0:T(8,128)(2,1)S(1)} %get-tuple-element.163), channel_id=1, source_target_pairs={{0,2},{1,3},{2,0},{3,1},{4,6},{5,7},{6,4},{7,5},{8,10},{9,11},{10,... | collective-permute-start | bytes 1179656 | tf_op jit(solution)/shard_map/ppermute | solution.py:736
  105.9 14.6 %collective-permute-start.33 = (bf16[4,96,768]{2,1,0:T(8,128)(2,1)S(1)}, bf16[4,96,768]{2,1,0:T(8,128)(2,1)S(1)}, u32[]{:S(2)}, u32[]{:S(2)}) collective-permute-start(bf16[4,96,768]{2,1,0:T(8,128)(2,1)S(1)} %get-tuple-element.158), channel_id=1, source_target_pairs={{0,32},{32,64},{64,96},{96,0},{1,33},{33,65},{65,97},{97,1},{2,34}... | collective-permute-start | bytes 1769480 | tf_op jit(solution)/shard_map/ppermute | solution.py:728
  106.7 13.8 %collective-permute-start.34 = (bf16[4,96,768]{2,1,0:T(8,128)(2,1)S(1)}, bf16[4,96,768]{2,1,0:T(8,128)(2,1)S(1)}, u32[]{:S(2)}, u32[]{:S(2)}) collective-permute-start(bf16[4,96,768]{2,1,0:T(8,128)(2,1)S(1)} %get-tuple-element.159), channel_id=1, source_target_pairs={{0,96},{32,0},{64,32},{96,64},{1,97},{33,1},{65,33},{97,65},{2,98}... | collective-permute-start | bytes 1769480 | tf_op jit(solution)/shard_map/ppermute | solution.py:728
  108.7 9.7 %collective-permute-start.35 = (bf16[4,96,512]{2,1,0:T(8,128)(2,1)S(1)}, bf16[4,96,512]{2,1,0:T(8,128)(2,1)S(1)}, u32[]{:S(2)}, u32[]{:S(2)}) collective-permute-start(bf16[4,96,512]{2,1,0:T(8,128)(2,1)S(1)} %get-tuple-element.161), channel_id=1, source_target_pairs={{0,8},{8,16},{16,24},{24,0},{1,9},{9,17},{17,25},{25,1},{2,10},{10... | collective-permute-start | bytes 1179656 | tf_op jit(solution)/shard_map/ppermute | solution.py:728
  108.7 9.7 %collective-permute-start.36 = (bf16[4,96,512]{2,1,0:T(8,128)(2,1)S(1)}, bf16[4,96,512]{2,1,0:T(8,128)(2,1)S(1)}, u32[]{:S(2)}, u32[]{:S(2)}) collective-permute-start(bf16[4,96,512]{2,1,0:T(8,128)(2,1)S(1)} %get-tuple-element.162), channel_id=1, source_target_pairs={{0,24},{8,0},{16,8},{24,16},{1,25},{9,1},{17,9},{25,17},{2,26},{10... | collective-permute-start | bytes 1179656 | tf_op jit(solution)/shard_map/ppermute | solution.py:728
  112.0 13.7 %collective-permute-start.41 = (bf16[64,1536]{1,0:T(8,128)(2,1)S(1)}, bf16[64,1536]{1,0:T(8,128)(2,1)S(1)}, u32[]{:S(2)}, u32[]{:S(2)}) collective-permute-start(bf16[64,1536]{1,0:T(8,128)(2,1)S(1)} %get-tuple-element.169), channel_id=1, source_target_pairs={{0,4},{1,5},{2,6},{3,7},{4,0},{5,1},{6,2},{7,3},{8,12},{9,13},{10,... | collective-permute-start | bytes 589832 | tf_op jit(solution)/shard_map/ppermute | solution.py:736
  125.7 9.0 %collective-permute-start.49 = (bf16[96,768]{1,0:T(8,128)(2,1)S(1)}, bf16[96,768]{1,0:T(8,128)(2,1)S(1)}, u32[]{:S(2)}, u32[]{:S(2)}) collective-permute-start(bf16[96,768]{1,0:T(8,128)(2,1)S(1)} %get-tuple-element.180), channel_id=1, source_target_pairs={{0,8},{8,16},{16,24},{24,0},{1,9},{9,17},{17,25},{25,1},{2,10},{10... | collective-permute-start | bytes 442376 | tf_op jit(solution)/shard_map/ppermute | solution.py:728
  130.2 15.0 %collective-permute-start.42 = (bf16[80,1536]{1,0:T(8,128)(2,1)S(1)}, bf16[80,1536]{1,0:T(8,128)(2,1)S(1)}, u32[]{:S(2)}, u32[]{:S(2)}) collective-permute-start(bf16[80,1536]{1,0:T(8,128)(2,1)S(1)} %get-tuple-element.172.refs_1_), channel_id=1, source_target_pairs={{0,2},{1,3},{2,4},{3,5},{4,6},{5,7},{6,0},{7,1},{8,10},{9,11},{10,... | collective-permute-start | bytes 737288 | tf_op jit(solution)/shard_map/ppermute | solution.py:732
  131.0 14.3 %collective-permute-start.43 = (bf16[80,1536]{1,0:T(8,128)(2,1)S(1)}, bf16[80,1536]{1,0:T(8,128)(2,1)S(1)}, u32[]{:S(2)}, u32[]{:S(2)}) collective-permute-start(bf16[80,1536]{1,0:T(8,128)(2,1)S(1)} %get-tuple-element.172.refs_1_), channel_id=1, source_target_pairs={{0,4},{1,5},{2,6},{3,7},{4,0},{5,1},{6,2},{7,3},{8,12},{9,13},{10,... | collective-permute-start | bytes 737288 | tf_op jit(solution)/shard_map/ppermute | solution.py:732
  132.4 13.3 %collective-permute-start.44 = (bf16[80,1536]{1,0:T(8,128)(2,1)S(1)}, bf16[80,1536]{1,0:T(8,128)(2,1)S(1)}, u32[]{:S(2)}, u32[]{:S(2)}) collective-permute-start(bf16[80,1536]{1,0:T(8,128)(2,1)S(1)} %get-tuple-element.172.refs_1_), channel_id=1, source_target_pairs={{0,6},{1,7},{2,0},{3,1},{4,2},{5,3},{6,4},{7,5},{8,14},{9,15},{10,... | collective-permute-start | bytes 737288 | tf_op jit(solution)/shard_map/ppermute | solution.py:732
  134.7 11.1 %collective-permute-start.51 = (bf16[96,768]{1,0:T(8,128)(2,1)S(1)}, bf16[96,768]{1,0:T(8,128)(2,1)S(1)}, u32[]{:S(2)}, u32[]{:S(2)}) collective-permute-start(bf16[96,768]{1,0:T(8,128)(2,1)S(1)} %get-tuple-element.182), channel_id=1, source_target_pairs={{0,24},{8,0},{16,8},{24,16},{1,25},{9,1},{17,9},{25,17},{2,26},{10... | collective-permute-start | bytes 442376 | tf_op jit(solution)/shard_map/ppermute | solution.py:728
  139.0 8.1 %collective-permute-start.45 = (bf16[80,1536]{1,0:T(8,128)(2,1)S(1)}, bf16[80,1536]{1,0:T(8,128)(2,1)S(1)}, u32[]{:S(2)}, u32[]{:S(2)}) collective-permute-start(bf16[80,1536]{1,0:T(8,128)(2,1)S(1)} %get-tuple-element.172.refs_1_), channel_id=1, source_target_pairs={{0,1},{1,0},{2,3},{3,2},{4,5},{5,4},{6,7},{7,6},{8,9},{9,8},{10,11... | collective-permute-start | bytes 737288 | tf_op jit(solution)/shard_map/ppermute | solution.py:736
  (28 other events, 278.8 us)

commit v6 on v5

--- a/solution.py
+++ b/solution.py
@@ -374,7 +374,8 @@
 
 
 def middle(
-    ids, hidden_in, gated_low, cotangent, gate_out, wide, narrow, grad_mixed, gate, out, grads, branch
+    ids, hidden_in, gated_low, cotangent, gate_out, wide, narrow, grad_mixed, state, spread, after,
+    gate, out, grads, branch, sums,
 ):
     gate[...] = dot_first(hidden_in[RIM:], gated_low[:, LOW_GATE]).astype(BF16)
     out[...] = dot_first(cotangent[...], gated_low[:, NORMED]).astype(BF16)
@@ -396,11 +397,19 @@
             grad_scores = grad_scores + twice(own, part, 1, 1) * weights
         grads[:, pair_columns(pair)] = jnp.where(lower, got[0], got[1])
     grads[:, WIDE : WIDE + STATE] = twice(grad_scores, cmat, 0, 0)
-    grads[:, WIDE + STATE :] = twice(grad_scores, bmat, 1, 0)
+    own = grad_mixed[...]
+    from_state = own * spread[:, GROWN]
+    grads[:, WIDE + STATE :] = twice(grad_scores, bmat, 1, 0) + sum(
+        dot_last(from_state, part) for part in split(state[:STATE], 2)
+    )
+    inputs = grads[:, :WIDE]
+    own = own.astype(BF16).astype(F32) * after[:, INSIDE] - weighted.astype(F32) * inputs
+    sums[:, :128] = head_sums(own)
+    sums[:, 128:] = head_sums(wide[:, VALUES] * inputs)
 
 
 def leave(
-    ids, g1, g2, g3, state, after, grad_mixed, grads, wide, spread, slope, narrow, consts, taken, grad_gain,
+    ids, g1, g2, g3, state, inner, grad_mixed, grads, wide, spread, slope, narrow, consts, taken, grad_gain,
     low, state_low, keep, send, small, turned,
 ):
     me = ids[0, 1]
@@ -422,17 +431,15 @@
     from_b = grads[:, WIDE : WIDE + STATE]
     from_b = from_b + sum(dot_last(weighted * to_end, part) for part in split(end, 2))
     from_c = grads[:, WIDE + STATE :]
-    from_c = from_c + sum(
-        dot_last(own * spread[:, GROWN], part) for part in split(state[:STATE], 2)
-    )
-    grad_log = head_sums(own.astype(BF16).astype(F32) * after[:, INSIDE] - weighted * inputs)
-    at_end = jnp.sum(weighted * from_end, axis=0, keepdims=True) + jnp.exp(
-        spread_heads(last)
-    ) * jnp.sum(end * state[:STATE], axis=0, keepdims=True)
+    sums = head_sums(values * from_end)
+    ended = step * sums
+    at_end = jnp.exp(spread_heads(last)) * jnp.sum(end * state[:STATE], axis=0, keepdims=True)
     at_end = head_sums(jnp.broadcast_to(at_end, (8, WIDE)))[0:1]
+    at_end = at_end + jnp.sum(ended, axis=0, keepdims=True)
+    grad_log = inner[:, :128] - ended
     grad_decay = pick(flag(iota((T, T), 0) <= iota((T, T), 1)), grad_log, 1, 0) + at_end
     rate = jnp.exp(consts[7:8, :128])
-    grad_step = head_sums(values * inputs) - rate * grad_decay
+    grad_step = inner[:, 128:] + sums - rate * grad_decay
     grad_step_pre = grad_step * step_slope
     grad_values = own * spread_heads(consts[8:9, :128]) + inputs * spread[:, STEPS]
     grad_pre = jnp.concatenate([grad_values, from_b, from_c], axis=1) * slope[...]
@@ -872,9 +879,9 @@
     )
     later = [shift(sensitivity, "ctx", -steps) for steps in range(1, 4)]
     square = ((D, WIDE), BF16)
-    gate, out, grads, branch = fuse(
+    gate, out, grads, branch, inner = fuse(
         middle,
-        [square, square, ((T, MIX), F32), ((T, D), BF16)],
+        [square, square, ((T, MIX), F32), ((T, D), BF16), ((T, 256), F32)],
         ids,
         hidden_in,
         gated_low,
@@ -883,6 +890,9 @@
         wide,
         narrow,
         grad_mixed,
+        state,
+        spread,
+        after,
     )
     low, state_low, keep, send, small = fuse(
         leave,
@@ -890,7 +900,7 @@
         ids,
         *later,
         state,
-        after,
+        inner,
         grad_mixed,
         grads,
         wide,

time: 150 us -> 150 us (level)
  no operation moved by 1% of the time
where the time goes in v6:
time: 150 us
  starting transfers between devices  76.4 us (51%)
  waiting for transfers between devices  35.9 us (24%)
  Pallas kernels  32.6 us (22%)
  other arithmetic  1.86 us (1%)
  local copies, waits for them, and re-layouts  1.81 us (1%)
    ppermute x34, starting transfers between devices, shift(): return lax.ppermute(array, axis, [(i, (i + steps) % 4) for i in range(4)])  44.5 us
    pallas_call x20, Pallas kernels, fuse(): return list(call(ids, *arrays))  32.6 us
    ppermute x34, waiting for transfers between devices, shift(): return lax.ppermute(array, axis, [(i, (i + steps) % 4) for i in range(4)])  32.6 us
    ppermute x9, starting transfers between devices, across(): return lax.ppermute(array, 'tp', [(i, i ^ bits) for i in range(8)])  20.1 us
    ppermute x9, starting transfers between devices, from_chip(): lax.ppermute(array, 'tp', [(i, (i + 2 * steps) % 8) for i in range(8)])  11.7 us
  transfers between devices with their start and end apart: 52, of which 22 were waited for; matrix products, arithmetic and copies ran while one was open for 2% of the time, Pallas kernels for 12%

profile of v6, /device:TPU:1, one launch (start us, length us, event | category | flops | bytes accessed | tf_op | source)
XLA Modules:
  0.0 149.5 jit_solution(17347292175435488510)
XLA Ops:
  2.6 2.5 %collective-permute-start.3 = (bf16[96,768]{1,0:T(8,128)(2,1)S(1)}, bf16[96,768]{1,0:T(8,128)(2,1)S(1)}, u32[]{:S(2)}, u32[]{:S(2)}) collective-permute-start(bf16[96,768]{1,0:T(8,128)(2,1)S(1)} %get-tuple-element.109.refs_5_), channel_id=1, source_target_pairs={{0,32},{32,64},{64,96},{96,0},{1,33},{33,65},{65,97},{97,1},{2,34}... | collective-permute-start | bytes 442376 | tf_op jit(solution)/shard_map/ppermute | solution.py:735
  6.4 3.3 %collective-permute-start.4 = (bf16[96,768]{1,0:T(8,128)(2,1)S(1)}, bf16[96,768]{1,0:T(8,128)(2,1)S(1)}, u32[]{:S(2)}, u32[]{:S(2)}) collective-permute-start(bf16[96,768]{1,0:T(8,128)(2,1)S(1)} %get-tuple-element.109.refs_5_), channel_id=1, source_target_pairs={{0,64},{32,96},{64,0},{96,32},{1,65},{33,97},{65,1},{97,33},{2,66}... | collective-permute-start | bytes 442376 | tf_op jit(solution)/shard_map/ppermute | solution.py:735
  10.5 2.7 %collective-permute-start.1 = (bf16[96,768]{1,0:T(8,128)(2,1)S(1)}, bf16[96,768]{1,0:T(8,128)(2,1)S(1)}, u32[]{:S(2)}, u32[]{:S(2)}) collective-permute-start(bf16[96,768]{1,0:T(8,128)(2,1)S(1)} %get-tuple-element.107.refs_1_), channel_id=1, source_target_pairs={{0,16},{8,24},{16,0},{24,8},{1,17},{9,25},{17,1},{25,9},{2,18},{10... | collective-permute-start | bytes 442376 | tf_op jit(solution)/shard_map/ppermute | solution.py:735
  16.1 2.6 %collective-permute-done.2.refs_4_ = bf16[96,768]{1,0:T(8,128)(2,1)S(1)} collective-permute-done((bf16[96,768]{1,0:T(8,128)(2,1)S(1)}, bf16[96,768]{1,0:T(8,128)(2,1)S(1)}, u32[]{:S(2)}, u32[]{:S(2)}) %collective-permute-start.2) | collective-permute-done | bytes 147488 | tf_op jit(solution)/shard_map/ppermute | solution.py:735
  22.9 1.9 %collective-permute-start.8 = (bf16[4,96,768]{2,1,0:T(8,128)(2,1)S(1)}, bf16[4,96,768]{2,1,0:T(8,128)(2,1)S(1)}, u32[]{:S(2)}, u32[]{:S(2)}) collective-permute-start(bf16[4,96,768]{2,1,0:T(8,128)(2,1)S(1)} %get-tuple-element.110.refs_1_), channel_id=1, source_target_pairs={{0,96},{32,0},{64,32},{96,64},{1,97},{33,1},{65,33},{97,65},{2,98}... | collective-permute-start | bytes 1769480 | tf_op jit(solution)/shard_map/ppermute | solution.py:735
  24.8 8.2 %collective-permute-done.10.refs_7_ = bf16[4,96,768]{2,1,0:T(8,128)(2,1)S(1)} collective-permute-done((bf16[4,96,768]{2,1,0:T(8,128)(2,1)S(1)}, bf16[4,96,768]{2,1,0:T(8,128)(2,1)S(1)}, u32[]{:S(2)}, u32[]{:S(2)}) %collective-permute-start.10) | collective-permute-done | bytes 589856 | tf_op jit(solution)/shard_map/ppermute | solution.py:735
  33.2 2.7 %collective-permute-start.13 = (bf16[2,96,768]{2,1,0:T(8,128)(2,1)S(1)}, bf16[2,96,768]{2,1,0:T(8,128)(2,1)S(1)}, u32[]{:S(2)}, u32[]{:S(2)}) collective-permute-start(bf16[2,96,768]{2,1,0:T(8,128)(2,1)S(1)} %slice.19), channel_id=1, source_target_pairs={{0,24},{8,0},{16,8},{24,16},{1,25},{9,1},{17,9},{25,17},{2,26},{10... | collective-permute-start | bytes 884744 | tf_op jit(solution)/shard_map/ppermute | solution.py:735
  36.8 2.0 %collective-permute-start.9 = (bf16[2,96,768]{2,1,0:T(8,128)(2,1)S(1)}, bf16[2,96,768]{2,1,0:T(8,128)(2,1)S(1)}, u32[]{:S(2)}, u32[]{:S(2)}) collective-permute-start(bf16[2,96,768]{2,1,0:T(8,128)(2,1)S(1)} %slice.17), channel_id=1, source_target_pairs={{0,96},{32,0},{64,32},{96,64},{1,97},{33,1},{65,33},{97,65},{2,98}... | collective-permute-start | bytes 884744 | tf_op jit(solution)/shard_map/ppermute | solution.py:735
  41.1 2.1 %tabulate.1 = (f32[16,768]{1,0:T(8,128)S(1)}, f32[256,1536]{1,0:T(8,128)S(1)}) custom-call(s32[1,3]{1,0:T(1,128)S(1)} %add_bitcast_fusion.refs_0_, bf16[4,384]{1,0:T(4,128)(2,1)} %refs_1_.3, bf16[4,256]{1,0:T(4,128)(2,1)} %refs_2_.3, bf16[1,384]{1,0:T(2,128)(2,1)} %broadcast_in_dim.19.refs_3_, bf16[1,256]{1,0:T(2,128)(2,1)} %broadcast_in_dim.20.refs_4_, ...), custom_call_target="tpu_custom_call" | custom-call | tf_op jit(solution)/shard_map/tabulate/pallas_call | solution.py:99
  43.2 2.9 %enter.1 = (bf16[1536,768]{1,0:T(8,128)(2,1)S(1)}, bf16[272,1536]{1,0:T(8,128)(2,1)S(1)}, bf16[272,640]{1,0:T(8,128)(2,1)S(1)}, f32[256,1408]{1,0:T(8,128)S(1)},...) custom-call(s32[1,3]{1,0:T(1,128)S(1)} %add_bitcast_fusion.refs_0_, ...), custom_call_target="tpu_custom_call" | custom-call | tf_op jit(solution)/shard_map/enter/pallas_call | solution.py:99
  46.2 2.3 %collective-permute-start.15 = (bf16[144,384]{1,0:T(8,128)(2,1)S(1)}, bf16[144,384]{1,0:T(8,128)(2,1)S(1)}, u32[]{:S(2)}, u32[]{:S(2)}) collective-permute-start(bf16[144,384]{1,0:T(8,128)(2,1)S(1)} %get-tuple-element.115), channel_id=1, source_target_pairs={{0,16},{8,24},{16,0},{24,8},{1,17},{9,25},{17,1},{25,9},{2,18},{10... | collective-permute-start | bytes 331784 | tf_op jit(solution)/shard_map/ppermute | solution.py:735
  48.9 2.4 %project.1 = (bf16[1536,768]{1,0:T(8,128)(2,1)S(1)}, f32[256,2304]{1,0:T(8,128)S(1)}, f32[256,640]{1,0:T(8,128)S(1)}, f32[256,1152]{1,0:T(8,128)S(1)}) custom-call(s32[1,3]{1,0:T(1,128)S(1)} %add_bitcast_fusion.refs_0_, bf16[4,96,768]{2,1,0:T(8,128)(2,1)S(1)} %get-tuple-element.110.refs_1_, bf16[4,96,768]{2,1,0:T(8,128)(2,1)S(1)} %collective-permute-done.6.refs_2_, ...), custom_call_target="tpu_custom_call" | custom-call | tf_op jit(solution)/shard_map/project/pallas_call | solution.py:99
  53.9 6.0 %collective-permute-start.17 = (f32[8,256]{1,0:T(8,128)S(1)}, f32[8,256]{1,0:T(8,128)S(1)}, u32[]{:S(2)}, u32[]{:S(2)}) collective-permute-start(f32[8,256]{1,0:T(8,128)S(1)} %get-tuple-element.121), channel_id=1, source_target_pairs={{0,1},{1,0},{2,3},{3,2},{4,5},{5,4},{6,7},{7,6},{8,9},{9,8},{10,11... | collective-permute-start | bytes 24584 | tf_op jit(solution)/shard_map/ppermute | solution.py:743
  61.9 2.4 %collective-permute-start.19 = (f32[8,256]{1,0:T(8,128)S(1)}, f32[8,256]{1,0:T(8,128)S(1)}, u32[]{:S(2)}, u32[]{:S(2)}) collective-permute-start(f32[8,256]{1,0:T(8,128)S(1)} %add.3.refs_1_), channel_id=1, source_target_pairs={{0,4},{1,5},{2,6},{3,7},{4,0},{5,1},{6,2},{7,3},{8,12},{9,13},{10,... | collective-permute-start | bytes 24584 | tf_op jit(solution)/shard_map/ppermute | solution.py:739
  68.4 2.2 %collective-permute-start.21 = (bf16[128,384]{1,0:T(8,128)(2,1)S(1)}, bf16[128,384]{1,0:T(8,128)(2,1)S(1)}, u32[]{:S(2)}, u32[]{:S(2)}) collective-permute-start(bf16[128,384]{1,0:T(8,128)(2,1)S(1)} %get-tuple-element.123), channel_id=1, source_target_pairs={{0,24},{8,0},{16,8},{24,16},{1,25},{9,1},{17,9},{25,17},{2,26},{10... | collective-permute-start | bytes 294920 | tf_op jit(solution)/shard_map/ppermute | solution.py:735
  71.3 3.6 %middle.1 = (bf16[1536,384]{1,0:T(8,128)(2,1)S(1)}, bf16[1536,384]{1,0:T(8,128)(2,1)S(1)}, f32[256,640]{1,0:T(8,128)S(1)}, bf16[256,1536]{1,0:T(8,128)(2,1)S(1)}, f32[256,256]{1,0:T(8,128)S(1)}) custom-call(s32[1,3]{1,0:T(1,128)S(1)} %add_bitcast_fusion.refs_0_, bf16[272,1536]{1,0:T(8,128)(2,1)S(1)} %get-tuple-element.116.refs_11_.refs_1_.refs_6_.refs_10_, ...), custom_call_target="tpu_custom_call" | custom-call | tf_op jit(solution)/shard_map/middle/pallas_call | solution.py:99
  76.5 2.0 %leave.1 = (bf16[272,512]{1,0:T(8,128)(2,1)S(1)}, f32[272,256]{1,0:T(8,128)S(1)}, f32[4,32,384]{2,1,0:T(8,128)S(1)}, f32[4,32,384]{2,1,0:T(8,128)S(1)}, f32[8,384]{1,0:T(8,128)S(1)}) custom-call(s32[1,3]{1,0:T(1,128)S(1)} %add_bitcast_fusion.refs_0_, bf16[128,384]{1,0:T(8,128)(2,1)S(1)} %collective-permute-done.21.refs_1_, ...), custom_call_target="tpu_custom_call" | custom-call | tf_op jit(solution)/shard_map/leave/pallas_call | solution.py:99
  78.5 3.4 %collective-permute-start.24 = (f32[4,32,384]{2,1,0:T(8,128)S(1)}, f32[4,32,384]{2,1,0:T(8,128)S(1)}, u32[]{:S(2)}, u32[]{:S(2)}) collective-permute-start(f32[4,32,384]{2,1,0:T(8,128)S(1)} %get-tuple-element.134), channel_id=1, source_target_pairs={{0,1},{1,0},{2,3},{3,2},{4,5},{5,4},{6,7},{7,6},{8,9},{9,8},{10,11... | collective-permute-start | bytes 589832 | tf_op jit(solution)/shard_map/ppermute | solution.py:743
  83.6 3.5 %collective-permute-start.26 = (f32[32,384]{1,0:T(8,128)S(1)}, f32[32,384]{1,0:T(8,128)S(1)}, u32[]{:S(2)}, u32[]{:S(2)}) collective-permute-start(f32[32,384]{1,0:T(8,128)S(1)} %get-tuple-element.137), channel_id=1, source_target_pairs={{0,4},{1,5},{2,6},{3,7},{4,0},{5,1},{6,2},{7,3},{8,12},{9,13},{10,... | collective-permute-start | bytes 147464 | tf_op jit(solution)/shard_map/ppermute | solution.py:739
  87.2 3.0 %value_grads.1 = (bf16[1536,384]{1,0:T(8,128)(2,1)S(1)}, f32[272,1536]{1,0:T(8,128)S(1)}) custom-call(s32[1,3]{1,0:T(1,128)S(1)} %add_bitcast_fusion.refs_0_, bf16[272,512]{1,0:T(8,128)(2,1)S(1)} %get-tuple-element.139.refs_1_.refs_5_, f32[272,256]{1,0:T(8,128)S(1)} %get-tuple-element.141.refs_2_, bf16[256,768]{1,0:T(8,128)(2,1)S(1)} %get-tuple-element.125.refs_2_.refs_3_, ...), custom_call_target="tpu_custom_call" | custom-call | tf_op jit(solution)/shard_map/value_grads/pallas_call | solution.py:99
  90.4 2.0 %late_grads.1 = (bf16[4,64,1536]{2,1,0:T(8,128)(2,1)S(1)}, bf16[4,64,1536]{2,1,0:T(8,128)(2,1)S(1)}, bf16[4,96,768]{2,1,0:T(8,128)(2,1)S(1)}, bf16[4,96,768]{2,1...) custom-call(s32[1,3]{1,0:T(1,128)S(1)} %add_bitcast_fusion.refs_0_, ...), custom_call_target="tpu_custom_call" | custom-call | tf_op jit(solution)/shard_map/late_grads/pallas_call | solution.py:99
  94.3 3.0 %collective-permute-start.29 = (bf16[2,96,768]{2,1,0:T(8,128)(2,1)S(1)}, bf16[2,96,768]{2,1,0:T(8,128)(2,1)S(1)}, u32[]{:S(2)}, u32[]{:S(2)}) collective-permute-start(bf16[2,96,768]{2,1,0:T(8,128)(2,1)S(1)} %get-tuple-element.152), channel_id=1, source_target_pairs={{0,96},{32,0},{64,32},{96,64},{1,97},{33,1},{65,33},{97,65},{2,98}... | collective-permute-start | bytes 884744 | tf_op jit(solution)/shard_map/ppermute | solution.py:735
  100.4 4.0 %collective-permute-done.30.refs_7_ = bf16[2,96,512]{2,1,0:T(8,128)(2,1)S(1)} collective-permute-done((bf16[2,96,512]{2,1,0:T(8,128)(2,1)S(1)}, bf16[2,96,512]{2,1,0:T(8,128)(2,1)S(1)}, u32[]{:S(2)}, u32[]{:S(2)}) %collective-permute-start.30) | collective-permute-done | bytes 196640 | tf_op jit(solution)/shard_map/ppermute | solution.py:735
  106.3 2.0 %collective-permute-start.34 = (bf16[4,96,768]{2,1,0:T(8,128)(2,1)S(1)}, bf16[4,96,768]{2,1,0:T(8,128)(2,1)S(1)}, u32[]{:S(2)}, u32[]{:S(2)}) collective-permute-start(bf16[4,96,768]{2,1,0:T(8,128)(2,1)S(1)} %get-tuple-element.161), channel_id=1, source_target_pairs={{0,96},{32,0},{64,32},{96,64},{1,97},{33,1},{65,33},{97,65},{2,98}... | collective-permute-start | bytes 1769480 | tf_op jit(solution)/shard_map/ppermute | solution.py:735
  108.3 2.7 %collective-permute-start.36 = (bf16[4,96,512]{2,1,0:T(8,128)(2,1)S(1)}, bf16[4,96,512]{2,1,0:T(8,128)(2,1)S(1)}, u32[]{:S(2)}, u32[]{:S(2)}) collective-permute-start(bf16[4,96,512]{2,1,0:T(8,128)(2,1)S(1)} %get-tuple-element.164), channel_id=1, source_target_pairs={{0,24},{8,0},{16,8},{24,16},{1,25},{9,1},{17,9},{25,17},{2,26},{10... | collective-permute-start | bytes 1179656 | tf_op jit(solution)/shard_map/ppermute | solution.py:735
  112.9 5.0 %collective-permute-done.35.refs_5_ = bf16[4,96,512]{2,1,0:T(8,128)(2,1)S(1)} collective-permute-done((bf16[4,96,512]{2,1,0:T(8,128)(2,1)S(1)}, bf16[4,96,512]{2,1,0:T(8,128)(2,1)S(1)}, u32[]{:S(2)}, u32[]{:S(2)}) %collective-permute-start.35) | collective-permute-done | bytes 393248 | tf_op jit(solution)/shard_map/ppermute | solution.py:735
  118.0 2.1 %collective-permute-done.33.refs_2_ = bf16[4,96,768]{2,1,0:T(8,128)(2,1)S(1)} collective-permute-done((bf16[4,96,768]{2,1,0:T(8,128)(2,1)S(1)}, bf16[4,96,768]{2,1,0:T(8,128)(2,1)S(1)}, u32[]{:S(2)}, u32[]{:S(2)}) %collective-permute-start.33) | collective-permute-done | bytes 589856 | tf_op jit(solution)/shard_map/ppermute | solution.py:735
  121.8 2.9 %collective-permute-start.39 = (bf16[96,512]{1,0:T(8,128)(2,1)S(1)}, bf16[96,512]{1,0:T(8,128)(2,1)S(1)}, u32[]{:S(2)}, u32[]{:S(2)}) collective-permute-start(bf16[96,512]{1,0:T(8,128)(2,1)S(1)} %get-tuple-element.169), channel_id=1, source_target_pairs={{0,64},{32,96},{64,0},{96,32},{1,65},{33,97},{65,1},{97,33},{2,66}... | collective-permute-start | bytes 294920 | tf_op jit(solution)/shard_map/ppermute | solution.py:735
  125.8 2.0 %collective-permute-done.39.refs_3_.refs_7_ = bf16[96,512]{1,0:T(8,128)(2,1)S(1)} collective-permute-done((bf16[96,512]{1,0:T(8,128)(2,1)S(1)}, bf16[96,512]{1,0:T(8,128)(2,1)S(1)}, u32[]{:S(2)}, u32[]{:S(2)}) %collective-permute-start.39) | collective-permute-done | bytes 98336 | tf_op jit(solution)/shard_map/ppermute | solution.py:735
  136.3 2.4 %collective-permute-done.50.refs_3_ = bf16[96,768]{1,0:T(8,128)(2,1)S(1)} collective-permute-done((bf16[96,768]{1,0:T(8,128)(2,1)S(1)}, bf16[96,768]{1,0:T(8,128)(2,1)S(1)}, u32[]{:S(2)}, u32[]{:S(2)}) %collective-permute-start.50) | collective-permute-done | bytes 147488 | tf_op jit(solution)/shard_map/ppermute | solution.py:735
  138.7 6.2 %collective-permute-start.45 = (bf16[80,1536]{1,0:T(8,128)(2,1)S(1)}, bf16[80,1536]{1,0:T(8,128)(2,1)S(1)}, u32[]{:S(2)}, u32[]{:S(2)}) collective-permute-start(bf16[80,1536]{1,0:T(8,128)(2,1)S(1)} %get-tuple-element.174.refs_1_), channel_id=1, source_target_pairs={{0,1},{1,0},{2,3},{3,2},{4,5},{5,4},{6,7},{7,6},{8,9},{9,8},{10,11... | collective-permute-start | bytes 737288 | tf_op jit(solution)/shard_map/ppermute | solution.py:743
  147.0 2.5 %finish.1 = (f32[256,1536]{1,0:T(8,128)}, bf16[256,1536]{1,0:T(8,128)(2,1)}, f32[96,256]{1,0:T(8,128)}, f32[1,96]{1,0:T(1,128)}, f32[4,256]{1,0:T(4,128)}, /*index=5*/f32[1,256]{1,0:T(1,128)}) custom-call(s32[1,3]{1,0:T(1,128)S(1)} %add_bitcast_fusion.refs_0_, bf16[80,1536]{1,0:T(8,128)(2,1)S(1)} %get-tuple-element.174.refs_1_, ...), custom_call_target="tpu_custom_call" | custom-call | tf_op jit(solution)/shard_map/finish/pallas_call | solution.py:99
  (120 shorter events, 49.9 us)
Async XLA Ops:
  2.6 10.6 %collective-permute-start.3 = (bf16[96,768]{1,0:T(8,128)(2,1)S(1)}, bf16[96,768]{1,0:T(8,128)(2,1)S(1)}, u32[]{:S(2)}, u32[]{:S(2)}) collective-permute-start(bf16[96,768]{1,0:T(8,128)(2,1)S(1)} %get-tuple-element.109.refs_5_), channel_id=1, source_target_pairs={{0,32},{32,64},{64,96},{96,0},{1,33},{33,65},{65,97},{97,1},{2,34}... | collective-permute-start | bytes 442376 | tf_op jit(solution)/shard_map/ppermute | solution.py:735
  5.1 13.5 %collective-permute-start = (bf16[112,768]{1,0:T(8,128)(2,1)S(1)}, bf16[112,768]{1,0:T(8,128)(2,1)S(1)}, u32[]{:S(2)}, u32[]{:S(2)}) collective-permute-start(bf16[112,768]{1,0:T(8,128)(2,1)S(1)} %get-tuple-element.108), channel_id=1, source_target_pairs={{0,8},{8,16},{16,24},{24,0},{1,9},{9,17},{17,25},{25,1},{2,10},{10... | collective-permute-start | bytes 516104 | tf_op jit(solution)/shard_map/ppermute | solution.py:735
  6.4 8.4 %collective-permute-start.4 = (bf16[96,768]{1,0:T(8,128)(2,1)S(1)}, bf16[96,768]{1,0:T(8,128)(2,1)S(1)}, u32[]{:S(2)}, u32[]{:S(2)}) collective-permute-start(bf16[96,768]{1,0:T(8,128)(2,1)S(1)} %get-tuple-element.109.refs_5_), channel_id=1, source_target_pairs={{0,64},{32,96},{64,0},{96,32},{1,65},{33,97},{65,1},{97,33},{2,66}... | collective-permute-start | bytes 442376 | tf_op jit(solution)/shard_map/ppermute | solution.py:735
  19.3 13.8 %collective-permute-start.10 = (bf16[4,96,768]{2,1,0:T(8,128)(2,1)S(1)}, bf16[4,96,768]{2,1,0:T(8,128)(2,1)S(1)}, u32[]{:S(2)}, u32[]{:S(2)}) collective-permute-start(bf16[4,96,768]{2,1,0:T(8,128)(2,1)S(1)} %get-tuple-element.111.refs_6_), channel_id=1, source_target_pairs={{0,8},{8,16},{16,24},{24,0},{1,9},{9,17},{17,25},{25,1},{2,10},{10... | collective-permute-start | bytes 1769480 | tf_op jit(solution)/shard_map/ppermute | solution.py:735
  20.4 12.7 %collective-permute-start.12 = (bf16[4,96,768]{2,1,0:T(8,128)(2,1)S(1)}, bf16[4,96,768]{2,1,0:T(8,128)(2,1)S(1)}, u32[]{:S(2)}, u32[]{:S(2)}) collective-permute-start(bf16[4,96,768]{2,1,0:T(8,128)(2,1)S(1)} %get-tuple-element.111.refs_6_), channel_id=1, source_target_pairs={{0,24},{8,0},{16,8},{24,16},{1,25},{9,1},{17,9},{25,17},{2,26},{10... | collective-permute-start | bytes 1769480 | tf_op jit(solution)/shard_map/ppermute | solution.py:735
  22.1 13.8 %collective-permute-start.6 = (bf16[4,96,768]{2,1,0:T(8,128)(2,1)S(1)}, bf16[4,96,768]{2,1,0:T(8,128)(2,1)S(1)}, u32[]{:S(2)}, u32[]{:S(2)}) collective-permute-start(bf16[4,96,768]{2,1,0:T(8,128)(2,1)S(1)} %get-tuple-element.110.refs_1_), channel_id=1, source_target_pairs={{0,32},{32,64},{64,96},{96,0},{1,33},{33,65},{65,97},{97,1},{2,34}... | collective-permute-start | bytes 1769480 | tf_op jit(solution)/shard_map/ppermute | solution.py:735
  22.9 13.9 %collective-permute-start.8 = (bf16[4,96,768]{2,1,0:T(8,128)(2,1)S(1)}, bf16[4,96,768]{2,1,0:T(8,128)(2,1)S(1)}, u32[]{:S(2)}, u32[]{:S(2)}) collective-permute-start(bf16[4,96,768]{2,1,0:T(8,128)(2,1)S(1)} %get-tuple-element.110.refs_1_), channel_id=1, source_target_pairs={{0,96},{32,0},{64,32},{96,64},{1,97},{33,1},{65,33},{97,65},{2,98}... | collective-permute-start | bytes 1769480 | tf_op jit(solution)/shard_map/ppermute | solution.py:735
  33.1 10.1 %collective-permute-start.11 = (bf16[2,96,768]{2,1,0:T(8,128)(2,1)S(1)}, bf16[2,96,768]{2,1,0:T(8,128)(2,1)S(1)}, u32[]{:S(2)}, u32[]{:S(2)}) collective-permute-start(bf16[2,96,768]{2,1,0:T(8,128)(2,1)S(1)} %slice.18), channel_id=1, source_target_pairs={{0,8},{8,16},{16,24},{24,0},{1,9},{9,17},{17,25},{25,1},{2,10},{10... | collective-permute-start | bytes 884744 | tf_op jit(solution)/shard_map/ppermute | solution.py:735
  33.2 10.0 %collective-permute-start.13 = (bf16[2,96,768]{2,1,0:T(8,128)(2,1)S(1)}, bf16[2,96,768]{2,1,0:T(8,128)(2,1)S(1)}, u32[]{:S(2)}, u32[]{:S(2)}) collective-permute-start(bf16[2,96,768]{2,1,0:T(8,128)(2,1)S(1)} %slice.19), channel_id=1, source_target_pairs={{0,24},{8,0},{16,8},{24,16},{1,25},{9,1},{17,9},{25,17},{2,26},{10... | collective-permute-start | bytes 884744 | tf_op jit(solution)/shard_map/ppermute | solution.py:735
  35.9 7.3 %collective-permute-start.7 = (bf16[2,96,768]{2,1,0:T(8,128)(2,1)S(1)}, bf16[2,96,768]{2,1,0:T(8,128)(2,1)S(1)}, u32[]{:S(2)}, u32[]{:S(2)}) collective-permute-start(bf16[2,96,768]{2,1,0:T(8,128)(2,1)S(1)} %slice.16), channel_id=1, source_target_pairs={{0,32},{32,64},{64,96},{96,0},{1,33},{33,65},{65,97},{97,1},{2,34}... | collective-permute-start | bytes 884744 | tf_op jit(solution)/shard_map/ppermute | solution.py:735
  36.8 6.4 %collective-permute-start.9 = (bf16[2,96,768]{2,1,0:T(8,128)(2,1)S(1)}, bf16[2,96,768]{2,1,0:T(8,128)(2,1)S(1)}, u32[]{:S(2)}, u32[]{:S(2)}) collective-permute-start(bf16[2,96,768]{2,1,0:T(8,128)(2,1)S(1)} %slice.17), channel_id=1, source_target_pairs={{0,96},{32,0},{64,32},{96,64},{1,97},{33,1},{65,33},{97,65},{2,98}... | collective-permute-start | bytes 884744 | tf_op jit(solution)/shard_map/ppermute | solution.py:735
  53.9 6.8 %collective-permute-start.17 = (f32[8,256]{1,0:T(8,128)S(1)}, f32[8,256]{1,0:T(8,128)S(1)}, u32[]{:S(2)}, u32[]{:S(2)}) collective-permute-start(f32[8,256]{1,0:T(8,128)S(1)} %get-tuple-element.121), channel_id=1, source_target_pairs={{0,1},{1,0},{2,3},{3,2},{4,5},{5,4},{6,7},{7,6},{8,9},{9,8},{10,11... | collective-permute-start | bytes 24584 | tf_op jit(solution)/shard_map/ppermute | solution.py:743
  68.4 6.6 %collective-permute-start.21 = (bf16[128,384]{1,0:T(8,128)(2,1)S(1)}, bf16[128,384]{1,0:T(8,128)(2,1)S(1)}, u32[]{:S(2)}, u32[]{:S(2)}) collective-permute-start(bf16[128,384]{1,0:T(8,128)(2,1)S(1)} %get-tuple-element.123), channel_id=1, source_target_pairs={{0,24},{8,0},{16,8},{24,16},{1,25},{9,1},{17,9},{25,17},{2,26},{10... | collective-permute-start | bytes 294920 | tf_op jit(solution)/shard_map/ppermute | solution.py:735
  83.6 6.6 %collective-permute-start.25 = (f32[32,384]{1,0:T(8,128)S(1)}, f32[32,384]{1,0:T(8,128)S(1)}, u32[]{:S(2)}, u32[]{:S(2)}) collective-permute-start(f32[32,384]{1,0:T(8,128)S(1)} %get-tuple-element.136), channel_id=1, source_target_pairs={{0,2},{1,3},{2,4},{3,5},{4,6},{5,7},{6,0},{7,1},{8,10},{9,11},{10,... | collective-permute-start | bytes 147464 | tf_op jit(solution)/shard_map/ppermute | solution.py:739
  83.6 6.6 %collective-permute-start.26 = (f32[32,384]{1,0:T(8,128)S(1)}, f32[32,384]{1,0:T(8,128)S(1)}, u32[]{:S(2)}, u32[]{:S(2)}) collective-permute-start(f32[32,384]{1,0:T(8,128)S(1)} %get-tuple-element.137), channel_id=1, source_target_pairs={{0,4},{1,5},{2,6},{3,7},{4,0},{5,1},{6,2},{7,3},{8,12},{9,13},{10,... | collective-permute-start | bytes 147464 | tf_op jit(solution)/shard_map/ppermute | solution.py:739
  92.5 6.4 %collective-permute-start.32 = (bf16[4,64,1536]{2,1,0:T(8,128)(2,1)S(1)}, bf16[4,64,1536]{2,1,0:T(8,128)(2,1)S(1)}, u32[]{:S(2)}, u32[]{:S(2)}) collective-permute-start(bf16[4,64,1536]{2,1,0:T(8,128)(2,1)S(1)} %get-tuple-element.158), channel_id=1, source_target_pairs={{0,1},{1,0},{2,3},{3,2},{4,5},{5,4},{6,7},{7,6},{8,9},{9,8},{10,11... | collective-permute-start | bytes 2359304 | tf_op jit(solution)/shard_map/ppermute | solution.py:743
  94.3 10.3 %collective-permute-start.28 = (bf16[2,96,768]{2,1,0:T(8,128)(2,1)S(1)}, bf16[2,96,768]{2,1,0:T(8,128)(2,1)S(1)}, u32[]{:S(2)}, u32[]{:S(2)}) collective-permute-start(bf16[2,96,768]{2,1,0:T(8,128)(2,1)S(1)} %get-tuple-element.151), channel_id=1, source_target_pairs={{0,32},{32,64},{64,96},{96,0},{1,33},{33,65},{65,97},{97,1},{2,34}... | collective-permute-start | bytes 884744 | tf_op jit(solution)/shard_map/ppermute | solution.py:735
  94.3 10.3 %collective-permute-start.29 = (bf16[2,96,768]{2,1,0:T(8,128)(2,1)S(1)}, bf16[2,96,768]{2,1,0:T(8,128)(2,1)S(1)}, u32[]{:S(2)}, u32[]{:S(2)}) collective-permute-start(bf16[2,96,768]{2,1,0:T(8,128)(2,1)S(1)} %get-tuple-element.152), channel_id=1, source_target_pairs={{0,96},{32,0},{64,32},{96,64},{1,97},{33,1},{65,33},{97,65},{2,98}... | collective-permute-start | bytes 884744 | tf_op jit(solution)/shard_map/ppermute | solution.py:735
  97.4 7.0 %collective-permute-start.31 = (bf16[2,112,512]{2,1,0:T(8,128)(2,1)S(1)}, bf16[2,112,512]{2,1,0:T(8,128)(2,1)S(1)}, u32[]{:S(2)}, u32[]{:S(2)}) collective-permute-start(bf16[2,112,512]{2,1,0:T(8,128)(2,1)S(1)} %get-tuple-element.156), channel_id=1, source_target_pairs={{0,24},{8,0},{16,8},{24,16},{1,25},{9,1},{17,9},{25,17},{2,26},{10... | collective-permute-start | bytes 688136 | tf_op jit(solution)/shard_map/ppermute | solution.py:735
  97.7 6.7 %collective-permute-start.30 = (bf16[2,96,512]{2,1,0:T(8,128)(2,1)S(1)}, bf16[2,96,512]{2,1,0:T(8,128)(2,1)S(1)}, u32[]{:S(2)}, u32[]{:S(2)}) collective-permute-start(bf16[2,96,512]{2,1,0:T(8,128)(2,1)S(1)} %get-tuple-element.155), channel_id=1, source_target_pairs={{0,8},{8,16},{16,24},{24,0},{1,9},{9,17},{17,25},{25,1},{2,10},{10... | collective-permute-start | bytes 589832 | tf_op jit(solution)/shard_map/ppermute | solution.py:735
  99.6 11.4 %collective-permute-start.37 = (bf16[2,64,1536]{2,1,0:T(8,128)(2,1)S(1)}, bf16[2,64,1536]{2,1,0:T(8,128)(2,1)S(1)}, u32[]{:S(2)}, u32[]{:S(2)}) collective-permute-start(bf16[2,64,1536]{2,1,0:T(8,128)(2,1)S(1)} %get-tuple-element.165), channel_id=1, source_target_pairs={{0,2},{1,3},{2,0},{3,1},{4,6},{5,7},{6,4},{7,5},{8,10},{9,11},{10,... | collective-permute-start | bytes 1179656 | tf_op jit(solution)/shard_map/ppermute | solution.py:743
  105.5 14.5 %collective-permute-start.33 = (bf16[4,96,768]{2,1,0:T(8,128)(2,1)S(1)}, bf16[4,96,768]{2,1,0:T(8,128)(2,1)S(1)}, u32[]{:S(2)}, u32[]{:S(2)}) collective-permute-start(bf16[4,96,768]{2,1,0:T(8,128)(2,1)S(1)} %get-tuple-element.160), channel_id=1, source_target_pairs={{0,32},{32,64},{64,96},{96,0},{1,33},{33,65},{65,97},{97,1},{2,34}... | collective-permute-start | bytes 1769480 | tf_op jit(solution)/shard_map/ppermute | solution.py:735
  106.3 13.8 %collective-permute-start.34 = (bf16[4,96,768]{2,1,0:T(8,128)(2,1)S(1)}, bf16[4,96,768]{2,1,0:T(8,128)(2,1)S(1)}, u32[]{:S(2)}, u32[]{:S(2)}) collective-permute-start(bf16[4,96,768]{2,1,0:T(8,128)(2,1)S(1)} %get-tuple-element.161), channel_id=1, source_target_pairs={{0,96},{32,0},{64,32},{96,64},{1,97},{33,1},{65,33},{97,65},{2,98}... | collective-permute-start | bytes 1769480 | tf_op jit(solution)/shard_map/ppermute | solution.py:735
  108.3 9.7 %collective-permute-start.35 = (bf16[4,96,512]{2,1,0:T(8,128)(2,1)S(1)}, bf16[4,96,512]{2,1,0:T(8,128)(2,1)S(1)}, u32[]{:S(2)}, u32[]{:S(2)}) collective-permute-start(bf16[4,96,512]{2,1,0:T(8,128)(2,1)S(1)} %get-tuple-element.163), channel_id=1, source_target_pairs={{0,8},{8,16},{16,24},{24,0},{1,9},{9,17},{17,25},{25,1},{2,10},{10... | collective-permute-start | bytes 1179656 | tf_op jit(solution)/shard_map/ppermute | solution.py:735
  108.3 9.7 %collective-permute-start.36 = (bf16[4,96,512]{2,1,0:T(8,128)(2,1)S(1)}, bf16[4,96,512]{2,1,0:T(8,128)(2,1)S(1)}, u32[]{:S(2)}, u32[]{:S(2)}) collective-permute-start(bf16[4,96,512]{2,1,0:T(8,128)(2,1)S(1)} %get-tuple-element.164), channel_id=1, source_target_pairs={{0,24},{8,0},{16,8},{24,16},{1,25},{9,1},{17,9},{25,17},{2,26},{10... | collective-permute-start | bytes 1179656 | tf_op jit(solution)/shard_map/ppermute | solution.py:735
  111.6 13.7 %collective-permute-start.41 = (bf16[64,1536]{1,0:T(8,128)(2,1)S(1)}, bf16[64,1536]{1,0:T(8,128)(2,1)S(1)}, u32[]{:S(2)}, u32[]{:S(2)}) collective-permute-start(bf16[64,1536]{1,0:T(8,128)(2,1)S(1)} %get-tuple-element.171), channel_id=1, source_target_pairs={{0,4},{1,5},{2,6},{3,7},{4,0},{5,1},{6,2},{7,3},{8,12},{9,13},{10,... | collective-permute-start | bytes 589832 | tf_op jit(solution)/shard_map/ppermute | solution.py:743
  125.3 9.0 %collective-permute-start.49 = (bf16[96,768]{1,0:T(8,128)(2,1)S(1)}, bf16[96,768]{1,0:T(8,128)(2,1)S(1)}, u32[]{:S(2)}, u32[]{:S(2)}) collective-permute-start(bf16[96,768]{1,0:T(8,128)(2,1)S(1)} %get-tuple-element.182), channel_id=1, source_target_pairs={{0,8},{8,16},{16,24},{24,0},{1,9},{9,17},{17,25},{25,1},{2,10},{10... | collective-permute-start | bytes 442376 | tf_op jit(solution)/shard_map/ppermute | solution.py:735
  129.9 15.0 %collective-permute-start.42 = (bf16[80,1536]{1,0:T(8,128)(2,1)S(1)}, bf16[80,1536]{1,0:T(8,128)(2,1)S(1)}, u32[]{:S(2)}, u32[]{:S(2)}) collective-permute-start(bf16[80,1536]{1,0:T(8,128)(2,1)S(1)} %get-tuple-element.174.refs_1_), channel_id=1, source_target_pairs={{0,2},{1,3},{2,4},{3,5},{4,6},{5,7},{6,0},{7,1},{8,10},{9,11},{10,... | collective-permute-start | bytes 737288 | tf_op jit(solution)/shard_map/ppermute | solution.py:739
  130.6 14.2 %collective-permute-start.43 = (bf16[80,1536]{1,0:T(8,128)(2,1)S(1)}, bf16[80,1536]{1,0:T(8,128)(2,1)S(1)}, u32[]{:S(2)}, u32[]{:S(2)}) collective-permute-start(bf16[80,1536]{1,0:T(8,128)(2,1)S(1)} %get-tuple-element.174.refs_1_), channel_id=1, source_target_pairs={{0,4},{1,5},{2,6},{3,7},{4,0},{5,1},{6,2},{7,3},{8,12},{9,13},{10,... | collective-permute-start | bytes 737288 | tf_op jit(solution)/shard_map/ppermute | solution.py:739
  132.0 13.3 %collective-permute-start.44 = (bf16[80,1536]{1,0:T(8,128)(2,1)S(1)}, bf16[80,1536]{1,0:T(8,128)(2,1)S(1)}, u32[]{:S(2)}, u32[]{:S(2)}) collective-permute-start(bf16[80,1536]{1,0:T(8,128)(2,1)S(1)} %get-tuple-element.174.refs_1_), channel_id=1, source_target_pairs={{0,6},{1,7},{2,0},{3,1},{4,2},{5,3},{6,4},{7,5},{8,14},{9,15},{10,... | collective-permute-start | bytes 737288 | tf_op jit(solution)/shard_map/ppermute | solution.py:739
  134.3 11.1 %collective-permute-start.51 = (bf16[96,768]{1,0:T(8,128)(2,1)S(1)}, bf16[96,768]{1,0:T(8,128)(2,1)S(1)}, u32[]{:S(2)}, u32[]{:S(2)}) collective-permute-start(bf16[96,768]{1,0:T(8,128)(2,1)S(1)} %get-tuple-element.184), channel_id=1, source_target_pairs={{0,24},{8,0},{16,8},{24,16},{1,25},{9,1},{17,9},{25,17},{2,26},{10... | collective-permute-start | bytes 442376 | tf_op jit(solution)/shard_map/ppermute | solution.py:735
  138.7 8.1 %collective-permute-start.45 = (bf16[80,1536]{1,0:T(8,128)(2,1)S(1)}, bf16[80,1536]{1,0:T(8,128)(2,1)S(1)}, u32[]{:S(2)}, u32[]{:S(2)}) collective-permute-start(bf16[80,1536]{1,0:T(8,128)(2,1)S(1)} %get-tuple-element.174.refs_1_), channel_id=1, source_target_pairs={{0,1},{1,0},{2,3},{3,2},{4,5},{5,4},{6,7},{7,6},{8,9},{9,8},{10,11... | collective-permute-start | bytes 737288 | tf_op jit(solution)/shard_map/ppermute | solution.py:743
  (28 other events, 278.8 us)

commit v7 on v6

--- a/solution.py
+++ b/solution.py
@@ -614,9 +614,12 @@
         put(target, total, side)
 
 
-def halfway_both(ids, l0, l1, l3, r0, r1, r3, own, *targets):
-    halfway(0, l0, l1, l3, *targets[:4])
-    halfway(1, r0, r1, r3, *targets[4:])
+def halfway_left(ids, own, one, three, right, *targets):
+    halfway(0, own, one, three, *targets)
+
+
+def halfway_right(ids, own, one, three, pair, *targets):
+    halfway(1, own, one, three, *targets)
 
 
 def pair_again(ids, near, got, cotangent, hidden, own, second, held, mine, last):
@@ -974,16 +977,10 @@
         cotangent,
         hidden,
     )
-    sums = fuse(
-        halfway_both,
-        [((ROWS, LEFT), BF16)] * 4 + [((ROWS, RIGHT), BF16)] * 4,
-        ids,
-        *left,
-        *right,
-        own,
-    )
-    left = sums[:1] + [shift(sums[steps], "ctx", steps) for steps in range(1, 4)]
-    right = sums[4:5] + [shift(sums[4 + steps], "dp", steps) for steps in range(1, 4)]
+    right = fuse(halfway_right, [((ROWS, RIGHT), BF16)] * 4, ids, *right, own)
+    left = fuse(halfway_left, [((ROWS, LEFT), BF16)] * 4, ids, *left, right[0])
+    left = left[:1] + [shift(left[steps], "ctx", steps) for steps in range(1, 4)]
+    right = right[:1] + [shift(right[steps], "dp", steps) for steps in range(1, 4)]
     few, line = ((1, HEADS), F32), ((1, WIDE), F32)
     message, gain_full, *few_grads = fuse(
         gather_up,

time: 150 us -> 147 us (0.980)
  waiting for transfers between devices: 35.9 us -> 32.2 us
    ppermute x34, waiting for transfers between devices: 32.6 us -> 29 us  [shift(): return lax.ppermute(array, axis, [(i, (i + steps) % 4) for i in range(4)])]
    pallas_call x20 -> x21, Pallas kernels: 32.6 us -> 33.2 us  [fuse(): return list(call(ids, *arrays))]
  transfers between devices with their start and end apart: 52 -> 52, of which waited for: 22 -> 21; matrix products, arithmetic and copies ran while one was open for 2% -> 2% of each run, Pallas kernels for 12% -> 13%
where the time goes in v7:
time: 147 us; the launch traced here: 146 us
  starting transfers between devices  76.4 us (52%)
  Pallas kernels  33.2 us (23%)
  waiting for transfers between devices  32.2 us (22%)
  other arithmetic  1.86 us (1%)
  local copies, waits for them, and re-layouts  1.81 us (1%)
    ppermute x34, starting transfers between devices, shift(): return lax.ppermute(array, axis, [(i, (i + steps) % 4) for i in range(4)])  44.3 us
    pallas_call x21, Pallas kernels, fuse(): return list(call(ids, *arrays))  33.2 us
    ppermute x34, waiting for transfers between devices, shift(): return lax.ppermute(array, axis, [(i, (i + steps) % 4) for i in range(4)])  29 us
    ppermute x9, starting transfers between devices, across(): return lax.ppermute(array, 'tp', [(i, i ^ bits) for i in range(8)])  20.4 us
    ppermute x9, starting transfers between devices, from_chip(): lax.ppermute(array, 'tp', [(i, (i + 2 * steps) % 8) for i in range(8)])  11.7 us
  transfers between devices with their start and end apart: 52, of which 21 were waited for; matrix products, arithmetic and copies ran while one was open for 2% of the time, Pallas kernels for 13%

profile of v7, /device:TPU:1, one launch (start us, length us, event | category | flops | bytes accessed | tf_op | source)
XLA Modules:
  0.0 146.5 jit_solution(5454976033305309087)
XLA Ops:
  0.7 1.8 %prepare.1 = (bf16[96,768]{1,0:T(8,128)(2,1)S(1)}, bf16[112,768]{1,0:T(8,128)(2,1)S(1)}, bf16[96,768]{1,0:T(8,128)(2,1)S(1)}) custom-call(s32[1,3]{1,0:T(1,128)S(1)} %add_bitcast_fusion.refs_0_, bf16[96,384]{1,0:T(8,128)(2,1)} %refs_1_.2, bf16[96,384]{1,0:T(8,128)(2,1)} %refs_2_.2, bf16[96,256]{1,0:T(8,128)(2,1)} %refs_3_.1, bf16[6,96]{1,0:T(8,128)(2,1)} %bitcast.29, ...), custom_call_target="tpu_custom_call" | custom-call | tf_op jit(solution)/shard_map/prepare/pallas_call | solution.py:99
  2.6 2.5 %collective-permute-start.3 = (bf16[96,768]{1,0:T(8,128)(2,1)S(1)}, bf16[96,768]{1,0:T(8,128)(2,1)S(1)}, u32[]{:S(2)}, u32[]{:S(2)}) collective-permute-start(bf16[96,768]{1,0:T(8,128)(2,1)S(1)} %get-tuple-element.109.refs_5_), channel_id=1, source_target_pairs={{0,32},{32,64},{64,96},{96,0},{1,33},{33,65},{65,97},{97,1},{2,34}... | collective-permute-start | bytes 442376 | tf_op jit(solution)/shard_map/ppermute | solution.py:738
  6.4 3.3 %collective-permute-start.4 = (bf16[96,768]{1,0:T(8,128)(2,1)S(1)}, bf16[96,768]{1,0:T(8,128)(2,1)S(1)}, u32[]{:S(2)}, u32[]{:S(2)}) collective-permute-start(bf16[96,768]{1,0:T(8,128)(2,1)S(1)} %get-tuple-element.109.refs_5_), channel_id=1, source_target_pairs={{0,64},{32,96},{64,0},{96,32},{1,65},{33,97},{65,1},{97,33},{2,66}... | collective-permute-start | bytes 442376 | tf_op jit(solution)/shard_map/ppermute | solution.py:738
  10.5 2.7 %collective-permute-start.1 = (bf16[96,768]{1,0:T(8,128)(2,1)S(1)}, bf16[96,768]{1,0:T(8,128)(2,1)S(1)}, u32[]{:S(2)}, u32[]{:S(2)}) collective-permute-start(bf16[96,768]{1,0:T(8,128)(2,1)S(1)} %get-tuple-element.107.refs_1_), channel_id=1, source_target_pairs={{0,16},{8,24},{16,0},{24,8},{1,17},{9,25},{17,1},{25,9},{2,18},{10... | collective-permute-start | bytes 442376 | tf_op jit(solution)/shard_map/ppermute | solution.py:738
  16.1 2.6 %collective-permute-done.2.refs_4_ = bf16[96,768]{1,0:T(8,128)(2,1)S(1)} collective-permute-done((bf16[96,768]{1,0:T(8,128)(2,1)S(1)}, bf16[96,768]{1,0:T(8,128)(2,1)S(1)}, u32[]{:S(2)}, u32[]{:S(2)}) %collective-permute-start.2) | collective-permute-done | bytes 147488 | tf_op jit(solution)/shard_map/ppermute | solution.py:738
  22.9 1.9 %collective-permute-start.8 = (bf16[4,96,768]{2,1,0:T(8,128)(2,1)S(1)}, bf16[4,96,768]{2,1,0:T(8,128)(2,1)S(1)}, u32[]{:S(2)}, u32[]{:S(2)}) collective-permute-start(bf16[4,96,768]{2,1,0:T(8,128)(2,1)S(1)} %get-tuple-element.110.refs_1_), channel_id=1, source_target_pairs={{0,96},{32,0},{64,32},{96,64},{1,97},{33,1},{65,33},{97,65},{2,98}... | collective-permute-start | bytes 1769480 | tf_op jit(solution)/shard_map/ppermute | solution.py:738
  24.8 8.2 %collective-permute-done.10.refs_7_ = bf16[4,96,768]{2,1,0:T(8,128)(2,1)S(1)} collective-permute-done((bf16[4,96,768]{2,1,0:T(8,128)(2,1)S(1)}, bf16[4,96,768]{2,1,0:T(8,128)(2,1)S(1)}, u32[]{:S(2)}, u32[]{:S(2)}) %collective-permute-start.10) | collective-permute-done | bytes 589856 | tf_op jit(solution)/shard_map/ppermute | solution.py:738
  33.2 2.7 %collective-permute-start.13 = (bf16[2,96,768]{2,1,0:T(8,128)(2,1)S(1)}, bf16[2,96,768]{2,1,0:T(8,128)(2,1)S(1)}, u32[]{:S(2)}, u32[]{:S(2)}) collective-permute-start(bf16[2,96,768]{2,1,0:T(8,128)(2,1)S(1)} %slice.19), channel_id=1, source_target_pairs={{0,24},{8,0},{16,8},{24,16},{1,25},{9,1},{17,9},{25,17},{2,26},{10... | collective-permute-start | bytes 884744 | tf_op jit(solution)/shard_map/ppermute | solution.py:738
  36.8 2.0 %collective-permute-start.9 = (bf16[2,96,768]{2,1,0:T(8,128)(2,1)S(1)}, bf16[2,96,768]{2,1,0:T(8,128)(2,1)S(1)}, u32[]{:S(2)}, u32[]{:S(2)}) collective-permute-start(bf16[2,96,768]{2,1,0:T(8,128)(2,1)S(1)} %slice.17), channel_id=1, source_target_pairs={{0,96},{32,0},{64,32},{96,64},{1,97},{33,1},{65,33},{97,65},{2,98}... | collective-permute-start | bytes 884744 | tf_op jit(solution)/shard_map/ppermute | solution.py:738
  41.1 2.1 %tabulate.1 = (f32[16,768]{1,0:T(8,128)S(1)}, f32[256,1536]{1,0:T(8,128)S(1)}) custom-call(s32[1,3]{1,0:T(1,128)S(1)} %add_bitcast_fusion.refs_0_, bf16[4,384]{1,0:T(4,128)(2,1)} %refs_1_.3, bf16[4,256]{1,0:T(4,128)(2,1)} %refs_2_.3, bf16[1,384]{1,0:T(2,128)(2,1)} %broadcast_in_dim.19.refs_3_, bf16[1,256]{1,0:T(2,128)(2,1)} %broadcast_in_dim.20.refs_4_, ...), custom_call_target="tpu_custom_call" | custom-call | tf_op jit(solution)/shard_map/tabulate/pallas_call | solution.py:99
  43.2 2.9 %enter.1 = (bf16[1536,768]{1,0:T(8,128)(2,1)S(1)}, bf16[272,1536]{1,0:T(8,128)(2,1)S(1)}, bf16[272,640]{1,0:T(8,128)(2,1)S(1)}, f32[256,1408]{1,0:T(8,128)S(1)},...) custom-call(s32[1,3]{1,0:T(1,128)S(1)} %add_bitcast_fusion.refs_0_, ...), custom_call_target="tpu_custom_call" | custom-call | tf_op jit(solution)/shard_map/enter/pallas_call | solution.py:99
  46.2 2.3 %collective-permute-start.15 = (bf16[144,384]{1,0:T(8,128)(2,1)S(1)}, bf16[144,384]{1,0:T(8,128)(2,1)S(1)}, u32[]{:S(2)}, u32[]{:S(2)}) collective-permute-start(bf16[144,384]{1,0:T(8,128)(2,1)S(1)} %get-tuple-element.115), channel_id=1, source_target_pairs={{0,16},{8,24},{16,0},{24,8},{1,17},{9,25},{17,1},{25,9},{2,18},{10... | collective-permute-start | bytes 331784 | tf_op jit(solution)/shard_map/ppermute | solution.py:738
  48.9 2.4 %project.1 = (bf16[1536,768]{1,0:T(8,128)(2,1)S(1)}, f32[256,2304]{1,0:T(8,128)S(1)}, f32[256,640]{1,0:T(8,128)S(1)}, f32[256,1152]{1,0:T(8,128)S(1)}) custom-call(s32[1,3]{1,0:T(1,128)S(1)} %add_bitcast_fusion.refs_0_, bf16[4,96,768]{2,1,0:T(8,128)(2,1)S(1)} %get-tuple-element.110.refs_1_, bf16[4,96,768]{2,1,0:T(8,128)(2,1)S(1)} %collective-permute-done.6.refs_2_, ...), custom_call_target="tpu_custom_call" | custom-call | tf_op jit(solution)/shard_map/project/pallas_call | solution.py:99
  53.9 6.0 %collective-permute-start.17 = (f32[8,256]{1,0:T(8,128)S(1)}, f32[8,256]{1,0:T(8,128)S(1)}, u32[]{:S(2)}, u32[]{:S(2)}) collective-permute-start(f32[8,256]{1,0:T(8,128)S(1)} %get-tuple-element.121), channel_id=1, source_target_pairs={{0,1},{1,0},{2,3},{3,2},{4,5},{5,4},{6,7},{7,6},{8,9},{9,8},{10,11... | collective-permute-start | bytes 24584 | tf_op jit(solution)/shard_map/ppermute | solution.py:746
  61.9 2.4 %collective-permute-start.19 = (f32[8,256]{1,0:T(8,128)S(1)}, f32[8,256]{1,0:T(8,128)S(1)}, u32[]{:S(2)}, u32[]{:S(2)}) collective-permute-start(f32[8,256]{1,0:T(8,128)S(1)} %add.3.refs_1_), channel_id=1, source_target_pairs={{0,4},{1,5},{2,6},{3,7},{4,0},{5,1},{6,2},{7,3},{8,12},{9,13},{10,... | collective-permute-start | bytes 24584 | tf_op jit(solution)/shard_map/ppermute | solution.py:742
  68.4 2.2 %collective-permute-start.21 = (bf16[128,384]{1,0:T(8,128)(2,1)S(1)}, bf16[128,384]{1,0:T(8,128)(2,1)S(1)}, u32[]{:S(2)}, u32[]{:S(2)}) collective-permute-start(bf16[128,384]{1,0:T(8,128)(2,1)S(1)} %get-tuple-element.123), channel_id=1, source_target_pairs={{0,24},{8,0},{16,8},{24,16},{1,25},{9,1},{17,9},{25,17},{2,26},{10... | collective-permute-start | bytes 294920 | tf_op jit(solution)/shard_map/ppermute | solution.py:738
  71.3 3.6 %middle.1 = (bf16[1536,384]{1,0:T(8,128)(2,1)S(1)}, bf16[1536,384]{1,0:T(8,128)(2,1)S(1)}, f32[256,640]{1,0:T(8,128)S(1)}, bf16[256,1536]{1,0:T(8,128)(2,1)S(1)}, f32[256,256]{1,0:T(8,128)S(1)}) custom-call(s32[1,3]{1,0:T(1,128)S(1)} %add_bitcast_fusion.refs_0_, bf16[272,1536]{1,0:T(8,128)(2,1)S(1)} %get-tuple-element.116.refs_11_.refs_1_.refs_6_.refs_10_, ...), custom_call_target="tpu_custom_call" | custom-call | tf_op jit(solution)/shard_map/middle/pallas_call | solution.py:99
  76.5 2.0 %leave.1 = (bf16[272,512]{1,0:T(8,128)(2,1)S(1)}, f32[272,256]{1,0:T(8,128)S(1)}, f32[4,32,384]{2,1,0:T(8,128)S(1)}, f32[4,32,384]{2,1,0:T(8,128)S(1)}, f32[8,384]{1,0:T(8,128)S(1)}) custom-call(s32[1,3]{1,0:T(1,128)S(1)} %add_bitcast_fusion.refs_0_, bf16[128,384]{1,0:T(8,128)(2,1)S(1)} %collective-permute-done.21.refs_1_, ...), custom_call_target="tpu_custom_call" | custom-call | tf_op jit(solution)/shard_map/leave/pallas_call | solution.py:99
  78.5 3.4 %collective-permute-start.24 = (f32[4,32,384]{2,1,0:T(8,128)S(1)}, f32[4,32,384]{2,1,0:T(8,128)S(1)}, u32[]{:S(2)}, u32[]{:S(2)}) collective-permute-start(f32[4,32,384]{2,1,0:T(8,128)S(1)} %get-tuple-element.134), channel_id=1, source_target_pairs={{0,1},{1,0},{2,3},{3,2},{4,5},{5,4},{6,7},{7,6},{8,9},{9,8},{10,11... | collective-permute-start | bytes 589832 | tf_op jit(solution)/shard_map/ppermute | solution.py:746
  83.6 3.5 %collective-permute-start.26 = (f32[32,384]{1,0:T(8,128)S(1)}, f32[32,384]{1,0:T(8,128)S(1)}, u32[]{:S(2)}, u32[]{:S(2)}) collective-permute-start(f32[32,384]{1,0:T(8,128)S(1)} %get-tuple-element.137), channel_id=1, source_target_pairs={{0,4},{1,5},{2,6},{3,7},{4,0},{5,1},{6,2},{7,3},{8,12},{9,13},{10,... | collective-permute-start | bytes 147464 | tf_op jit(solution)/shard_map/ppermute | solution.py:742
  87.2 3.0 %value_grads.1 = (bf16[1536,384]{1,0:T(8,128)(2,1)S(1)}, f32[272,1536]{1,0:T(8,128)S(1)}) custom-call(s32[1,3]{1,0:T(1,128)S(1)} %add_bitcast_fusion.refs_0_, bf16[272,512]{1,0:T(8,128)(2,1)S(1)} %get-tuple-element.139.refs_1_.refs_5_, f32[272,256]{1,0:T(8,128)S(1)} %get-tuple-element.141.refs_2_, bf16[256,768]{1,0:T(8,128)(2,1)S(1)} %get-tuple-element.125.refs_2_.refs_3_, ...), custom_call_target="tpu_custom_call" | custom-call | tf_op jit(solution)/shard_map/value_grads/pallas_call | solution.py:99
  90.4 2.0 %late_grads.1 = (bf16[4,64,1536]{2,1,0:T(8,128)(2,1)S(1)}, bf16[4,64,1536]{2,1,0:T(8,128)(2,1)S(1)}, bf16[4,96,768]{2,1,0:T(8,128)(2,1)S(1)}, bf16[4,96,768]{2,1...) custom-call(s32[1,3]{1,0:T(1,128)S(1)} %add_bitcast_fusion.refs_0_, ...), custom_call_target="tpu_custom_call" | custom-call | tf_op jit(solution)/shard_map/late_grads/pallas_call | solution.py:99
  92.5 1.9 %collective-permute-start.32 = (bf16[4,64,1536]{2,1,0:T(8,128)(2,1)S(1)}, bf16[4,64,1536]{2,1,0:T(8,128)(2,1)S(1)}, u32[]{:S(2)}, u32[]{:S(2)}) collective-permute-start(bf16[4,64,1536]{2,1,0:T(8,128)(2,1)S(1)} %get-tuple-element.158), channel_id=1, source_target_pairs={{0,1},{1,0},{2,3},{3,2},{4,5},{5,4},{6,7},{7,6},{8,9},{9,8},{10,11... | collective-permute-start | bytes 2359304 | tf_op jit(solution)/shard_map/ppermute | solution.py:746
  94.3 3.0 %collective-permute-start.29 = (bf16[2,96,768]{2,1,0:T(8,128)(2,1)S(1)}, bf16[2,96,768]{2,1,0:T(8,128)(2,1)S(1)}, u32[]{:S(2)}, u32[]{:S(2)}) collective-permute-start(bf16[2,96,768]{2,1,0:T(8,128)(2,1)S(1)} %get-tuple-element.152), channel_id=1, source_target_pairs={{0,96},{32,0},{64,32},{96,64},{1,97},{33,1},{65,33},{97,65},{2,98}... | collective-permute-start | bytes 884744 | tf_op jit(solution)/shard_map/ppermute | solution.py:738
  100.4 4.0 %collective-permute-done.30.refs_7_ = bf16[2,96,512]{2,1,0:T(8,128)(2,1)S(1)} collective-permute-done((bf16[2,96,512]{2,1,0:T(8,128)(2,1)S(1)}, bf16[2,96,512]{2,1,0:T(8,128)(2,1)S(1)}, u32[]{:S(2)}, u32[]{:S(2)}) %collective-permute-start.30) | collective-permute-done | bytes 196640 | tf_op jit(solution)/shard_map/ppermute | solution.py:738
  106.3 2.0 %collective-permute-start.48 = (bf16[4,96,768]{2,1,0:T(8,128)(2,1)S(1)}, bf16[4,96,768]{2,1,0:T(8,128)(2,1)S(1)}, u32[]{:S(2)}, u32[]{:S(2)}) collective-permute-start(bf16[4,96,768]{2,1,0:T(8,128)(2,1)S(1)} %get-tuple-element.180), channel_id=1, source_target_pairs={{0,96},{32,0},{64,32},{96,64},{1,97},{33,1},{65,33},{97,65},{2,98}... | collective-permute-start | bytes 1769480 | tf_op jit(solution)/shard_map/ppermute | solution.py:738
  108.3 2.7 %collective-permute-start.34 = (bf16[4,96,512]{2,1,0:T(8,128)(2,1)S(1)}, bf16[4,96,512]{2,1,0:T(8,128)(2,1)S(1)}, u32[]{:S(2)}, u32[]{:S(2)}) collective-permute-start(bf16[4,96,512]{2,1,0:T(8,128)(2,1)S(1)} %get-tuple-element.161), channel_id=1, source_target_pairs={{0,24},{8,0},{16,8},{24,16},{1,25},{9,1},{17,9},{25,17},{2,26},{10... | collective-permute-start | bytes 1179656 | tf_op jit(solution)/shard_map/ppermute | solution.py:738
  112.9 5.0 %collective-permute-done.33.refs_2_ = bf16[4,96,512]{2,1,0:T(8,128)(2,1)S(1)} collective-permute-done((bf16[4,96,512]{2,1,0:T(8,128)(2,1)S(1)}, bf16[4,96,512]{2,1,0:T(8,128)(2,1)S(1)}, u32[]{:S(2)}, u32[]{:S(2)}) %collective-permute-start.33) | collective-permute-done | bytes 393248 | tf_op jit(solution)/shard_map/ppermute | solution.py:738
  118.9 2.3 %collective-permute-start.37 = (bf16[96,512]{1,0:T(8,128)(2,1)S(1)}, bf16[96,512]{1,0:T(8,128)(2,1)S(1)}, u32[]{:S(2)}, u32[]{:S(2)}) collective-permute-start(bf16[96,512]{1,0:T(8,128)(2,1)S(1)} %get-tuple-element.166), channel_id=1, source_target_pairs={{0,64},{32,96},{64,0},{96,32},{1,65},{33,97},{65,1},{97,33},{2,66}... | collective-permute-start | bytes 294920 | tf_op jit(solution)/shard_map/ppermute | solution.py:738
  133.4 1.9 %collective-permute-done.50.refs_3_ = bf16[96,768]{1,0:T(8,128)(2,1)S(1)} collective-permute-done((bf16[96,768]{1,0:T(8,128)(2,1)S(1)}, bf16[96,768]{1,0:T(8,128)(2,1)S(1)}, u32[]{:S(2)}, u32[]{:S(2)}) %collective-permute-start.50) | collective-permute-done | bytes 147488 | tf_op jit(solution)/shard_map/ppermute | solution.py:738
  135.3 6.5 %collective-permute-start.43 = (bf16[80,1536]{1,0:T(8,128)(2,1)S(1)}, bf16[80,1536]{1,0:T(8,128)(2,1)S(1)}, u32[]{:S(2)}, u32[]{:S(2)}) collective-permute-start(bf16[80,1536]{1,0:T(8,128)(2,1)S(1)} %get-tuple-element.171.refs_1_), channel_id=1, source_target_pairs={{0,1},{1,0},{2,3},{3,2},{4,5},{5,4},{6,7},{7,6},{8,9},{9,8},{10,11... | collective-permute-start | bytes 737288 | tf_op jit(solution)/shard_map/ppermute | solution.py:746
  144.0 2.5 %finish.1 = (f32[256,1536]{1,0:T(8,128)}, bf16[256,1536]{1,0:T(8,128)(2,1)}, f32[96,256]{1,0:T(8,128)}, f32[1,96]{1,0:T(1,128)}, f32[4,256]{1,0:T(4,128)}, /*index=5*/f32[1,256]{1,0:T(1,128)}) custom-call(s32[1,3]{1,0:T(1,128)S(1)} %add_bitcast_fusion.refs_0_, bf16[80,1536]{1,0:T(8,128)(2,1)S(1)} %get-tuple-element.171.refs_1_, ...), custom_call_target="tpu_custom_call" | custom-call | tf_op jit(solution)/shard_map/finish/pallas_call | solution.py:99
  (121 shorter events, 48.0 us)
Async XLA Ops:
  2.6 10.6 %collective-permute-start.3 = (bf16[96,768]{1,0:T(8,128)(2,1)S(1)}, bf16[96,768]{1,0:T(8,128)(2,1)S(1)}, u32[]{:S(2)}, u32[]{:S(2)}) collective-permute-start(bf16[96,768]{1,0:T(8,128)(2,1)S(1)} %get-tuple-element.109.refs_5_), channel_id=1, source_target_pairs={{0,32},{32,64},{64,96},{96,0},{1,33},{33,65},{65,97},{97,1},{2,34}... | collective-permute-start | bytes 442376 | tf_op jit(solution)/shard_map/ppermute | solution.py:738
  5.1 13.5 %collective-permute-start = (bf16[112,768]{1,0:T(8,128)(2,1)S(1)}, bf16[112,768]{1,0:T(8,128)(2,1)S(1)}, u32[]{:S(2)}, u32[]{:S(2)}) collective-permute-start(bf16[112,768]{1,0:T(8,128)(2,1)S(1)} %get-tuple-element.108), channel_id=1, source_target_pairs={{0,8},{8,16},{16,24},{24,0},{1,9},{9,17},{17,25},{25,1},{2,10},{10... | collective-permute-start | bytes 516104 | tf_op jit(solution)/shard_map/ppermute | solution.py:738
  6.4 8.4 %collective-permute-start.4 = (bf16[96,768]{1,0:T(8,128)(2,1)S(1)}, bf16[96,768]{1,0:T(8,128)(2,1)S(1)}, u32[]{:S(2)}, u32[]{:S(2)}) collective-permute-start(bf16[96,768]{1,0:T(8,128)(2,1)S(1)} %get-tuple-element.109.refs_5_), channel_id=1, source_target_pairs={{0,64},{32,96},{64,0},{96,32},{1,65},{33,97},{65,1},{97,33},{2,66}... | collective-permute-start | bytes 442376 | tf_op jit(solution)/shard_map/ppermute | solution.py:738
  19.3 13.8 %collective-permute-start.10 = (bf16[4,96,768]{2,1,0:T(8,128)(2,1)S(1)}, bf16[4,96,768]{2,1,0:T(8,128)(2,1)S(1)}, u32[]{:S(2)}, u32[]{:S(2)}) collective-permute-start(bf16[4,96,768]{2,1,0:T(8,128)(2,1)S(1)} %get-tuple-element.111.refs_6_), channel_id=1, source_target_pairs={{0,8},{8,16},{16,24},{24,0},{1,9},{9,17},{17,25},{25,1},{2,10},{10... | collective-permute-start | bytes 1769480 | tf_op jit(solution)/shard_map/ppermute | solution.py:738
  20.4 12.7 %collective-permute-start.12 = (bf16[4,96,768]{2,1,0:T(8,128)(2,1)S(1)}, bf16[4,96,768]{2,1,0:T(8,128)(2,1)S(1)}, u32[]{:S(2)}, u32[]{:S(2)}) collective-permute-start(bf16[4,96,768]{2,1,0:T(8,128)(2,1)S(1)} %get-tuple-element.111.refs_6_), channel_id=1, source_target_pairs={{0,24},{8,0},{16,8},{24,16},{1,25},{9,1},{17,9},{25,17},{2,26},{10... | collective-permute-start | bytes 1769480 | tf_op jit(solution)/shard_map/ppermute | solution.py:738
  22.1 13.8 %collective-permute-start.6 = (bf16[4,96,768]{2,1,0:T(8,128)(2,1)S(1)}, bf16[4,96,768]{2,1,0:T(8,128)(2,1)S(1)}, u32[]{:S(2)}, u32[]{:S(2)}) collective-permute-start(bf16[4,96,768]{2,1,0:T(8,128)(2,1)S(1)} %get-tuple-element.110.refs_1_), channel_id=1, source_target_pairs={{0,32},{32,64},{64,96},{96,0},{1,33},{33,65},{65,97},{97,1},{2,34}... | collective-permute-start | bytes 1769480 | tf_op jit(solution)/shard_map/ppermute | solution.py:738
  22.9 13.9 %collective-permute-start.8 = (bf16[4,96,768]{2,1,0:T(8,128)(2,1)S(1)}, bf16[4,96,768]{2,1,0:T(8,128)(2,1)S(1)}, u32[]{:S(2)}, u32[]{:S(2)}) collective-permute-start(bf16[4,96,768]{2,1,0:T(8,128)(2,1)S(1)} %get-tuple-element.110.refs_1_), channel_id=1, source_target_pairs={{0,96},{32,0},{64,32},{96,64},{1,97},{33,1},{65,33},{97,65},{2,98}... | collective-permute-start | bytes 1769480 | tf_op jit(solution)/shard_map/ppermute | solution.py:738
  33.1 10.1 %collective-permute-start.11 = (bf16[2,96,768]{2,1,0:T(8,128)(2,1)S(1)}, bf16[2,96,768]{2,1,0:T(8,128)(2,1)S(1)}, u32[]{:S(2)}, u32[]{:S(2)}) collective-permute-start(bf16[2,96,768]{2,1,0:T(8,128)(2,1)S(1)} %slice.18), channel_id=1, source_target_pairs={{0,8},{8,16},{16,24},{24,0},{1,9},{9,17},{17,25},{25,1},{2,10},{10... | collective-permute-start | bytes 884744 | tf_op jit(solution)/shard_map/ppermute | solution.py:738
  33.2 10.0 %collective-permute-start.13 = (bf16[2,96,768]{2,1,0:T(8,128)(2,1)S(1)}, bf16[2,96,768]{2,1,0:T(8,128)(2,1)S(1)}, u32[]{:S(2)}, u32[]{:S(2)}) collective-permute-start(bf16[2,96,768]{2,1,0:T(8,128)(2,1)S(1)} %slice.19), channel_id=1, source_target_pairs={{0,24},{8,0},{16,8},{24,16},{1,25},{9,1},{17,9},{25,17},{2,26},{10... | collective-permute-start | bytes 884744 | tf_op jit(solution)/shard_map/ppermute | solution.py:738
  35.9 7.3 %collective-permute-start.7 = (bf16[2,96,768]{2,1,0:T(8,128)(2,1)S(1)}, bf16[2,96,768]{2,1,0:T(8,128)(2,1)S(1)}, u32[]{:S(2)}, u32[]{:S(2)}) collective-permute-start(bf16[2,96,768]{2,1,0:T(8,128)(2,1)S(1)} %slice.16), channel_id=1, source_target_pairs={{0,32},{32,64},{64,96},{96,0},{1,33},{33,65},{65,97},{97,1},{2,34}... | collective-permute-start | bytes 884744 | tf_op jit(solution)/shard_map/ppermute | solution.py:738
  36.8 6.4 %collective-permute-start.9 = (bf16[2,96,768]{2,1,0:T(8,128)(2,1)S(1)}, bf16[2,96,768]{2,1,0:T(8,128)(2,1)S(1)}, u32[]{:S(2)}, u32[]{:S(2)}) collective-permute-start(bf16[2,96,768]{2,1,0:T(8,128)(2,1)S(1)} %slice.17), channel_id=1, source_target_pairs={{0,96},{32,0},{64,32},{96,64},{1,97},{33,1},{65,33},{97,65},{2,98}... | collective-permute-start | bytes 884744 | tf_op jit(solution)/shard_map/ppermute | solution.py:738
  53.9 6.8 %collective-permute-start.17 = (f32[8,256]{1,0:T(8,128)S(1)}, f32[8,256]{1,0:T(8,128)S(1)}, u32[]{:S(2)}, u32[]{:S(2)}) collective-permute-start(f32[8,256]{1,0:T(8,128)S(1)} %get-tuple-element.121), channel_id=1, source_target_pairs={{0,1},{1,0},{2,3},{3,2},{4,5},{5,4},{6,7},{7,6},{8,9},{9,8},{10,11... | collective-permute-start | bytes 24584 | tf_op jit(solution)/shard_map/ppermute | solution.py:746
  68.4 6.6 %collective-permute-start.21 = (bf16[128,384]{1,0:T(8,128)(2,1)S(1)}, bf16[128,384]{1,0:T(8,128)(2,1)S(1)}, u32[]{:S(2)}, u32[]{:S(2)}) collective-permute-start(bf16[128,384]{1,0:T(8,128)(2,1)S(1)} %get-tuple-element.123), channel_id=1, source_target_pairs={{0,24},{8,0},{16,8},{24,16},{1,25},{9,1},{17,9},{25,17},{2,26},{10... | collective-permute-start | bytes 294920 | tf_op jit(solution)/shard_map/ppermute | solution.py:738
  83.6 6.6 %collective-permute-start.25 = (f32[32,384]{1,0:T(8,128)S(1)}, f32[32,384]{1,0:T(8,128)S(1)}, u32[]{:S(2)}, u32[]{:S(2)}) collective-permute-start(f32[32,384]{1,0:T(8,128)S(1)} %get-tuple-element.136), channel_id=1, source_target_pairs={{0,2},{1,3},{2,4},{3,5},{4,6},{5,7},{6,0},{7,1},{8,10},{9,11},{10,... | collective-permute-start | bytes 147464 | tf_op jit(solution)/shard_map/ppermute | solution.py:742
  83.6 6.6 %collective-permute-start.26 = (f32[32,384]{1,0:T(8,128)S(1)}, f32[32,384]{1,0:T(8,128)S(1)}, u32[]{:S(2)}, u32[]{:S(2)}) collective-permute-start(f32[32,384]{1,0:T(8,128)S(1)} %get-tuple-element.137), channel_id=1, source_target_pairs={{0,4},{1,5},{2,6},{3,7},{4,0},{5,1},{6,2},{7,3},{8,12},{9,13},{10,... | collective-permute-start | bytes 147464 | tf_op jit(solution)/shard_map/ppermute | solution.py:742
  92.5 6.4 %collective-permute-start.32 = (bf16[4,64,1536]{2,1,0:T(8,128)(2,1)S(1)}, bf16[4,64,1536]{2,1,0:T(8,128)(2,1)S(1)}, u32[]{:S(2)}, u32[]{:S(2)}) collective-permute-start(bf16[4,64,1536]{2,1,0:T(8,128)(2,1)S(1)} %get-tuple-element.158), channel_id=1, source_target_pairs={{0,1},{1,0},{2,3},{3,2},{4,5},{5,4},{6,7},{7,6},{8,9},{9,8},{10,11... | collective-permute-start | bytes 2359304 | tf_op jit(solution)/shard_map/ppermute | solution.py:746
  94.3 10.3 %collective-permute-start.28 = (bf16[2,96,768]{2,1,0:T(8,128)(2,1)S(1)}, bf16[2,96,768]{2,1,0:T(8,128)(2,1)S(1)}, u32[]{:S(2)}, u32[]{:S(2)}) collective-permute-start(bf16[2,96,768]{2,1,0:T(8,128)(2,1)S(1)} %get-tuple-element.151), channel_id=1, source_target_pairs={{0,32},{32,64},{64,96},{96,0},{1,33},{33,65},{65,97},{97,1},{2,34}... | collective-permute-start | bytes 884744 | tf_op jit(solution)/shard_map/ppermute | solution.py:738
  94.3 10.3 %collective-permute-start.29 = (bf16[2,96,768]{2,1,0:T(8,128)(2,1)S(1)}, bf16[2,96,768]{2,1,0:T(8,128)(2,1)S(1)}, u32[]{:S(2)}, u32[]{:S(2)}) collective-permute-start(bf16[2,96,768]{2,1,0:T(8,128)(2,1)S(1)} %get-tuple-element.152), channel_id=1, source_target_pairs={{0,96},{32,0},{64,32},{96,64},{1,97},{33,1},{65,33},{97,65},{2,98}... | collective-permute-start | bytes 884744 | tf_op jit(solution)/shard_map/ppermute | solution.py:738
  97.4 7.0 %collective-permute-start.31 = (bf16[2,112,512]{2,1,0:T(8,128)(2,1)S(1)}, bf16[2,112,512]{2,1,0:T(8,128)(2,1)S(1)}, u32[]{:S(2)}, u32[]{:S(2)}) collective-permute-start(bf16[2,112,512]{2,1,0:T(8,128)(2,1)S(1)} %get-tuple-element.156), channel_id=1, source_target_pairs={{0,24},{8,0},{16,8},{24,16},{1,25},{9,1},{17,9},{25,17},{2,26},{10... | collective-permute-start | bytes 688136 | tf_op jit(solution)/shard_map/ppermute | solution.py:738
  97.7 6.7 %collective-permute-start.30 = (bf16[2,96,512]{2,1,0:T(8,128)(2,1)S(1)}, bf16[2,96,512]{2,1,0:T(8,128)(2,1)S(1)}, u32[]{:S(2)}, u32[]{:S(2)}) collective-permute-start(bf16[2,96,512]{2,1,0:T(8,128)(2,1)S(1)} %get-tuple-element.155), channel_id=1, source_target_pairs={{0,8},{8,16},{16,24},{24,0},{1,9},{9,17},{17,25},{25,1},{2,10},{10... | collective-permute-start | bytes 589832 | tf_op jit(solution)/shard_map/ppermute | solution.py:738
  99.6 11.3 %collective-permute-start.35 = (bf16[2,64,1536]{2,1,0:T(8,128)(2,1)S(1)}, bf16[2,64,1536]{2,1,0:T(8,128)(2,1)S(1)}, u32[]{:S(2)}, u32[]{:S(2)}) collective-permute-start(bf16[2,64,1536]{2,1,0:T(8,128)(2,1)S(1)} %get-tuple-element.162), channel_id=1, source_target_pairs={{0,2},{1,3},{2,0},{3,1},{4,6},{5,7},{6,4},{7,5},{8,10},{9,11},{10,... | collective-permute-start | bytes 1179656 | tf_op jit(solution)/shard_map/ppermute | solution.py:746
  105.5 15.7 %collective-permute-start.47 = (bf16[4,96,768]{2,1,0:T(8,128)(2,1)S(1)}, bf16[4,96,768]{2,1,0:T(8,128)(2,1)S(1)}, u32[]{:S(2)}, u32[]{:S(2)}) collective-permute-start(bf16[4,96,768]{2,1,0:T(8,128)(2,1)S(1)} %get-tuple-element.179), channel_id=1, source_target_pairs={{0,32},{32,64},{64,96},{96,0},{1,33},{33,65},{65,97},{97,1},{2,34}... | collective-permute-start | bytes 1769480 | tf_op jit(solution)/shard_map/ppermute | solution.py:738
  106.3 15.9 %collective-permute-start.48 = (bf16[4,96,768]{2,1,0:T(8,128)(2,1)S(1)}, bf16[4,96,768]{2,1,0:T(8,128)(2,1)S(1)}, u32[]{:S(2)}, u32[]{:S(2)}) collective-permute-start(bf16[4,96,768]{2,1,0:T(8,128)(2,1)S(1)} %get-tuple-element.180), channel_id=1, source_target_pairs={{0,96},{32,0},{64,32},{96,64},{1,97},{33,1},{65,33},{97,65},{2,98}... | collective-permute-start | bytes 1769480 | tf_op jit(solution)/shard_map/ppermute | solution.py:738
  108.3 9.7 %collective-permute-start.33 = (bf16[4,96,512]{2,1,0:T(8,128)(2,1)S(1)}, bf16[4,96,512]{2,1,0:T(8,128)(2,1)S(1)}, u32[]{:S(2)}, u32[]{:S(2)}) collective-permute-start(bf16[4,96,512]{2,1,0:T(8,128)(2,1)S(1)} %get-tuple-element.160), channel_id=1, source_target_pairs={{0,8},{8,16},{16,24},{24,0},{1,9},{9,17},{17,25},{25,1},{2,10},{10... | collective-permute-start | bytes 1179656 | tf_op jit(solution)/shard_map/ppermute | solution.py:738
  108.3 9.7 %collective-permute-start.34 = (bf16[4,96,512]{2,1,0:T(8,128)(2,1)S(1)}, bf16[4,96,512]{2,1,0:T(8,128)(2,1)S(1)}, u32[]{:S(2)}, u32[]{:S(2)}) collective-permute-start(bf16[4,96,512]{2,1,0:T(8,128)(2,1)S(1)} %get-tuple-element.161), channel_id=1, source_target_pairs={{0,24},{8,0},{16,8},{24,16},{1,25},{9,1},{17,9},{25,17},{2,26},{10... | collective-permute-start | bytes 1179656 | tf_op jit(solution)/shard_map/ppermute | solution.py:738
  111.6 13.5 %collective-permute-start.39 = (bf16[64,1536]{1,0:T(8,128)(2,1)S(1)}, bf16[64,1536]{1,0:T(8,128)(2,1)S(1)}, u32[]{:S(2)}, u32[]{:S(2)}) collective-permute-start(bf16[64,1536]{1,0:T(8,128)(2,1)S(1)} %get-tuple-element.168), channel_id=1, source_target_pairs={{0,4},{1,5},{2,6},{3,7},{4,0},{5,1},{6,2},{7,3},{8,12},{9,13},{10,... | collective-permute-start | bytes 589832 | tf_op jit(solution)/shard_map/ppermute | solution.py:746
  122.9 8.4 %collective-permute-start.49 = (bf16[96,768]{1,0:T(8,128)(2,1)S(1)}, bf16[96,768]{1,0:T(8,128)(2,1)S(1)}, u32[]{:S(2)}, u32[]{:S(2)}) collective-permute-start(bf16[96,768]{1,0:T(8,128)(2,1)S(1)} %get-tuple-element.182), channel_id=1, source_target_pairs={{0,8},{8,16},{16,24},{24,0},{1,9},{9,17},{17,25},{25,1},{2,10},{10... | collective-permute-start | bytes 442376 | tf_op jit(solution)/shard_map/ppermute | solution.py:738
  126.5 15.3 %collective-permute-start.40 = (bf16[80,1536]{1,0:T(8,128)(2,1)S(1)}, bf16[80,1536]{1,0:T(8,128)(2,1)S(1)}, u32[]{:S(2)}, u32[]{:S(2)}) collective-permute-start(bf16[80,1536]{1,0:T(8,128)(2,1)S(1)} %get-tuple-element.171.refs_1_), channel_id=1, source_target_pairs={{0,2},{1,3},{2,4},{3,5},{4,6},{5,7},{6,0},{7,1},{8,10},{9,11},{10,... | collective-permute-start | bytes 737288 | tf_op jit(solution)/shard_map/ppermute | solution.py:742
  127.2 14.5 %collective-permute-start.41 = (bf16[80,1536]{1,0:T(8,128)(2,1)S(1)}, bf16[80,1536]{1,0:T(8,128)(2,1)S(1)}, u32[]{:S(2)}, u32[]{:S(2)}) collective-permute-start(bf16[80,1536]{1,0:T(8,128)(2,1)S(1)} %get-tuple-element.171.refs_1_), channel_id=1, source_target_pairs={{0,4},{1,5},{2,6},{3,7},{4,0},{5,1},{6,2},{7,3},{8,12},{9,13},{10,... | collective-permute-start | bytes 737288 | tf_op jit(solution)/shard_map/ppermute | solution.py:742
  128.7 13.6 %collective-permute-start.42 = (bf16[80,1536]{1,0:T(8,128)(2,1)S(1)}, bf16[80,1536]{1,0:T(8,128)(2,1)S(1)}, u32[]{:S(2)}, u32[]{:S(2)}) collective-permute-start(bf16[80,1536]{1,0:T(8,128)(2,1)S(1)} %get-tuple-element.171.refs_1_), channel_id=1, source_target_pairs={{0,6},{1,7},{2,0},{3,1},{4,2},{5,3},{6,4},{7,5},{8,14},{9,15},{10,... | collective-permute-start | bytes 737288 | tf_op jit(solution)/shard_map/ppermute | solution.py:742
  131.3 11.0 %collective-permute-start.51 = (bf16[96,768]{1,0:T(8,128)(2,1)S(1)}, bf16[96,768]{1,0:T(8,128)(2,1)S(1)}, u32[]{:S(2)}, u32[]{:S(2)}) collective-permute-start(bf16[96,768]{1,0:T(8,128)(2,1)S(1)} %get-tuple-element.184), channel_id=1, source_target_pairs={{0,24},{8,0},{16,8},{24,16},{1,25},{9,1},{17,9},{25,17},{2,26},{10... | collective-permute-start | bytes 442376 | tf_op jit(solution)/shard_map/ppermute | solution.py:738
  135.3 8.4 %collective-permute-start.43 = (bf16[80,1536]{1,0:T(8,128)(2,1)S(1)}, bf16[80,1536]{1,0:T(8,128)(2,1)S(1)}, u32[]{:S(2)}, u32[]{:S(2)}) collective-permute-start(bf16[80,1536]{1,0:T(8,128)(2,1)S(1)} %get-tuple-element.171.refs_1_), channel_id=1, source_target_pairs={{0,1},{1,0},{2,3},{3,2},{4,5},{5,4},{6,7},{7,6},{8,9},{9,8},{10,11... | collective-permute-start | bytes 737288 | tf_op jit(solution)/shard_map/ppermute | solution.py:746
  (28 other events, 278.6 us)

commit v8 on v7

--- a/solution.py
+++ b/solution.py
@@ -597,10 +597,12 @@
             to_one[near] = one[near]
 
 
-def relay_both(ids, *refs):
-    relay(0, *refs[:4], *refs[9:11])
-    relay(1, *refs[4:8], *refs[11:13])
-    second, behind = refs[7], refs[13]
+def relay_left(ids, *refs):
+    relay(0, *refs)
+
+
+def relay_right(ids, one, three, first, second, left, pair, to_one, to_three, behind):
+    relay(1, one, three, first, second, to_one, to_three)
     inside = jnp.where(ids[0, 1] < 3, 1.0, 0.0)
     for chunk in range(D // RIGHT):
         got = second[chunk // 2, ROWS:].astype(F32) * inside
@@ -958,14 +960,21 @@
     )
     left, right = blocks[:5], blocks[5:]
     near, far = fuse(pair_halves, [two] * 2, ids, keep, across(send, 1))
-    *sides, behind = fuse(
-        relay_both,
-        [stage(4, ROWS, LEFT)] * 2 + [stage(4, ROWS, RIGHT)] * 2 + [((8, D), F32)],
+    sides = fuse(
+        relay_left,
+        [stage(4, ROWS, LEFT)] * 2,
         ids,
         *(left[1], left[4], shift(left[2], "dp", 1), shift(left[3], "dp", 3)),
+    )
+    *others, behind = fuse(
+        relay_right,
+        [stage(4, ROWS, RIGHT)] * 2 + [((8, D), F32)],
+        ids,
         *(right[1], right[4], shift(right[2], "ctx", 1), shift(right[3], "ctx", 3)),
+        sides[0],
         near,
     )
+    sides += others
     left = [left[0], shift(sides[0], "dp", 1), shift(sides[1], "dp", 3)]
     right = [right[0], shift(sides[2], "ctx", 1), shift(sides[3], "ctx", 3)]
     own, second, held, mine, last = fuse(

time: 147 us -> 149 us (1.014)
  waiting for transfers between devices: 32.2 us -> 35.4 us
    ppermute x34, waiting for transfers between devices: 29 us -> 32.4 us  [shift(): return lax.ppermute(array, axis, [(i, (i + steps) % 4) for i in range(4)])]
    pallas_call x21 -> x22, Pallas kernels: 33.2 us -> 33.7 us  [fuse(): return list(call(ids, *arrays))]
  transfers between devices with their start and end apart: 52 -> 52, of which waited for: 21 -> 18; matrix products, arithmetic and copies ran while one was open for 2% -> 2% of each run, Pallas kernels for 13% -> 13%
where the time goes in v8:
time: 149 us
  starting transfers between devices  75.1 us (50%)
  waiting for transfers between devices  35.4 us (24%)
  Pallas kernels  33.7 us (23%)
  other arithmetic  1.86 us (1%)
  local copies, waits for them, and re-layouts  1.81 us (1%)
    ppermute x34, starting transfers between devices, shift(): return lax.ppermute(array, axis, [(i, (i + steps) % 4) for i in range(4)])  43.3 us
    pallas_call x22, Pallas kernels, fuse(): return list(call(ids, *arrays))  33.7 us
    ppermute x34, waiting for transfers between devices, shift(): return lax.ppermute(array, axis, [(i, (i + steps) % 4) for i in range(4)])  32.4 us
    ppermute x9, starting transfers between devices, across(): return lax.ppermute(array, 'tp', [(i, i ^ bits) for i in range(8)])  20.1 us
    ppermute x9, starting transfers between devices, from_chip(): lax.ppermute(array, 'tp', [(i, (i + 2 * steps) % 8) for i in range(8)])  11.7 us
  transfers between devices with their start and end apart: 52, of which 18 were waited for; matrix products, arithmetic and copies ran while one was open for 2% of the time, Pallas kernels for 13%

profile of v8, /device:TPU:1, one launch (start us, length us, event | category | flops | bytes accessed | tf_op | source)
XLA Modules:
  0.0 148.9 jit_solution(3742328634137775745)
XLA Ops:
  0.7 1.8 %prepare.1 = (bf16[96,768]{1,0:T(8,128)(2,1)S(1)}, bf16[112,768]{1,0:T(8,128)(2,1)S(1)}, bf16[96,768]{1,0:T(8,128)(2,1)S(1)}) custom-call(s32[1,3]{1,0:T(1,128)S(1)} %add_bitcast_fusion.refs_0_, bf16[96,384]{1,0:T(8,128)(2,1)} %refs_1_.2, bf16[96,384]{1,0:T(8,128)(2,1)} %refs_2_.2, bf16[96,256]{1,0:T(8,128)(2,1)} %refs_3_.1, bf16[6,96]{1,0:T(8,128)(2,1)} %bitcast.29, ...), custom_call_target="tpu_custom_call" | custom-call | tf_op jit(solution)/shard_map/prepare/pallas_call | solution.py:99
  2.6 2.5 %collective-permute-start.3 = (bf16[96,768]{1,0:T(8,128)(2,1)S(1)}, bf16[96,768]{1,0:T(8,128)(2,1)S(1)}, u32[]{:S(2)}, u32[]{:S(2)}) collective-permute-start(bf16[96,768]{1,0:T(8,128)(2,1)S(1)} %get-tuple-element.109.refs_5_), channel_id=1, source_target_pairs={{0,32},{32,64},{64,96},{96,0},{1,33},{33,65},{65,97},{97,1},{2,34}... | collective-permute-start | bytes 442376 | tf_op jit(solution)/shard_map/ppermute | solution.py:740
  6.4 3.3 %collective-permute-start.4 = (bf16[96,768]{1,0:T(8,128)(2,1)S(1)}, bf16[96,768]{1,0:T(8,128)(2,1)S(1)}, u32[]{:S(2)}, u32[]{:S(2)}) collective-permute-start(bf16[96,768]{1,0:T(8,128)(2,1)S(1)} %get-tuple-element.109.refs_5_), channel_id=1, source_target_pairs={{0,64},{32,96},{64,0},{96,32},{1,65},{33,97},{65,1},{97,33},{2,66}... | collective-permute-start | bytes 442376 | tf_op jit(solution)/shard_map/ppermute | solution.py:740
  10.5 2.7 %collective-permute-start.1 = (bf16[96,768]{1,0:T(8,128)(2,1)S(1)}, bf16[96,768]{1,0:T(8,128)(2,1)S(1)}, u32[]{:S(2)}, u32[]{:S(2)}) collective-permute-start(bf16[96,768]{1,0:T(8,128)(2,1)S(1)} %get-tuple-element.107.refs_1_), channel_id=1, source_target_pairs={{0,16},{8,24},{16,0},{24,8},{1,17},{9,25},{17,1},{25,9},{2,18},{10... | collective-permute-start | bytes 442376 | tf_op jit(solution)/shard_map/ppermute | solution.py:740
  16.1 2.6 %collective-permute-done.2.refs_4_ = bf16[96,768]{1,0:T(8,128)(2,1)S(1)} collective-permute-done((bf16[96,768]{1,0:T(8,128)(2,1)S(1)}, bf16[96,768]{1,0:T(8,128)(2,1)S(1)}, u32[]{:S(2)}, u32[]{:S(2)}) %collective-permute-start.2) | collective-permute-done | bytes 147488 | tf_op jit(solution)/shard_map/ppermute | solution.py:740
  22.9 1.9 %collective-permute-start.8 = (bf16[4,96,768]{2,1,0:T(8,128)(2,1)S(1)}, bf16[4,96,768]{2,1,0:T(8,128)(2,1)S(1)}, u32[]{:S(2)}, u32[]{:S(2)}) collective-permute-start(bf16[4,96,768]{2,1,0:T(8,128)(2,1)S(1)} %get-tuple-element.110.refs_1_), channel_id=1, source_target_pairs={{0,96},{32,0},{64,32},{96,64},{1,97},{33,1},{65,33},{97,65},{2,98}... | collective-permute-start | bytes 1769480 | tf_op jit(solution)/shard_map/ppermute | solution.py:740
  24.8 8.2 %collective-permute-done.10.refs_7_ = bf16[4,96,768]{2,1,0:T(8,128)(2,1)S(1)} collective-permute-done((bf16[4,96,768]{2,1,0:T(8,128)(2,1)S(1)}, bf16[4,96,768]{2,1,0:T(8,128)(2,1)S(1)}, u32[]{:S(2)}, u32[]{:S(2)}) %collective-permute-start.10) | collective-permute-done | bytes 589856 | tf_op jit(solution)/shard_map/ppermute | solution.py:740
  33.2 2.7 %collective-permute-start.13 = (bf16[2,96,768]{2,1,0:T(8,128)(2,1)S(1)}, bf16[2,96,768]{2,1,0:T(8,128)(2,1)S(1)}, u32[]{:S(2)}, u32[]{:S(2)}) collective-permute-start(bf16[2,96,768]{2,1,0:T(8,128)(2,1)S(1)} %slice.19), channel_id=1, source_target_pairs={{0,24},{8,0},{16,8},{24,16},{1,25},{9,1},{17,9},{25,17},{2,26},{10... | collective-permute-start | bytes 884744 | tf_op jit(solution)/shard_map/ppermute | solution.py:740
  36.8 2.0 %collective-permute-start.9 = (bf16[2,96,768]{2,1,0:T(8,128)(2,1)S(1)}, bf16[2,96,768]{2,1,0:T(8,128)(2,1)S(1)}, u32[]{:S(2)}, u32[]{:S(2)}) collective-permute-start(bf16[2,96,768]{2,1,0:T(8,128)(2,1)S(1)} %slice.17), channel_id=1, source_target_pairs={{0,96},{32,0},{64,32},{96,64},{1,97},{33,1},{65,33},{97,65},{2,98}... | collective-permute-start | bytes 884744 | tf_op jit(solution)/shard_map/ppermute | solution.py:740
  41.1 2.1 %tabulate.1 = (f32[16,768]{1,0:T(8,128)S(1)}, f32[256,1536]{1,0:T(8,128)S(1)}) custom-call(s32[1,3]{1,0:T(1,128)S(1)} %add_bitcast_fusion.refs_0_, bf16[4,384]{1,0:T(4,128)(2,1)} %refs_1_.3, bf16[4,256]{1,0:T(4,128)(2,1)} %refs_2_.3, bf16[1,384]{1,0:T(2,128)(2,1)} %broadcast_in_dim.19.refs_3_, bf16[1,256]{1,0:T(2,128)(2,1)} %broadcast_in_dim.20.refs_4_, ...), custom_call_target="tpu_custom_call" | custom-call | tf_op jit(solution)/shard_map/tabulate/pallas_call | solution.py:99
  43.2 2.9 %enter.1 = (bf16[1536,768]{1,0:T(8,128)(2,1)S(1)}, bf16[272,1536]{1,0:T(8,128)(2,1)S(1)}, bf16[272,640]{1,0:T(8,128)(2,1)S(1)}, f32[256,1408]{1,0:T(8,128)S(1)},...) custom-call(s32[1,3]{1,0:T(1,128)S(1)} %add_bitcast_fusion.refs_0_, ...), custom_call_target="tpu_custom_call" | custom-call | tf_op jit(solution)/shard_map/enter/pallas_call | solution.py:99
  46.2 2.3 %collective-permute-start.15 = (bf16[144,384]{1,0:T(8,128)(2,1)S(1)}, bf16[144,384]{1,0:T(8,128)(2,1)S(1)}, u32[]{:S(2)}, u32[]{:S(2)}) collective-permute-start(bf16[144,384]{1,0:T(8,128)(2,1)S(1)} %get-tuple-element.115), channel_id=1, source_target_pairs={{0,16},{8,24},{16,0},{24,8},{1,17},{9,25},{17,1},{25,9},{2,18},{10... | collective-permute-start | bytes 331784 | tf_op jit(solution)/shard_map/ppermute | solution.py:740
  48.9 2.4 %project.1 = (bf16[1536,768]{1,0:T(8,128)(2,1)S(1)}, f32[256,2304]{1,0:T(8,128)S(1)}, f32[256,640]{1,0:T(8,128)S(1)}, f32[256,1152]{1,0:T(8,128)S(1)}) custom-call(s32[1,3]{1,0:T(1,128)S(1)} %add_bitcast_fusion.refs_0_, bf16[4,96,768]{2,1,0:T(8,128)(2,1)S(1)} %get-tuple-element.110.refs_1_, bf16[4,96,768]{2,1,0:T(8,128)(2,1)S(1)} %collective-permute-done.6.refs_2_, ...), custom_call_target="tpu_custom_call" | custom-call | tf_op jit(solution)/shard_map/project/pallas_call | solution.py:99
  53.9 6.0 %collective-permute-start.17 = (f32[8,256]{1,0:T(8,128)S(1)}, f32[8,256]{1,0:T(8,128)S(1)}, u32[]{:S(2)}, u32[]{:S(2)}) collective-permute-start(f32[8,256]{1,0:T(8,128)S(1)} %get-tuple-element.121), channel_id=1, source_target_pairs={{0,1},{1,0},{2,3},{3,2},{4,5},{5,4},{6,7},{7,6},{8,9},{9,8},{10,11... | collective-permute-start | bytes 24584 | tf_op jit(solution)/shard_map/ppermute | solution.py:748
  61.9 2.4 %collective-permute-start.19 = (f32[8,256]{1,0:T(8,128)S(1)}, f32[8,256]{1,0:T(8,128)S(1)}, u32[]{:S(2)}, u32[]{:S(2)}) collective-permute-start(f32[8,256]{1,0:T(8,128)S(1)} %add.3.refs_1_), channel_id=1, source_target_pairs={{0,4},{1,5},{2,6},{3,7},{4,0},{5,1},{6,2},{7,3},{8,12},{9,13},{10,... | collective-permute-start | bytes 24584 | tf_op jit(solution)/shard_map/ppermute | solution.py:744
  68.4 2.2 %collective-permute-start.21 = (bf16[128,384]{1,0:T(8,128)(2,1)S(1)}, bf16[128,384]{1,0:T(8,128)(2,1)S(1)}, u32[]{:S(2)}, u32[]{:S(2)}) collective-permute-start(bf16[128,384]{1,0:T(8,128)(2,1)S(1)} %get-tuple-element.123), channel_id=1, source_target_pairs={{0,24},{8,0},{16,8},{24,16},{1,25},{9,1},{17,9},{25,17},{2,26},{10... | collective-permute-start | bytes 294920 | tf_op jit(solution)/shard_map/ppermute | solution.py:740
  71.3 3.6 %middle.1 = (bf16[1536,384]{1,0:T(8,128)(2,1)S(1)}, bf16[1536,384]{1,0:T(8,128)(2,1)S(1)}, f32[256,640]{1,0:T(8,128)S(1)}, bf16[256,1536]{1,0:T(8,128)(2,1)S(1)}, f32[256,256]{1,0:T(8,128)S(1)}) custom-call(s32[1,3]{1,0:T(1,128)S(1)} %add_bitcast_fusion.refs_0_, bf16[272,1536]{1,0:T(8,128)(2,1)S(1)} %get-tuple-element.116.refs_11_.refs_1_.refs_6_.refs_10_, ...), custom_call_target="tpu_custom_call" | custom-call | tf_op jit(solution)/shard_map/middle/pallas_call | solution.py:99
  76.5 2.0 %leave.1 = (bf16[272,512]{1,0:T(8,128)(2,1)S(1)}, f32[272,256]{1,0:T(8,128)S(1)}, f32[4,32,384]{2,1,0:T(8,128)S(1)}, f32[4,32,384]{2,1,0:T(8,128)S(1)}, f32[8,384]{1,0:T(8,128)S(1)}) custom-call(s32[1,3]{1,0:T(1,128)S(1)} %add_bitcast_fusion.refs_0_, bf16[128,384]{1,0:T(8,128)(2,1)S(1)} %collective-permute-done.21.refs_1_, ...), custom_call_target="tpu_custom_call" | custom-call | tf_op jit(solution)/shard_map/leave/pallas_call | solution.py:99
  78.5 3.4 %collective-permute-start.24 = (f32[4,32,384]{2,1,0:T(8,128)S(1)}, f32[4,32,384]{2,1,0:T(8,128)S(1)}, u32[]{:S(2)}, u32[]{:S(2)}) collective-permute-start(f32[4,32,384]{2,1,0:T(8,128)S(1)} %get-tuple-element.134), channel_id=1, source_target_pairs={{0,1},{1,0},{2,3},{3,2},{4,5},{5,4},{6,7},{7,6},{8,9},{9,8},{10,11... | collective-permute-start | bytes 589832 | tf_op jit(solution)/shard_map/ppermute | solution.py:748
  83.6 3.5 %collective-permute-start.26 = (f32[32,384]{1,0:T(8,128)S(1)}, f32[32,384]{1,0:T(8,128)S(1)}, u32[]{:S(2)}, u32[]{:S(2)}) collective-permute-start(f32[32,384]{1,0:T(8,128)S(1)} %get-tuple-element.137), channel_id=1, source_target_pairs={{0,4},{1,5},{2,6},{3,7},{4,0},{5,1},{6,2},{7,3},{8,12},{9,13},{10,... | collective-permute-start | bytes 147464 | tf_op jit(solution)/shard_map/ppermute | solution.py:744
  87.2 3.0 %value_grads.1 = (bf16[1536,384]{1,0:T(8,128)(2,1)S(1)}, f32[272,1536]{1,0:T(8,128)S(1)}) custom-call(s32[1,3]{1,0:T(1,128)S(1)} %add_bitcast_fusion.refs_0_, bf16[272,512]{1,0:T(8,128)(2,1)S(1)} %get-tuple-element.139.refs_1_.refs_5_, f32[272,256]{1,0:T(8,128)S(1)} %get-tuple-element.141.refs_2_, bf16[256,768]{1,0:T(8,128)(2,1)S(1)} %get-tuple-element.125.refs_2_.refs_3_, ...), custom_call_target="tpu_custom_call" | custom-call | tf_op jit(solution)/shard_map/value_grads/pallas_call | solution.py:99
  90.4 2.0 %late_grads.1 = (bf16[4,64,1536]{2,1,0:T(8,128)(2,1)S(1)}, bf16[4,64,1536]{2,1,0:T(8,128)(2,1)S(1)}, bf16[4,96,768]{2,1,0:T(8,128)(2,1)S(1)}, bf16[4,96,768]{2,1...) custom-call(s32[1,3]{1,0:T(1,128)S(1)} %add_bitcast_fusion.refs_0_, ...), custom_call_target="tpu_custom_call" | custom-call | tf_op jit(solution)/shard_map/late_grads/pallas_call | solution.py:99
  92.5 1.9 %collective-permute-start.32 = (bf16[4,64,1536]{2,1,0:T(8,128)(2,1)S(1)}, bf16[4,64,1536]{2,1,0:T(8,128)(2,1)S(1)}, u32[]{:S(2)}, u32[]{:S(2)}) collective-permute-start(bf16[4,64,1536]{2,1,0:T(8,128)(2,1)S(1)} %get-tuple-element.159), channel_id=1, source_target_pairs={{0,1},{1,0},{2,3},{3,2},{4,5},{5,4},{6,7},{7,6},{8,9},{9,8},{10,11... | collective-permute-start | bytes 2359304 | tf_op jit(solution)/shard_map/ppermute | solution.py:748
  94.3 3.0 %collective-permute-start.31 = (bf16[2,96,768]{2,1,0:T(8,128)(2,1)S(1)}, bf16[2,96,768]{2,1,0:T(8,128)(2,1)S(1)}, u32[]{:S(2)}, u32[]{:S(2)}) collective-permute-start(bf16[2,96,768]{2,1,0:T(8,128)(2,1)S(1)} %get-tuple-element.156), channel_id=1, source_target_pairs={{0,96},{32,0},{64,32},{96,64},{1,97},{33,1},{65,33},{97,65},{2,98}... | collective-permute-start | bytes 884744 | tf_op jit(solution)/shard_map/ppermute | solution.py:740
  100.4 4.3 %collective-permute-done.30.refs_3_ = bf16[2,96,768]{2,1,0:T(8,128)(2,1)S(1)} collective-permute-done((bf16[2,96,768]{2,1,0:T(8,128)(2,1)S(1)}, bf16[2,96,768]{2,1,0:T(8,128)(2,1)S(1)}, u32[]{:S(2)}, u32[]{:S(2)}) %collective-permute-start.30) | collective-permute-done | bytes 294944 | tf_op jit(solution)/shard_map/ppermute | solution.py:740
  106.1 2.0 %collective-permute-start.48 = (bf16[4,96,768]{2,1,0:T(8,128)(2,1)S(1)}, bf16[4,96,768]{2,1,0:T(8,128)(2,1)S(1)}, u32[]{:S(2)}, u32[]{:S(2)}) collective-permute-start(bf16[4,96,768]{2,1,0:T(8,128)(2,1)S(1)} %get-tuple-element.180), channel_id=1, source_target_pairs={{0,96},{32,0},{64,32},{96,64},{1,97},{33,1},{65,33},{97,65},{2,98}... | collective-permute-start | bytes 1769480 | tf_op jit(solution)/shard_map/ppermute | solution.py:740
  108.9 2.7 %collective-permute-start.34 = (bf16[4,96,512]{2,1,0:T(8,128)(2,1)S(1)}, bf16[4,96,512]{2,1,0:T(8,128)(2,1)S(1)}, u32[]{:S(2)}, u32[]{:S(2)}) collective-permute-start(bf16[4,96,512]{2,1,0:T(8,128)(2,1)S(1)} %get-tuple-element.162), channel_id=1, source_target_pairs={{0,24},{8,0},{16,8},{24,16},{1,25},{9,1},{17,9},{25,17},{2,26},{10... | collective-permute-start | bytes 1179656 | tf_op jit(solution)/shard_map/ppermute | solution.py:740
  113.5 5.9 %collective-permute-done.33.refs_2_ = bf16[4,96,512]{2,1,0:T(8,128)(2,1)S(1)} collective-permute-done((bf16[4,96,512]{2,1,0:T(8,128)(2,1)S(1)}, bf16[4,96,512]{2,1,0:T(8,128)(2,1)S(1)}, u32[]{:S(2)}, u32[]{:S(2)}) %collective-permute-start.33) | collective-permute-done | bytes 393248 | tf_op jit(solution)/shard_map/ppermute | solution.py:740
  123.8 2.2 %collective-permute-done.36.refs_2_.refs_6_ = bf16[96,512]{1,0:T(8,128)(2,1)S(1)} collective-permute-done((bf16[96,512]{1,0:T(8,128)(2,1)S(1)}, bf16[96,512]{1,0:T(8,128)(2,1)S(1)}, u32[]{:S(2)}, u32[]{:S(2)}) %collective-permute-start.36) | collective-permute-done | bytes 98336 | tf_op jit(solution)/shard_map/ppermute | solution.py:740
  133.8 3.4 %collective-permute-done.50.refs_3_ = bf16[96,768]{1,0:T(8,128)(2,1)S(1)} collective-permute-done((bf16[96,768]{1,0:T(8,128)(2,1)S(1)}, bf16[96,768]{1,0:T(8,128)(2,1)S(1)}, u32[]{:S(2)}, u32[]{:S(2)}) %collective-permute-start.50) | collective-permute-done | bytes 147488 | tf_op jit(solution)/shard_map/ppermute | solution.py:740
  137.1 5.2 %collective-permute-start.43 = (bf16[80,1536]{1,0:T(8,128)(2,1)S(1)}, bf16[80,1536]{1,0:T(8,128)(2,1)S(1)}, u32[]{:S(2)}, u32[]{:S(2)}) collective-permute-start(bf16[80,1536]{1,0:T(8,128)(2,1)S(1)} %get-tuple-element.172.refs_1_), channel_id=1, source_target_pairs={{0,1},{1,0},{2,3},{3,2},{4,5},{5,4},{6,7},{7,6},{8,9},{9,8},{10,11... | collective-permute-start | bytes 737288 | tf_op jit(solution)/shard_map/ppermute | solution.py:748
  146.4 2.5 %finish.1 = (f32[256,1536]{1,0:T(8,128)}, bf16[256,1536]{1,0:T(8,128)(2,1)}, f32[96,256]{1,0:T(8,128)}, f32[1,96]{1,0:T(1,128)}, f32[4,256]{1,0:T(4,128)}, /*index=5*/f32[1,256]{1,0:T(1,128)}) custom-call(s32[1,3]{1,0:T(1,128)S(1)} %add_bitcast_fusion.refs_0_, bf16[80,1536]{1,0:T(8,128)(2,1)S(1)} %get-tuple-element.172.refs_1_, ...), custom_call_target="tpu_custom_call" | custom-call | tf_op jit(solution)/shard_map/finish/pallas_call | solution.py:99
  (122 shorter events, 49.0 us)
Async XLA Ops:
  2.6 10.6 %collective-permute-start.3 = (bf16[96,768]{1,0:T(8,128)(2,1)S(1)}, bf16[96,768]{1,0:T(8,128)(2,1)S(1)}, u32[]{:S(2)}, u32[]{:S(2)}) collective-permute-start(bf16[96,768]{1,0:T(8,128)(2,1)S(1)} %get-tuple-element.109.refs_5_), channel_id=1, source_target_pairs={{0,32},{32,64},{64,96},{96,0},{1,33},{33,65},{65,97},{97,1},{2,34}... | collective-permute-start | bytes 442376 | tf_op jit(solution)/shard_map/ppermute | solution.py:740
  5.1 13.5 %collective-permute-start = (bf16[112,768]{1,0:T(8,128)(2,1)S(1)}, bf16[112,768]{1,0:T(8,128)(2,1)S(1)}, u32[]{:S(2)}, u32[]{:S(2)}) collective-permute-start(bf16[112,768]{1,0:T(8,128)(2,1)S(1)} %get-tuple-element.108), channel_id=1, source_target_pairs={{0,8},{8,16},{16,24},{24,0},{1,9},{9,17},{17,25},{25,1},{2,10},{10... | collective-permute-start | bytes 516104 | tf_op jit(solution)/shard_map/ppermute | solution.py:740
  6.4 8.4 %collective-permute-start.4 = (bf16[96,768]{1,0:T(8,128)(2,1)S(1)}, bf16[96,768]{1,0:T(8,128)(2,1)S(1)}, u32[]{:S(2)}, u32[]{:S(2)}) collective-permute-start(bf16[96,768]{1,0:T(8,128)(2,1)S(1)} %get-tuple-element.109.refs_5_), channel_id=1, source_target_pairs={{0,64},{32,96},{64,0},{96,32},{1,65},{33,97},{65,1},{97,33},{2,66}... | collective-permute-start | bytes 442376 | tf_op jit(solution)/shard_map/ppermute | solution.py:740
  19.3 13.8 %collective-permute-start.10 = (bf16[4,96,768]{2,1,0:T(8,128)(2,1)S(1)}, bf16[4,96,768]{2,1,0:T(8,128)(2,1)S(1)}, u32[]{:S(2)}, u32[]{:S(2)}) collective-permute-start(bf16[4,96,768]{2,1,0:T(8,128)(2,1)S(1)} %get-tuple-element.111.refs_6_), channel_id=1, source_target_pairs={{0,8},{8,16},{16,24},{24,0},{1,9},{9,17},{17,25},{25,1},{2,10},{10... | collective-permute-start | bytes 1769480 | tf_op jit(solution)/shard_map/ppermute | solution.py:740
  20.4 12.7 %collective-permute-start.12 = (bf16[4,96,768]{2,1,0:T(8,128)(2,1)S(1)}, bf16[4,96,768]{2,1,0:T(8,128)(2,1)S(1)}, u32[]{:S(2)}, u32[]{:S(2)}) collective-permute-start(bf16[4,96,768]{2,1,0:T(8,128)(2,1)S(1)} %get-tuple-element.111.refs_6_), channel_id=1, source_target_pairs={{0,24},{8,0},{16,8},{24,16},{1,25},{9,1},{17,9},{25,17},{2,26},{10... | collective-permute-start | bytes 1769480 | tf_op jit(solution)/shard_map/ppermute | solution.py:740
  22.1 13.8 %collective-permute-start.6 = (bf16[4,96,768]{2,1,0:T(8,128)(2,1)S(1)}, bf16[4,96,768]{2,1,0:T(8,128)(2,1)S(1)}, u32[]{:S(2)}, u32[]{:S(2)}) collective-permute-start(bf16[4,96,768]{2,1,0:T(8,128)(2,1)S(1)} %get-tuple-element.110.refs_1_), channel_id=1, source_target_pairs={{0,32},{32,64},{64,96},{96,0},{1,33},{33,65},{65,97},{97,1},{2,34}... | collective-permute-start | bytes 1769480 | tf_op jit(solution)/shard_map/ppermute | solution.py:740
  22.9 13.9 %collective-permute-start.8 = (bf16[4,96,768]{2,1,0:T(8,128)(2,1)S(1)}, bf16[4,96,768]{2,1,0:T(8,128)(2,1)S(1)}, u32[]{:S(2)}, u32[]{:S(2)}) collective-permute-start(bf16[4,96,768]{2,1,0:T(8,128)(2,1)S(1)} %get-tuple-element.110.refs_1_), channel_id=1, source_target_pairs={{0,96},{32,0},{64,32},{96,64},{1,97},{33,1},{65,33},{97,65},{2,98}... | collective-permute-start | bytes 1769480 | tf_op jit(solution)/shard_map/ppermute | solution.py:740
  33.1 10.1 %collective-permute-start.11 = (bf16[2,96,768]{2,1,0:T(8,128)(2,1)S(1)}, bf16[2,96,768]{2,1,0:T(8,128)(2,1)S(1)}, u32[]{:S(2)}, u32[]{:S(2)}) collective-permute-start(bf16[2,96,768]{2,1,0:T(8,128)(2,1)S(1)} %slice.18), channel_id=1, source_target_pairs={{0,8},{8,16},{16,24},{24,0},{1,9},{9,17},{17,25},{25,1},{2,10},{10... | collective-permute-start | bytes 884744 | tf_op jit(solution)/shard_map/ppermute | solution.py:740
  33.2 10.0 %collective-permute-start.13 = (bf16[2,96,768]{2,1,0:T(8,128)(2,1)S(1)}, bf16[2,96,768]{2,1,0:T(8,128)(2,1)S(1)}, u32[]{:S(2)}, u32[]{:S(2)}) collective-permute-start(bf16[2,96,768]{2,1,0:T(8,128)(2,1)S(1)} %slice.19), channel_id=1, source_target_pairs={{0,24},{8,0},{16,8},{24,16},{1,25},{9,1},{17,9},{25,17},{2,26},{10... | collective-permute-start | bytes 884744 | tf_op jit(solution)/shard_map/ppermute | solution.py:740
  35.9 7.3 %collective-permute-start.7 = (bf16[2,96,768]{2,1,0:T(8,128)(2,1)S(1)}, bf16[2,96,768]{2,1,0:T(8,128)(2,1)S(1)}, u32[]{:S(2)}, u32[]{:S(2)}) collective-permute-start(bf16[2,96,768]{2,1,0:T(8,128)(2,1)S(1)} %slice.16), channel_id=1, source_target_pairs={{0,32},{32,64},{64,96},{96,0},{1,33},{33,65},{65,97},{97,1},{2,34}... | collective-permute-start | bytes 884744 | tf_op jit(solution)/shard_map/ppermute | solution.py:740
  36.8 6.4 %collective-permute-start.9 = (bf16[2,96,768]{2,1,0:T(8,128)(2,1)S(1)}, bf16[2,96,768]{2,1,0:T(8,128)(2,1)S(1)}, u32[]{:S(2)}, u32[]{:S(2)}) collective-permute-start(bf16[2,96,768]{2,1,0:T(8,128)(2,1)S(1)} %slice.17), channel_id=1, source_target_pairs={{0,96},{32,0},{64,32},{96,64},{1,97},{33,1},{65,33},{97,65},{2,98}... | collective-permute-start | bytes 884744 | tf_op jit(solution)/shard_map/ppermute | solution.py:740
  46.1 6.1 %collective-permute-start.14 = (bf16[144,384]{1,0:T(8,128)(2,1)S(1)}, bf16[144,384]{1,0:T(8,128)(2,1)S(1)}, u32[]{:S(2)}, u32[]{:S(2)}) collective-permute-start(bf16[144,384]{1,0:T(8,128)(2,1)S(1)} %get-tuple-element.115), channel_id=1, source_target_pairs={{0,8},{8,16},{16,24},{24,0},{1,9},{9,17},{17,25},{25,1},{2,10},{10... | collective-permute-start | bytes 331784 | tf_op jit(solution)/shard_map/ppermute | solution.py:740
  53.9 6.8 %collective-permute-start.17 = (f32[8,256]{1,0:T(8,128)S(1)}, f32[8,256]{1,0:T(8,128)S(1)}, u32[]{:S(2)}, u32[]{:S(2)}) collective-permute-start(f32[8,256]{1,0:T(8,128)S(1)} %get-tuple-element.121), channel_id=1, source_target_pairs={{0,1},{1,0},{2,3},{3,2},{4,5},{5,4},{6,7},{7,6},{8,9},{9,8},{10,11... | collective-permute-start | bytes 24584 | tf_op jit(solution)/shard_map/ppermute | solution.py:748
  68.4 6.6 %collective-permute-start.21 = (bf16[128,384]{1,0:T(8,128)(2,1)S(1)}, bf16[128,384]{1,0:T(8,128)(2,1)S(1)}, u32[]{:S(2)}, u32[]{:S(2)}) collective-permute-start(bf16[128,384]{1,0:T(8,128)(2,1)S(1)} %get-tuple-element.123), channel_id=1, source_target_pairs={{0,24},{8,0},{16,8},{24,16},{1,25},{9,1},{17,9},{25,17},{2,26},{10... | collective-permute-start | bytes 294920 | tf_op jit(solution)/shard_map/ppermute | solution.py:740
  83.6 6.6 %collective-permute-start.25 = (f32[32,384]{1,0:T(8,128)S(1)}, f32[32,384]{1,0:T(8,128)S(1)}, u32[]{:S(2)}, u32[]{:S(2)}) collective-permute-start(f32[32,384]{1,0:T(8,128)S(1)} %get-tuple-element.136), channel_id=1, source_target_pairs={{0,2},{1,3},{2,4},{3,5},{4,6},{5,7},{6,0},{7,1},{8,10},{9,11},{10,... | collective-permute-start | bytes 147464 | tf_op jit(solution)/shard_map/ppermute | solution.py:744
  83.6 6.6 %collective-permute-start.26 = (f32[32,384]{1,0:T(8,128)S(1)}, f32[32,384]{1,0:T(8,128)S(1)}, u32[]{:S(2)}, u32[]{:S(2)}) collective-permute-start(f32[32,384]{1,0:T(8,128)S(1)} %get-tuple-element.137), channel_id=1, source_target_pairs={{0,4},{1,5},{2,6},{3,7},{4,0},{5,1},{6,2},{7,3},{8,12},{9,13},{10,... | collective-permute-start | bytes 147464 | tf_op jit(solution)/shard_map/ppermute | solution.py:744
  94.3 10.3 %collective-permute-start.30 = (bf16[2,96,768]{2,1,0:T(8,128)(2,1)S(1)}, bf16[2,96,768]{2,1,0:T(8,128)(2,1)S(1)}, u32[]{:S(2)}, u32[]{:S(2)}) collective-permute-start(bf16[2,96,768]{2,1,0:T(8,128)(2,1)S(1)} %get-tuple-element.155), channel_id=1, source_target_pairs={{0,32},{32,64},{64,96},{96,0},{1,33},{33,65},{65,97},{97,1},{2,34}... | collective-permute-start | bytes 884744 | tf_op jit(solution)/shard_map/ppermute | solution.py:740
  94.3 10.3 %collective-permute-start.31 = (bf16[2,96,768]{2,1,0:T(8,128)(2,1)S(1)}, bf16[2,96,768]{2,1,0:T(8,128)(2,1)S(1)}, u32[]{:S(2)}, u32[]{:S(2)}) collective-permute-start(bf16[2,96,768]{2,1,0:T(8,128)(2,1)S(1)} %get-tuple-element.156), channel_id=1, source_target_pairs={{0,96},{32,0},{64,32},{96,64},{1,97},{33,1},{65,33},{97,65},{2,98}... | collective-permute-start | bytes 884744 | tf_op jit(solution)/shard_map/ppermute | solution.py:740
  98.1 13.4 %collective-permute-start.35 = (bf16[2,64,1536]{2,1,0:T(8,128)(2,1)S(1)}, bf16[2,64,1536]{2,1,0:T(8,128)(2,1)S(1)}, u32[]{:S(2)}, u32[]{:S(2)}) collective-permute-start(bf16[2,64,1536]{2,1,0:T(8,128)(2,1)S(1)} %get-tuple-element.163), channel_id=1, source_target_pairs={{0,2},{1,3},{2,0},{3,1},{4,6},{5,7},{6,4},{7,5},{8,10},{9,11},{10,... | collective-permute-start | bytes 1179656 | tf_op jit(solution)/shard_map/ppermute | solution.py:748
  98.9 9.2 %collective-permute-start.29 = (bf16[2,112,512]{2,1,0:T(8,128)(2,1)S(1)}, bf16[2,112,512]{2,1,0:T(8,128)(2,1)S(1)}, u32[]{:S(2)}, u32[]{:S(2)}) collective-permute-start(bf16[2,112,512]{2,1,0:T(8,128)(2,1)S(1)} %get-tuple-element.152), channel_id=1, source_target_pairs={{0,24},{8,0},{16,8},{24,16},{1,25},{9,1},{17,9},{25,17},{2,26},{10... | collective-permute-start | bytes 688136 | tf_op jit(solution)/shard_map/ppermute | solution.py:740
  99.2 8.9 %collective-permute-start.28 = (bf16[2,96,512]{2,1,0:T(8,128)(2,1)S(1)}, bf16[2,96,512]{2,1,0:T(8,128)(2,1)S(1)}, u32[]{:S(2)}, u32[]{:S(2)}) collective-permute-start(bf16[2,96,512]{2,1,0:T(8,128)(2,1)S(1)} %get-tuple-element.151), channel_id=1, source_target_pairs={{0,8},{8,16},{16,24},{24,0},{1,9},{9,17},{17,25},{25,1},{2,10},{10... | collective-permute-start | bytes 589832 | tf_op jit(solution)/shard_map/ppermute | solution.py:740
  105.4 16.4 %collective-permute-start.47 = (bf16[4,96,768]{2,1,0:T(8,128)(2,1)S(1)}, bf16[4,96,768]{2,1,0:T(8,128)(2,1)S(1)}, u32[]{:S(2)}, u32[]{:S(2)}) collective-permute-start(bf16[4,96,768]{2,1,0:T(8,128)(2,1)S(1)} %get-tuple-element.157.refs_5_), channel_id=1, source_target_pairs={{0,32},{32,64},{64,96},{96,0},{1,33},{33,65},{65,97},{97,1},{2,34}... | collective-permute-start | bytes 1769480 | tf_op jit(solution)/shard_map/ppermute | solution.py:740
  106.1 16.8 %collective-permute-start.48 = (bf16[4,96,768]{2,1,0:T(8,128)(2,1)S(1)}, bf16[4,96,768]{2,1,0:T(8,128)(2,1)S(1)}, u32[]{:S(2)}, u32[]{:S(2)}) collective-permute-start(bf16[4,96,768]{2,1,0:T(8,128)(2,1)S(1)} %get-tuple-element.180), channel_id=1, source_target_pairs={{0,96},{32,0},{64,32},{96,64},{1,97},{33,1},{65,33},{97,65},{2,98}... | collective-permute-start | bytes 1769480 | tf_op jit(solution)/shard_map/ppermute | solution.py:740
  108.8 10.7 %collective-permute-start.33 = (bf16[4,96,512]{2,1,0:T(8,128)(2,1)S(1)}, bf16[4,96,512]{2,1,0:T(8,128)(2,1)S(1)}, u32[]{:S(2)}, u32[]{:S(2)}) collective-permute-start(bf16[4,96,512]{2,1,0:T(8,128)(2,1)S(1)} %get-tuple-element.161), channel_id=1, source_target_pairs={{0,8},{8,16},{16,24},{24,0},{1,9},{9,17},{17,25},{25,1},{2,10},{10... | collective-permute-start | bytes 1179656 | tf_op jit(solution)/shard_map/ppermute | solution.py:740
  108.9 10.6 %collective-permute-start.34 = (bf16[4,96,512]{2,1,0:T(8,128)(2,1)S(1)}, bf16[4,96,512]{2,1,0:T(8,128)(2,1)S(1)}, u32[]{:S(2)}, u32[]{:S(2)}) collective-permute-start(bf16[4,96,512]{2,1,0:T(8,128)(2,1)S(1)} %get-tuple-element.162), channel_id=1, source_target_pairs={{0,24},{8,0},{16,8},{24,16},{1,25},{9,1},{17,9},{25,17},{2,26},{10... | collective-permute-start | bytes 1179656 | tf_op jit(solution)/shard_map/ppermute | solution.py:740
  112.2 14.7 %collective-permute-start.39 = (bf16[64,1536]{1,0:T(8,128)(2,1)S(1)}, bf16[64,1536]{1,0:T(8,128)(2,1)S(1)}, u32[]{:S(2)}, u32[]{:S(2)}) collective-permute-start(bf16[64,1536]{1,0:T(8,128)(2,1)S(1)} %get-tuple-element.169), channel_id=1, source_target_pairs={{0,4},{1,5},{2,6},{3,7},{4,0},{5,1},{6,2},{7,3},{8,12},{9,13},{10,... | collective-permute-start | bytes 589832 | tf_op jit(solution)/shard_map/ppermute | solution.py:748
  123.7 9.1 %collective-permute-start.49 = (bf16[96,768]{1,0:T(8,128)(2,1)S(1)}, bf16[96,768]{1,0:T(8,128)(2,1)S(1)}, u32[]{:S(2)}, u32[]{:S(2)}) collective-permute-start(bf16[96,768]{1,0:T(8,128)(2,1)S(1)} %get-tuple-element.182), channel_id=1, source_target_pairs={{0,8},{8,16},{16,24},{24,0},{1,9},{9,17},{17,25},{25,1},{2,10},{10... | collective-permute-start | bytes 442376 | tf_op jit(solution)/shard_map/ppermute | solution.py:740
  128.3 14.0 %collective-permute-start.40 = (bf16[80,1536]{1,0:T(8,128)(2,1)S(1)}, bf16[80,1536]{1,0:T(8,128)(2,1)S(1)}, u32[]{:S(2)}, u32[]{:S(2)}) collective-permute-start(bf16[80,1536]{1,0:T(8,128)(2,1)S(1)} %get-tuple-element.172.refs_1_), channel_id=1, source_target_pairs={{0,2},{1,3},{2,4},{3,5},{4,6},{5,7},{6,0},{7,1},{8,10},{9,11},{10,... | collective-permute-start | bytes 737288 | tf_op jit(solution)/shard_map/ppermute | solution.py:744
  129.1 14.1 %collective-permute-start.41 = (bf16[80,1536]{1,0:T(8,128)(2,1)S(1)}, bf16[80,1536]{1,0:T(8,128)(2,1)S(1)}, u32[]{:S(2)}, u32[]{:S(2)}) collective-permute-start(bf16[80,1536]{1,0:T(8,128)(2,1)S(1)} %get-tuple-element.172.refs_1_), channel_id=1, source_target_pairs={{0,4},{1,5},{2,6},{3,7},{4,0},{5,1},{6,2},{7,3},{8,12},{9,13},{10,... | collective-permute-start | bytes 737288 | tf_op jit(solution)/shard_map/ppermute | solution.py:744
  130.5 12.7 %collective-permute-start.42 = (bf16[80,1536]{1,0:T(8,128)(2,1)S(1)}, bf16[80,1536]{1,0:T(8,128)(2,1)S(1)}, u32[]{:S(2)}, u32[]{:S(2)}) collective-permute-start(bf16[80,1536]{1,0:T(8,128)(2,1)S(1)} %get-tuple-element.172.refs_1_), channel_id=1, source_target_pairs={{0,6},{1,7},{2,0},{3,1},{4,2},{5,3},{6,4},{7,5},{8,14},{9,15},{10,... | collective-permute-start | bytes 737288 | tf_op jit(solution)/shard_map/ppermute | solution.py:744
  132.8 11.0 %collective-permute-start.51 = (bf16[96,768]{1,0:T(8,128)(2,1)S(1)}, bf16[96,768]{1,0:T(8,128)(2,1)S(1)}, u32[]{:S(2)}, u32[]{:S(2)}) collective-permute-start(bf16[96,768]{1,0:T(8,128)(2,1)S(1)} %get-tuple-element.184), channel_id=1, source_target_pairs={{0,24},{8,0},{16,8},{24,16},{1,25},{9,1},{17,9},{25,17},{2,26},{10... | collective-permute-start | bytes 442376 | tf_op jit(solution)/shard_map/ppermute | solution.py:740
  137.1 9.2 %collective-permute-start.43 = (bf16[80,1536]{1,0:T(8,128)(2,1)S(1)}, bf16[80,1536]{1,0:T(8,128)(2,1)S(1)}, u32[]{:S(2)}, u32[]{:S(2)}) collective-permute-start(bf16[80,1536]{1,0:T(8,128)(2,1)S(1)} %get-tuple-element.172.refs_1_), channel_id=1, source_target_pairs={{0,1},{1,0},{2,3},{3,2},{4,5},{5,4},{6,7},{7,6},{8,9},{9,8},{10,11... | collective-permute-start | bytes 737288 | tf_op jit(solution)/shard_map/ppermute | solution.py:748
  (28 other events, 285.3 us)
